TPU v7x, 32 devices: a whole 2x2x4 slice. The times are simulated.
32 devices in a mesh: chord: 4 (over x, core), normal: 8 (over z, y).
Axes of the slice: x: 2, y: 2, z: 4, core: 2. Of those that a mesh axis runs over, the one named last changes fastest.
Arguments:
- direct_modes: bfloat16 [16, 5, 64, 128, 256], P(None, None, 'chord', 'normal'), may hold values from -62 to 62
- adjoint_modes: bfloat16 [16, 5, 64, 128, 256], P(None, None, 'chord', 'normal'), may hold values from -5 to 5
- base_flow: float32 [5, 64, 128, 256], P(None, 'chord', 'normal'), may hold values from -5 to 5
- cell_type: int32 [64, 128, 256], P('chord', 'normal'), may hold values from 0 to 2
- mode_pick: int32 [16], replicated, may hold values from 0 to 15, each once
- flux_mix: float32 [3, 5, 5], replicated, may hold values from -2.5 to 2.5
Outputs:
- sensitivity: float32 [5, 64, 128, 256], P(None, 'chord', 'normal')
Inputs may be any that keep to these rules, and one draw needn't show every extreme that they name: `mode_pick`: each mode once.
All inputs are finite; a program needn't handle non-finite values.
Results may differ from a plain program's by a relative error of at most 0.0003.
Values may be sent and summed in bfloat16 or wider, within the bound.
No kernel may reach another device: no remote copies, remote signals or barrier semaphores. Data moves between devices by JAX's collectives and lax.ppermute only.
A program may use at most 256 MiB of HBM per device.

v0:
```python
import jax
import jax.numpy as jnp
from jax import lax
from jax.sharding import PartitionSpec as P


def with_halo(cells, sides, width):
    for axis, dim in sides:
        count = lax.axis_size(axis)
        ends = count - 1
        head = lax.slice_in_dim(cells, 0, width, axis=dim)
        tail = lax.slice_in_dim(cells, cells.shape[dim] - width, cells.shape[dim], axis=dim)
        cells = jnp.concatenate(
            [
                lax.ppermute(tail, axis, [(i, (i + 1) % count) for i in range(ends)]),
                cells,
                lax.ppermute(head, axis, [((i + 1) % count, i) for i in range(ends)]),
            ],
            axis=dim,
        )
    return cells


def mixing(matrix, field_in):
    return jnp.einsum("ij,i...->j...", matrix, field_in, precision=lax.Precision.HIGHEST)


def diff_chord(padded):
    return padded[..., 2:, 1:-1, :] - padded[..., :-2, 1:-1, :]


def diff_normal(padded):
    return padded[..., 1:-1, 2:, :] - padded[..., 1:-1, :-2, :]


def inner_cells(padded):
    return padded[..., 1:-1, 1:-1, :]


def diff_span(field_in):
    return jnp.roll(field_in, -1, -1) - jnp.roll(field_in, 1, -1)


def bilinear_term(left_pad, right_pad, flux_mix):
    summed = jnp.zeros(inner_cells(left_pad).shape, jnp.float32)
    for axis_num, differ in ((0, diff_chord), (1, diff_normal)):
        mixed_adj = mixing(flux_mix[axis_num], right_pad)
        summed = summed + differ(left_pad) * inner_cells(mixed_adj) - differ(left_pad * mixed_adj)
    left_in = inner_cells(left_pad)
    mixed_adj = mixing(flux_mix[2], inner_cells(right_pad))
    return summed + diff_span(left_in) * mixed_adj - diff_span(left_in * mixed_adj)


def cell_weight(cell_type):
    return jnp.where(cell_type == 0, 1.0, jnp.where(cell_type == 1, 0.5, 0.0)).astype(jnp.float32)


def per_device(direct_modes, adjoint_modes, base_flow, cell_type, mode_pick, flux_mix):
    modes_count = direct_modes.shape[0]
    cells_all = direct_modes[0].size * lax.axis_size("chord") * lax.axis_size("normal")
    local_sums = jnp.sum(jnp.square(direct_modes.astype(jnp.float32)), axis=(1, 2, 3, 4))
    energy = lax.psum(local_sums, ("chord", "normal")) / cells_all
    amplitude = lax.rsqrt(energy + 1e-06)
    zeros_field = jnp.zeros(base_flow.shape, jnp.float32)
    direct_pad, adjoint_pad = (
        with_halo(direct_modes, (("chord", 2), ("normal", 3)), 1),
        with_halo(adjoint_modes, (("chord", 2), ("normal", 3)), 1),
    )

    def accumulate(number, summed):
        direct = direct_pad[number].astype(jnp.float32)
        adjoint = adjoint_pad[mode_pick[number]].astype(jnp.float32)
        return summed + amplitude[number] * bilinear_term(direct, adjoint, flux_mix)

    gradient = lax.fori_loop(0, modes_count, accumulate, zeros_field) / modes_count
    weight = cell_weight(cell_type)
    base_pad = with_halo(base_flow, (("chord", 1), ("normal", 2)), 1)

    def transpose_step(field_in):
        weighted = with_halo(weight * field_in, (("chord", 1), ("normal", 2)), 1)
        return bilinear_term(base_pad, weighted, flux_mix)

    once_applied = transpose_step(gradient)
    twice_applied = transpose_step(once_applied)
    return twice_applied


def solution(mesh):
    return jax.shard_map(
        per_device,
        mesh=mesh,
        in_specs=(
            P(None, None, "chord", "normal", None),
            P(None, None, "chord", "normal", None),
            P(None, "chord", "normal", None),
            P("chord", "normal", None),
            P(),
            P(),
        ),
        out_specs=P(None, "chord", "normal", None),
        check_vma=False,
    )
```

profile of v0, /device:TPU:5, one launch (start us, length us, event | category | flops | bytes accessed | tf_op | source)
XLA Modules:
  0.0 909.6 jit_solution(4840779016358689285)
XLA Ops:
  21.3 6.3 multiply_reduce_fusion
  31.0 37.9 %psum.7 = f32[16]{0:T(128)S(1)} all-reduce(f32[16]{0:T(128)S(1)} %multiply_reduce_fusion), channel_id=1, replica_groups=mesh['chord'=4,'normal'=8] {'chord','normal'}, use_global_device_ids=true, to_apply=%region_1.0 | all-reduce | flops 16 | bytes 128 | tf_op jit(solution)/shard_map/psum | solution.py:62
  70.7 4.4 collective-permute-start
  78.0 19.8 %copy_dynamic-update-slice_fusion = bf16[16,5,18,16,256]{4,0,3,2,1:T(8,128)(2,1)} fusion(bf16[16,5,18,16,256]{4,0,3,2,1:T(8,128)(2,1)} %copy_dynamic-update-slice_fusion.4, bf16[16,5,16,16,256]{4,3,2,1,0:T(8,128)(2,1)} %param.9), kind=kLoop, calls=%fused_computation.41 | loop fusion | bytes 20971520
  109.0 19.5 %copy_dynamic-update-slice_fusion.1 = bf16[16,5,18,16,256]{4,0,3,2,1:T(8,128)(2,1)} fusion(bf16[16,5,18,16,256]{4,0,3,2,1:T(8,128)(2,1)} %copy_dynamic-update-slice_fusion.6, bf16[16,5,16,16,256]{4,3,2,1,0:T(8,128)(2,1)} %param.8), kind=kLoop, calls=%fused_computation.42 | loop fusion | bytes 20971520
  137.6 7.8 pad_maximum_fusion.1
  145.4 13.5 %copy.52 = bf16[16,5,18,18,256]{4,1,3,2,0:T(8,128)(2,1)} copy(bf16[16,5,18,18,256]{4,0,3,2,1:T(8,128)(2,1)S(1)} %pad_maximum_fusion.1) | data formatting | bytes 26542080
  159.0 9.9 %collective-permute-done.4 = bf16[16,5,18,1,256]{4,0,3,2,1:T(8,128)(2,1)S(1)} collective-permute-done((bf16[16,5,18,1,256]{4,0,3,2,1:T(8,128)(2,1)S(1)}, bf16[16,5,18,1,256]{4,0,3,2,1:T(8,128)(2,1)S(1)}, u32[]{:S(2)}, u32[]{:S(2)}) %collective-permute-start.4) | collective-permute-done | bytes 737312 | tf_op jit(solution)/shard_map/ppermute | solution.py:15
  170.7 13.6 %copy.51 = bf16[16,5,18,18,256]{4,1,3,2,0:T(8,128)(2,1)} copy(bf16[16,5,18,18,256]{4,0,3,2,1:T(8,128)(2,1)S(1)} %pad_maximum_fusion) | data formatting | bytes 26542080
  184.3 629.3 %while.14 = (s32[]{:T(128)}, f32[5,16,16,256]{3,0,2,1:T(8,128)}, f32[16]{0:T(128)S(1)}, bf16[16,5,18,18,256]{4,1,3,2,0:T(8,128)(2,1)}, s32[16]{0:T(128)S(1)}, /*...) while((s32[]{:T(128)}, f32[5,16,16,256]{3,0,2,1:T(8,128)}, ...), condition=%wide.region_3.4_spmd.clone, body=%wide.region_2.3_spmd.clone.sunk | while | flops 78295040 | bytes 61221592 | solution.py:75
  192.1 4.5 fusion.75
  201.9 7.6 convert_multiply_fusion.3
  210.2 12.8 %fusion.76 = f32[5,16,16,256]{3,0,2,1:T(8,128)} fusion(f32[5,18,18,256]{3,0,2,1:T(8,128)} %get-tuple-element.300, f32[5,18,18,256]{3,0,2,1:T(8,128)} %copy-done, f32[5,18,18,256]{3,0,2,1:T(8,128)S(1)} %bitcast_convert_fusion.2, f32[5,18,18,256]{3,0,2,1:T(8,128)} %get-tuple-element.301, f32[5,18,18,256]{3,0,2,1:T(8,128)} %get-tuple-element.302, ...), kind=kLoop, calls=%fused_computation.6.clone.1 | loop fusion | flops 6881280 | bytes 22282244 | tf_op jit(solution)/shard_map/while/body/eval_jaxpr/add | solution.py:73
  230.9 4.5 fusion.75
  240.7 7.6 convert_multiply_fusion.3
  249.0 13.4 %fusion.76 = f32[5,16,16,256]{3,0,2,1:T(8,128)} fusion(f32[5,18,18,256]{3,0,2,1:T(8,128)} %get-tuple-element.300, f32[5,18,18,256]{3,0,2,1:T(8,128)} %copy-done, f32[5,18,18,256]{3,0,2,1:T(8,128)S(1)} %bitcast_convert_fusion.2, f32[5,18,18,256]{3,0,2,1:T(8,128)} %get-tuple-element.301, f32[5,18,18,256]{3,0,2,1:T(8,128)} %get-tuple-element.302, ...), kind=kLoop, calls=%fused_computation.6.clone.1 | loop fusion | flops 6881280 | bytes 22282244 | tf_op jit(solution)/shard_map/while/body/eval_jaxpr/add | solution.py:73
  270.3 4.5 fusion.75
  280.0 7.6 convert_multiply_fusion.3
  288.3 13.4 %fusion.76 = f32[5,16,16,256]{3,0,2,1:T(8,128)} fusion(f32[5,18,18,256]{3,0,2,1:T(8,128)} %get-tuple-element.300, f32[5,18,18,256]{3,0,2,1:T(8,128)} %copy-done, f32[5,18,18,256]{3,0,2,1:T(8,128)S(1)} %bitcast_convert_fusion.2, f32[5,18,18,256]{3,0,2,1:T(8,128)} %get-tuple-element.301, f32[5,18,18,256]{3,0,2,1:T(8,128)} %get-tuple-element.302, ...), kind=kLoop, calls=%fused_computation.6.clone.1 | loop fusion | flops 6881280 | bytes 22282244 | tf_op jit(solution)/shard_map/while/body/eval_jaxpr/add | solution.py:73
  309.6 4.5 fusion.75
  319.4 7.6 convert_multiply_fusion.3
  327.7 13.4 %fusion.76 = f32[5,16,16,256]{3,0,2,1:T(8,128)} fusion(f32[5,18,18,256]{3,0,2,1:T(8,128)} %get-tuple-element.300, f32[5,18,18,256]{3,0,2,1:T(8,128)} %copy-done, f32[5,18,18,256]{3,0,2,1:T(8,128)S(1)} %bitcast_convert_fusion.2, f32[5,18,18,256]{3,0,2,1:T(8,128)} %get-tuple-element.301, f32[5,18,18,256]{3,0,2,1:T(8,128)} %get-tuple-element.302, ...), kind=kLoop, calls=%fused_computation.6.clone.1 | loop fusion | flops 6881280 | bytes 22282244 | tf_op jit(solution)/shard_map/while/body/eval_jaxpr/add | solution.py:73
  349.0 4.5 fusion.75
  358.8 7.6 convert_multiply_fusion.3
  367.0 13.4 %fusion.76 = f32[5,16,16,256]{3,0,2,1:T(8,128)} fusion(f32[5,18,18,256]{3,0,2,1:T(8,128)} %get-tuple-element.300, f32[5,18,18,256]{3,0,2,1:T(8,128)} %copy-done, f32[5,18,18,256]{3,0,2,1:T(8,128)S(1)} %bitcast_convert_fusion.2, f32[5,18,18,256]{3,0,2,1:T(8,128)} %get-tuple-element.301, f32[5,18,18,256]{3,0,2,1:T(8,128)} %get-tuple-element.302, ...), kind=kLoop, calls=%fused_computation.6.clone.1 | loop fusion | flops 6881280 | bytes 22282244 | tf_op jit(solution)/shard_map/while/body/eval_jaxpr/add | solution.py:73
  388.3 4.5 fusion.75
  398.1 7.6 convert_multiply_fusion.3
  406.4 13.4 %fusion.76 = f32[5,16,16,256]{3,0,2,1:T(8,128)} fusion(f32[5,18,18,256]{3,0,2,1:T(8,128)} %get-tuple-element.300, f32[5,18,18,256]{3,0,2,1:T(8,128)} %copy-done, f32[5,18,18,256]{3,0,2,1:T(8,128)S(1)} %bitcast_convert_fusion.2, f32[5,18,18,256]{3,0,2,1:T(8,128)} %get-tuple-element.301, f32[5,18,18,256]{3,0,2,1:T(8,128)} %get-tuple-element.302, ...), kind=kLoop, calls=%fused_computation.6.clone.1 | loop fusion | flops 6881280 | bytes 22282244 | tf_op jit(solution)/shard_map/while/body/eval_jaxpr/add | solution.py:73
  427.7 4.5 fusion.75
  437.5 7.6 convert_multiply_fusion.3
  445.8 13.4 %fusion.76 = f32[5,16,16,256]{3,0,2,1:T(8,128)} fusion(f32[5,18,18,256]{3,0,2,1:T(8,128)} %get-tuple-element.300, f32[5,18,18,256]{3,0,2,1:T(8,128)} %copy-done, f32[5,18,18,256]{3,0,2,1:T(8,128)S(1)} %bitcast_convert_fusion.2, f32[5,18,18,256]{3,0,2,1:T(8,128)} %get-tuple-element.301, f32[5,18,18,256]{3,0,2,1:T(8,128)} %get-tuple-element.302, ...), kind=kLoop, calls=%fused_computation.6.clone.1 | loop fusion | flops 6881280 | bytes 22282244 | tf_op jit(solution)/shard_map/while/body/eval_jaxpr/add | solution.py:73
  467.1 4.5 fusion.75
  476.8 7.6 convert_multiply_fusion.3
  485.1 13.4 %fusion.76 = f32[5,16,16,256]{3,0,2,1:T(8,128)} fusion(f32[5,18,18,256]{3,0,2,1:T(8,128)} %get-tuple-element.300, f32[5,18,18,256]{3,0,2,1:T(8,128)} %copy-done, f32[5,18,18,256]{3,0,2,1:T(8,128)S(1)} %bitcast_convert_fusion.2, f32[5,18,18,256]{3,0,2,1:T(8,128)} %get-tuple-element.301, f32[5,18,18,256]{3,0,2,1:T(8,128)} %get-tuple-element.302, ...), kind=kLoop, calls=%fused_computation.6.clone.1 | loop fusion | flops 6881280 | bytes 22282244 | tf_op jit(solution)/shard_map/while/body/eval_jaxpr/add | solution.py:73
  506.4 4.5 fusion.75
  516.2 7.6 convert_multiply_fusion.3
  524.5 13.4 %fusion.76 = f32[5,16,16,256]{3,0,2,1:T(8,128)} fusion(f32[5,18,18,256]{3,0,2,1:T(8,128)} %get-tuple-element.300, f32[5,18,18,256]{3,0,2,1:T(8,128)} %copy-done, f32[5,18,18,256]{3,0,2,1:T(8,128)S(1)} %bitcast_convert_fusion.2, f32[5,18,18,256]{3,0,2,1:T(8,128)} %get-tuple-element.301, f32[5,18,18,256]{3,0,2,1:T(8,128)} %get-tuple-element.302, ...), kind=kLoop, calls=%fused_computation.6.clone.1 | loop fusion | flops 6881280 | bytes 22282244 | tf_op jit(solution)/shard_map/while/body/eval_jaxpr/add | solution.py:73
  545.8 4.5 fusion.75
  555.6 7.6 convert_multiply_fusion.3
  563.8 13.4 %fusion.76 = f32[5,16,16,256]{3,0,2,1:T(8,128)} fusion(f32[5,18,18,256]{3,0,2,1:T(8,128)} %get-tuple-element.300, f32[5,18,18,256]{3,0,2,1:T(8,128)} %copy-done, f32[5,18,18,256]{3,0,2,1:T(8,128)S(1)} %bitcast_convert_fusion.2, f32[5,18,18,256]{3,0,2,1:T(8,128)} %get-tuple-element.301, f32[5,18,18,256]{3,0,2,1:T(8,128)} %get-tuple-element.302, ...), kind=kLoop, calls=%fused_computation.6.clone.1 | loop fusion | flops 6881280 | bytes 22282244 | tf_op jit(solution)/shard_map/while/body/eval_jaxpr/add | solution.py:73
  585.1 4.5 fusion.75
  594.9 7.6 convert_multiply_fusion.3
  603.2 13.4 %fusion.76 = f32[5,16,16,256]{3,0,2,1:T(8,128)} fusion(f32[5,18,18,256]{3,0,2,1:T(8,128)} %get-tuple-element.300, f32[5,18,18,256]{3,0,2,1:T(8,128)} %copy-done, f32[5,18,18,256]{3,0,2,1:T(8,128)S(1)} %bitcast_convert_fusion.2, f32[5,18,18,256]{3,0,2,1:T(8,128)} %get-tuple-element.301, f32[5,18,18,256]{3,0,2,1:T(8,128)} %get-tuple-element.302, ...), kind=kLoop, calls=%fused_computation.6.clone.1 | loop fusion | flops 6881280 | bytes 22282244 | tf_op jit(solution)/shard_map/while/body/eval_jaxpr/add | solution.py:73
  624.5 4.5 fusion.75
  634.3 7.6 convert_multiply_fusion.3
  642.6 13.4 %fusion.76 = f32[5,16,16,256]{3,0,2,1:T(8,128)} fusion(f32[5,18,18,256]{3,0,2,1:T(8,128)} %get-tuple-element.300, f32[5,18,18,256]{3,0,2,1:T(8,128)} %copy-done, f32[5,18,18,256]{3,0,2,1:T(8,128)S(1)} %bitcast_convert_fusion.2, f32[5,18,18,256]{3,0,2,1:T(8,128)} %get-tuple-element.301, f32[5,18,18,256]{3,0,2,1:T(8,128)} %get-tuple-element.302, ...), kind=kLoop, calls=%fused_computation.6.clone.1 | loop fusion | flops 6881280 | bytes 22282244 | tf_op jit(solution)/shard_map/while/body/eval_jaxpr/add | solution.py:73
  663.9 4.5 fusion.75
  673.6 7.6 convert_multiply_fusion.3
  681.9 13.4 %fusion.76 = f32[5,16,16,256]{3,0,2,1:T(8,128)} fusion(f32[5,18,18,256]{3,0,2,1:T(8,128)} %get-tuple-element.300, f32[5,18,18,256]{3,0,2,1:T(8,128)} %copy-done, f32[5,18,18,256]{3,0,2,1:T(8,128)S(1)} %bitcast_convert_fusion.2, f32[5,18,18,256]{3,0,2,1:T(8,128)} %get-tuple-element.301, f32[5,18,18,256]{3,0,2,1:T(8,128)} %get-tuple-element.302, ...), kind=kLoop, calls=%fused_computation.6.clone.1 | loop fusion | flops 6881280 | bytes 22282244 | tf_op jit(solution)/shard_map/while/body/eval_jaxpr/add | solution.py:73
  703.2 4.5 fusion.75
  713.0 7.6 convert_multiply_fusion.3
  721.3 13.4 %fusion.76 = f32[5,16,16,256]{3,0,2,1:T(8,128)} fusion(f32[5,18,18,256]{3,0,2,1:T(8,128)} %get-tuple-element.300, f32[5,18,18,256]{3,0,2,1:T(8,128)} %copy-done, f32[5,18,18,256]{3,0,2,1:T(8,128)S(1)} %bitcast_convert_fusion.2, f32[5,18,18,256]{3,0,2,1:T(8,128)} %get-tuple-element.301, f32[5,18,18,256]{3,0,2,1:T(8,128)} %get-tuple-element.302, ...), kind=kLoop, calls=%fused_computation.6.clone.1 | loop fusion | flops 6881280 | bytes 22282244 | tf_op jit(solution)/shard_map/while/body/eval_jaxpr/add | solution.py:73
  742.6 4.5 fusion.75
  752.4 7.6 convert_multiply_fusion.3
  760.6 13.4 %fusion.76 = f32[5,16,16,256]{3,0,2,1:T(8,128)} fusion(f32[5,18,18,256]{3,0,2,1:T(8,128)} %get-tuple-element.300, f32[5,18,18,256]{3,0,2,1:T(8,128)} %copy-done, f32[5,18,18,256]{3,0,2,1:T(8,128)S(1)} %bitcast_convert_fusion.2, f32[5,18,18,256]{3,0,2,1:T(8,128)} %get-tuple-element.301, f32[5,18,18,256]{3,0,2,1:T(8,128)} %get-tuple-element.302, ...), kind=kLoop, calls=%fused_computation.6.clone.1 | loop fusion | flops 6881280 | bytes 22282244 | tf_op jit(solution)/shard_map/while/body/eval_jaxpr/add | solution.py:73
  781.9 4.5 fusion.75
  791.7 7.6 convert_multiply_fusion.3
  800.0 13.4 %fusion.76 = f32[5,16,16,256]{3,0,2,1:T(8,128)} fusion(f32[5,18,18,256]{3,0,2,1:T(8,128)} %get-tuple-element.300, f32[5,18,18,256]{3,0,2,1:T(8,128)} %copy-done, f32[5,18,18,256]{3,0,2,1:T(8,128)S(1)} %bitcast_convert_fusion.2, f32[5,18,18,256]{3,0,2,1:T(8,128)} %get-tuple-element.301, f32[5,18,18,256]{3,0,2,1:T(8,128)} %get-tuple-element.302, ...), kind=kLoop, calls=%fused_computation.6.clone.1 | loop fusion | flops 6881280 | bytes 22282244 | tf_op jit(solution)/shard_map/while/body/eval_jaxpr/add | solution.py:73
  834.5 5.0 collective-permute-start.12
  841.5 4.3 collective-permute-start.14
  852.5 5.4 fusion.40
  858.0 9.5 %fusion.32 = f32[5,16,16,256]{3,0,2,1:T(8,128)S(1)} fusion(f32[5,18,18,256]{3,0,2,1:T(8,128)} %get-tuple-element.210, f32[5,18,18,256]{3,0,2,1:T(8,128)} %copy-done.10, f32[5,18,18,256]{3,0,2,1:T(8,128)} %get-tuple-element.209, f32[5,18,18,256]{3,0,2,1:T(8,128)} %get-tuple-element.240, f32[5,16,16,1]{3,0,2,1:T(8,128)} %get-tuple-element.228, ...), kind=kLoop, calls=%fused_computation.59 | loop fusion | flops 7536640 | bytes 19124224 | tf_op jit(solution)/shard_map/mul | solution.py:80
  893.6 5.5 fusion.38
  899.1 8.6 fusion.26
  (239 shorter events, 297.7 us)
Async XLA Ops:
  0.0 16.0 %copy-start.4 = (f32[5,16,16,256]{3,2,1,0:T(8,128)S(1)}, f32[5,16,16,256]{3,2,1,0:T(8,128)}, u32[]{:S(2)}) copy-start(f32[5,16,16,256]{3,2,1,0:T(8,128)} %param.10) | copy-start | bytes 3932164
  2.3 73.4 %collective-permute-start.6 = (bf16[16,5,1,16,256]{4,3,2,1,0:T(8,128)(2,1)}, bf16[16,5,1,16,256]{4,3,2,1,0:T(8,128)(2,1)}, u32[]{:S(2)}, u32[]{:S(2)}) collective-permute-start(bf16[16,5,1,16,256]{4,3,2,1,0:T(8,128)(2,1)} %get-tuple-element.204), channel_id=1, source_target_pairs={{0,8},{8,16},{16,24},{1,9},{9,17},{17,25},{2,10},{10,18},{18,26},{... | collective-permute-start | bytes 1966088 | tf_op jit(solution)/shard_map/ppermute | solution.py:15
  6.0 91.8 %collective-permute-start.7 = (bf16[16,5,1,16,256]{4,3,2,1,0:T(8,128)(2,1)S(1)}, bf16[16,5,1,16,256]{4,3,2,1,0:T(8,128)(2,1)}, u32[]{:S(2)}, u32[]{:S(2)}) collective-permute-start(bf16[16,5,1,16,256]{4,3,2,1,0:T(8,128)(2,1)S(1)} %get-tuple-element.203), channel_id=1, source_target_pairs={{8,0},{16,8},{24,16},{9,1},{17,9},{25,17},{10,2},{18,10},{26,18},{... | collective-permute-start | bytes 1966088 | tf_op jit(solution)/shard_map/ppermute | solution.py:17
  10.4 96.3 %collective-permute-start.2 = (bf16[16,5,1,16,256]{4,3,2,1,0:T(8,128)(2,1)}, bf16[16,5,1,16,256]{4,3,2,1,0:T(8,128)(2,1)}, u32[]{:S(2)}, u32[]{:S(2)}) collective-permute-start(bf16[16,5,1,16,256]{4,3,2,1,0:T(8,128)(2,1)} %get-tuple-element.206), channel_id=1, source_target_pairs={{0,8},{8,16},{16,24},{1,9},{9,17},{17,25},{2,10},{10,18},{18,26},{... | collective-permute-start | bytes 1966088 | tf_op jit(solution)/shard_map/ppermute | solution.py:15
  14.1 114.4 %collective-permute-start.3 = (bf16[16,5,1,16,256]{4,3,2,1,0:T(8,128)(2,1)}, bf16[16,5,1,16,256]{4,3,2,1,0:T(8,128)(2,1)}, u32[]{:S(2)}, u32[]{:S(2)}) collective-permute-start(bf16[16,5,1,16,256]{4,3,2,1,0:T(8,128)(2,1)} %get-tuple-element.205), channel_id=1, source_target_pairs={{8,0},{16,8},{24,16},{9,1},{17,9},{25,17},{10,2},{18,10},{26,18},{... | collective-permute-start | bytes 1966088 | tf_op jit(solution)/shard_map/ppermute | solution.py:17
  16.9 52.0 %copy-start.1 = (f32[5,16,16,256]{3,0,2,1:T(8,128)}, f32[5,16,16,256]{3,0,2,1:T(8,128)S(1)}, u32[]{:S(2)}) copy-start(f32[5,16,16,256]{3,0,2,1:T(8,128)S(1)} %copy.42) | copy-start | bytes 3932164
  17.6 53.0 %collective-permute-start.1 = (f32[5,1,16,256]{3,0,2,1:T(8,128)S(1)}, f32[5,1,16,256]{3,0,2,1:T(8,128)S(1)}, u32[]{:S(2)}, u32[]{:S(2)}) collective-permute-start(f32[5,1,16,256]{3,0,2,1:T(8,128)S(1)} %get-tuple-element.232), channel_id=1, source_target_pairs={{0,8},{8,16},{16,24},{1,9},{9,17},{17,25},{2,10},{10,18},{18,26},{... | collective-permute-start | bytes 245768 | tf_op jit(solution)/shard_map/ppermute | solution.py:15
  27.5 2.7 copy-start.15
  68.9 1.7 copy-start.16
  70.7 27.1 %copy-start.12 = (f32[5,1,16,256]{3,0,2,1:T(8,128)}, f32[5,1,16,256]{3,0,2,1:T(8,128)S(1)}, u32[]{:S(2)}) copy-start(f32[5,1,16,256]{3,0,2,1:T(8,128)S(1)} %collective-permute-done.1) | copy-start | bytes 245764
  70.7 759.4 %collective-permute-start = (f32[5,1,16,256]{3,0,2,1:T(8,128)}, f32[5,1,16,256]{3,0,2,1:T(8,128)}, u32[]{:S(2)}, u32[]{:S(2)}) collective-permute-start(f32[5,1,16,256]{3,0,2,1:T(8,128)} %get-tuple-element.231), channel_id=1, source_target_pairs={{8,0},{16,8},{24,16},{9,1},{17,9},{25,17},{10,2},{18,10},{26,18},{... | collective-permute-start | bytes 245768 | tf_op jit(solution)/shard_map/ppermute | solution.py:17
  101.4 36.2 %collective-permute-start.8 = (bf16[16,5,18,1,256]{4,0,3,2,1:T(8,128)(2,1)S(1)}, bf16[16,5,18,1,256]{4,0,3,2,1:T(8,128)(2,1)S(1)}, u32[]{:S(2)}, u32[]{:S(2)}) collective-permute-start(bf16[16,5,18,1,256]{4,0,3,2,1:T(8,128)(2,1)S(1)} %get-tuple-element.199), channel_id=1, source_target_pairs={{0,1},{1,2},{2,3},{3,4},{4,5},{5,6},{6,7},{8,9},{9,10},{10,11},{11... | collective-permute-start | bytes 2211848 | tf_op jit(solution)/shard_map/ppermute | solution.py:15
  103.9 33.8 %collective-permute-start.9 = (bf16[16,5,18,1,256]{4,0,3,2,1:T(8,128)(2,1)S(1)}, bf16[16,5,18,1,256]{4,0,3,2,1:T(8,128)(2,1)S(1)}, u32[]{:S(2)}, u32[]{:S(2)}) collective-permute-start(bf16[16,5,18,1,256]{4,0,3,2,1:T(8,128)(2,1)S(1)} %get-tuple-element.200), channel_id=1, source_target_pairs={{1,0},{2,1},{3,2},{4,3},{5,4},{6,5},{7,6},{9,8},{10,9},{11,10},{12... | collective-permute-start | bytes 2211848 | tf_op jit(solution)/shard_map/ppermute | solution.py:17
  132.1 36.8 %collective-permute-start.4 = (bf16[16,5,18,1,256]{4,0,3,2,1:T(8,128)(2,1)S(1)}, bf16[16,5,18,1,256]{4,0,3,2,1:T(8,128)(2,1)S(1)}, u32[]{:S(2)}, u32[]{:S(2)}) collective-permute-start(bf16[16,5,18,1,256]{4,0,3,2,1:T(8,128)(2,1)S(1)} %get-tuple-element.201), channel_id=1, source_target_pairs={{0,1},{1,2},{2,3},{3,4},{4,5},{5,6},{6,7},{8,9},{9,10},{10,11},{11... | collective-permute-start | bytes 2211848 | tf_op jit(solution)/shard_map/ppermute | solution.py:15
  135.4 33.6 %collective-permute-start.5 = (bf16[16,5,18,1,256]{4,0,3,2,1:T(8,128)(2,1)S(1)}, bf16[16,5,18,1,256]{4,0,3,2,1:T(8,128)(2,1)S(1)}, u32[]{:S(2)}, u32[]{:S(2)}) collective-permute-start(bf16[16,5,18,1,256]{4,0,3,2,1:T(8,128)(2,1)S(1)} %get-tuple-element.202), channel_id=1, source_target_pairs={{1,0},{2,1},{3,2},{4,3},{5,4},{6,5},{7,6},{9,8},{10,9},{11,10},{12... | collective-permute-start | bytes 2211848 | tf_op jit(solution)/shard_map/ppermute | solution.py:17
  137.6 31.3 %slice-start = ((s8[11796480]{0:T(1024)(128)(4,1)}), s8[4194304]{0:T(1024)(128)(4,1)S(1)}, s32[]{:S(2)}) async-start(s8[11796480]{0:T(1024)(128)(4,1)} %bitcast.119), calls=%async_computation | async-start | bytes 8388608
  137.6 31.3 %slice-start.1 = ((s8[11796480]{0:T(1024)(128)(4,1)}), s8[4194304]{0:T(1024)(128)(4,1)S(1)}, s32[]{:S(2)}) async-start(s8[11796480]{0:T(1024)(128)(4,1)} %bitcast.119), calls=%async_computation.1 | async-start | bytes 8388608
  145.4 23.5 %slice-start.2 = ((s8[11796480]{0:T(1024)(128)(4,1)}), s8[3407872]{0:T(1024)(128)(4,1)S(1)}, s32[]{:S(2)}) async-start(s8[11796480]{0:T(1024)(128)(4,1)} %bitcast.119), calls=%async_computation.2 | async-start | bytes 6815744
  170.7 13.6 %copy-start.17 = (s32[16]{0:T(128)S(1)}, s32[16]{0:T(128)}, u32[]{:S(2)}) copy-start(s32[16]{0:T(128)} %param.12) | copy-start | bytes 196
  184.3 629.4 %copy-start.14 = (f32[16,16,256]{2,1,0:T(8,128)S(1)}, f32[16,16,256]{2,1,0:T(8,128)}, u32[]{:S(2)}) copy-start(f32[16,16,256]{2,1,0:T(8,128)} %get-tuple-element.238) | copy-start | bytes 786436
  201.9 7.6 copy-start
  240.7 7.6 copy-start
  280.0 7.6 copy-start
  319.4 7.6 copy-start
  358.7 7.6 copy-start
  398.1 7.6 copy-start
  437.5 7.6 copy-start
  476.8 7.6 copy-start
  516.2 7.6 copy-start
  555.5 7.6 copy-start
  594.9 7.6 copy-start
  634.3 7.6 copy-start
  673.6 7.6 copy-start
  713.0 7.6 copy-start
  752.3 7.6 copy-start
  791.7 7.6 copy-start
  813.7 2.3 copy-start.3
  813.7 2.6 copy-start.5
  824.8 6.2 collective-permute-start.10
  828.2 6.3 collective-permute-start.11
  834.5 13.2 %collective-permute-start.12 = (f32[5,18,1,256]{3,0,2,1:T(8,128)S(1)}, f32[5,18,1,256]{3,0,2,1:T(8,128)S(1)}, u32[]{:S(2)}, u32[]{:S(2)}) collective-permute-start(f32[5,18,1,256]{3,0,2,1:T(8,128)S(1)} %get-tuple-element.215), channel_id=1, source_target_pairs={{0,1},{1,2},{2,3},{3,4},{4,5},{5,6},{6,7},{8,9},{9,10},{10,11},{11... | collective-permute-start | bytes 276488 | tf_op jit(solution)/shard_map/ppermute | solution.py:15
  839.5 8.2 collective-permute-start.13
  841.5 8.8 collective-permute-start.14
  845.7 6.8 collective-permute-start.15
  850.2 7.7 copy-start.10
  850.2 7.7 copy-start.2
  850.2 7.7 copy-start.6
  850.2 7.7 copy-start.7
  850.2 7.7 copy-start.8
  850.2 7.7 copy-start.9
  850.2 7.7 copy-start.13
  871.6 8.4 collective-permute-start.16
  875.4 6.3 collective-permute-start.17
  881.7 7.5 collective-permute-start.18
  884.3 6.8 collective-permute-start.19
  893.6 5.5 copy-start.11
where the time goes:
time: 919 us; the launch traced here: 910 us
  other arithmetic  277 us (30%)
  matrix products  247 us (27%)
  local copies, waits for them, and re-layouts  235 us (26%)
  starting transfers between devices  59.2 us (6%)
  blocking collectives  37.9 us (4%)
  loops' own time  32 us (3%)
  waiting for transfers between devices  21.3 us (2%)
    dot_general x54, matrix products, mixing(): jnp.einsum('ij,i...->j...', matrix, field_in, precision=lax.Precision.HIG...  247 us
    add x16, other arithmetic, accumulate(): return summed + amplitude[number] * bilinear_term(direct, adjoint, flux_mix)  214 us
    slice x38, local copies, waits for them, and re-layouts, diff_span(): return jnp.roll(field_in, -1, -1) - jnp.roll(field_in, 1, -1)  127 us
    unnamed x49, local copies, waits for them, and re-layouts  73 us
    psum x1, blocking collectives, per_device(): energy = lax.psum(local_sums, ('chord', 'normal')) / cells_all  37.9 us
    ppermute x10, starting transfers between devices, with_halo(): lax.ppermute(tail, axis, [(i, (i + 1) % count) for i in range(ends)])  35.6 us
    another operation x1, loops' own time, per_device(): lax.fori_loop(0, modes_count, accumulate, zeros_field) / modes_count  32 us
    convert_element_type x16, other arithmetic, accumulate(): direct = direct_pad[number].astype(jnp.float32)  25.6 us
  transfers between devices with their start and end apart: 20, of which 7 were waited for; matrix products, arithmetic and copies ran while one was open for 79% of the time, Pallas kernels for 0%

commit v1 on v0

v1 whole, which is shorter than its diff:
```python
import jax
import jax.numpy as jnp
import numpy as np
from jax import lax
from jax.experimental import pallas as pl
from jax.experimental.pallas import tpu as pltpu
from jax.sharding import PartitionSpec as P

F32 = jnp.float32
BF16 = jnp.bfloat16
VMEM = pltpu.VMEM
SMEM = pltpu.SMEM
LIMIT = 56 * 1024 * 1024


def in_vmem():
    return pl.BlockSpec(memory_space=VMEM)


def in_smem():
    return pl.BlockSpec(memory_space=SMEM)


def sds(shape, dtype):
    return jax.ShapeDtypeStruct(shape, dtype)


def params():
    return pltpu.CompilerParams(vmem_limit_bytes=LIMIT)


def pack_kernel(with_energy, src, xlo, xhi, ylo, yhi, *energy):
    nv, nx, ny, nz = src.shape[1:]
    xlo[0] = src[0, :, 0]
    xhi[0] = src[0, :, nx - 1]
    total = jnp.zeros((ny, nz), F32)
    for i in range(nv):
        cells = src[0, i].astype(F32)
        ylo[0, i] = cells[:, 0, :].astype(BF16)
        yhi[0, i] = cells[:, ny - 1, :].astype(BF16)
        if with_energy:
            total = total + jnp.sum(cells * cells, axis=0)
    if with_energy:
        energy[0][pl.program_id(0)] = jnp.sum(total)


def pack(modes, with_energy):
    nm, nv, nx, ny, nz = modes.shape
    face_x = sds((nm, nv, ny, nz), BF16)
    face_y = sds((nm, nv, nx, nz), BF16)
    spec_x = pl.BlockSpec((1, nv, ny, nz), lambda m: (m, 0, 0, 0))
    spec_y = pl.BlockSpec((1, nv, nx, nz), lambda m: (m, 0, 0, 0))
    return pl.pallas_call(
        lambda *refs: pack_kernel(with_energy, *refs),
        grid=(nm,),
        in_specs=[pl.BlockSpec((1, nv, nx, ny, nz), lambda m: (m, 0, 0, 0, 0))],
        out_specs=[spec_x, spec_x, spec_y, spec_y] + ([in_smem()] if with_energy else []),
        out_shape=[face_x, face_x, face_y, face_y] + ([sds((nm,), F32)] if with_energy else []),
        compiler_params=params(),
        name="pack_direct" if with_energy else "pack_adjoint",
    )(modes)


def faces_kernel(pick, amp, lw, base, *refs):
    u = refs[0:4]
    q = refs[4:8]
    w_out = refs[8:12]
    send = refs[12:16]
    nm, nv = u[0].shape[:2]
    nx, ny, nz = base.shape[1:]
    for f in range(4):
        d = f // 2
        n = u[f].shape[2]
        rows = nv * n

        def body(m, acc):
            qm = q[f][pick[m]].reshape(rows, nz)
            w = jnp.dot(lw[d], jnp.concatenate([qm, qm], axis=0), preferred_element_type=F32)
            w = w * amp[m]
            w_out[f][m] = w
            return acc + u[f][m].reshape(rows, nz).astype(F32) * w

        acc = lax.fori_loop(0, nm, body, jnp.zeros((rows, nz), F32))
        send[f][0:nv] = acc.reshape(nv, n, nz)
    for j in range(nv):
        send[0][nv + j] = base[j, 0]
        send[1][nv + j] = base[j, nx - 1]
        send[2][nv + j] = base[j][:, 0, :]
        send[3][nv + j] = base[j][:, ny - 1, :]


def faces(pick, amp, lw, base, u_faces, q_faces):
    nm, nv = u_faces[0].shape[:2]
    sizes = [f.shape[2] for f in u_faces]
    nz = base.shape[-1]
    return pl.pallas_call(
        faces_kernel,
        in_specs=[in_smem(), in_smem()] + [in_vmem()] * 10,
        out_specs=[in_vmem()] * 8,
        out_shape=[sds((nm, nv * n, nz), F32) for n in sizes] + [sds((2 * nv, n, nz), F32) for n in sizes],
        compiler_params=params(),
        name="faces",
    )(pick, amp, lw, base, *u_faces, *q_faces)


def shift_up(a):
    n = a.shape[0]
    row = lax.broadcasted_iota(jnp.int32, a.shape, 0)
    return jnp.where(row == n - 1, 0.0, pltpu.roll(a, n - 1, 0))


def shift_down(a):
    row = lax.broadcasted_iota(jnp.int32, a.shape, 0)
    return jnp.where(row == 0, 0.0, pltpu.roll(a, 1, 0))


def diff_lanes(a):
    n = a.shape[-1]
    return pltpu.roll(a, n - 1, a.ndim - 1) - pltpu.roll(a, 1, a.ndim - 1)


UNROLL = 4


def main_kernel(pick, amp, lw, ld, rz, um, uc, up, q, h_out, c0_out, acc):
    nm, nv, _, ny, nz = uc.shape
    rows = nv * ny
    acc[...] = jnp.zeros_like(acc)

    def body(step, carry):
        parts = [None] * 4
        for k in range(UNROLL):
            m = step * UNROLL + k
            qm = q[pick[m], :, 0].reshape(rows, nz)
            u = uc[m, :, 0].reshape(rows, nz)
            w = jnp.dot(lw[...], jnp.concatenate([qm, qm], axis=0), preferred_element_type=F32)
            stacked = jnp.concatenate([um[m, :, 0].reshape(rows, nz), up[m, :, 0].reshape(rows, nz), u], axis=0)
            dxy = jnp.dot(ld[0], stacked, preferred_element_type=F32)
            dz = jnp.dot(u, rz[...], preferred_element_type=F32)
            a = amp[m]
            uf = u.astype(F32) * a
            w0, w1, w2 = w[:rows], w[rows : 2 * rows], w[2 * rows :]
            terms = [(dxy[:rows] * w0 + dxy[rows:] * w1 + dz * w2) * a, uf * w0, uf * w1, uf * w2]
            parts = [t if p is None else p + t for p, t in zip(parts, terms)]
        for n in range(4):
            acc[n] += parts[n]
        return carry

    lax.fori_loop(0, nm // UNROLL, body, 0)
    c0_out[:, 0] = acc[1].reshape(nv, ny, nz)
    h = acc[0] - diff_lanes(acc[3])
    for j in range(nv):
        c1 = acc[2, j * ny : (j + 1) * ny]
        h_out[j, 0] = h[j * ny : (j + 1) * ny] - shift_up(c1) + shift_down(c1)


def main(pick, amp, lw, ld, rz, direct, adjoint):
    nm, nv, nx, ny, nz = direct.shape
    rows = nv * ny
    block = (nm, nv, 1, ny, nz)
    out_spec = pl.BlockSpec((nv, 1, ny, nz), lambda p: (0, p, 0, 0))
    whole = lambda shape: pl.BlockSpec(shape, lambda p: (0,) * len(shape))
    return pl.pallas_call(
        main_kernel,
        grid=(nx,),
        in_specs=[
            in_smem(),
            in_smem(),
            whole(lw.shape),
            pl.BlockSpec((1,) + ld.shape[1:], lambda p: (jnp.where(p == 0, 0, jnp.where(p == nx - 1, 2, 1)), 0, 0)),
            whole(rz.shape),
            pl.BlockSpec(block, lambda p: (0, 0, jnp.maximum(p - 1, 0), 0, 0)),
            pl.BlockSpec(block, lambda p: (0, 0, p, 0, 0)),
            pl.BlockSpec(block, lambda p: (0, 0, jnp.minimum(p + 1, nx - 1), 0, 0)),
            pl.BlockSpec(block, lambda p: (0, 0, p, 0, 0)),
        ],
        out_specs=[out_spec, out_spec],
        out_shape=[sds((nv, nx, ny, nz), F32)] * 2,
        scratch_shapes=[pltpu.VMEM((4, rows, nz), F32)],
        compiler_params=params(),
        cost_estimate=pl.CostEstimate(flops=2 * nm * nx * 480 * 256 * 256, bytes_accessed=4 * direct.size * 2, transcendentals=0),
        name="main",
    )(pick, amp, lw, ld, rz, direct, direct, direct, adjoint)


def weight_of(cells):
    return jnp.where(cells == 0, 1.0, jnp.where(cells == 1, 0.5, 0.0)).astype(F32)


def write_faces(values, j, x, nx, outs):
    ny = values.shape[0]
    if x == 0:
        outs[0][j] = values
    if x == nx - 1:
        outs[1][j] = values
    outs[2][j, x : x + 1] = values[0:1]
    outs[3][j, x : x + 1] = values[ny - 1 : ny]


def edge_rows(lo, hi, shape):
    row = lax.broadcasted_iota(jnp.int32, shape, 0)
    return jnp.where(row == 0, lo, 0.0) + jnp.where(row == shape[0] - 1, hi, 0.0)


def boundary_kernel(scale, h, c0, cell, *refs):
    w = refs[0:4]
    u = refs[4:8]
    got = refs[8:12]
    field = refs[12]
    outs = refs[13:17]
    add = refs[17:21]
    nv, nx, ny, nz = h.shape
    nm = u[0].shape[0]
    for f in range(4):
        n = u[f].shape[2]

        def body(m, acc):
            return acc + u[f][m].reshape(nv * n, nz).astype(F32) * w[f][m]

        total = lax.fori_loop(0, nm, body, jnp.zeros((nv * n, nz), F32))
        sign = -1.0 if f % 2 == 0 else 1.0
        add[f][...] = (sign * total).reshape(nv, n, nz) - sign * got[f][0:nv]
    for x in range(nx):
        weight = weight_of(cell[x]) * scale
        for j in range(nv):
            g = h[j, x]
            if x > 0:
                g = g + c0[j, x - 1]
            else:
                g = g + add[0][j]
            if x < nx - 1:
                g = g - c0[j, x + 1]
            else:
                g = g + add[1][j]
            g = g + edge_rows(add[2][j, x : x + 1], add[3][j, x : x + 1], (ny, nz))
            g = g * weight
            field[j, x] = g
            write_faces(g, j, x, nx, outs)


def boundary(scale, h, c0, cell, w_faces, u_halo, got):
    nv, nx, ny, nz = h.shape
    face = [sds((nv, n, nz), F32) for n in (ny, ny, nx, nx)]
    return pl.pallas_call(
        lambda *refs: boundary_kernel(scale, *refs),
        in_specs=[in_vmem()] * 15,
        out_specs=[in_vmem()] * 5,
        out_shape=[sds(h.shape, F32)] + face,
        scratch_shapes=[pltpu.VMEM(f.shape, F32) for f in face],
        compiler_params=params(),
        name="boundary",
    )(h, c0, cell, *w_faces, *u_halo, *got)


def mixed(mix, d, j, values):
    total = mix[d, 0, j] * values[0]
    for i in range(1, len(values)):
        total = total + mix[d, i, j] * values[i]
    return total


def step_kernel(last, mix, base, cell, *refs):
    field = refs[0]
    got_base = refs[1:5]
    got = refs[5:9]
    out = refs[9]
    outs = refs[10:14]
    wx, wyh = refs[-2:]
    nv, nx, ny, nz = base.shape
    for x in range(-1, nx + 1):
        values = [got[0][i] if x < 0 else got[1][i] if x == nx else field[i, x] for i in range(nv)]
        for j in range(nv):
            wx[j, x + 1] = mixed(mix, 0, j, values)
    for s in range(2):
        values = [got[2 + s][i] for i in range(nv)]
        for j in range(nv):
            wyh[s, j] = mixed(mix, 1, j, values)
    row = lax.broadcasted_iota(jnp.int32, (ny, nz), 0)
    for x in range(nx):
        values = [field[i, x] for i in range(nv)]
        weight = None if last else weight_of(cell[x])
        for j in range(nv):
            b = base[j, x]
            w = wx[j, x + 1]
            b_hi = base[j, x + 1] if x < nx - 1 else got_base[1][nv + j]
            b_lo = base[j, x - 1] if x > 0 else got_base[0][nv + j]
            total = b_hi * (w - wx[j, x + 2]) + b_lo * (wx[j, x] - w)
            w = mixed(mix, 1, j, values)
            b_hi = jnp.where(row == ny - 1, got_base[3][nv + j, x : x + 1], pltpu.roll(b, ny - 1, 0))
            b_lo = jnp.where(row == 0, got_base[2][nv + j, x : x + 1], pltpu.roll(b, 1, 0))
            w_hi = jnp.where(row == ny - 1, wyh[1, j, x : x + 1], pltpu.roll(w, ny - 1, 0))
            w_lo = jnp.where(row == 0, wyh[0, j, x : x + 1], pltpu.roll(w, 1, 0))
            total = total + b_hi * (w - w_hi) + b_lo * (w_lo - w)
            w = mixed(mix, 2, j, values)
            flux = w - pltpu.roll(w, nz - 1, 1)
            total = total + pltpu.roll(b, nz - 1, 1) * flux + pltpu.roll(b, 1, 1) * pltpu.roll(flux, 1, 1)
            if not last:
                total = total * weight
                write_faces(total, j, x, nx, outs)
            out[j, x] = total


def apply_step(last, mix, base, cell, field, got_base, got):
    nv, nx, ny, nz = base.shape
    face = [] if last else [sds((nv, n, nz), F32) for n in (ny, ny, nx, nx)]
    return pl.pallas_call(
        lambda *refs: step_kernel(last, *refs),
        in_specs=[in_smem()] + [in_vmem()] * 11,
        out_specs=[in_vmem()] * (1 + len(face)),
        out_shape=[sds(base.shape, F32)] + face,
        scratch_shapes=[pltpu.VMEM((nv, nx + 2, ny, nz), F32), pltpu.VMEM((2, nv, nx, nz), F32)],
        compiler_params=params(),
        name="step_two" if last else "step_one",
    )(mix, base, cell, field, *got_base, *got)


def exchange(arrays):
    out = []
    for k, axis in enumerate(("chord", "normal")):
        count = lax.axis_size(axis)
        up = [(i, i + 1) for i in range(count - 1)]
        down = [(i + 1, i) for i in range(count - 1)]
        out.append(lax.ppermute(arrays[2 * k + 1], axis, up))
        out.append(lax.ppermute(arrays[2 * k], axis, down))
    return out


def kron_rows(mix, ny):
    nv = mix.shape[1]
    hi = lax.reduce_precision(mix, 8, 7)
    lo = lax.reduce_precision(mix - hi, 8, 7)
    both = jnp.stack([hi, lo], axis=1)
    small = both.transpose(0, 3, 1, 2).reshape(3, nv, 2 * nv)
    rows, cols = np.arange(nv * ny), np.arange(2 * nv * ny)
    left = jnp.asarray((rows[:, None] // ny == np.arange(nv)[None]).astype(np.float32))
    right = jnp.asarray((cols[None] // ny == np.arange(2 * nv)[:, None]).astype(np.float32))
    mask = jnp.asarray((rows[:, None] % ny == cols[None] % ny).astype(np.float32))
    wide = jnp.einsum("rj,djc,ck->drk", left, small, right, precision=lax.Precision.HIGHEST)
    return (wide * mask).astype(BF16)


def difference_rows(nv, ny):
    eye = np.eye(nv * ny, dtype=np.float32)
    dy = np.kron(np.eye(nv, dtype=np.float32), np.eye(ny, k=1, dtype=np.float32) - np.eye(ny, k=-1, dtype=np.float32))
    zero = np.zeros_like(eye)
    kinds = []
    for lo, hi in ((0.0, 1.0), (1.0, 1.0), (1.0, 0.0)):
        kinds.append(np.block([[-lo * eye, hi * eye, zero], [zero, zero, dy]]))
    return jnp.asarray(np.stack(kinds), BF16)


def span_difference(nz):
    eye = np.eye(nz, dtype=np.float32)
    return jnp.asarray(np.roll(eye, -1, 1) - np.roll(eye, 1, 1), BF16)


def per_device(direct, adjoint, base, cell, pick, mix):
    nm, nv, nx, ny, nz = direct.shape
    cells_all = nv * nx * ny * nz * lax.axis_size("chord") * lax.axis_size("normal")
    *u_faces, sums = pack(direct, True)
    u_halo = exchange(u_faces)
    energy = lax.psum(sums, ("chord", "normal")) / cells_all
    amp = lax.rsqrt(energy + 1e-06)
    q_faces = pack(adjoint, False)
    lw_y = kron_rows(mix, ny)
    lw_x = lw_y if nx == ny else kron_rows(mix, nx)
    lw_faces = jnp.stack([lw_y[0], lw_x[1]])
    out = faces(pick, amp, lw_faces, base, u_faces, q_faces)
    w_faces, send = out[:4], out[4:]
    got = exchange(send)
    lw = lw_y.reshape(3 * nv * ny, 2 * nv * ny)
    h, c0 = main(pick, amp, lw, difference_rows(nv, ny), span_difference(nz), direct, adjoint)
    field, *sides = boundary(1.0 / nm, h, c0, cell, w_faces, u_halo, got)
    halo = exchange(sides)
    field, *sides = apply_step(False, mix, base, cell, field, got, halo)
    halo = exchange(sides)
    return apply_step(True, mix, base, cell, field, got, halo)[0]


def solution(mesh):
    return jax.shard_map(
        per_device,
        mesh=mesh,
        in_specs=(
            P(None, None, "chord", "normal", None),
            P(None, None, "chord", "normal", None),
            P(None, "chord", "normal", None),
            P("chord", "normal", None),
            P(),
            P(),
        ),
        out_specs=P(None, "chord", "normal", None),
        check_vma=False,
    )
```

time: 919 us -> 204 us (0.22)
  other arithmetic: 277 us -> 0.55 us
  matrix products: 247 us -> 0.62 us
  local copies, waits for them, and re-layouts: 235 us -> 4.09 us
  Pallas kernels: 0 us -> 101 us
  loops' own time: 32 us -> 0 us
  waiting for transfers between devices: 21.3 us -> 8.8 us
  starting transfers between devices: 59.2 us -> 47.1 us
    dot_general x54 -> x2, matrix products: 247 us -> 0.62 us  [kron_rows(): jnp.einsum('rj,djc,ck->drk', left, small, right, precision=lax.Precision....]
    add x16 -> x0, other arithmetic: 214 us -> none  [accumulate(): return summed + amplitude[number] * bilinear_term(direct, adjoint, flux_mix)]
    slice x46 -> x0, local copies, waits for them, and re-layouts: 135 us -> none  [the longest x38 127 us: diff_span(): return jnp.roll(field_in, -1, -1) - jnp.roll(field_in, 1, -1)]
    pallas_call x0 -> x7, Pallas kernels: none -> 101 us  [the longest x1 36.9 us: main(): pl.pallas_call(main_kernel, grid=(nx,), in_specs=[in_smem(), in_smem(), w...]
    unnamed x49 -> x51, local copies, waits for them, and re-layouts: 73 us -> 3.42 us
    another operation x1 -> x0, loops' own time: 32 us -> none  [per_device(): lax.fori_loop(0, modes_count, accumulate, zeros_field) / modes_count]
    convert_element_type x16 -> x0, other arithmetic: 25.6 us -> none  [accumulate(): direct = direct_pad[number].astype(jnp.float32)]
    dynamic_slice x32 -> x0, local copies, waits for them, and re-layouts: 19.8 us -> none  [the longest x16 10.4 us: accumulate(): return summed + amplitude[number] * bilinear_term(direct, adjoint, flux_mix)]
  transfers between devices with their start and end apart: 20 -> 16, of which waited for: 7 -> 3; matrix products, arithmetic and copies ran while one was open for 79% -> 0% of each run, Pallas kernels for 0% -> 18%
where the time goes in v1:
time: 204 us; the launch traced here: 203 us
  Pallas kernels  101 us (50%)
  starting transfers between devices  47.1 us (23%)
  blocking collectives  39.8 us (20%)
  waiting for transfers between devices  8.8 us (4%)
  local copies, waits for them, and re-layouts  4.09 us (2%)
    psum x1, blocking collectives, per_device(): energy = lax.psum(sums, ('chord', 'normal')) / cells_all  39.8 us
    pallas_call x1, Pallas kernels, main(): pl.pallas_call(main_kernel, grid=(nx,), in_specs=[in_smem(), in_smem(), w...  36.9 us
    ppermute x8, starting transfers between devices, exchange(): out.append(lax.ppermute(arrays[2 * k + 1], axis, up))  30.1 us
    pallas_call x2, Pallas kernels, pack(): pl.pallas_call(lambda *refs: pack_kernel(with_energy, *refs), grid=(nm,),...  24.6 us
    pallas_call x2, Pallas kernels, apply_step(): pl.pallas_call(lambda *refs: step_kernel(last, *refs), in_specs=[in_smem(...  17.9 us
    ppermute x8, starting transfers between devices, exchange(): out.append(lax.ppermute(arrays[2 * k], axis, down))  17 us
    pallas_call x1, Pallas kernels, faces(): pl.pallas_call(faces_kernel, in_specs=[in_smem(), in_smem()] + [in_vmem()...  15.3 us
    ppermute x8, waiting for transfers between devices, exchange(): out.append(lax.ppermute(arrays[2 * k], axis, down))  8.35 us
  transfers between devices with their start and end apart: 16, of which 3 were waited for; matrix products, arithmetic and copies ran while one was open for 0% of the time, Pallas kernels for 18%

profile of v1, /device:TPU:5, one launch (start us, length us, event | category | flops | bytes accessed | tf_op | source)
XLA Modules:
  0.0 203.0 jit_solution(18244575045458059768)
XLA Ops:
  0.0 12.8 %pack_direct.1 = (bf16[16,5,16,256]{3,2,1,0:T(8,128)(2,1)}, bf16[16,5,16,256]{3,2,1,0:T(8,128)(2,1)}, bf16[16,5,16,256]{3,2,1,0:T(8,128)(2,1)}, bf16[16,5,16,256]{3,2,1,0:T(8,128)(2,1)}, f32[16]{0:T(128)}) custom-call(bf16[16,5,16,16,256]{4,3,2,1,0:T(8,128)(2,1)} %up.1), custom_call_target="tpu_custom_call" | custom-call | tf_op jit(solution)/shard_map/pack_direct/pallas_call | solution.py:53
  12.8 39.8 %psum.7 = f32[16]{0:T(128)S(1)} all-reduce(f32[16]{0:T(128)} %get-tuple-element.34), channel_id=1, replica_groups=mesh['chord'=4,'normal'=8] {'chord','normal'}, use_global_device_ids=true, to_apply=%region_0.0 | all-reduce | flops 16 | bytes 128 | tf_op jit(solution)/shard_map/psum | solution.py:362
  52.6 0.5 add_rsqrt_fusion.amp
  53.2 11.9 %pack_adjoint.1 = (bf16[16,5,16,256]{3,2,1,0:T(8,128)(2,1)}, bf16[16,5,16,256]{3,2,1,0:T(8,128)(2,1)}, bf16[16,5,16,256]{3,2,1,0:T(8,128)(2,1)}, bf16[16,5,16,256]{3,2,1,0:T(8,128)(2,1)}) custom-call(bf16[16,5,16,16,256]{4,3,2,1,0:T(8,128)(2,1)} %refs_0_.5), custom_call_target="tpu_custom_call" | custom-call | tf_op jit(solution)/shard_map/pack_adjoint/pallas_call | solution.py:53
  65.0 0.0 copy-done.22
  65.1 0.0 copy-done.23
  65.1 0.2 fusion.2
  65.3 0.0 copy-done.13
  65.3 0.0 copy-done.24
  65.3 0.4 fusion.1
  65.7 0.0 copy-start.12
  65.7 0.7 stack.16.lw
  66.4 15.3 %faces.1 = (f32[16,80,256]{2,1,0:T(8,128)}, f32[16,80,256]{2,1,0:T(8,128)}, f32[16,80,256]{2,1,0:T(8,128)}, f32[16,80,256]{2,1,0:T(8,128)}, f32[10,16,256]{2,1,0...) custom-call(s32[16]{0:T(128)} %pick.3, f32[16]{0:T(128)} %add_rsqrt_fusion.amp, ...), custom_call_target="tpu_custom_call" | custom-call | tf_op jit(solution)/shard_map/faces/pallas_call | solution.py:96
  81.7 0.0 copy-done.12
  81.7 4.5 %collective-permute-start.4 = (f32[10,16,256]{2,1,0:T(8,128)}, f32[10,16,256]{2,1,0:T(8,128)S(1)}, u32[]{:S(2)}, u32[]{:S(2)}) collective-permute-start(f32[10,16,256]{2,1,0:T(8,128)} %get-tuple-element.49), channel_id=1, source_target_pairs={{0,8},{8,16},{16,24},{1,9},{9,17},{17,25},{2,10},{10,18},{18,26},{... | collective-permute-start | bytes 491528 | tf_op jit(solution)/shard_map/ppermute | solution.py:323
  86.2 1.9 collective-permute-start.5
  88.1 4.0 %collective-permute-start.6 = (f32[10,16,256]{2,1,0:T(8,128)}, f32[10,16,256]{2,1,0:T(8,128)S(1)}, u32[]{:S(2)}, u32[]{:S(2)}) collective-permute-start(f32[10,16,256]{2,1,0:T(8,128)} %get-tuple-element.51), channel_id=1, source_target_pairs={{0,1},{1,2},{2,3},{3,4},{4,5},{5,6},{6,7},{8,9},{9,10},{10,11},{11... | collective-permute-start | bytes 491528 | tf_op jit(solution)/shard_map/ppermute | solution.py:323
  92.1 0.0 copy-done.11
  92.2 3.9 %collective-permute-start = (bf16[16,5,16,256]{3,2,1,0:T(8,128)(2,1)S(1)}, bf16[16,5,16,256]{3,2,1,0:T(8,128)(2,1)S(1)}, u32[]{:S(2)}, u32[]{:S(2)}) collective-permute-start(bf16[16,5,16,256]{3,2,1,0:T(8,128)(2,1)S(1)} %copy-done.11), channel_id=1, source_target_pairs={{0,8},{8,16},{16,24},{1,9},{9,17},{17,25},{2,10},{10,18},{18,26},{... | collective-permute-start | bytes 1966088 | tf_op jit(solution)/shard_map/ppermute | solution.py:323
  96.1 0.0 copy-done.10
  96.1 1.9 collective-permute-start.1
  98.0 0.0 collective-permute-done.4.refs_11_.refs_4_
  98.0 2.2 %collective-permute-start.2 = (bf16[16,5,16,256]{3,2,1,0:T(8,128)(2,1)S(1)}, bf16[16,5,16,256]{3,2,1,0:T(8,128)(2,1)S(1)}, u32[]{:S(2)}, u32[]{:S(2)}) collective-permute-start(bf16[16,5,16,256]{3,2,1,0:T(8,128)(2,1)S(1)} %copy-done.9), channel_id=1, source_target_pairs={{0,1},{1,2},{2,3},{3,4},{4,5},{5,6},{6,7},{8,9},{9,10},{10,11},{11... | collective-permute-start | bytes 1966088 | tf_op jit(solution)/shard_map/ppermute | solution.py:323
  100.2 0.0 collective-permute-done.5.refs_12_.refs_5_
  100.3 3.1 %collective-permute-start.3 = (bf16[16,5,16,256]{3,2,1,0:T(8,128)(2,1)S(1)}, bf16[16,5,16,256]{3,2,1,0:T(8,128)(2,1)S(1)}, u32[]{:S(2)}, u32[]{:S(2)}) collective-permute-start(bf16[16,5,16,256]{3,2,1,0:T(8,128)(2,1)S(1)} %copy-done.8), channel_id=1, source_target_pairs={{1,0},{2,1},{3,2},{4,3},{5,4},{6,5},{7,6},{9,8},{10,9},{11,10},{12... | collective-permute-start | bytes 1966088 | tf_op jit(solution)/shard_map/ppermute | solution.py:324
  103.4 0.0 collective-permute-done.6.refs_13_.refs_6_
  103.4 1.9 collective-permute-start.7
  105.4 36.9 %main.1 = (f32[5,16,16,256]{3,2,1,0:T(8,128)}, f32[5,16,16,256]{3,2,1,0:T(8,128)}) custom-call(s32[16]{0:T(128)} %pick.3, f32[16]{0:T(128)} %add_rsqrt_fusion.amp, bf16[240,160]{1,0:T(8,128)(2,1)} %bitcast.19, bf16[3,160,240]{2,1,0:T(8,128)(2,1)} %constant.18.clone.ld, bf16[256,256]{1,0:T(8,128)(2,1)} %constant.19.clone.rz, ...), custom_call_target="tpu_custom_call" | custom-call | flops 16106127360 | bytes 41943040 | tf_op jit(solution)/shard_map/main/pallas_call | solution.py:163
  142.2 0.0 copy-done
  142.3 0.0 collective-permute-done.7.refs_14_.refs_7_
  142.3 0.0 collective-permute-done.refs_7_
  142.3 0.0 collective-permute-done.1.refs_8_
  142.3 0.0 copy-start.5
  142.3 0.0 collective-permute-done.2.refs_9_
  142.3 0.0 collective-permute-done.3.refs_10_
  142.4 0.6 copy-done.3
  142.9 0.3 copy-done.4
  143.2 0.3 copy-done.5
  143.5 0.2 copy-done.6
  143.6 0.2 copy-done.7
  143.9 6.8 %boundary.1 = (f32[5,16,16,256]{3,2,1,0:T(8,128)}, f32[5,16,256]{2,1,0:T(8,128)}, f32[5,16,256]{2,1,0:T(8,128)}, f32[5,16,256]{2,1,0:T(8,128)}, f32[5,16,256]{2,1,0:T(8,128)}) custom-call(f32[5,16,16,256]{3,2,1,0:T(8,128)} %get-tuple-element.35.refs_0_, f32[5,16,16,256]{3,2,1,0:T(8,128)} %get-tuple-element.36.refs_1_, s32[16,16,256]{2,1,0:T(8,128)} %refs_2_.5, ...), custom_call_target="tpu_custom_call" | custom-call | tf_op jit(solution)/shard_map/boundary/pallas_call | solution.py:244
  150.7 4.3 %collective-permute-start.10 = (f32[5,16,256]{2,1,0:T(8,128)}, f32[5,16,256]{2,1,0:T(8,128)S(1)}, u32[]{:S(2)}, u32[]{:S(2)}) collective-permute-start(f32[5,16,256]{2,1,0:T(8,128)} %get-tuple-element.56), channel_id=1, source_target_pairs={{0,1},{1,2},{2,3},{3,4},{4,5},{5,6},{6,7},{8,9},{9,10},{10,11},{11... | collective-permute-start | bytes 245768 | tf_op jit(solution)/shard_map/ppermute | solution.py:323
  154.9 1.9 collective-permute-start.11
  156.9 4.8 %collective-permute-start.8 = (f32[5,16,256]{2,1,0:T(8,128)}, f32[5,16,256]{2,1,0:T(8,128)S(1)}, u32[]{:S(2)}, u32[]{:S(2)}) collective-permute-start(f32[5,16,256]{2,1,0:T(8,128)} %get-tuple-element.54), channel_id=1, source_target_pairs={{0,8},{8,16},{16,24},{1,9},{9,17},{17,25},{2,10},{10,18},{18,26},{... | collective-permute-start | bytes 245768 | tf_op jit(solution)/shard_map/ppermute | solution.py:323
  161.6 1.9 collective-permute-start.9
  163.5 0.6 copy.13.refs_0_
  164.1 0.0 collective-permute-done.10.refs_10_
  164.2 0.0 collective-permute-done.11.refs_11_
  164.2 0.0 collective-permute-done.8.refs_8_
  164.2 0.0 copy-start.18
  164.2 3.4 %collective-permute-done.9.refs_9_ = f32[5,16,256]{2,1,0:T(8,128)S(1)} collective-permute-done((f32[5,16,256]{2,1,0:T(8,128)}, f32[5,16,256]{2,1,0:T(8,128)S(1)}, u32[]{:S(2)}, u32[]{:S(2)}) %collective-permute-start.9) | collective-permute-done | bytes 81952 | tf_op jit(solution)/shard_map/ppermute | solution.py:324
  167.6 0.6 copy-done.20
  168.2 9.0 %step_one.1 = (f32[5,16,16,256]{3,2,1,0:T(8,128)}, f32[5,16,256]{2,1,0:T(8,128)}, f32[5,16,256]{2,1,0:T(8,128)}, f32[5,16,256]{2,1,0:T(8,128)}, f32[5,16,256]{2,1,0:T(8,128)}) custom-call(f32[3,5,5]{2,1,0:T(8,128)} %copy.13.refs_0_, f32[5,16,16,256]{3,2,1,0:T(8,128)} %refs_1_.3, s32[16,16,256]{2,1,0:T(8,128)} %refs_2_.5, ...), custom_call_target="tpu_custom_call" | custom-call | tf_op jit(solution)/shard_map/step_one/pallas_call | solution.py:306
  177.2 1.9 collective-permute-start.12
  179.2 2.4 %collective-permute-start.13 = (f32[5,16,256]{2,1,0:T(8,128)}, f32[5,16,256]{2,1,0:T(8,128)S(1)}, u32[]{:S(2)}, u32[]{:S(2)}) collective-permute-start(f32[5,16,256]{2,1,0:T(8,128)} %get-tuple-element.60), channel_id=1, source_target_pairs={{8,0},{16,8},{24,16},{9,1},{17,9},{25,17},{10,2},{18,10},{26,18},{... | collective-permute-start | bytes 245768 | tf_op jit(solution)/shard_map/ppermute | solution.py:324
  181.6 4.5 %collective-permute-start.14 = (f32[5,16,256]{2,1,0:T(8,128)}, f32[5,16,256]{2,1,0:T(8,128)S(1)}, u32[]{:S(2)}, u32[]{:S(2)}) collective-permute-start(f32[5,16,256]{2,1,0:T(8,128)} %get-tuple-element.61), channel_id=1, source_target_pairs={{0,1},{1,2},{2,3},{3,4},{4,5},{5,6},{6,7},{8,9},{9,10},{10,11},{11... | collective-permute-start | bytes 245768 | tf_op jit(solution)/shard_map/ppermute | solution.py:323
  186.1 1.9 collective-permute-start.15
  188.1 0.0 collective-permute-done.12.refs_8_
  188.1 0.0 collective-permute-done.13.refs_9_
  188.1 0.4 collective-permute-done.14.refs_10_
  188.5 4.9 %collective-permute-done.15.refs_11_ = f32[5,16,256]{2,1,0:T(8,128)S(1)} collective-permute-done((f32[5,16,256]{2,1,0:T(8,128)}, f32[5,16,256]{2,1,0:T(8,128)S(1)}, u32[]{:S(2)}, u32[]{:S(2)}) %collective-permute-start.15) | collective-permute-done | bytes 81952 | tf_op jit(solution)/shard_map/ppermute | solution.py:324
  193.5 0.0 copy-done.15
  193.5 0.6 copy-done.21
  194.1 8.9 %step_two.1 = f32[5,16,16,256]{3,2,1,0:T(8,128)} custom-call(f32[3,5,5]{2,1,0:T(8,128)} %copy.13.refs_0_, f32[5,16,16,256]{3,2,1,0:T(8,128)} %refs_1_.3, s32[16,16,256]{2,1,0:T(8,128)} %refs_2_.5, f32[5,16,16,256]{3,2,1,0:T(8,128)} %get-tuple-element.58.refs_3_, f32[10,16,256]{2,1,0:T(8,128)} %copy-done, f32[10,16,256]{2,1,0:T(8,128)} %copy-done.1, ...), custom_call_target="tpu_custom_call" | custom-call | tf_op jit(solution)/shard_map/step_two/pallas_call | solution.py:306
  (33 shorter events, 0.1 us)
Async XLA Ops:
  53.2 11.9 %copy-start.22 = (f32[3,5,5]{2,0,1:T(4,128)S(1)}, f32[3,5,5]{2,0,1:T(4,128)}, u32[]{:S(2)}) copy-start(f32[3,5,5]{2,0,1:T(4,128)} %param.16) | copy-start | bytes 904
  53.2 11.9 %copy-start.23 = (f32[10,160,1]{1,0,2:T(8,128)S(1)}, f32[10,160,1]{1,0,2:T(8,128)}, u32[]{:S(2)}) copy-start(f32[10,160,1]{1,0,2:T(8,128)} %constant.20) | copy-start | bytes 19204
  53.2 12.1 %copy-start.13 = (f32[80,160]{1,0:T(8,128)S(1)}, f32[80,160]{1,0:T(8,128)}, u32[]{:S(2)}) copy-start(f32[80,160]{1,0:T(8,128)} %constant.17.clone) | copy-start | bytes 153604
  53.2 12.1 %copy-start.24 = (f32[80,5,1]{0,1,2:T(8,128)S(1)}, f32[80,5,1]{0,1,2:T(8,128)}, u32[]{:S(2)}) copy-start(f32[80,5,1]{0,1,2:T(8,128)} %constant.21) | copy-start | bytes 4804
  65.7 15.9 %copy-start.12 = (bf16[3,80,160]{2,1,0:T(8,128)(2,1)}, bf16[3,80,160]{2,1,0:T(8,128)(2,1)S(1)}, u32[]{:S(2)}) copy-start(bf16[3,80,160]{2,1,0:T(8,128)(2,1)S(1)} %fusion.1) | copy-start | bytes 230404
  66.4 25.7 %copy-start.11 = (bf16[16,5,16,256]{3,2,1,0:T(8,128)(2,1)S(1)}, bf16[16,5,16,256]{3,2,1,0:T(8,128)(2,1)}, u32[]{:S(2)}) copy-start(bf16[16,5,16,256]{3,2,1,0:T(8,128)(2,1)} %get-tuple-element.38.refs_1_) | copy-start | bytes 1966084
  66.4 29.7 %copy-start.10 = (bf16[16,5,16,256]{3,2,1,0:T(8,128)(2,1)S(1)}, bf16[16,5,16,256]{3,2,1,0:T(8,128)(2,1)}, u32[]{:S(2)}) copy-start(bf16[16,5,16,256]{3,2,1,0:T(8,128)(2,1)} %get-tuple-element.37.refs_0_) | copy-start | bytes 1966084
  66.4 31.6 %copy-start.9 = (bf16[16,5,16,256]{3,2,1,0:T(8,128)(2,1)S(1)}, bf16[16,5,16,256]{3,2,1,0:T(8,128)(2,1)}, u32[]{:S(2)}) copy-start(bf16[16,5,16,256]{3,2,1,0:T(8,128)(2,1)} %get-tuple-element.40.refs_3_) | copy-start | bytes 1966084
  66.4 33.8 %copy-start.8 = (bf16[16,5,16,256]{3,2,1,0:T(8,128)(2,1)S(1)}, bf16[16,5,16,256]{3,2,1,0:T(8,128)(2,1)}, u32[]{:S(2)}) copy-start(bf16[16,5,16,256]{3,2,1,0:T(8,128)(2,1)} %get-tuple-element.39.refs_2_) | copy-start | bytes 1966084
  81.7 16.3 %collective-permute-start.4 = (f32[10,16,256]{2,1,0:T(8,128)}, f32[10,16,256]{2,1,0:T(8,128)S(1)}, u32[]{:S(2)}, u32[]{:S(2)}) collective-permute-start(f32[10,16,256]{2,1,0:T(8,128)} %get-tuple-element.49), channel_id=1, source_target_pairs={{0,8},{8,16},{16,24},{1,9},{9,17},{17,25},{2,10},{10,18},{18,26},{... | collective-permute-start | bytes 491528 | tf_op jit(solution)/shard_map/ppermute | solution.py:323
  86.2 14.1 %collective-permute-start.5 = (f32[10,16,256]{2,1,0:T(8,128)}, f32[10,16,256]{2,1,0:T(8,128)S(1)}, u32[]{:S(2)}, u32[]{:S(2)}) collective-permute-start(f32[10,16,256]{2,1,0:T(8,128)} %get-tuple-element.50), channel_id=1, source_target_pairs={{8,0},{16,8},{24,16},{9,1},{17,9},{25,17},{10,2},{18,10},{26,18},{... | collective-permute-start | bytes 491528 | tf_op jit(solution)/shard_map/ppermute | solution.py:324
  88.1 15.3 %collective-permute-start.6 = (f32[10,16,256]{2,1,0:T(8,128)}, f32[10,16,256]{2,1,0:T(8,128)S(1)}, u32[]{:S(2)}, u32[]{:S(2)}) collective-permute-start(f32[10,16,256]{2,1,0:T(8,128)} %get-tuple-element.51), channel_id=1, source_target_pairs={{0,1},{1,2},{2,3},{3,4},{4,5},{5,6},{6,7},{8,9},{9,10},{10,11},{11... | collective-permute-start | bytes 491528 | tf_op jit(solution)/shard_map/ppermute | solution.py:323
  92.2 50.1 %collective-permute-start = (bf16[16,5,16,256]{3,2,1,0:T(8,128)(2,1)S(1)}, bf16[16,5,16,256]{3,2,1,0:T(8,128)(2,1)S(1)}, u32[]{:S(2)}, u32[]{:S(2)}) collective-permute-start(bf16[16,5,16,256]{3,2,1,0:T(8,128)(2,1)S(1)} %copy-done.11), channel_id=1, source_target_pairs={{0,8},{8,16},{16,24},{1,9},{9,17},{17,25},{2,10},{10,18},{18,26},{... | collective-permute-start | bytes 1966088 | tf_op jit(solution)/shard_map/ppermute | solution.py:323
  96.1 46.2 %collective-permute-start.1 = (bf16[16,5,16,256]{3,2,1,0:T(8,128)(2,1)S(1)}, bf16[16,5,16,256]{3,2,1,0:T(8,128)(2,1)S(1)}, u32[]{:S(2)}, u32[]{:S(2)}) collective-permute-start(bf16[16,5,16,256]{3,2,1,0:T(8,128)(2,1)S(1)} %copy-done.10), channel_id=1, source_target_pairs={{8,0},{16,8},{24,16},{9,1},{17,9},{25,17},{10,2},{18,10},{26,18},{... | collective-permute-start | bytes 1966088 | tf_op jit(solution)/shard_map/ppermute | solution.py:324
  98.0 44.2 %copy-start = (f32[10,16,256]{2,1,0:T(8,128)}, f32[10,16,256]{2,1,0:T(8,128)S(1)}, u32[]{:S(2)}) copy-start(f32[10,16,256]{2,1,0:T(8,128)S(1)} %collective-permute-done.4.refs_11_.refs_4_) | copy-start | bytes 491524
  98.0 44.3 %collective-permute-start.2 = (bf16[16,5,16,256]{3,2,1,0:T(8,128)(2,1)S(1)}, bf16[16,5,16,256]{3,2,1,0:T(8,128)(2,1)S(1)}, u32[]{:S(2)}, u32[]{:S(2)}) collective-permute-start(bf16[16,5,16,256]{3,2,1,0:T(8,128)(2,1)S(1)} %copy-done.9), channel_id=1, source_target_pairs={{0,1},{1,2},{2,3},{3,4},{4,5},{5,6},{6,7},{8,9},{9,10},{10,11},{11... | collective-permute-start | bytes 1966088 | tf_op jit(solution)/shard_map/ppermute | solution.py:323
  100.3 42.0 %copy-start.1 = (f32[10,16,256]{2,1,0:T(8,128)}, f32[10,16,256]{2,1,0:T(8,128)S(1)}, u32[]{:S(2)}) copy-start(f32[10,16,256]{2,1,0:T(8,128)S(1)} %collective-permute-done.5.refs_12_.refs_5_) | copy-start | bytes 491524
  100.3 42.1 %collective-permute-start.3 = (bf16[16,5,16,256]{3,2,1,0:T(8,128)(2,1)S(1)}, bf16[16,5,16,256]{3,2,1,0:T(8,128)(2,1)S(1)}, u32[]{:S(2)}, u32[]{:S(2)}) collective-permute-start(bf16[16,5,16,256]{3,2,1,0:T(8,128)(2,1)S(1)} %copy-done.8), channel_id=1, source_target_pairs={{1,0},{2,1},{3,2},{4,3},{5,4},{6,5},{7,6},{9,8},{10,9},{11,10},{12... | collective-permute-start | bytes 1966088 | tf_op jit(solution)/shard_map/ppermute | solution.py:324
  103.4 38.8 %copy-start.2 = (f32[10,16,256]{2,1,0:T(8,128)}, f32[10,16,256]{2,1,0:T(8,128)S(1)}, u32[]{:S(2)}) copy-start(f32[10,16,256]{2,1,0:T(8,128)S(1)} %collective-permute-done.6.refs_13_.refs_6_) | copy-start | bytes 491524
  103.4 38.8 %collective-permute-start.7 = (f32[10,16,256]{2,1,0:T(8,128)}, f32[10,16,256]{2,1,0:T(8,128)S(1)}, u32[]{:S(2)}, u32[]{:S(2)}) collective-permute-start(f32[10,16,256]{2,1,0:T(8,128)} %get-tuple-element.52), channel_id=1, source_target_pairs={{1,0},{2,1},{3,2},{4,3},{5,4},{6,5},{7,6},{9,8},{10,9},{11,10},{12... | collective-permute-start | bytes 491528 | tf_op jit(solution)/shard_map/ppermute | solution.py:324
  142.3 0.7 copy-start.3
  142.3 0.9 copy-start.4
  142.3 1.2 copy-start.5
  142.3 1.3 copy-start.6
  142.4 1.5 copy-start.7
  150.7 13.5 %collective-permute-start.10 = (f32[5,16,256]{2,1,0:T(8,128)}, f32[5,16,256]{2,1,0:T(8,128)S(1)}, u32[]{:S(2)}, u32[]{:S(2)}) collective-permute-start(f32[5,16,256]{2,1,0:T(8,128)} %get-tuple-element.56), channel_id=1, source_target_pairs={{0,1},{1,2},{2,3},{3,4},{4,5},{5,6},{6,7},{8,9},{9,10},{10,11},{11... | collective-permute-start | bytes 245768 | tf_op jit(solution)/shard_map/ppermute | solution.py:323
  154.9 9.2 %collective-permute-start.11 = (f32[5,16,256]{2,1,0:T(8,128)}, f32[5,16,256]{2,1,0:T(8,128)S(1)}, u32[]{:S(2)}, u32[]{:S(2)}) collective-permute-start(f32[5,16,256]{2,1,0:T(8,128)} %get-tuple-element.57), channel_id=1, source_target_pairs={{1,0},{2,1},{3,2},{4,3},{5,4},{6,5},{7,6},{9,8},{10,9},{11,10},{12... | collective-permute-start | bytes 245768 | tf_op jit(solution)/shard_map/ppermute | solution.py:324
  156.9 7.3 %collective-permute-start.8 = (f32[5,16,256]{2,1,0:T(8,128)}, f32[5,16,256]{2,1,0:T(8,128)S(1)}, u32[]{:S(2)}, u32[]{:S(2)}) collective-permute-start(f32[5,16,256]{2,1,0:T(8,128)} %get-tuple-element.54), channel_id=1, source_target_pairs={{0,8},{8,16},{16,24},{1,9},{9,17},{17,25},{2,10},{10,18},{18,26},{... | collective-permute-start | bytes 245768 | tf_op jit(solution)/shard_map/ppermute | solution.py:323
  161.6 6.0 %collective-permute-start.9 = (f32[5,16,256]{2,1,0:T(8,128)}, f32[5,16,256]{2,1,0:T(8,128)S(1)}, u32[]{:S(2)}, u32[]{:S(2)}) collective-permute-start(f32[5,16,256]{2,1,0:T(8,128)} %get-tuple-element.55), channel_id=1, source_target_pairs={{8,0},{16,8},{24,16},{9,1},{17,9},{25,17},{10,2},{18,10},{26,18},{... | collective-permute-start | bytes 245768 | tf_op jit(solution)/shard_map/ppermute | solution.py:324
  164.2 3.4 %copy-start.14 = (f32[5,16,256]{2,1,0:T(8,128)}, f32[5,16,256]{2,1,0:T(8,128)S(1)}, u32[]{:S(2)}) copy-start(f32[5,16,256]{2,1,0:T(8,128)S(1)} %collective-permute-done.10.refs_10_) | copy-start | bytes 245764
  164.2 3.4 %copy-start.16 = (f32[5,16,256]{2,1,0:T(8,128)}, f32[5,16,256]{2,1,0:T(8,128)S(1)}, u32[]{:S(2)}) copy-start(f32[5,16,256]{2,1,0:T(8,128)S(1)} %collective-permute-done.11.refs_11_) | copy-start | bytes 245764
  164.2 3.4 %copy-start.18 = (f32[5,16,256]{2,1,0:T(8,128)}, f32[5,16,256]{2,1,0:T(8,128)S(1)}, u32[]{:S(2)}) copy-start(f32[5,16,256]{2,1,0:T(8,128)S(1)} %collective-permute-done.8.refs_8_) | copy-start | bytes 245764
  167.6 0.6 copy-start.20
  177.2 10.8 %collective-permute-start.12 = (f32[5,16,256]{2,1,0:T(8,128)}, f32[5,16,256]{2,1,0:T(8,128)S(1)}, u32[]{:S(2)}, u32[]{:S(2)}) collective-permute-start(f32[5,16,256]{2,1,0:T(8,128)} %get-tuple-element.59), channel_id=1, source_target_pairs={{0,8},{8,16},{16,24},{1,9},{9,17},{17,25},{2,10},{10,18},{18,26},{... | collective-permute-start | bytes 245768 | tf_op jit(solution)/shard_map/ppermute | solution.py:323
  179.2 8.9 %collective-permute-start.13 = (f32[5,16,256]{2,1,0:T(8,128)}, f32[5,16,256]{2,1,0:T(8,128)S(1)}, u32[]{:S(2)}, u32[]{:S(2)}) collective-permute-start(f32[5,16,256]{2,1,0:T(8,128)} %get-tuple-element.60), channel_id=1, source_target_pairs={{8,0},{16,8},{24,16},{9,1},{17,9},{25,17},{10,2},{18,10},{26,18},{... | collective-permute-start | bytes 245768 | tf_op jit(solution)/shard_map/ppermute | solution.py:324
  181.6 7.0 %collective-permute-start.14 = (f32[5,16,256]{2,1,0:T(8,128)}, f32[5,16,256]{2,1,0:T(8,128)S(1)}, u32[]{:S(2)}, u32[]{:S(2)}) collective-permute-start(f32[5,16,256]{2,1,0:T(8,128)} %get-tuple-element.61), channel_id=1, source_target_pairs={{0,1},{1,2},{2,3},{3,4},{4,5},{5,6},{6,7},{8,9},{9,10},{10,11},{11... | collective-permute-start | bytes 245768 | tf_op jit(solution)/shard_map/ppermute | solution.py:323
  186.1 7.3 %collective-permute-start.15 = (f32[5,16,256]{2,1,0:T(8,128)}, f32[5,16,256]{2,1,0:T(8,128)S(1)}, u32[]{:S(2)}, u32[]{:S(2)}) collective-permute-start(f32[5,16,256]{2,1,0:T(8,128)} %get-tuple-element.62), channel_id=1, source_target_pairs={{1,0},{2,1},{3,2},{4,3},{5,4},{6,5},{7,6},{9,8},{10,9},{11,10},{12... | collective-permute-start | bytes 245768 | tf_op jit(solution)/shard_map/ppermute | solution.py:324
  188.1 5.4 %copy-start.15 = (f32[5,16,256]{2,1,0:T(8,128)}, f32[5,16,256]{2,1,0:T(8,128)S(1)}, u32[]{:S(2)}) copy-start(f32[5,16,256]{2,1,0:T(8,128)S(1)} %collective-permute-done.12.refs_8_) | copy-start | bytes 245764
  188.1 5.4 %copy-start.17 = (f32[5,16,256]{2,1,0:T(8,128)}, f32[5,16,256]{2,1,0:T(8,128)S(1)}, u32[]{:S(2)}) copy-start(f32[5,16,256]{2,1,0:T(8,128)S(1)} %collective-permute-done.13.refs_9_) | copy-start | bytes 245764
  188.5 4.9 %copy-start.19 = (f32[5,16,256]{2,1,0:T(8,128)}, f32[5,16,256]{2,1,0:T(8,128)S(1)}, u32[]{:S(2)}) copy-start(f32[5,16,256]{2,1,0:T(8,128)S(1)} %collective-permute-done.14.refs_10_) | copy-start | bytes 245764
  193.5 0.6 copy-start.21

commit v2 on v1

--- a/solution.py
+++ b/solution.py
@@ -29,59 +29,103 @@
     return pltpu.CompilerParams(vmem_limit_bytes=LIMIT)
 
 
-def pack_kernel(with_energy, src, xlo, xhi, ylo, yhi, *energy):
+LANES = 128
+
+
+def edge_lines(cells, scratch):
+    nx, ny, nz = cells.shape
+    flat = cells.reshape(nx * ny, nz)
+    out = ([], [])
+    for h in range(nz // LANES):
+        scratch[h] = flat[:, h * LANES : (h + 1) * LANES]
+        for side, first in enumerate((0, ny - 1)):
+            out[side].append(scratch[h, pl.ds(first, nx, stride=ny), :])
+    return [jnp.concatenate(o, axis=1) for o in out]
+
+
+def direct_kernel(src, xlo, xhi, ylo, yhi, energy, scratch):
     nv, nx, ny, nz = src.shape[1:]
     xlo[0] = src[0, :, 0]
     xhi[0] = src[0, :, nx - 1]
     total = jnp.zeros((ny, nz), F32)
     for i in range(nv):
         cells = src[0, i].astype(F32)
-        ylo[0, i] = cells[:, 0, :].astype(BF16)
-        yhi[0, i] = cells[:, ny - 1, :].astype(BF16)
-        if with_energy:
-            total = total + jnp.sum(cells * cells, axis=0)
-    if with_energy:
-        energy[0][pl.program_id(0)] = jnp.sum(total)
-
-
-def pack(modes, with_energy):
+        lo, hi = edge_lines(cells, scratch.at[i])
+        ylo[0, i] = lo.astype(BF16)
+        yhi[0, i] = hi.astype(BF16)
+        total = total + jnp.sum(cells * cells, axis=0)
+    line = jnp.sum(total, axis=0, keepdims=True)
+    energy[pl.ds(pl.program_id(0), 1), :] = sum(line[:, h : h + LANES] for h in range(0, nz, LANES))
+
+
+def pack_direct(modes):
     nm, nv, nx, ny, nz = modes.shape
     face_x = sds((nm, nv, ny, nz), BF16)
     face_y = sds((nm, nv, nx, nz), BF16)
     spec_x = pl.BlockSpec((1, nv, ny, nz), lambda m: (m, 0, 0, 0))
     spec_y = pl.BlockSpec((1, nv, nx, nz), lambda m: (m, 0, 0, 0))
     return pl.pallas_call(
-        lambda *refs: pack_kernel(with_energy, *refs),
+        direct_kernel,
         grid=(nm,),
         in_specs=[pl.BlockSpec((1, nv, nx, ny, nz), lambda m: (m, 0, 0, 0, 0))],
-        out_specs=[spec_x, spec_x, spec_y, spec_y] + ([in_smem()] if with_energy else []),
-        out_shape=[face_x, face_x, face_y, face_y] + ([sds((nm,), F32)] if with_energy else []),
-        compiler_params=params(),
-        name="pack_direct" if with_energy else "pack_adjoint",
+        out_specs=[spec_x, spec_x, spec_y, spec_y, pl.BlockSpec((nm, LANES), lambda m: (0, 0))],
+        out_shape=[face_x, face_x, face_y, face_y, sds((nm, LANES), F32)],
+        scratch_shapes=[pltpu.VMEM((nv, nz // LANES, nx * ny, LANES), F32)],
+        compiler_params=params(),
+        cost_estimate=pl.CostEstimate(flops=3 * modes.size, bytes_accessed=2 * modes.size, transcendentals=0),
+        name="pack_direct",
     )(modes)
 
 
-def faces_kernel(pick, amp, lw, base, *refs):
+def adjoint_kernel(pick, src, lw_x, lw_y, *refs):
+    w_out, scratch = refs[:4], refs[4]
+    nv, nx, ny, nz = src.shape[1:]
+    lines = [edge_lines(src[0, i].astype(F32), scratch.at[i]) for i in range(nv)]
+    for f in range(4):
+        if f < 2:
+            face = src[0, :, 0 if f == 0 else nx - 1].reshape(nv * ny, nz)
+        else:
+            face = jnp.concatenate([line[f - 2] for line in lines], axis=0).astype(BF16)
+        lw = lw_x if f < 2 else lw_y
+        w_out[f][0] = jnp.dot(lw[...], jnp.concatenate([face, face], axis=0), preferred_element_type=F32)
+
+
+def mix_faces(pick, modes, lw_x, lw_y):
+    nm, nv, nx, ny, nz = modes.shape
+    rows = [nv * ny, nv * ny, nv * nx, nv * nx]
+    return pl.pallas_call(
+        adjoint_kernel,
+        grid_spec=pltpu.PrefetchScalarGridSpec(
+            num_scalar_prefetch=1,
+            grid=(nm,),
+            in_specs=[
+                pl.BlockSpec((1, nv, nx, ny, nz), lambda m, pick: (pick[m], 0, 0, 0, 0)),
+                pl.BlockSpec(lw_x.shape, lambda m, pick: (0, 0)),
+                pl.BlockSpec(lw_y.shape, lambda m, pick: (0, 0)),
+            ],
+            out_specs=[pl.BlockSpec((1, r, nz), lambda m, pick: (m, 0, 0)) for r in rows],
+            scratch_shapes=[pltpu.VMEM((nv, nz // LANES, nx * ny, LANES), F32)],
+        ),
+        out_shape=[sds((nm, r, nz), F32) for r in rows],
+        compiler_params=params(),
+        cost_estimate=pl.CostEstimate(flops=4 * modes.size, bytes_accessed=3 * modes.size, transcendentals=0),
+        name="mix_faces",
+    )(pick, modes, lw_x, lw_y)
+
+
+def faces_kernel(amp, base, *refs):
     u = refs[0:4]
-    q = refs[4:8]
-    w_out = refs[8:12]
-    send = refs[12:16]
+    w = refs[4:8]
+    send = refs[8:12]
     nm, nv = u[0].shape[:2]
     nx, ny, nz = base.shape[1:]
     for f in range(4):
-        d = f // 2
         n = u[f].shape[2]
-        rows = nv * n
-
-        def body(m, acc):
-            qm = q[f][pick[m]].reshape(rows, nz)
-            w = jnp.dot(lw[d], jnp.concatenate([qm, qm], axis=0), preferred_element_type=F32)
-            w = w * amp[m]
-            w_out[f][m] = w
-            return acc + u[f][m].reshape(rows, nz).astype(F32) * w
-
-        acc = lax.fori_loop(0, nm, body, jnp.zeros((rows, nz), F32))
-        send[f][0:nv] = acc.reshape(nv, n, nz)
+        for j in range(nv):
+            total = jnp.zeros((n, nz), F32)
+            for m in range(nm):
+                total = total + amp[m] * (u[f][m, j].astype(F32) * w[f][m, j * n : (j + 1) * n])
+            send[f][j] = total
     for j in range(nv):
         send[0][nv + j] = base[j, 0]
         send[1][nv + j] = base[j, nx - 1]
@@ -89,18 +133,17 @@
         send[3][nv + j] = base[j][:, ny - 1, :]
 
 
-def faces(pick, amp, lw, base, u_faces, q_faces):
-    nm, nv = u_faces[0].shape[:2]
+def faces(amp, base, u_faces, w_faces):
+    nv, nz = base.shape[0], base.shape[-1]
     sizes = [f.shape[2] for f in u_faces]
-    nz = base.shape[-1]
     return pl.pallas_call(
         faces_kernel,
-        in_specs=[in_smem(), in_smem()] + [in_vmem()] * 10,
-        out_specs=[in_vmem()] * 8,
-        out_shape=[sds((nm, nv * n, nz), F32) for n in sizes] + [sds((2 * nv, n, nz), F32) for n in sizes],
+        in_specs=[in_smem()] + [in_vmem()] * 9,
+        out_specs=[in_vmem()] * 4,
+        out_shape=[sds((2 * nv, n, nz), F32) for n in sizes],
         compiler_params=params(),
         name="faces",
-    )(pick, amp, lw, base, *u_faces, *q_faces)
+    )(amp, base, *u_faces, *w_faces)
 
 
 def shift_up(a):
@@ -122,7 +165,7 @@
 UNROLL = 4
 
 
-def main_kernel(pick, amp, lw, ld, rz, um, uc, up, q, h_out, c0_out, acc):
+def main_kernel(pick, amp, lw, um, uc, up, q, h_out, c0_out, acc):
     nm, nv, _, ny, nz = uc.shape
     rows = nv * ny
     acc[...] = jnp.zeros_like(acc)
@@ -133,42 +176,41 @@
             m = step * UNROLL + k
             qm = q[pick[m], :, 0].reshape(rows, nz)
             u = uc[m, :, 0].reshape(rows, nz)
-            w = jnp.dot(lw[...], jnp.concatenate([qm, qm], axis=0), preferred_element_type=F32)
-            stacked = jnp.concatenate([um[m, :, 0].reshape(rows, nz), up[m, :, 0].reshape(rows, nz), u], axis=0)
-            dxy = jnp.dot(ld[0], stacked, preferred_element_type=F32)
-            dz = jnp.dot(u, rz[...], preferred_element_type=F32)
+            w = jnp.dot(lw[...], jnp.concatenate([qm, qm, u], axis=0), preferred_element_type=F32)
+            w0, w1, w2, dy = (w[n * rows : (n + 1) * rows] for n in range(4))
+            dx = up[m, :, 0].reshape(rows, nz).astype(F32) - um[m, :, 0].reshape(rows, nz).astype(F32)
             a = amp[m]
-            uf = u.astype(F32) * a
-            w0, w1, w2 = w[:rows], w[rows : 2 * rows], w[2 * rows :]
-            terms = [(dxy[:rows] * w0 + dxy[rows:] * w1 + dz * w2) * a, uf * w0, uf * w1, uf * w2]
+            uf = u.astype(F32)
+            dz = diff_lanes(uf)
+            uf = uf * a
+            terms = [(dx * w0 + dy * w1 + dz * w2) * a, uf * w0, uf * w1, uf * w2]
             parts = [t if p is None else p + t for p, t in zip(parts, terms)]
         for n in range(4):
             acc[n] += parts[n]
         return carry
 
     lax.fori_loop(0, nm // UNROLL, body, 0)
+    p = pl.program_id(0)
+    ends = jnp.where(p == 0, 1.0, 0.0) - jnp.where(p == pl.num_programs(0) - 1, 1.0, 0.0)
     c0_out[:, 0] = acc[1].reshape(nv, ny, nz)
-    h = acc[0] - diff_lanes(acc[3])
+    h = acc[0] - diff_lanes(acc[3]) + ends * acc[1]
     for j in range(nv):
         c1 = acc[2, j * ny : (j + 1) * ny]
         h_out[j, 0] = h[j * ny : (j + 1) * ny] - shift_up(c1) + shift_down(c1)
 
 
-def main(pick, amp, lw, ld, rz, direct, adjoint):
+def main(pick, amp, lw, direct, adjoint):
     nm, nv, nx, ny, nz = direct.shape
     rows = nv * ny
     block = (nm, nv, 1, ny, nz)
     out_spec = pl.BlockSpec((nv, 1, ny, nz), lambda p: (0, p, 0, 0))
-    whole = lambda shape: pl.BlockSpec(shape, lambda p: (0,) * len(shape))
     return pl.pallas_call(
         main_kernel,
         grid=(nx,),
         in_specs=[
             in_smem(),
             in_smem(),
-            whole(lw.shape),
-            pl.BlockSpec((1,) + ld.shape[1:], lambda p: (jnp.where(p == 0, 0, jnp.where(p == nx - 1, 2, 1)), 0, 0)),
-            whole(rz.shape),
+            pl.BlockSpec(lw.shape, lambda p: (0, 0)),
             pl.BlockSpec(block, lambda p: (0, 0, jnp.maximum(p - 1, 0), 0, 0)),
             pl.BlockSpec(block, lambda p: (0, 0, p, 0, 0)),
             pl.BlockSpec(block, lambda p: (0, 0, jnp.minimum(p + 1, nx - 1), 0, 0)),
@@ -180,7 +222,7 @@
         compiler_params=params(),
         cost_estimate=pl.CostEstimate(flops=2 * nm * nx * 480 * 256 * 256, bytes_accessed=4 * direct.size * 2, transcendentals=0),
         name="main",
-    )(pick, amp, lw, ld, rz, direct, direct, direct, adjoint)
+    )(pick, amp, lw, direct, direct, direct, adjoint)
 
 
 def weight_of(cells):
@@ -202,7 +244,7 @@
     return jnp.where(row == 0, lo, 0.0) + jnp.where(row == shape[0] - 1, hi, 0.0)
 
 
-def boundary_kernel(scale, h, c0, cell, *refs):
+def boundary_kernel(scale, amp, h, c0, cell, *refs):
     w = refs[0:4]
     u = refs[4:8]
     got = refs[8:12]
@@ -213,13 +255,12 @@
     nm = u[0].shape[0]
     for f in range(4):
         n = u[f].shape[2]
-
-        def body(m, acc):
-            return acc + u[f][m].reshape(nv * n, nz).astype(F32) * w[f][m]
-
-        total = lax.fori_loop(0, nm, body, jnp.zeros((nv * n, nz), F32))
         sign = -1.0 if f % 2 == 0 else 1.0
-        add[f][...] = (sign * total).reshape(nv, n, nz) - sign * got[f][0:nv]
+        for j in range(nv):
+            total = jnp.zeros((n, nz), F32)
+            for m in range(nm):
+                total = total + amp[m] * (u[f][m, j].astype(F32) * w[f][m, j * n : (j + 1) * n])
+            add[f][j] = sign * (total - got[f][j])
     for x in range(nx):
         weight = weight_of(cell[x]) * scale
         for j in range(nv):
@@ -238,18 +279,18 @@
             write_faces(g, j, x, nx, outs)
 
 
-def boundary(scale, h, c0, cell, w_faces, u_halo, got):
+def boundary(scale, amp, h, c0, cell, w_faces, u_halo, got):
     nv, nx, ny, nz = h.shape
     face = [sds((nv, n, nz), F32) for n in (ny, ny, nx, nx)]
     return pl.pallas_call(
         lambda *refs: boundary_kernel(scale, *refs),
-        in_specs=[in_vmem()] * 15,
+        in_specs=[in_smem()] + [in_vmem()] * 15,
         out_specs=[in_vmem()] * 5,
         out_shape=[sds(h.shape, F32)] + face,
         scratch_shapes=[pltpu.VMEM(f.shape, F32) for f in face],
         compiler_params=params(),
         name="boundary",
-    )(h, c0, cell, *w_faces, *u_halo, *got)
+    )(amp, h, c0, cell, *w_faces, *u_halo, *got)
 
 
 def mixed(mix, d, j, values):
@@ -339,38 +380,26 @@
     return (wide * mask).astype(BF16)
 
 
-def difference_rows(nv, ny):
-    eye = np.eye(nv * ny, dtype=np.float32)
+def main_rows(lw, nv, ny):
     dy = np.kron(np.eye(nv, dtype=np.float32), np.eye(ny, k=1, dtype=np.float32) - np.eye(ny, k=-1, dtype=np.float32))
-    zero = np.zeros_like(eye)
-    kinds = []
-    for lo, hi in ((0.0, 1.0), (1.0, 1.0), (1.0, 0.0)):
-        kinds.append(np.block([[-lo * eye, hi * eye, zero], [zero, zero, dy]]))
-    return jnp.asarray(np.stack(kinds), BF16)
-
-
-def span_difference(nz):
-    eye = np.eye(nz, dtype=np.float32)
-    return jnp.asarray(np.roll(eye, -1, 1) - np.roll(eye, 1, 1), BF16)
+    rows = nv * ny
+    top = jnp.pad(lw.reshape(3 * rows, 2 * rows), ((0, 0), (0, rows)))
+    return jnp.concatenate([top, jnp.pad(jnp.asarray(dy, BF16), ((0, 0), (2 * rows, 0)))], axis=0)
 
 
 def per_device(direct, adjoint, base, cell, pick, mix):
     nm, nv, nx, ny, nz = direct.shape
     cells_all = nv * nx * ny * nz * lax.axis_size("chord") * lax.axis_size("normal")
-    *u_faces, sums = pack(direct, True)
+    *u_faces, sums = pack_direct(direct)
     u_halo = exchange(u_faces)
-    energy = lax.psum(sums, ("chord", "normal")) / cells_all
+    energy = jnp.sum(lax.all_gather(sums, ("chord", "normal")), axis=(0, 2)) / cells_all
     amp = lax.rsqrt(energy + 1e-06)
-    q_faces = pack(adjoint, False)
     lw_y = kron_rows(mix, ny)
     lw_x = lw_y if nx == ny else kron_rows(mix, nx)
-    lw_faces = jnp.stack([lw_y[0], lw_x[1]])
-    out = faces(pick, amp, lw_faces, base, u_faces, q_faces)
-    w_faces, send = out[:4], out[4:]
-    got = exchange(send)
-    lw = lw_y.reshape(3 * nv * ny, 2 * nv * ny)
-    h, c0 = main(pick, amp, lw, difference_rows(nv, ny), span_difference(nz), direct, adjoint)
-    field, *sides = boundary(1.0 / nm, h, c0, cell, w_faces, u_halo, got)
+    w_faces = mix_faces(pick, adjoint, lw_y[0], lw_x[1])
+    got = exchange(faces(amp, base, u_faces, w_faces))
+    h, c0 = main(pick, amp, main_rows(lw_y, nv, ny), direct, adjoint)
+    field, *sides = boundary(1.0 / nm, amp, h, c0, cell, w_faces, u_halo, got)
     halo = exchange(sides)
     field, *sides = apply_step(False, mix, base, cell, field, got, halo)
     halo = exchange(sides)

time: 204 us -> 219 us (1.074)
  blocking collectives: 39.8 us -> 58.9 us
  Pallas kernels: 101 us -> 88.4 us
  starting transfers between devices: 47.1 us -> 52.9 us
    all_gather x0 -> x1, blocking collectives: none -> 58.9 us  [per_device(): lax.all_gather(sums, ('chord', 'normal'))]
    psum x1 -> x0, blocking collectives: 39.8 us -> none  [per_device(): energy = lax.psum(sums, ('chord', 'normal')) / cells_all]
    pallas_call x4, Pallas kernels: 76.8 us -> 64.1 us  [the longest x1 33.2 us: main(): pl.pallas_call(main_kernel, grid=(nx,), in_specs=[in_smem(), in_smem(), p...]
    ppermute x8, starting transfers between devices: 30.1 us -> 35.5 us  [exchange(): out.append(lax.ppermute(arrays[2 * k + 1], axis, up))]
  transfers between devices with their start and end apart: 16 -> 16, of which waited for: 3 -> 3; matrix products, arithmetic and copies ran while one was open for 0% -> 1% of each run, Pallas kernels for 18% -> 15%
where the time goes in v2:
time: 219 us; the launch traced here: 218 us
  Pallas kernels  88.4 us (40%)
  blocking collectives  58.9 us (27%)
  starting transfers between devices  52.9 us (24%)
  waiting for transfers between devices  8.61 us (4%)
  local copies, waits for them, and re-layouts  4.13 us (2%)
  matrix products  2.24 us (1%)
    all_gather x1, blocking collectives, per_device(): lax.all_gather(sums, ('chord', 'normal'))  58.9 us
    ppermute x8, starting transfers between devices, exchange(): out.append(lax.ppermute(arrays[2 * k + 1], axis, up))  35.5 us
    pallas_call x1, Pallas kernels, main(): pl.pallas_call(main_kernel, grid=(nx,), in_specs=[in_smem(), in_smem(), p...  33.2 us
    pallas_call x2, Pallas kernels, apply_step(): pl.pallas_call(lambda *refs: step_kernel(last, *refs), in_specs=[in_smem(...  17.9 us
    ppermute x8, starting transfers between devices, exchange(): out.append(lax.ppermute(arrays[2 * k], axis, down))  17.5 us
    pallas_call x1, Pallas kernels, mix_faces(): pl.pallas_call(adjoint_kernel, grid_spec=pltpu.PrefetchScalarGridSpec(num...  13.9 us
    pallas_call x1, Pallas kernels, pack_direct(): pl.pallas_call(direct_kernel, grid=(nm,), in_specs=[pl.BlockSpec((1, nv,...  11.7 us
    ppermute x8, waiting for transfers between devices, exchange(): out.append(lax.ppermute(arrays[2 * k], axis, down))  8.34 us
  transfers between devices with their start and end apart: 16, of which 3 were waited for; matrix products, arithmetic and copies ran while one was open for 1% of the time, Pallas kernels for 15%

profile of v2, /device:TPU:5, one launch (start us, length us, event | category | flops | bytes accessed | tf_op | source)
XLA Modules:
  0.0 217.8 jit_solution(11129893650874566101)
XLA Ops:
  0.0 0.7 reduce-precision_bitcast_fusion
  0.7 0.9 fusion.4
  1.7 1.3 fusion.1
  3.0 0.6 slice_bitcast_fusion
  3.6 11.7 %pack_direct.1 = (bf16[16,5,16,256]{3,2,1,0:T(8,128)(2,1)}, bf16[16,5,16,256]{3,2,1,0:T(8,128)(2,1)}, bf16[16,5,16,256]{3,2,1,0:T(8,128)(2,1)}, bf16[16,5,16,256]{3,2,1,0:T(8,128)(2,1)}, f32[16,128]{1,0:T(8,128)}) custom-call(bf16[16,5,16,16,256]{4,3,2,1,0:T(8,128)(2,1)} %up.1), custom_call_target="tpu_custom_call" | custom-call | flops 15728640 | bytes 10485760 | tf_op jit(solution)/shard_map/pack_direct/pallas_call | solution.py:67
  15.3 58.9 %all-gather = f32[512,128]{1,0:T(8,128)S(1)} all-gather(f32[16,128]{1,0:T(8,128)} %get-tuple-element.30), channel_id=2, replica_groups=mesh['chord'=4,'normal'=8] {'chord','normal'}, dimensions={0}, use_global_device_ids=true | all-gather | bytes 270336 | tf_op jit(solution)/shard_map/all_gather | solution.py:395
  74.3 0.1 reduce
  74.4 0.1 reshape.10
  74.5 0.6 add_rsqrt_fusion.amp.refs_0_
  75.1 13.9 %mix_faces.1 = (f32[16,80,256]{2,1,0:T(8,128)}, f32[16,80,256]{2,1,0:T(8,128)}, f32[16,80,256]{2,1,0:T(8,128)}, f32[16,80,256]{2,1,0:T(8,128)}) custom-call(s32[16]{0:T(128)} %pick.3, bf16[16,5,16,16,256]{4,3,2,1,0:T(8,128)(2,1)} %src.3, bf16[80,160]{1,0:T(8,128)(2,1)} %get-tuple-element.56.lw_x, bf16[80,160]{1,0:T(8,128)(2,1)} %get-tuple-element.55.lw_y), custom_call_target="tpu_custom_call" | custom-call | flops 20971520 | bytes 15728640 | tf_op jit(solution)/shard_map/mix_faces/pallas_call | solution.py:96
  89.0 0.0 copy-start.20
  89.0 0.0 copy-start.5
  89.0 0.0 copy-start.4
  89.0 5.3 %faces.1 = (f32[10,16,256]{2,1,0:T(8,128)}, f32[10,16,256]{2,1,0:T(8,128)}, f32[10,16,256]{2,1,0:T(8,128)}, f32[10,16,256]{2,1,0:T(8,128)}) custom-call(f32[16]{0:T(128)} %add_rsqrt_fusion.amp.refs_0_, f32[5,16,16,256]{3,2,1,0:T(8,128)} %refs_1_.3, bf16[16,5,16,256]{3,2,1,0:T(8,128)(2,1)} %get-tuple-element.38.refs_0_, ...), custom_call_target="tpu_custom_call" | custom-call | tf_op jit(solution)/shard_map/faces/pallas_call | solution.py:139
  94.3 10.5 %collective-permute-start.4 = (f32[10,16,256]{2,1,0:T(8,128)}, f32[10,16,256]{2,1,0:T(8,128)S(1)}, u32[]{:S(2)}, u32[]{:S(2)}) collective-permute-start(f32[10,16,256]{2,1,0:T(8,128)} %get-tuple-element.41), channel_id=1, source_target_pairs={{0,8},{8,16},{16,24},{1,9},{9,17},{17,25},{2,10},{10,18},{18,26},{... | collective-permute-start | bytes 491528 | tf_op jit(solution)/shard_map/ppermute | solution.py:364
  104.8 1.9 collective-permute-start.5
  106.8 3.6 %collective-permute-start.6 = (f32[10,16,256]{2,1,0:T(8,128)}, f32[10,16,256]{2,1,0:T(8,128)S(1)}, u32[]{:S(2)}, u32[]{:S(2)}) collective-permute-start(f32[10,16,256]{2,1,0:T(8,128)} %get-tuple-element.43), channel_id=1, source_target_pairs={{0,1},{1,2},{2,3},{3,4},{4,5},{5,6},{6,7},{8,9},{9,10},{10,11},{11... | collective-permute-start | bytes 491528 | tf_op jit(solution)/shard_map/ppermute | solution.py:364
  110.4 0.0 copy-done.7
  110.4 3.9 %collective-permute-start = (bf16[16,5,16,256]{3,2,1,0:T(8,128)(2,1)S(1)}, bf16[16,5,16,256]{3,2,1,0:T(8,128)(2,1)S(1)}, u32[]{:S(2)}, u32[]{:S(2)}) collective-permute-start(bf16[16,5,16,256]{3,2,1,0:T(8,128)(2,1)S(1)} %copy-done.7), channel_id=1, source_target_pairs={{0,8},{8,16},{16,24},{1,9},{9,17},{17,25},{2,10},{10,18},{18,26},{... | collective-permute-start | bytes 1966088 | tf_op jit(solution)/shard_map/ppermute | solution.py:364
  114.3 0.0 copy-done.6
  114.3 1.9 collective-permute-start.1
  116.2 0.0 copy-done.20
  116.3 0.7 fusion.3.lw
  117.0 0.0 collective-permute-done.4.refs_12_.refs_4_
  117.0 1.9 collective-permute-start.2
  118.9 0.0 collective-permute-done.5.refs_13_.refs_5_
  118.9 0.0 copy-done.4
  118.9 3.4 %collective-permute-start.3 = (bf16[16,5,16,256]{3,2,1,0:T(8,128)(2,1)S(1)}, bf16[16,5,16,256]{3,2,1,0:T(8,128)(2,1)S(1)}, u32[]{:S(2)}, u32[]{:S(2)}) collective-permute-start(bf16[16,5,16,256]{3,2,1,0:T(8,128)(2,1)S(1)} %copy-done.4), channel_id=1, source_target_pairs={{1,0},{2,1},{3,2},{4,3},{5,4},{6,5},{7,6},{9,8},{10,9},{11,10},{12... | collective-permute-start | bytes 1966088 | tf_op jit(solution)/shard_map/ppermute | solution.py:365
  122.3 0.0 collective-permute-done.6.refs_14_.refs_6_
  122.3 1.9 collective-permute-start.7
  124.3 33.2 %main.1 = (f32[5,16,16,256]{3,2,1,0:T(8,128)}, f32[5,16,16,256]{3,2,1,0:T(8,128)}) custom-call(s32[16]{0:T(128)} %pick.3, f32[16]{0:T(128)} %add_rsqrt_fusion.amp.refs_0_, bf16[320,240]{1,0:T(8,128)(2,1)} %fusion.3.lw, bf16[16,5,16,16,256]{4,3,2,1,0:T(8,128)(2,1)} %up.1, bf16[16,5,16,16,256]{4,3,2,1,0:T(8,128)(2,1)} %up.1, bf16[16,5,16,16,256]{4,3,2,1,0:T(8,128)(2,1)} %up.1, ...), custom_call_target="tpu_custom_call" | custom-call | flops 16106127360 | bytes 41943040 | tf_op jit(solution)/shard_map/main/pallas_call | solution.py:207
  157.5 0.0 collective-permute-done.7.refs_15_.refs_7_
  157.5 0.0 collective-permute-done.refs_8_
  157.5 0.0 collective-permute-done.1.refs_9_
  157.6 0.0 collective-permute-done.2.refs_10_
  157.6 0.0 collective-permute-done.3.refs_11_
  157.6 0.6 copy-done.3
  158.2 0.3 copy-done.8
  158.4 0.3 copy-done.9
  158.7 0.2 copy-done.10
  158.9 0.2 copy-done.11
  159.1 6.4 %boundary.1 = (f32[5,16,16,256]{3,2,1,0:T(8,128)}, f32[5,16,256]{2,1,0:T(8,128)}, f32[5,16,256]{2,1,0:T(8,128)}, f32[5,16,256]{2,1,0:T(8,128)}, f32[5,16,256]{2,1,0:T(8,128)}) custom-call(f32[16]{0:T(128)} %add_rsqrt_fusion.amp.refs_0_, f32[5,16,16,256]{3,2,1,0:T(8,128)} %get-tuple-element.31.refs_1_, f32[5,16,16,256]{3,2,1,0:T(8,128)} %get-tuple-element.32.refs_2_, ...), custom_call_target="tpu_custom_call" | custom-call | tf_op jit(solution)/shard_map/boundary/pallas_call | solution.py:285
  165.5 4.2 %collective-permute-start.10 = (f32[5,16,256]{2,1,0:T(8,128)}, f32[5,16,256]{2,1,0:T(8,128)S(1)}, u32[]{:S(2)}, u32[]{:S(2)}) collective-permute-start(f32[5,16,256]{2,1,0:T(8,128)} %get-tuple-element.48), channel_id=1, source_target_pairs={{0,1},{1,2},{2,3},{3,4},{4,5},{5,6},{6,7},{8,9},{9,10},{10,11},{11... | collective-permute-start | bytes 245768 | tf_op jit(solution)/shard_map/ppermute | solution.py:364
  169.8 1.9 collective-permute-start.11
  171.7 4.8 %collective-permute-start.8 = (f32[5,16,256]{2,1,0:T(8,128)}, f32[5,16,256]{2,1,0:T(8,128)S(1)}, u32[]{:S(2)}, u32[]{:S(2)}) collective-permute-start(f32[5,16,256]{2,1,0:T(8,128)} %get-tuple-element.46), channel_id=1, source_target_pairs={{0,8},{8,16},{16,24},{1,9},{9,17},{17,25},{2,10},{10,18},{18,26},{... | collective-permute-start | bytes 245768 | tf_op jit(solution)/shard_map/ppermute | solution.py:364
  176.5 1.9 collective-permute-start.9
  178.4 0.6 copy.14.refs_0_
  179.0 0.0 collective-permute-done.10.refs_10_
  179.0 0.0 collective-permute-done.11.refs_11_
  179.0 0.0 collective-permute-done.8.refs_8_
  179.1 0.0 copy-start.16
  179.1 3.4 %collective-permute-done.9.refs_9_ = f32[5,16,256]{2,1,0:T(8,128)S(1)} collective-permute-done((f32[5,16,256]{2,1,0:T(8,128)}, f32[5,16,256]{2,1,0:T(8,128)S(1)}, u32[]{:S(2)}, u32[]{:S(2)}) %collective-permute-start.9) | collective-permute-done | bytes 81952 | tf_op jit(solution)/shard_map/ppermute | solution.py:365
  182.5 0.6 copy-done.18
  183.1 9.0 %step_one.1 = (f32[5,16,16,256]{3,2,1,0:T(8,128)}, f32[5,16,256]{2,1,0:T(8,128)}, f32[5,16,256]{2,1,0:T(8,128)}, f32[5,16,256]{2,1,0:T(8,128)}, f32[5,16,256]{2,1,0:T(8,128)}) custom-call(f32[3,5,5]{2,1,0:T(8,128)} %copy.14.refs_0_, f32[5,16,16,256]{3,2,1,0:T(8,128)} %refs_1_.3, s32[16,16,256]{2,1,0:T(8,128)} %refs_2_.3, ...), custom_call_target="tpu_custom_call" | custom-call | tf_op jit(solution)/shard_map/step_one/pallas_call | solution.py:347
  192.1 1.9 collective-permute-start.12
  194.0 2.4 %collective-permute-start.13 = (f32[5,16,256]{2,1,0:T(8,128)}, f32[5,16,256]{2,1,0:T(8,128)S(1)}, u32[]{:S(2)}, u32[]{:S(2)}) collective-permute-start(f32[5,16,256]{2,1,0:T(8,128)} %get-tuple-element.52), channel_id=1, source_target_pairs={{8,0},{16,8},{24,16},{9,1},{17,9},{25,17},{10,2},{18,10},{26,18},{... | collective-permute-start | bytes 245768 | tf_op jit(solution)/shard_map/ppermute | solution.py:365
  196.4 4.5 %collective-permute-start.14 = (f32[5,16,256]{2,1,0:T(8,128)}, f32[5,16,256]{2,1,0:T(8,128)S(1)}, u32[]{:S(2)}, u32[]{:S(2)}) collective-permute-start(f32[5,16,256]{2,1,0:T(8,128)} %get-tuple-element.53), channel_id=1, source_target_pairs={{0,1},{1,2},{2,3},{3,4},{4,5},{5,6},{6,7},{8,9},{9,10},{10,11},{11... | collective-permute-start | bytes 245768 | tf_op jit(solution)/shard_map/ppermute | solution.py:364
  200.9 2.1 collective-permute-start.15
  203.1 0.0 collective-permute-done.12.refs_8_
  203.1 0.0 collective-permute-done.13.refs_9_
  203.1 0.3 collective-permute-done.14.refs_10_
  203.3 4.9 %collective-permute-done.15.refs_11_ = f32[5,16,256]{2,1,0:T(8,128)S(1)} collective-permute-done((f32[5,16,256]{2,1,0:T(8,128)}, f32[5,16,256]{2,1,0:T(8,128)S(1)}, u32[]{:S(2)}, u32[]{:S(2)}) %collective-permute-start.15) | collective-permute-done | bytes 81952 | tf_op jit(solution)/shard_map/ppermute | solution.py:365
  208.3 0.6 copy-done.19
  208.9 8.9 %step_two.1 = f32[5,16,16,256]{3,2,1,0:T(8,128)} custom-call(f32[3,5,5]{2,1,0:T(8,128)} %copy.14.refs_0_, f32[5,16,16,256]{3,2,1,0:T(8,128)} %refs_1_.3, s32[16,16,256]{2,1,0:T(8,128)} %refs_2_.3, f32[5,16,16,256]{3,2,1,0:T(8,128)} %get-tuple-element.50.refs_3_, f32[10,16,256]{2,1,0:T(8,128)} %copy-done, f32[10,16,256]{2,1,0:T(8,128)} %copy-done.1, ...), custom_call_target="tpu_custom_call" | custom-call | tf_op jit(solution)/shard_map/step_two/pallas_call | solution.py:347
  (31 shorter events, 0.1 us)
Async XLA Ops:
  89.0 21.4 %copy-start.7 = (bf16[16,5,16,256]{3,2,1,0:T(8,128)(2,1)S(1)}, bf16[16,5,16,256]{3,2,1,0:T(8,128)(2,1)}, u32[]{:S(2)}) copy-start(bf16[16,5,16,256]{3,2,1,0:T(8,128)(2,1)} %get-tuple-element.37.refs_1_) | copy-start | bytes 1966084
  89.0 25.3 %copy-start.6 = (bf16[16,5,16,256]{3,2,1,0:T(8,128)(2,1)S(1)}, bf16[16,5,16,256]{3,2,1,0:T(8,128)(2,1)}, u32[]{:S(2)}) copy-start(bf16[16,5,16,256]{3,2,1,0:T(8,128)(2,1)} %get-tuple-element.38.refs_0_) | copy-start | bytes 1966084
  89.0 27.3 %copy-start.20 = (bf16[80,240]{1,0:T(8,128)(2,1)S(1)}, bf16[80,240]{1,0:T(8,128)(2,1)}, u32[]{:S(2)}) copy-start(bf16[80,240]{1,0:T(8,128)(2,1)} %constant.26) | copy-start | bytes 115204
  89.0 28.0 %copy-start.5 = (bf16[16,5,16,256]{3,2,1,0:T(8,128)(2,1)S(1)}, bf16[16,5,16,256]{3,2,1,0:T(8,128)(2,1)}, u32[]{:S(2)}) copy-start(bf16[16,5,16,256]{3,2,1,0:T(8,128)(2,1)} %get-tuple-element.39.refs_3_) | copy-start | bytes 1966084
  89.0 29.9 %copy-start.4 = (bf16[16,5,16,256]{3,2,1,0:T(8,128)(2,1)S(1)}, bf16[16,5,16,256]{3,2,1,0:T(8,128)(2,1)}, u32[]{:S(2)}) copy-start(bf16[16,5,16,256]{3,2,1,0:T(8,128)(2,1)} %get-tuple-element.40.refs_2_) | copy-start | bytes 1966084
  94.3 22.7 %collective-permute-start.4 = (f32[10,16,256]{2,1,0:T(8,128)}, f32[10,16,256]{2,1,0:T(8,128)S(1)}, u32[]{:S(2)}, u32[]{:S(2)}) collective-permute-start(f32[10,16,256]{2,1,0:T(8,128)} %get-tuple-element.41), channel_id=1, source_target_pairs={{0,8},{8,16},{16,24},{1,9},{9,17},{17,25},{2,10},{10,18},{18,26},{... | collective-permute-start | bytes 491528 | tf_op jit(solution)/shard_map/ppermute | solution.py:364
  104.8 14.1 %collective-permute-start.5 = (f32[10,16,256]{2,1,0:T(8,128)}, f32[10,16,256]{2,1,0:T(8,128)S(1)}, u32[]{:S(2)}, u32[]{:S(2)}) collective-permute-start(f32[10,16,256]{2,1,0:T(8,128)} %get-tuple-element.42), channel_id=1, source_target_pairs={{8,0},{16,8},{24,16},{9,1},{17,9},{25,17},{10,2},{18,10},{26,18},{... | collective-permute-start | bytes 491528 | tf_op jit(solution)/shard_map/ppermute | solution.py:365
  106.8 15.6 %collective-permute-start.6 = (f32[10,16,256]{2,1,0:T(8,128)}, f32[10,16,256]{2,1,0:T(8,128)S(1)}, u32[]{:S(2)}, u32[]{:S(2)}) collective-permute-start(f32[10,16,256]{2,1,0:T(8,128)} %get-tuple-element.43), channel_id=1, source_target_pairs={{0,1},{1,2},{2,3},{3,4},{4,5},{5,6},{6,7},{8,9},{9,10},{10,11},{11... | collective-permute-start | bytes 491528 | tf_op jit(solution)/shard_map/ppermute | solution.py:364
  110.4 47.1 %collective-permute-start = (bf16[16,5,16,256]{3,2,1,0:T(8,128)(2,1)S(1)}, bf16[16,5,16,256]{3,2,1,0:T(8,128)(2,1)S(1)}, u32[]{:S(2)}, u32[]{:S(2)}) collective-permute-start(bf16[16,5,16,256]{3,2,1,0:T(8,128)(2,1)S(1)} %copy-done.7), channel_id=1, source_target_pairs={{0,8},{8,16},{16,24},{1,9},{9,17},{17,25},{2,10},{10,18},{18,26},{... | collective-permute-start | bytes 1966088 | tf_op jit(solution)/shard_map/ppermute | solution.py:364
  114.3 43.2 %collective-permute-start.1 = (bf16[16,5,16,256]{3,2,1,0:T(8,128)(2,1)S(1)}, bf16[16,5,16,256]{3,2,1,0:T(8,128)(2,1)S(1)}, u32[]{:S(2)}, u32[]{:S(2)}) collective-permute-start(bf16[16,5,16,256]{3,2,1,0:T(8,128)(2,1)S(1)} %copy-done.6), channel_id=1, source_target_pairs={{8,0},{16,8},{24,16},{9,1},{17,9},{25,17},{10,2},{18,10},{26,18},{... | collective-permute-start | bytes 1966088 | tf_op jit(solution)/shard_map/ppermute | solution.py:365
  117.0 40.5 %copy-start = (f32[10,16,256]{2,1,0:T(8,128)}, f32[10,16,256]{2,1,0:T(8,128)S(1)}, u32[]{:S(2)}) copy-start(f32[10,16,256]{2,1,0:T(8,128)S(1)} %collective-permute-done.4.refs_12_.refs_4_) | copy-start | bytes 491524
  117.0 40.6 %collective-permute-start.2 = (bf16[16,5,16,256]{3,2,1,0:T(8,128)(2,1)S(1)}, bf16[16,5,16,256]{3,2,1,0:T(8,128)(2,1)S(1)}, u32[]{:S(2)}, u32[]{:S(2)}) collective-permute-start(bf16[16,5,16,256]{3,2,1,0:T(8,128)(2,1)S(1)} %copy-done.5), channel_id=1, source_target_pairs={{0,1},{1,2},{2,3},{3,4},{4,5},{5,6},{6,7},{8,9},{9,10},{10,11},{11... | collective-permute-start | bytes 1966088 | tf_op jit(solution)/shard_map/ppermute | solution.py:364
  118.9 38.6 %copy-start.1 = (f32[10,16,256]{2,1,0:T(8,128)}, f32[10,16,256]{2,1,0:T(8,128)S(1)}, u32[]{:S(2)}) copy-start(f32[10,16,256]{2,1,0:T(8,128)S(1)} %collective-permute-done.5.refs_13_.refs_5_) | copy-start | bytes 491524
  118.9 38.7 %collective-permute-start.3 = (bf16[16,5,16,256]{3,2,1,0:T(8,128)(2,1)S(1)}, bf16[16,5,16,256]{3,2,1,0:T(8,128)(2,1)S(1)}, u32[]{:S(2)}, u32[]{:S(2)}) collective-permute-start(bf16[16,5,16,256]{3,2,1,0:T(8,128)(2,1)S(1)} %copy-done.4), channel_id=1, source_target_pairs={{1,0},{2,1},{3,2},{4,3},{5,4},{6,5},{7,6},{9,8},{10,9},{11,10},{12... | collective-permute-start | bytes 1966088 | tf_op jit(solution)/shard_map/ppermute | solution.py:365
  122.3 35.2 %copy-start.2 = (f32[10,16,256]{2,1,0:T(8,128)}, f32[10,16,256]{2,1,0:T(8,128)S(1)}, u32[]{:S(2)}) copy-start(f32[10,16,256]{2,1,0:T(8,128)S(1)} %collective-permute-done.6.refs_14_.refs_6_) | copy-start | bytes 491524
  122.3 35.2 %collective-permute-start.7 = (f32[10,16,256]{2,1,0:T(8,128)}, f32[10,16,256]{2,1,0:T(8,128)S(1)}, u32[]{:S(2)}, u32[]{:S(2)}) collective-permute-start(f32[10,16,256]{2,1,0:T(8,128)} %get-tuple-element.44), channel_id=1, source_target_pairs={{1,0},{2,1},{3,2},{4,3},{5,4},{6,5},{7,6},{9,8},{10,9},{11,10},{12... | collective-permute-start | bytes 491528 | tf_op jit(solution)/shard_map/ppermute | solution.py:365
  157.5 0.7 copy-start.3
  157.5 0.9 copy-start.8
  157.6 1.1 copy-start.9
  157.6 1.3 copy-start.10
  157.6 1.5 copy-start.11
  159.1 19.3 %copy-start.21 = (f32[3,5,5]{2,0,1:T(4,128)S(1)}, f32[3,5,5]{2,0,1:T(4,128)}, u32[]{:S(2)}) copy-start(f32[3,5,5]{2,0,1:T(4,128)} %param.15) | copy-start | bytes 904
  165.5 13.5 %collective-permute-start.10 = (f32[5,16,256]{2,1,0:T(8,128)}, f32[5,16,256]{2,1,0:T(8,128)S(1)}, u32[]{:S(2)}, u32[]{:S(2)}) collective-permute-start(f32[5,16,256]{2,1,0:T(8,128)} %get-tuple-element.48), channel_id=1, source_target_pairs={{0,1},{1,2},{2,3},{3,4},{4,5},{5,6},{6,7},{8,9},{9,10},{10,11},{11... | collective-permute-start | bytes 245768 | tf_op jit(solution)/shard_map/ppermute | solution.py:364
  169.8 9.2 %collective-permute-start.11 = (f32[5,16,256]{2,1,0:T(8,128)}, f32[5,16,256]{2,1,0:T(8,128)S(1)}, u32[]{:S(2)}, u32[]{:S(2)}) collective-permute-start(f32[5,16,256]{2,1,0:T(8,128)} %get-tuple-element.49), channel_id=1, source_target_pairs={{1,0},{2,1},{3,2},{4,3},{5,4},{6,5},{7,6},{9,8},{10,9},{11,10},{12... | collective-permute-start | bytes 245768 | tf_op jit(solution)/shard_map/ppermute | solution.py:365
  171.7 7.3 %collective-permute-start.8 = (f32[5,16,256]{2,1,0:T(8,128)}, f32[5,16,256]{2,1,0:T(8,128)S(1)}, u32[]{:S(2)}, u32[]{:S(2)}) collective-permute-start(f32[5,16,256]{2,1,0:T(8,128)} %get-tuple-element.46), channel_id=1, source_target_pairs={{0,8},{8,16},{16,24},{1,9},{9,17},{17,25},{2,10},{10,18},{18,26},{... | collective-permute-start | bytes 245768 | tf_op jit(solution)/shard_map/ppermute | solution.py:364
  176.5 6.0 %collective-permute-start.9 = (f32[5,16,256]{2,1,0:T(8,128)}, f32[5,16,256]{2,1,0:T(8,128)S(1)}, u32[]{:S(2)}, u32[]{:S(2)}) collective-permute-start(f32[5,16,256]{2,1,0:T(8,128)} %get-tuple-element.47), channel_id=1, source_target_pairs={{8,0},{16,8},{24,16},{9,1},{17,9},{25,17},{10,2},{18,10},{26,18},{... | collective-permute-start | bytes 245768 | tf_op jit(solution)/shard_map/ppermute | solution.py:365
  179.0 3.4 %copy-start.12 = (f32[5,16,256]{2,1,0:T(8,128)}, f32[5,16,256]{2,1,0:T(8,128)S(1)}, u32[]{:S(2)}) copy-start(f32[5,16,256]{2,1,0:T(8,128)S(1)} %collective-permute-done.10.refs_10_) | copy-start | bytes 245764
  179.0 3.4 %copy-start.14 = (f32[5,16,256]{2,1,0:T(8,128)}, f32[5,16,256]{2,1,0:T(8,128)S(1)}, u32[]{:S(2)}) copy-start(f32[5,16,256]{2,1,0:T(8,128)S(1)} %collective-permute-done.11.refs_11_) | copy-start | bytes 245764
  179.1 3.4 %copy-start.16 = (f32[5,16,256]{2,1,0:T(8,128)}, f32[5,16,256]{2,1,0:T(8,128)S(1)}, u32[]{:S(2)}) copy-start(f32[5,16,256]{2,1,0:T(8,128)S(1)} %collective-permute-done.8.refs_8_) | copy-start | bytes 245764
  182.5 0.6 copy-start.18
  192.1 11.0 %collective-permute-start.12 = (f32[5,16,256]{2,1,0:T(8,128)}, f32[5,16,256]{2,1,0:T(8,128)S(1)}, u32[]{:S(2)}, u32[]{:S(2)}) collective-permute-start(f32[5,16,256]{2,1,0:T(8,128)} %get-tuple-element.51), channel_id=1, source_target_pairs={{0,8},{8,16},{16,24},{1,9},{9,17},{17,25},{2,10},{10,18},{18,26},{... | collective-permute-start | bytes 245768 | tf_op jit(solution)/shard_map/ppermute | solution.py:364
  194.0 9.1 %collective-permute-start.13 = (f32[5,16,256]{2,1,0:T(8,128)}, f32[5,16,256]{2,1,0:T(8,128)S(1)}, u32[]{:S(2)}, u32[]{:S(2)}) collective-permute-start(f32[5,16,256]{2,1,0:T(8,128)} %get-tuple-element.52), channel_id=1, source_target_pairs={{8,0},{16,8},{24,16},{9,1},{17,9},{25,17},{10,2},{18,10},{26,18},{... | collective-permute-start | bytes 245768 | tf_op jit(solution)/shard_map/ppermute | solution.py:365
  196.4 7.0 %collective-permute-start.14 = (f32[5,16,256]{2,1,0:T(8,128)}, f32[5,16,256]{2,1,0:T(8,128)S(1)}, u32[]{:S(2)}, u32[]{:S(2)}) collective-permute-start(f32[5,16,256]{2,1,0:T(8,128)} %get-tuple-element.53), channel_id=1, source_target_pairs={{0,1},{1,2},{2,3},{3,4},{4,5},{5,6},{6,7},{8,9},{9,10},{10,11},{11... | collective-permute-start | bytes 245768 | tf_op jit(solution)/shard_map/ppermute | solution.py:364
  200.9 7.3 %collective-permute-start.15 = (f32[5,16,256]{2,1,0:T(8,128)}, f32[5,16,256]{2,1,0:T(8,128)S(1)}, u32[]{:S(2)}, u32[]{:S(2)}) collective-permute-start(f32[5,16,256]{2,1,0:T(8,128)} %get-tuple-element.54), channel_id=1, source_target_pairs={{1,0},{2,1},{3,2},{4,3},{5,4},{6,5},{7,6},{9,8},{10,9},{11,10},{12... | collective-permute-start | bytes 245768 | tf_op jit(solution)/shard_map/ppermute | solution.py:365
  203.1 5.2 %copy-start.13 = (f32[5,16,256]{2,1,0:T(8,128)}, f32[5,16,256]{2,1,0:T(8,128)S(1)}, u32[]{:S(2)}) copy-start(f32[5,16,256]{2,1,0:T(8,128)S(1)} %collective-permute-done.12.refs_8_) | copy-start | bytes 245764
  203.1 5.2 %copy-start.15 = (f32[5,16,256]{2,1,0:T(8,128)}, f32[5,16,256]{2,1,0:T(8,128)S(1)}, u32[]{:S(2)}) copy-start(f32[5,16,256]{2,1,0:T(8,128)S(1)} %collective-permute-done.13.refs_9_) | copy-start | bytes 245764
  203.3 4.9 %copy-start.17 = (f32[5,16,256]{2,1,0:T(8,128)}, f32[5,16,256]{2,1,0:T(8,128)S(1)}, u32[]{:S(2)}) copy-start(f32[5,16,256]{2,1,0:T(8,128)S(1)} %collective-permute-done.14.refs_10_) | copy-start | bytes 245764
  208.3 0.6 copy-start.19

commit v3 on v0

v3 whole, which is shorter than its diff:
```python
import jax
import jax.numpy as jnp
import numpy as np
from jax import lax
from jax.experimental import pallas as pl
from jax.experimental.pallas import tpu as pltpu
from jax.sharding import PartitionSpec as P

F32 = jnp.float32
BF16 = jnp.bfloat16
LANES = 128
MIB = 1024 * 1024
GROUP = 4


def in_vmem():
    return pl.BlockSpec(memory_space=pltpu.VMEM)


def in_smem():
    return pl.BlockSpec(memory_space=pltpu.SMEM)


def in_hbm():
    return pl.BlockSpec(memory_space=pl.ANY)


def sds(shape, dtype):
    return jax.ShapeDtypeStruct(shape, dtype)


def params(mib):
    return pltpu.CompilerParams(vmem_limit_bytes=mib * MIB)


def edge_lines(cells, scratch):
    nx, ny, nz = cells.shape
    flat = cells.reshape(nx * ny, nz)
    out = ([], [])
    for h in range(nz // LANES):
        scratch[h] = flat[:, h * LANES : (h + 1) * LANES]
        for side, first in enumerate((0, ny - 1)):
            out[side].append(scratch[h, pl.ds(first, nx, stride=ny), :])
    return [jnp.concatenate(o, axis=1) for o in out]


def copy_faces(src, outs, scratch, energy):
    group, nv, nx, ny, nz = src.shape

    def body(m, carry):
        outs[0][m] = src[m, :, 0]
        outs[1][m] = src[m, :, nx - 1]
        total = jnp.zeros((ny, nz), F32)
        for i in range(nv):
            cells = src[m, i].astype(F32)
            lo, hi = edge_lines(cells, scratch.at[i])
            outs[2][m, i] = lo.astype(BF16)
            outs[3][m, i] = hi.astype(BF16)
            if energy is not None:
                total = total + jnp.sum(cells * cells, axis=0)
        if energy is not None:
            line = jnp.sum(total, axis=0, keepdims=True)
            line = sum(line[:, h : h + LANES] for h in range(0, nz, LANES))
            energy[pl.ds(pl.program_id(0) * group + m, 1), :] = line
        return carry

    lax.fori_loop(0, group, body, 0)


def direct_kernel(src, xlo, xhi, ylo, yhi, energy, scratch):
    copy_faces(src, (xlo, xhi, ylo, yhi), scratch, energy)


def adjoint_kernel(steps, src, base, *refs):
    xlo, xhi, ylo, yhi = outs = refs[4:8]
    scratch = refs[8]
    nv, nx, ny, nz = base.shape

    @pl.when(pl.program_id(0) < steps)
    def _():
        copy_faces(src, outs, scratch, None)

    @pl.when(pl.program_id(0) == steps)
    def _():
        for j in range(nv):
            lines = [base[j, 0], base[j, nx - 1], *edge_lines(base[j], scratch.at[j])]
            for out, line in zip(outs, lines):
                for part in range(3):
                    rounded = line.astype(BF16)
                    out[part, j] = rounded
                    line = line - rounded.astype(F32)
                out[3, j] = jnp.zeros(out.shape[2:], BF16)


def face_spec(n, nv, nz, first):
    return pl.BlockSpec((GROUP, nv, n, nz), lambda s: (s + first, 0, 0, 0))


def pack(direct, adjoint, base):
    nm, nv, nx, ny, nz = direct.shape
    steps = nm // GROUP
    sizes = (ny, ny, nx, nx)
    shapes = [sds((2 * nm + GROUP, nv, n, nz), BF16) for n in sizes]
    block = (GROUP, nv, nx, ny, nz)
    scratch = [pltpu.VMEM((nv, nz // LANES, nx * ny, LANES), F32)]
    cost = pl.CostEstimate(flops=3 * direct.size, bytes_accessed=2 * direct.size, transcendentals=0)
    *partial, energy = pl.pallas_call(
        direct_kernel,
        grid=(steps,),
        in_specs=[pl.BlockSpec(block, lambda s: (s, 0, 0, 0, 0))],
        out_specs=[face_spec(n, nv, nz, 0) for n in sizes] + [pl.BlockSpec((nm, LANES), lambda s: (0, 0))],
        out_shape=shapes + [sds((nm, LANES), F32)],
        scratch_shapes=scratch,
        compiler_params=params(24),
        cost_estimate=cost,
        name="pack_direct",
    )(direct)
    full = pl.pallas_call(
        lambda *refs: adjoint_kernel(steps, *refs),
        grid=(steps + 1,),
        in_specs=[
            pl.BlockSpec(block, lambda s: (jnp.minimum(s, steps - 1), 0, 0, 0, 0)),
            pl.BlockSpec(base.shape, lambda s: (0, 0, 0, 0)),
        ]
        + [in_hbm()] * 4,
        out_specs=[face_spec(n, nv, nz, steps) for n in sizes],
        out_shape=shapes,
        input_output_aliases={2: 0, 3: 1, 4: 2, 5: 3},
        scratch_shapes=scratch,
        compiler_params=params(24),
        cost_estimate=cost,
        name="pack_adjoint",
    )(adjoint, base, *partial)
    return full, energy


def row_of(shape, n):
    return lax.broadcasted_iota(jnp.int32, shape, 0) % n


def diff_lanes(a):
    n = a.shape[-1]
    return pltpu.roll(a, n - 1, a.ndim - 1) - pltpu.roll(a, 1, a.ndim - 1)


def diff_rows(a, n, lo, hi):
    rows = a.shape[0]
    row = row_of(a.shape, n)
    return jnp.where(row == n - 1, hi, pltpu.roll(a, rows - 1, 0)) - jnp.where(row == 0, lo, pltpu.roll(a, 1, 0))


UNROLL = 4


def main_kernel(pick, amp, lw, u_hbm, q_hbm, out, u_buf, q_buf, acc, c0, u_sem, q_sem):
    nx, nm, nv, ny, nz = u_buf.shape
    rows = nv * ny

    def u_copy(p):
        return pltpu.make_async_copy(u_hbm.at[:, :, p], u_buf.at[p], u_sem.at[p])

    def q_copy(p):
        return pltpu.make_async_copy(q_hbm.at[:, :, p], q_buf.at[p], q_sem.at[p])

    for p in range(nx):
        u_copy(p).start()
        q_copy(p).start()
    c0[0] = jnp.zeros((rows, nz), F32)
    c0[nx + 1] = jnp.zeros((rows, nz), F32)
    u_copy(0).wait()

    def plane(p, carry):
        @pl.when(p < nx - 1)
        def _():
            u_copy(p + 1).wait()

        q_copy(p).wait()
        acc[...] = jnp.zeros_like(acc)
        below, above = jnp.maximum(p - 1, 0), jnp.minimum(p + 1, nx - 1)

        def body(step, carry):
            parts = [None] * 4
            for k in range(UNROLL):
                m = step * UNROLL + k
                qm = q_buf[p, pick[m]].reshape(rows, nz)
                u = u_buf[p, m].reshape(rows, nz)
                w = jnp.dot(lw[...], jnp.concatenate([qm, qm, u], axis=0), preferred_element_type=F32)
                w0, w1, w2, dy = (w[n * rows : (n + 1) * rows] for n in range(4))
                dx = u_buf[above, m].reshape(rows, nz).astype(F32) - u_buf[below, m].reshape(rows, nz).astype(F32)
                a = amp[m]
                uf = u.astype(F32)
                dz = diff_lanes(uf)
                uf = uf * a
                terms = [(dx * w0 + dy * w1 + dz * w2) * a, uf * w0, uf * w1, uf * w2]
                parts = [t if v is None else v + t for v, t in zip(parts, terms)]
            for n in range(4):
                acc[n] += parts[n]
            return carry

        lax.fori_loop(0, nm // UNROLL, body, 0)
        ends = jnp.where(p == 0, 1.0, 0.0) - jnp.where(p == nx - 1, 1.0, 0.0)
        c0[p + 1] = acc[1]
        h = acc[0] - diff_lanes(acc[3]) + ends * acc[1] - diff_rows(acc[2], ny, 0.0, 0.0)
        out[p] = h
        return carry

    lax.fori_loop(0, nx, plane, 0)

    def finish(p, carry):
        out[p] = out[p] - c0[p + 2] + c0[p]
        return carry

    lax.fori_loop(0, nx, finish, 0)


def main(pick, amp, lw, direct, adjoint):
    nm, nv, nx, ny, nz = direct.shape
    rows = nv * ny
    buf = pltpu.VMEM((nx, nm, nv, ny, nz), BF16)
    return pl.pallas_call(
        main_kernel,
        in_specs=[in_smem(), in_smem(), in_vmem(), in_hbm(), in_hbm()],
        out_specs=in_vmem(),
        out_shape=sds((nx, rows, nz), F32),
        scratch_shapes=[
            buf,
            buf,
            pltpu.VMEM((4, rows, nz), F32),
            pltpu.VMEM((nx + 2, rows, nz), F32),
            pltpu.SemaphoreType.DMA((nx,)),
            pltpu.SemaphoreType.DMA((nx,)),
        ],
        compiler_params=params(36),
        cost_estimate=pl.CostEstimate(flops=2 * nm * nx * 480 * 256 * 256, bytes_accessed=4 * direct.size, transcendentals=0),
        name="main",
    )(pick, amp, lw, direct, adjoint)


def weight_of(cells):
    return jnp.where(cells == 0, 1.0, jnp.where(cells == 1, 0.5, 0.0)).astype(F32)


def spread(ref, x, n):
    nv, _, nz = ref.shape
    return jnp.concatenate([jnp.broadcast_to(ref[j, pl.ds(x, 1), :], (n, nz)) for j in range(nv)], axis=0)


def write_lines(values, x, n, lo, hi):
    for j in range(lo.shape[0]):
        lo[j, pl.ds(x, 1), :] = values[j * n : j * n + 1]
        hi[j, pl.ds(x, 1), :] = values[(j + 1) * n - 1 : (j + 1) * n]


def boundary_kernel(scale, pick, amp, lw_x, lw_y, local, cell, *refs):
    own = refs[0:4]
    got = refs[4:8]
    field, xlo, xhi, ylo, yhi = refs[8:13]
    add = refs[13:17]
    nx, rows, nz = local.shape
    nm = (own[0].shape[0] - GROUP) // 2
    nv = own[0].shape[1]
    ny = rows // nv
    for f in range(4):
        add[f][...] = jnp.zeros_like(add[f])

    def body(step, carry):
        for k in range(2):
            m = step * 2 + k
            at = pick[m] + nm
            for f in range(4):
                n = nv * own[f].shape[2]
                outer = got[f][at].reshape(n, nz)
                inner = own[f][at].reshape(n, nz)
                lw = lw_x if f < 2 else lw_y
                diff = jnp.dot(lw[...], jnp.concatenate([outer, outer, inner, inner], axis=0), preferred_element_type=F32)
                add[f][...] += (amp[m] * got[f][m].reshape(n, nz).astype(F32) * diff).reshape(add[f].shape)
        return carry

    lax.fori_loop(0, nm // 2, body, 0)

    row = row_of((rows, nz), ny)

    def plane(x, carry):
        lo, hi = spread(add[2], x, ny), spread(add[3], x, ny)
        field[x] = local[x] + jnp.where(row == 0, lo, 0.0) - jnp.where(row == ny - 1, hi, 0.0)
        return carry

    lax.fori_loop(0, nx, plane, 0)
    field[0] += add[0][...].reshape(rows, nz)
    field[nx - 1] -= add[1][...].reshape(rows, nz)

    def weigh(x, carry):
        weight = weight_of(cell[x]) * scale
        g = field[x] * jnp.concatenate([weight] * nv, axis=0)
        field[x] = g
        write_lines(g, x, ny, ylo, yhi)
        return carry

    lax.fori_loop(0, nx, weigh, 0)
    xlo[...] = field[0].reshape(xlo.shape)
    xhi[...] = field[nx - 1].reshape(xhi.shape)


def boundary(scale, pick, amp, lw_x, lw_y, local, cell, own, got):
    nx, rows, nz = local.shape
    nv, ny = own[0].shape[1:3]
    face = [sds((nv, n, nz), F32) for n in (ny, ny, nx, nx)]
    return pl.pallas_call(
        lambda *refs: boundary_kernel(scale, *refs),
        in_specs=[in_smem()] * 2 + [in_vmem()] * 12,
        out_specs=[in_vmem()] * 5,
        out_shape=[sds(local.shape, F32)] + face,
        scratch_shapes=[pltpu.VMEM(f.shape, F32) for f in face],
        compiler_params=params(28),
        name="boundary",
    )(pick, amp, lw_x, lw_y, local, cell, *own, *got)


def mix_rows(lw, values):
    hi = values.astype(BF16)
    lo = (values - hi.astype(F32)).astype(BF16)
    return jnp.dot(lw, jnp.concatenate([hi, lo, hi], axis=0), preferred_element_type=F32)


def base_part(ref):
    n = ref.shape[0] - GROUP
    return ref[n].astype(F32) + (ref[n + 1].astype(F32) + ref[n + 2].astype(F32))


def step_kernel(last, lw, lw_y, base, cell, field, *refs):
    got_base = refs[0:4]
    got = refs[4:8]
    out = refs[8]
    faces = refs[9:13]
    b_pad, c0, bh_lo, bh_hi, ch_lo, ch_hi = refs[-6:]
    nv, nx, ny, nz = base.shape
    rows = nv * ny
    for f, at in ((0, 0), (1, nx + 1)):
        b = base_part(got_base[f]).reshape(rows, nz)
        b_pad[at] = b
        c0[at] = b * mix_rows(lw[:rows], got[f][...].reshape(rows, nz))
    for f, bh, ch in ((2, bh_lo, ch_lo), (3, bh_hi, ch_hi)):
        b = base_part(got_base[f])
        bh[...] = b
        ch[...] = b * mix_rows(lw_y[...], got[f][...].reshape(nv * nx, nz)).reshape(nv, nx, nz)

    def fill(x, carry):
        b_pad[x + 1] = base[:, x].reshape(rows, nz)
        return carry

    lax.fori_loop(0, nx, fill, 0)

    def plane(x, carry):
        w = mix_rows(lw[...], field[x])
        w0, w1, w2 = (w[n * rows : (n + 1) * rows] for n in range(3))
        b = b_pad[x + 1]
        c0[x + 1] = b * w0
        h = (b_pad[x + 2] - b_pad[x]) * w0
        h = h + diff_rows(b, ny, spread(bh_lo, x, ny), spread(bh_hi, x, ny)) * w1
        h = h - diff_rows(b * w1, ny, spread(ch_lo, x, ny), spread(ch_hi, x, ny))
        h = h + diff_lanes(b) * w2 - diff_lanes(b * w2)
        if last:
            out[:, x] = h.reshape(nv, ny, nz)
        else:
            out[x] = h
        return carry

    lax.fori_loop(0, nx, plane, 0)

    def finish(x, carry):
        change = c0[x] - c0[x + 2]
        if last:
            out[:, x] = out[:, x] + change.reshape(nv, ny, nz)
        else:
            g = (out[x] + change) * jnp.concatenate([weight_of(cell[x])] * nv, axis=0)
            out[x] = g
            write_lines(g, x, ny, faces[2], faces[3])
        return carry

    lax.fori_loop(0, nx, finish, 0)
    if not last:
        faces[0][...] = out[0].reshape(nv, ny, nz)
        faces[1][...] = out[nx - 1].reshape(nv, ny, nz)


def apply_step(last, lw, lw_y, base, cell, field, got_base, got):
    nv, nx, ny, nz = base.shape
    rows = nv * ny
    face = [] if last else [sds((nv, n, nz), F32) for n in (ny, ny, nx, nx)]
    line = pltpu.VMEM((nv, nx, nz), F32)
    padded = pltpu.VMEM((nx + 2, rows, nz), F32)
    return pl.pallas_call(
        lambda *refs: step_kernel(last, *refs),
        in_specs=[in_vmem()] * 13,
        out_specs=[in_vmem()] * (1 + len(face)),
        out_shape=[sds(base.shape if last else field.shape, F32)] + face,
        scratch_shapes=[padded, padded, line, line, line, line],
        compiler_params=params(28),
        name="step_two" if last else "step_one",
    )(lw, lw_y, base, cell, field, *got_base, *got)


def exchange(arrays):
    out = []
    for k, axis in enumerate(("chord", "normal")):
        count = lax.axis_size(axis)
        up = [(i, i + 1) for i in range(count - 1)]
        down = [(i + 1, i) for i in range(count - 1)]
        out.append(lax.ppermute(arrays[2 * k + 1], axis, up))
        out.append(lax.ppermute(arrays[2 * k], axis, down))
    return out


def sum_everywhere(values):
    for axis in ("chord", "normal"):
        count = lax.axis_size(axis)
        if count & (count - 1):
            values = lax.psum(values, axis)
            continue
        bit = 1
        while bit < count:
            values = values + lax.ppermute(values, axis, [(i, i ^ bit) for i in range(count)])
            bit *= 2
    return values


def kron_rows(mix, n):
    nv = mix.shape[1]
    hi = lax.reduce_precision(mix, 8, 7)
    lo = lax.reduce_precision(mix - hi, 8, 7)
    small = jnp.concatenate([hi.transpose(0, 2, 1), lo.transpose(0, 2, 1)], axis=2)
    rows, cols = np.arange(nv * n), np.arange(2 * nv * n)
    left = jnp.asarray((rows[:, None] // n == np.arange(nv)[None]).astype(np.float32))
    right = jnp.asarray((cols[None] // n == np.arange(2 * nv)[:, None]).astype(np.float32))
    mask = jnp.asarray((rows[:, None] % n == cols[None] % n).astype(np.float32))
    wide = jnp.einsum("rj,djc,ck->drk", left, small, right, precision=lax.Precision.HIGHEST)
    return (wide * mask).astype(BF16)


def main_rows(lw, nv, ny):
    dy = np.kron(np.eye(nv, dtype=np.float32), np.eye(ny, k=1, dtype=np.float32) - np.eye(ny, k=-1, dtype=np.float32))
    rows = nv * ny
    top = jnp.pad(lw.reshape(3 * rows, 2 * rows), ((0, 0), (0, rows)))
    return jnp.concatenate([top, jnp.pad(jnp.asarray(dy, BF16), ((0, 0), (2 * rows, 0)))], axis=0)


def step_rows(lw):
    half = lw.shape[-1] // 2
    return jnp.concatenate([lw[..., :half], lw[..., :half], lw[..., half:]], axis=-1)


def per_device(direct, adjoint, base, cell, pick, mix):
    nm, nv, nx, ny, nz = direct.shape
    cells_all = nv * nx * ny * nz * lax.axis_size("chord") * lax.axis_size("normal")
    own, sums = pack(direct, adjoint, base)
    energy = sum_everywhere(jnp.sum(sums, axis=1)) / cells_all
    got = exchange(own)
    amp = lax.rsqrt(energy + 1e-06)
    lw_y = kron_rows(mix, ny)
    lw_x = lw_y if nx == ny else kron_rows(mix, nx)
    local = main(pick, amp, main_rows(lw_y, nv, ny), direct, adjoint)
    across = [jnp.concatenate([lw, -lw], axis=1) for lw in (lw_y[0], lw_x[1])]
    field, *sides = boundary(1.0 / nm, pick, amp, *across, local, cell, own, got)
    lw_step = step_rows(lw_y.reshape(3 * nv * ny, -1))
    lw_line = step_rows(lw_x[1])
    field, *sides = apply_step(False, lw_step, lw_line, base, cell, field, got, exchange(sides))
    return apply_step(True, lw_step, lw_line, base, cell, field, got, exchange(sides))[0]


def solution(mesh):
    return jax.shard_map(
        per_device,
        mesh=mesh,
        in_specs=(
            P(None, None, "chord", "normal", None),
            P(None, None, "chord", "normal", None),
            P(None, "chord", "normal", None),
            P("chord", "normal", None),
            P(),
            P(),
        ),
        out_specs=P(None, "chord", "normal", None),
        check_vma=False,
    )
```

time: 919 us -> 184 us (0.20)
  other arithmetic: 277 us -> 0.47 us
  matrix products: 247 us -> 0.62 us
  local copies, waits for them, and re-layouts: 235 us -> 12.1 us
  Pallas kernels: 0 us -> 59 us
  waiting for transfers between devices: 21.3 us -> 70.8 us
  blocking collectives: 37.9 us -> 0 us
  loops' own time: 32 us -> 0 us
  starting transfers between devices: 59.2 us -> 39 us
    dot_general x54 -> x2, matrix products: 247 us -> 0.62 us  [kron_rows(): jnp.einsum('rj,djc,ck->drk', left, small, right, precision=lax.Precision....]
    add x16 -> x4, other arithmetic: 214 us -> 0.01 us  [sum_everywhere(): values + lax.ppermute(values, axis, [(i, i ^ bit) for i in range(count)])]
    slice x46 -> x2, local copies, waits for them, and re-layouts: 135 us -> 0.01 us  [step_rows(): lw[..., :half]]
    unnamed x49 -> x22, local copies, waits for them, and re-layouts: 73 us -> 12.1 us
    pallas_call x0 -> x6, Pallas kernels: none -> 59 us  [the longest x1 34 us: main(): pl.pallas_call(main_kernel, in_specs=[in_smem(), in_smem(), in_vmem(), in...]
    ppermute x20 -> x17, waiting for transfers between devices: 21.3 us -> 70.8 us  [the longest x5 62.9 us: sum_everywhere(): lax.ppermute(values, axis, [(i, i ^ bit) for i in range(count)])]
    psum x1 -> x0, blocking collectives: 37.9 us -> none  [per_device(): energy = lax.psum(local_sums, ('chord', 'normal')) / cells_all]
    another operation x1 -> x0, loops' own time: 32 us -> none  [per_device(): lax.fori_loop(0, modes_count, accumulate, zeros_field) / modes_count]
  transfers between devices with their start and end apart: 20 -> 17, of which waited for: 7 -> 7; matrix products, arithmetic and copies ran while one was open for 79% -> 1% of each run, Pallas kernels for 0% -> 21%
where the time goes in v3:
time: 184 us; the launch traced here: 182 us
  waiting for transfers between devices  70.8 us (38%)
  Pallas kernels  59 us (32%)
  starting transfers between devices  39 us (21%)
  local copies, waits for them, and re-layouts  12.1 us (7%)
    ppermute x5, waiting for transfers between devices, sum_everywhere(): lax.ppermute(values, axis, [(i, i ^ bit) for i in range(count)])  62.9 us
    pallas_call x1, Pallas kernels, main(): pl.pallas_call(main_kernel, in_specs=[in_smem(), in_smem(), in_vmem(), in...  34 us
    ppermute x6, starting transfers between devices, exchange(): out.append(lax.ppermute(arrays[2 * k + 1], axis, up))  21.6 us
    ppermute x6, starting transfers between devices, exchange(): out.append(lax.ppermute(arrays[2 * k], axis, down))  13 us
    unnamed x22, local copies, waits for them, and re-layouts  12.1 us
    pallas_call x2, Pallas kernels, apply_step(): pl.pallas_call(lambda *refs: step_kernel(last, *refs), in_specs=[in_vmem(...  11.8 us
    ppermute x6, waiting for transfers between devices, exchange(): out.append(lax.ppermute(arrays[2 * k], axis, down))  7.56 us
    pallas_call x1, Pallas kernels, boundary(): pl.pallas_call(lambda *refs: boundary_kernel(scale, *refs), in_specs=[in_...  6.24 us
  transfers between devices with their start and end apart: 17, of which 7 were waited for; matrix products, arithmetic and copies ran while one was open for 1% of the time, Pallas kernels for 21%

profile of v3, /device:TPU:5, one launch (start us, length us, event | category | flops | bytes accessed | tf_op | source)
XLA Modules:
  0.0 182.4 jit_solution(17529868528954472311)
XLA Ops:
  0.0 0.0 copy-start
  0.0 0.0 copy-start.1
  0.0 4.1 %copy-done.1 = bf16[16,5,16,16,256]{4,3,2,1,0:T(8,128)(2,1)S(1)} copy-done((bf16[16,5,16,16,256]{4,3,2,1,0:T(8,128)(2,1)S(1)}, bf16[16,5,16,16,256]{4,3,2,1,0:T(8,128)(2,1)}, u32[]{:S(2)}) %copy-start.1) | copy-done | bytes 10485784
  4.1 3.4 %pack_direct.1 = (bf16[36,5,16,256]{3,2,1,0:T(8,128)(2,1)S(1)}, bf16[36,5,16,256]{3,2,1,0:T(8,128)(2,1)}, bf16[36,5,16,256]{3,2,1,0:T(8,128)(2,1)}, bf16[36,5,16,256]{3,2,1,0:T(8,128)(2,1)}, f32[16,128]{1,0:T(8,128)S(1)}) custom-call(bf16[16,5,16,16,256]{4,3,2,1,0:T(8,128)(2,1)S(1)} %copy-done.1), custom_call_target="tpu_custom_call" | custom-call | flops 15728640 | bytes 10485760 | tf_op jit(solution)/shard_map/pack_direct/pallas_call | solution.py:107
  7.5 0.1 reduce_sum.9
  7.6 0.7 collective-permute-start
  8.3 0.0 copy-done
  8.3 0.0 copy-start.3
  8.3 4.0 %copy-done.3 = bf16[16,5,16,16,256]{4,3,2,1,0:T(8,128)(2,1)S(1)} copy-done((bf16[16,5,16,16,256]{4,3,2,1,0:T(8,128)(2,1)S(1)}, bf16[16,5,16,16,256]{4,3,2,1,0:T(8,128)(2,1)}, u32[]{:S(2)}) %copy-start.3) | copy-done | bytes 10485784
  12.3 0.0 copy-start.9
  12.3 0.0 copy-start.8
  12.3 0.0 copy-start.7
  12.3 3.6 %pack_adjoint.1 = (bf16[36,5,16,256]{3,2,1,0:T(8,128)(2,1)S(1)}, bf16[36,5,16,256]{3,2,1,0:T(8,128)(2,1)}, bf16[36,5,16,256]{3,2,1,0:T(8,128)(2,1)}, bf16[36,5,16,256]{3,2,1,0:T(8,128)(2,1)}) custom-call(bf16[16,5,16,16,256]{4,3,2,1,0:T(8,128)(2,1)S(1)} %copy-done.3, ...), custom_call_target="tpu_custom_call", output_to_operand_aliasing={{0}: (2, {}), {1}: (3, {}), {2}: (4, {}), {3}: (5, {})} | custom-call | flops 15728640 | bytes 10485760 | tf_op jit(solution)/shard_map/pack_adjoint/pallas_call | solution.py:118
  15.9 2.1 %collective-permute-start.6 = (bf16[36,5,16,256]{3,2,1,0:T(8,128)(2,1)S(1)}, bf16[36,5,16,256]{3,2,1,0:T(8,128)(2,1)S(1)}, u32[]{:S(2)}, u32[]{:S(2)}) collective-permute-start(bf16[36,5,16,256]{3,2,1,0:T(8,128)(2,1)S(1)} %get-tuple-element.29.refs_6_), channel_id=1, source_target_pairs={{8,0},{16,8},{24,16},{9,1},{17,9},{25,17},{10,2},{18,10},{26,18},{... | collective-permute-start | bytes 4423688 | tf_op jit(solution)/shard_map/ppermute | solution.py:410
  18.0 3.6 %collective-permute-start.5 = (bf16[36,5,16,256]{3,2,1,0:T(8,128)(2,1)}, bf16[36,5,16,256]{3,2,1,0:T(8,128)(2,1)S(1)}, u32[]{:S(2)}, u32[]{:S(2)}) collective-permute-start(bf16[36,5,16,256]{3,2,1,0:T(8,128)(2,1)} %get-tuple-element.30.refs_7_), channel_id=1, source_target_pairs={{0,8},{8,16},{16,24},{1,9},{9,17},{17,25},{2,10},{10,18},{18,26},{... | collective-permute-start | bytes 4423688 | tf_op jit(solution)/shard_map/ppermute | solution.py:409
  21.6 1.9 %collective-permute-start.8 = (bf16[36,5,16,256]{3,2,1,0:T(8,128)(2,1)}, bf16[36,5,16,256]{3,2,1,0:T(8,128)(2,1)S(1)}, u32[]{:S(2)}, u32[]{:S(2)}) collective-permute-start(bf16[36,5,16,256]{3,2,1,0:T(8,128)(2,1)} %get-tuple-element.31.refs_8_), channel_id=1, source_target_pairs={{1,0},{2,1},{3,2},{4,3},{5,4},{6,5},{7,6},{9,8},{10,9},{11,10},{12... | collective-permute-start | bytes 4423688 | tf_op jit(solution)/shard_map/ppermute | solution.py:410
  23.6 4.3 %collective-permute-start.7 = (bf16[36,5,16,256]{3,2,1,0:T(8,128)(2,1)}, bf16[36,5,16,256]{3,2,1,0:T(8,128)(2,1)S(1)}, u32[]{:S(2)}, u32[]{:S(2)}) collective-permute-start(bf16[36,5,16,256]{3,2,1,0:T(8,128)(2,1)} %get-tuple-element.32.refs_9_), channel_id=1, source_target_pairs={{0,1},{1,2},{2,3},{3,4},{4,5},{5,6},{6,7},{8,9},{9,10},{10,11},{11... | collective-permute-start | bytes 4423688 | tf_op jit(solution)/shard_map/ppermute | solution.py:409
  27.8 0.0 copy-done.9
  27.9 0.0 copy-done.8
  27.9 0.2 fusion.4
  28.1 0.0 copy-done.6
  28.1 0.0 copy-done.10
  28.1 0.4 fusion.1
  28.6 0.0 copy-done.7
  28.6 0.0 collective-permute-done
  28.6 0.1 collective-permute-start.1
  28.7 9.5 %collective-permute-done.1 = f32[16]{0:T(128)S(1)} collective-permute-done((f32[16]{0:T(128)S(1)}, f32[16]{0:T(128)S(1)}, u32[]{:S(2)}, u32[]{:S(2)}) %collective-permute-start.1) | collective-permute-done | bytes 96 | tf_op jit(solution)/shard_map/ppermute | solution.py:422
  38.2 0.0 collective-permute-start.2
  38.3 0.1 pad_maximum_fusion.refs_0_
  38.4 51.5 %collective-permute-done.2 = f32[16]{0:T(128)S(1)} collective-permute-done((f32[16]{0:T(128)S(1)}, f32[16]{0:T(128)S(1)}, u32[]{:S(2)}, u32[]{:S(2)}) %collective-permute-start.2) | collective-permute-done | bytes 96 | tf_op jit(solution)/shard_map/ppermute | solution.py:422
  89.8 1.3 collective-permute-start.3
  91.2 0.1 pad_maximum_fusion.1
  91.2 1.0 collective-permute-done.3
  92.2 2.3 %collective-permute-start.4 = (f32[16]{0:T(128)S(1)}, f32[16]{0:T(128)S(1)}, u32[]{:S(2)}, u32[]{:S(2)}) collective-permute-start(f32[16]{0:T(128)S(1)} %add.25), channel_id=1, source_target_pairs={{0,4},{1,5},{2,6},{3,7},{4,0},{5,1},{6,2},{7,3},{8,12},{9,13},{10,... | collective-permute-start | bytes 200 | tf_op jit(solution)/shard_map/ppermute | solution.py:422
  94.6 0.9 collective-permute-done.4
  95.5 0.0 copy-done.5
  95.5 0.0 copy-start.2
  95.5 4.0 %copy-done.2 = bf16[16,5,16,16,256]{4,3,2,1,0:T(8,128)(2,1)S(1)} copy-done((bf16[16,5,16,16,256]{4,3,2,1,0:T(8,128)(2,1)S(1)}, bf16[16,5,16,16,256]{4,3,2,1,0:T(8,128)(2,1)}, u32[]{:S(2)}) %copy-start.2) | copy-done | bytes 10485784
  99.5 34.0 %main.1.refs_4_ = f32[16,80,256]{2,1,0:T(8,128)S(1)} custom-call(s32[16]{0:T(128)S(1)} %copy-done.5, f32[16]{0:T(128)S(1)} %add_rsqrt_fusion.amp.refs_1_, bf16[320,240]{1,0:T(8,128)(2,1)S(1)} %fusion.3.lw, bf16[16,5,16,16,256]{4,3,2,1,0:T(8,128)(2,1)S(1)} %copy-done.2, bf16[16,5,16,16,256]{4,3,2,1,0:T(8,128)(2,1)} %refs_0_.2), custom_call_target="tpu_custom_call" | custom-call | flops 16106127360 | bytes 20971520 | tf_op jit(solution)/shard_map/main/pallas_call | solution.py:220
  133.5 0.0 collective-permute-done.6.refs_11_.refs_6_
  133.5 0.0 collective-permute-done.5.refs_10_.refs_5_
  133.5 0.0 collective-permute-done.8.refs_13_.refs_8_
  133.5 0.0 collective-permute-done.7.refs_12_.refs_7_
  133.6 0.0 copy-done.4
  133.6 6.2 %boundary.1 = (f32[16,80,256]{2,1,0:T(8,128)S(1)}, f32[5,16,256]{2,1,0:T(8,128)S(1)}, f32[5,16,256]{2,1,0:T(8,128)S(1)}, f32[5,16,256]{2,1,0:T(8,128)S(1)}, f32[5,16,256]{2,1,0:T(8,128)S(1)}) custom-call(s32[16]{0:T(128)S(1)} %copy-done.5, f32[16]{0:T(128)S(1)} %add_rsqrt_fusion.amp.refs_1_, bf16[80,320]{1,0:T(8,128)(2,1)S(1)} %get-tuple-element.49.refs_2_, ...), custom_call_target="tpu_custom_call" | custom-call | tf_op jit(solution)/shard_map/boundary/pallas_call | solution.py:308
  139.8 4.2 %collective-permute-start.9 = (f32[5,16,256]{2,1,0:T(8,128)S(1)}, f32[5,16,256]{2,1,0:T(8,128)S(1)}, u32[]{:S(2)}, u32[]{:S(2)}) collective-permute-start(f32[5,16,256]{2,1,0:T(8,128)S(1)} %get-tuple-element.34), channel_id=1, source_target_pairs={{0,8},{8,16},{16,24},{1,9},{9,17},{17,25},{2,10},{10,18},{18,26},{... | collective-permute-start | bytes 245768 | tf_op jit(solution)/shard_map/ppermute | solution.py:409
  144.1 1.9 %collective-permute-start.10 = (f32[5,16,256]{2,1,0:T(8,128)S(1)}, f32[5,16,256]{2,1,0:T(8,128)S(1)}, u32[]{:S(2)}, u32[]{:S(2)}) collective-permute-start(f32[5,16,256]{2,1,0:T(8,128)S(1)} %get-tuple-element.35), channel_id=1, source_target_pairs={{8,0},{16,8},{24,16},{9,1},{17,9},{25,17},{10,2},{18,10},{26,18},{... | collective-permute-start | bytes 245768 | tf_op jit(solution)/shard_map/ppermute | solution.py:410
  146.0 2.2 %collective-permute-start.11 = (f32[5,16,256]{2,1,0:T(8,128)S(1)}, f32[5,16,256]{2,1,0:T(8,128)S(1)}, u32[]{:S(2)}, u32[]{:S(2)}) collective-permute-start(f32[5,16,256]{2,1,0:T(8,128)S(1)} %get-tuple-element.36), channel_id=1, source_target_pairs={{0,1},{1,2},{2,3},{3,4},{4,5},{5,6},{6,7},{8,9},{9,10},{10,11},{11... | collective-permute-start | bytes 245768 | tf_op jit(solution)/shard_map/ppermute | solution.py:409
  148.2 3.0 %collective-permute-start.12 = (f32[5,16,256]{2,1,0:T(8,128)S(1)}, f32[5,16,256]{2,1,0:T(8,128)S(1)}, u32[]{:S(2)}, u32[]{:S(2)}) collective-permute-start(f32[5,16,256]{2,1,0:T(8,128)S(1)} %get-tuple-element.37), channel_id=1, source_target_pairs={{1,0},{2,1},{3,2},{4,3},{5,4},{6,5},{7,6},{9,8},{10,9},{11,10},{12... | collective-permute-start | bytes 245768 | tf_op jit(solution)/shard_map/ppermute | solution.py:410
  151.3 0.1 pad_maximum_fusion.3.refs_1_
  151.4 0.0 collective-permute-done.9.refs_9_
  151.4 0.0 collective-permute-done.10.refs_10_
  151.4 0.3 collective-permute-done.11.refs_11_
  151.7 3.6 %collective-permute-done.12.refs_12_ = f32[5,16,256]{2,1,0:T(8,128)S(1)} collective-permute-done((f32[5,16,256]{2,1,0:T(8,128)S(1)}, f32[5,16,256]{2,1,0:T(8,128)S(1)}, u32[]{:S(2)}, u32[]{:S(2)}) %collective-permute-start.12) | collective-permute-done | bytes 81952 | tf_op jit(solution)/shard_map/ppermute | solution.py:410
  155.4 5.5 %step_one.1 = (f32[16,80,256]{2,1,0:T(8,128)S(1)}, f32[5,16,256]{2,1,0:T(8,128)S(1)}, f32[5,16,256]{2,1,0:T(8,128)S(1)}, f32[5,16,256]{2,1,0:T(8,128)S(1)}, f32[5,16,256]{2,1,0:T(8,128)S(1)}) custom-call(bf16[240,240]{1,0:T(8,128)(2,1)S(1)} %pad_maximum_fusion.refs_0_, bf16[80,240]{1,0:T(8,128)(2,1)S(1)} %pad_maximum_fusion.3.refs_1_, ...), custom_call_target="tpu_custom_call" | custom-call | tf_op jit(solution)/shard_map/step_one/pallas_call | solution.py:392
  160.8 4.0 %collective-permute-start.13 = (f32[5,16,256]{2,1,0:T(8,128)S(1)}, f32[5,16,256]{2,1,0:T(8,128)S(1)}, u32[]{:S(2)}, u32[]{:S(2)}) collective-permute-start(f32[5,16,256]{2,1,0:T(8,128)S(1)} %get-tuple-element.39), channel_id=1, source_target_pairs={{0,8},{8,16},{16,24},{1,9},{9,17},{17,25},{2,10},{10,18},{18,26},{... | collective-permute-start | bytes 245768 | tf_op jit(solution)/shard_map/ppermute | solution.py:409
  164.9 1.9 %collective-permute-start.14 = (f32[5,16,256]{2,1,0:T(8,128)S(1)}, f32[5,16,256]{2,1,0:T(8,128)S(1)}, u32[]{:S(2)}, u32[]{:S(2)}) collective-permute-start(f32[5,16,256]{2,1,0:T(8,128)S(1)} %get-tuple-element.40), channel_id=1, source_target_pairs={{8,0},{16,8},{24,16},{9,1},{17,9},{25,17},{10,2},{18,10},{26,18},{... | collective-permute-start | bytes 245768 | tf_op jit(solution)/shard_map/ppermute | solution.py:410
  166.8 3.1 %collective-permute-start.15 = (f32[5,16,256]{2,1,0:T(8,128)S(1)}, f32[5,16,256]{2,1,0:T(8,128)S(1)}, u32[]{:S(2)}, u32[]{:S(2)}) collective-permute-start(f32[5,16,256]{2,1,0:T(8,128)S(1)} %get-tuple-element.41), channel_id=1, source_target_pairs={{0,1},{1,2},{2,3},{3,4},{4,5},{5,6},{6,7},{8,9},{9,10},{10,11},{11... | collective-permute-start | bytes 245768 | tf_op jit(solution)/shard_map/ppermute | solution.py:409
  170.0 2.1 %collective-permute-start.16 = (f32[5,16,256]{2,1,0:T(8,128)S(1)}, f32[5,16,256]{2,1,0:T(8,128)S(1)}, u32[]{:S(2)}, u32[]{:S(2)}) collective-permute-start(f32[5,16,256]{2,1,0:T(8,128)S(1)} %get-tuple-element.42), channel_id=1, source_target_pairs={{1,0},{2,1},{3,2},{4,3},{5,4},{6,5},{7,6},{9,8},{10,9},{11,10},{12... | collective-permute-start | bytes 245768 | tf_op jit(solution)/shard_map/ppermute | solution.py:410
  172.1 0.0 collective-permute-done.13.refs_9_
  172.1 0.0 collective-permute-done.14.refs_10_
  172.1 0.0 collective-permute-done.15.refs_11_
  172.1 3.9 %collective-permute-done.16.refs_12_ = f32[5,16,256]{2,1,0:T(8,128)S(1)} collective-permute-done((f32[5,16,256]{2,1,0:T(8,128)S(1)}, f32[5,16,256]{2,1,0:T(8,128)S(1)}, u32[]{:S(2)}, u32[]{:S(2)}) %collective-permute-start.16) | collective-permute-done | bytes 81952 | tf_op jit(solution)/shard_map/ppermute | solution.py:410
  176.0 6.3 %step_two.1 = f32[5,16,16,256]{3,2,1,0:T(8,128)} custom-call(bf16[240,240]{1,0:T(8,128)(2,1)S(1)} %pad_maximum_fusion.refs_0_, bf16[80,240]{1,0:T(8,128)(2,1)S(1)} %pad_maximum_fusion.3.refs_1_, f32[5,16,16,256]{3,2,1,0:T(8,128)S(1)} %copy-done, s32[16,16,256]{2,1,0:T(8,128)S(1)} %copy-done.4, f32[16,80,256]{2,1,0:T(8,128)S(1)} %get-tuple-element.38.refs_4_, ...), custom_call_target="tpu_custom_call" | custom-call | tf_op jit(solution)/shard_map/step_two/pallas_call | solution.py:392
  (16 shorter events, 0.1 us)
Async XLA Ops:
  0.0 8.3 %copy-start = (f32[5,16,16,256]{3,2,1,0:T(8,128)S(1)}, f32[5,16,16,256]{3,2,1,0:T(8,128)}, u32[]{:S(2)}) copy-start(f32[5,16,16,256]{3,2,1,0:T(8,128)} %refs_2_.3) | copy-start | bytes 3932164
  0.0 4.1 %copy-start.1 = (bf16[16,5,16,16,256]{4,3,2,1,0:T(8,128)(2,1)S(1)}, bf16[16,5,16,16,256]{4,3,2,1,0:T(8,128)(2,1)}, u32[]{:S(2)}) copy-start(bf16[16,5,16,16,256]{4,3,2,1,0:T(8,128)(2,1)} %u_hbm.1) | copy-start | bytes 31457284
  7.6 21.0 %collective-permute-start = (f32[16]{0:T(128)S(1)}, f32[16]{0:T(128)S(1)}, u32[]{:S(2)}, u32[]{:S(2)}) collective-permute-start(f32[16]{0:T(128)S(1)} %reduce_sum.9), channel_id=1, source_target_pairs={{0,8},{8,0},{16,24},{24,16},{1,9},{9,1},{17,25},{25,17},{2,10},{10... | collective-permute-start | bytes 200 | tf_op jit(solution)/shard_map/ppermute | solution.py:422
  8.3 4.0 %copy-start.3 = (bf16[16,5,16,16,256]{4,3,2,1,0:T(8,128)(2,1)S(1)}, bf16[16,5,16,16,256]{4,3,2,1,0:T(8,128)(2,1)}, u32[]{:S(2)}) copy-start(bf16[16,5,16,16,256]{4,3,2,1,0:T(8,128)(2,1)} %refs_0_.2) | copy-start | bytes 31457284
  12.3 15.5 %copy-start.9 = (f32[3,5,5]{2,0,1:T(4,128)S(1)}, f32[3,5,5]{2,0,1:T(4,128)}, u32[]{:S(2)}) copy-start(f32[3,5,5]{2,0,1:T(4,128)} %param.15) | copy-start | bytes 904
  12.3 15.6 %copy-start.8 = (f32[10,160,1]{1,0,2:T(8,128)S(1)}, f32[10,160,1]{1,0,2:T(8,128)}, u32[]{:S(2)}) copy-start(f32[10,160,1]{1,0,2:T(8,128)} %constant.27) | copy-start | bytes 19204
  12.3 15.8 %copy-start.6 = (f32[80,160]{1,0:T(8,128)S(1)}, f32[80,160]{1,0:T(8,128)}, u32[]{:S(2)}) copy-start(f32[80,160]{1,0:T(8,128)} %constant.20.clone) | copy-start | bytes 153604
  12.3 15.8 %copy-start.10 = (f32[80,5,1]{0,1,2:T(8,128)S(1)}, f32[80,5,1]{0,1,2:T(8,128)}, u32[]{:S(2)}) copy-start(f32[80,5,1]{0,1,2:T(8,128)} %constant.28) | copy-start | bytes 4804
  12.3 16.2 %copy-start.7 = (bf16[80,240]{1,0:T(8,128)(2,1)S(1)}, bf16[80,240]{1,0:T(8,128)(2,1)}, u32[]{:S(2)}) copy-start(bf16[80,240]{1,0:T(8,128)(2,1)} %constant.26) | copy-start | bytes 115204
  15.9 79.6 %copy-start.5 = (s32[16]{0:T(128)S(1)}, s32[16]{0:T(128)}, u32[]{:S(2)}) copy-start(s32[16]{0:T(128)} %refs_0_.3) | copy-start | bytes 196
  15.9 117.6 %collective-permute-start.6 = (bf16[36,5,16,256]{3,2,1,0:T(8,128)(2,1)S(1)}, bf16[36,5,16,256]{3,2,1,0:T(8,128)(2,1)S(1)}, u32[]{:S(2)}, u32[]{:S(2)}) collective-permute-start(bf16[36,5,16,256]{3,2,1,0:T(8,128)(2,1)S(1)} %get-tuple-element.29.refs_6_), channel_id=1, source_target_pairs={{8,0},{16,8},{24,16},{9,1},{17,9},{25,17},{10,2},{18,10},{26,18},{... | collective-permute-start | bytes 4423688 | tf_op jit(solution)/shard_map/ppermute | solution.py:410
  18.0 115.5 %collective-permute-start.5 = (bf16[36,5,16,256]{3,2,1,0:T(8,128)(2,1)}, bf16[36,5,16,256]{3,2,1,0:T(8,128)(2,1)S(1)}, u32[]{:S(2)}, u32[]{:S(2)}) collective-permute-start(bf16[36,5,16,256]{3,2,1,0:T(8,128)(2,1)} %get-tuple-element.30.refs_7_), channel_id=1, source_target_pairs={{0,8},{8,16},{16,24},{1,9},{9,17},{17,25},{2,10},{10,18},{18,26},{... | collective-permute-start | bytes 4423688 | tf_op jit(solution)/shard_map/ppermute | solution.py:409
  21.6 111.9 %collective-permute-start.8 = (bf16[36,5,16,256]{3,2,1,0:T(8,128)(2,1)}, bf16[36,5,16,256]{3,2,1,0:T(8,128)(2,1)S(1)}, u32[]{:S(2)}, u32[]{:S(2)}) collective-permute-start(bf16[36,5,16,256]{3,2,1,0:T(8,128)(2,1)} %get-tuple-element.31.refs_8_), channel_id=1, source_target_pairs={{1,0},{2,1},{3,2},{4,3},{5,4},{6,5},{7,6},{9,8},{10,9},{11,10},{12... | collective-permute-start | bytes 4423688 | tf_op jit(solution)/shard_map/ppermute | solution.py:410
  23.6 110.0 %collective-permute-start.7 = (bf16[36,5,16,256]{3,2,1,0:T(8,128)(2,1)}, bf16[36,5,16,256]{3,2,1,0:T(8,128)(2,1)S(1)}, u32[]{:S(2)}, u32[]{:S(2)}) collective-permute-start(bf16[36,5,16,256]{3,2,1,0:T(8,128)(2,1)} %get-tuple-element.32.refs_9_), channel_id=1, source_target_pairs={{0,1},{1,2},{2,3},{3,4},{4,5},{5,6},{6,7},{8,9},{9,10},{10,11},{11... | collective-permute-start | bytes 4423688 | tf_op jit(solution)/shard_map/ppermute | solution.py:409
  28.6 9.6 %collective-permute-start.1 = (f32[16]{0:T(128)S(1)}, f32[16]{0:T(128)S(1)}, u32[]{:S(2)}, u32[]{:S(2)}) collective-permute-start(f32[16]{0:T(128)S(1)} %add.22), channel_id=1, source_target_pairs={{0,16},{8,24},{16,0},{24,8},{1,17},{9,25},{17,1},{25,9},{2,18},{10... | collective-permute-start | bytes 200 | tf_op jit(solution)/shard_map/ppermute | solution.py:422
  38.2 51.6 %collective-permute-start.2 = (f32[16]{0:T(128)S(1)}, f32[16]{0:T(128)S(1)}, u32[]{:S(2)}, u32[]{:S(2)}) collective-permute-start(f32[16]{0:T(128)S(1)} %add.23), channel_id=1, source_target_pairs={{0,1},{1,0},{2,3},{3,2},{4,5},{5,4},{6,7},{7,6},{8,9},{9,8},{10,11... | collective-permute-start | bytes 200 | tf_op jit(solution)/shard_map/ppermute | solution.py:422
  89.8 2.4 %collective-permute-start.3 = (f32[16]{0:T(128)S(1)}, f32[16]{0:T(128)S(1)}, u32[]{:S(2)}, u32[]{:S(2)}) collective-permute-start(f32[16]{0:T(128)S(1)} %add.24), channel_id=1, source_target_pairs={{0,2},{1,3},{2,0},{3,1},{4,6},{5,7},{6,4},{7,5},{8,10},{9,11},{10,... | collective-permute-start | bytes 200 | tf_op jit(solution)/shard_map/ppermute | solution.py:422
  92.2 3.3 %collective-permute-start.4 = (f32[16]{0:T(128)S(1)}, f32[16]{0:T(128)S(1)}, u32[]{:S(2)}, u32[]{:S(2)}) collective-permute-start(f32[16]{0:T(128)S(1)} %add.25), channel_id=1, source_target_pairs={{0,4},{1,5},{2,6},{3,7},{4,0},{5,1},{6,2},{7,3},{8,12},{9,13},{10,... | collective-permute-start | bytes 200 | tf_op jit(solution)/shard_map/ppermute | solution.py:422
  95.5 4.0 %copy-start.2 = (bf16[16,5,16,16,256]{4,3,2,1,0:T(8,128)(2,1)S(1)}, bf16[16,5,16,16,256]{4,3,2,1,0:T(8,128)(2,1)}, u32[]{:S(2)}) copy-start(bf16[16,5,16,16,256]{4,3,2,1,0:T(8,128)(2,1)} %u_hbm.1) | copy-start | bytes 31457284
  99.5 34.1 %copy-start.4 = (s32[16,16,256]{2,1,0:T(8,128)S(1)}, s32[16,16,256]{2,1,0:T(8,128)}, u32[]{:S(2)}) copy-start(s32[16,16,256]{2,1,0:T(8,128)} %refs_3_.3) | copy-start | bytes 786436
  139.8 11.6 %collective-permute-start.9 = (f32[5,16,256]{2,1,0:T(8,128)S(1)}, f32[5,16,256]{2,1,0:T(8,128)S(1)}, u32[]{:S(2)}, u32[]{:S(2)}) collective-permute-start(f32[5,16,256]{2,1,0:T(8,128)S(1)} %get-tuple-element.34), channel_id=1, source_target_pairs={{0,8},{8,16},{16,24},{1,9},{9,17},{17,25},{2,10},{10,18},{18,26},{... | collective-permute-start | bytes 245768 | tf_op jit(solution)/shard_map/ppermute | solution.py:409
  144.1 7.3 %collective-permute-start.10 = (f32[5,16,256]{2,1,0:T(8,128)S(1)}, f32[5,16,256]{2,1,0:T(8,128)S(1)}, u32[]{:S(2)}, u32[]{:S(2)}) collective-permute-start(f32[5,16,256]{2,1,0:T(8,128)S(1)} %get-tuple-element.35), channel_id=1, source_target_pairs={{8,0},{16,8},{24,16},{9,1},{17,9},{25,17},{10,2},{18,10},{26,18},{... | collective-permute-start | bytes 245768 | tf_op jit(solution)/shard_map/ppermute | solution.py:410
  146.0 5.7 %collective-permute-start.11 = (f32[5,16,256]{2,1,0:T(8,128)S(1)}, f32[5,16,256]{2,1,0:T(8,128)S(1)}, u32[]{:S(2)}, u32[]{:S(2)}) collective-permute-start(f32[5,16,256]{2,1,0:T(8,128)S(1)} %get-tuple-element.36), channel_id=1, source_target_pairs={{0,1},{1,2},{2,3},{3,4},{4,5},{5,6},{6,7},{8,9},{9,10},{10,11},{11... | collective-permute-start | bytes 245768 | tf_op jit(solution)/shard_map/ppermute | solution.py:409
  148.2 7.1 %collective-permute-start.12 = (f32[5,16,256]{2,1,0:T(8,128)S(1)}, f32[5,16,256]{2,1,0:T(8,128)S(1)}, u32[]{:S(2)}, u32[]{:S(2)}) collective-permute-start(f32[5,16,256]{2,1,0:T(8,128)S(1)} %get-tuple-element.37), channel_id=1, source_target_pairs={{1,0},{2,1},{3,2},{4,3},{5,4},{6,5},{7,6},{9,8},{10,9},{11,10},{12... | collective-permute-start | bytes 245768 | tf_op jit(solution)/shard_map/ppermute | solution.py:410
  160.8 11.3 %collective-permute-start.13 = (f32[5,16,256]{2,1,0:T(8,128)S(1)}, f32[5,16,256]{2,1,0:T(8,128)S(1)}, u32[]{:S(2)}, u32[]{:S(2)}) collective-permute-start(f32[5,16,256]{2,1,0:T(8,128)S(1)} %get-tuple-element.39), channel_id=1, source_target_pairs={{0,8},{8,16},{16,24},{1,9},{9,17},{17,25},{2,10},{10,18},{18,26},{... | collective-permute-start | bytes 245768 | tf_op jit(solution)/shard_map/ppermute | solution.py:409
  164.9 7.2 %collective-permute-start.14 = (f32[5,16,256]{2,1,0:T(8,128)S(1)}, f32[5,16,256]{2,1,0:T(8,128)S(1)}, u32[]{:S(2)}, u32[]{:S(2)}) collective-permute-start(f32[5,16,256]{2,1,0:T(8,128)S(1)} %get-tuple-element.40), channel_id=1, source_target_pairs={{8,0},{16,8},{24,16},{9,1},{17,9},{25,17},{10,2},{18,10},{26,18},{... | collective-permute-start | bytes 245768 | tf_op jit(solution)/shard_map/ppermute | solution.py:410
  166.8 5.3 %collective-permute-start.15 = (f32[5,16,256]{2,1,0:T(8,128)S(1)}, f32[5,16,256]{2,1,0:T(8,128)S(1)}, u32[]{:S(2)}, u32[]{:S(2)}) collective-permute-start(f32[5,16,256]{2,1,0:T(8,128)S(1)} %get-tuple-element.41), channel_id=1, source_target_pairs={{0,1},{1,2},{2,3},{3,4},{4,5},{5,6},{6,7},{8,9},{9,10},{10,11},{11... | collective-permute-start | bytes 245768 | tf_op jit(solution)/shard_map/ppermute | solution.py:409
  170.0 6.1 %collective-permute-start.16 = (f32[5,16,256]{2,1,0:T(8,128)S(1)}, f32[5,16,256]{2,1,0:T(8,128)S(1)}, u32[]{:S(2)}, u32[]{:S(2)}) collective-permute-start(f32[5,16,256]{2,1,0:T(8,128)S(1)} %get-tuple-element.42), channel_id=1, source_target_pairs={{1,0},{2,1},{3,2},{4,3},{5,4},{6,5},{7,6},{9,8},{10,9},{11,10},{12... | collective-permute-start | bytes 245768 | tf_op jit(solution)/shard_map/ppermute | solution.py:410

commit v4 on v3

v4 whole, which is shorter than its diff:
```python
import jax
import jax.numpy as jnp
import numpy as np
from jax import lax
from jax.experimental import pallas as pl
from jax.experimental.pallas import tpu as pltpu
from jax.sharding import PartitionSpec as P

F32 = jnp.float32
BF16 = jnp.bfloat16
LANES = 128
MIB = 1024 * 1024
GROUP = 4
TAIL = 4


def in_vmem():
    return pl.BlockSpec(memory_space=pltpu.VMEM)


def in_smem():
    return pl.BlockSpec(memory_space=pltpu.SMEM)


def in_hbm():
    return pl.BlockSpec(memory_space=pl.ANY)


def sds(shape, dtype):
    return jax.ShapeDtypeStruct(shape, dtype)


def params(mib):
    return pltpu.CompilerParams(vmem_limit_bytes=mib * MIB)


def edge_lines(cells, scratch):
    nx, ny, nz = cells.shape
    flat = cells.reshape(nx * ny, nz)
    out = ([], [])
    for h in range(nz // LANES):
        scratch[h] = flat[:, h * LANES : (h + 1) * LANES]
        for side, first in enumerate((0, ny - 1)):
            out[side].append(scratch[h, pl.ds(first, nx, stride=ny), :])
    return [jnp.concatenate(o, axis=1) for o in out]


def direct_kernel(half, src, xlo, xhi, ylo_a, yhi_a, ylo_b, yhi_b, energy, scratch):
    group, nv, nx, ny, nz = src.shape
    step = pl.program_id(0)

    def body(m, carry):
        xlo[m] = src[m, :, 0]
        xhi[m] = src[m, :, nx - 1]
        total = jnp.zeros((ny, nz), F32)
        for i in range(nv):
            cells = src[m, i].astype(F32)
            lo, hi = (line.astype(BF16) for line in edge_lines(cells, scratch.at[i]))

            @pl.when(step < half)
            def _():
                ylo_a[m, i] = lo
                yhi_a[m, i] = hi

            @pl.when(step >= half)
            def _():
                ylo_b[m, i] = lo
                yhi_b[m, i] = hi

            total = total + jnp.sum(cells * cells, axis=0)
        line = jnp.sum(total, axis=0, keepdims=True)
        line = sum(line[:, h : h + LANES] for h in range(0, nz, LANES))
        energy[pl.ds(step * group + m, 1), :] = line
        return carry

    lax.fori_loop(0, group, body, 0)


def pack(direct):
    nm, nv, nx, ny, nz = direct.shape
    steps = nm // GROUP
    half = steps // 2
    kinds = [(ny, nm + TAIL, lambda s: s)] * 2
    kinds += [(nx, half * GROUP, lambda s: jnp.minimum(s, half - 1))] * 2
    kinds += [(nx, nm - half * GROUP + TAIL, lambda s: jnp.maximum(s - half, 0))] * 2
    face_spec = lambda n, at: pl.BlockSpec((GROUP, nv, n, nz), lambda s: (at(s), 0, 0, 0))
    return pl.pallas_call(
        lambda *refs: direct_kernel(half, *refs),
        grid=(steps,),
        in_specs=[pl.BlockSpec((GROUP, nv, nx, ny, nz), lambda s: (s, 0, 0, 0, 0))],
        out_specs=[face_spec(n, at) for n, _, at in kinds] + [pl.BlockSpec((nm, LANES), lambda s: (0, 0))],
        out_shape=[sds((count, nv, n, nz), BF16) for n, count, _ in kinds] + [sds((nm, LANES), F32)],
        scratch_shapes=[pltpu.VMEM((nv, nz // LANES, nx * ny, LANES), F32)],
        compiler_params=params(56),
        cost_estimate=pl.CostEstimate(flops=3 * direct.size, bytes_accessed=2 * direct.size, transcendentals=0),
        name="pack_direct",
    )(direct)


def mix_chord_kernel(lw, lo, hi, w_lo, w_hi):
    nm, nv, _, ny, nz = lo.shape
    rows = nv * ny

    def body(m, carry):
        for src, out in ((lo, w_lo), (hi, w_hi)):
            face = src[m, :, 0].reshape(rows, nz)
            out[m] = jnp.dot(lw[...], jnp.concatenate([face, face], axis=0), preferred_element_type=F32)
        return carry

    lax.fori_loop(0, nm, body, 0, unroll=4)


def mix_chord(lw, modes):
    nm, nv, nx, ny, nz = modes.shape
    block = (nm, nv, 1, ny, nz)
    w = sds((nm, nv * ny, nz), F32)
    whole = pl.BlockSpec(w.shape, lambda s: (0, 0, 0))
    return pl.pallas_call(
        mix_chord_kernel,
        grid=(1,),
        in_specs=[
            pl.BlockSpec(lw.shape, lambda s: (0, 0)),
            pl.BlockSpec(block, lambda s: (0, 0, 0, 0, 0)),
            pl.BlockSpec(block, lambda s: (0, 0, nx - 1, 0, 0)),
        ],
        out_specs=[whole, whole],
        out_shape=[w, w],
        compiler_params=params(56),
        cost_estimate=pl.CostEstimate(flops=10**8, bytes_accessed=6 * 10**6, transcendentals=0),
        name="mix_chord",
    )(lw, modes, modes)


def mix_normal_kernel(lw, src, w_lo, w_hi, scratch):
    group, nv, nx, ny, nz = src.shape

    def body(m, carry):
        lines = [edge_lines(src[m, i].astype(F32), scratch.at[i]) for i in range(nv)]
        for side, out in enumerate((w_lo, w_hi)):
            face = jnp.concatenate([line[side] for line in lines], axis=0).astype(BF16)
            out[m] = jnp.dot(lw[...], jnp.concatenate([face, face], axis=0), preferred_element_type=F32)
        return carry

    lax.fori_loop(0, group, body, 0)


def mix_normal(lw, modes):
    nm, nv, nx, ny, nz = modes.shape
    w = sds((nm, nv * nx, nz), F32)
    out = pl.BlockSpec((GROUP, nv * nx, nz), lambda s: (s, 0, 0))
    return pl.pallas_call(
        mix_normal_kernel,
        grid=(nm // GROUP,),
        in_specs=[
            pl.BlockSpec(lw.shape, lambda s: (0, 0)),
            pl.BlockSpec((GROUP, nv, nx, ny, nz), lambda s: (s, 0, 0, 0, 0)),
        ],
        out_specs=[out, out],
        out_shape=[w, w],
        scratch_shapes=[pltpu.VMEM((nv, nz // LANES, nx * ny, LANES), F32)],
        compiler_params=params(56),
        cost_estimate=pl.CostEstimate(flops=3 * modes.size, bytes_accessed=3 * modes.size, transcendentals=0),
        name="mix_normal",
    )(lw, modes)


def summed(pick, amp, parts, w, j):
    nm = w.shape[0]
    n, nz = parts[0][0].shape[2:]
    total = jnp.zeros((n, nz), F32)
    m = 0
    for u, count in parts:
        for k in range(count):
            total = total + amp[m] * (u[k, j].astype(F32) * w[pick[m], pl.ds(pl.multiple_of(j * n, n), n), :])
            m += 1
    return total


def by_face(refs):
    modes = [ref.shape[0] - TAIL for ref in refs]
    parts = [[(refs[f], modes[f])] for f in range(2)]
    parts += [[(refs[f], refs[f].shape[0]), (refs[f + 2], modes[f + 2])] for f in (2, 3)]
    return parts, [refs[0], refs[1], refs[4], refs[5]]


def whole_of(ref, part):
    n = ref.shape[0] - TAIL + 2 * part
    return ref[n].astype(F32) + ref[n + 1].astype(F32)


def faces_kernel(pick, amp, base, *refs):
    u = refs[0:6]
    w = refs[6:10]
    tails = refs[10:14]
    scratch = refs[14]
    nv, nx, ny, nz = base.shape
    parts, _ = by_face(u)

    def body(j, carry):
        lines = [base[j, 0], base[j, nx - 1], *edge_lines(base[j], scratch)]
        for f in range(4):
            for n, value in enumerate((summed(pick, amp, parts[f], w[f], j), lines[f])):
                hi = value.astype(BF16)
                tails[f][2 * n, j] = hi
                tails[f][2 * n + 1, j] = (value - hi.astype(F32)).astype(BF16)
        return carry

    lax.fori_loop(0, nv, body, 0)


def faces(pick, amp, base, u_faces, w_faces):
    nv, nx, ny, nz = base.shape
    whole = lambda a: pl.BlockSpec(a.shape, lambda s: (0,) * a.ndim)
    tailed = [u_faces[f] for f in (0, 1, 4, 5)]
    at = [a.shape[0] // TAIL - 1 for a in tailed]
    return pl.pallas_call(
        faces_kernel,
        grid=(1,),
        in_specs=[in_smem()] * 2 + [whole(a) for a in (base, *u_faces, *w_faces)],
        out_specs=[pl.BlockSpec((TAIL,) + a.shape[1:], lambda s, n=n: (n, 0, 0, 0)) for a, n in zip(tailed, at)],
        out_shape=[sds(a.shape, BF16) for a in tailed],
        input_output_aliases={3: 0, 4: 1, 7: 2, 8: 3},
        scratch_shapes=[pltpu.VMEM((nz // LANES, nx * ny, LANES), F32)],
        compiler_params=params(40),
        name="faces",
    )(pick, amp, base, *u_faces, *w_faces)


def row_of(shape, n):
    return lax.broadcasted_iota(jnp.int32, shape, 0) % n


def diff_lanes(a):
    n = a.shape[-1]
    return pltpu.roll(a, n - 1, a.ndim - 1) - pltpu.roll(a, 1, a.ndim - 1)


def diff_rows(a, n, lo, hi):
    rows = a.shape[0]
    row = row_of(a.shape, n)
    return jnp.where(row == n - 1, hi, pltpu.roll(a, rows - 1, 0)) - jnp.where(row == 0, lo, pltpu.roll(a, 1, 0))


def main_kernel(pick, amp, lw, u_hbm, q_hbm, out, u_buf, q_buf, even, odd, acc, c0, u_sem, q_sem):
    nx, nm, nv, ny, nz = u_buf.shape
    rows = nv * ny

    def u_copy(p):
        return pltpu.make_async_copy(u_hbm.at[:, :, p], u_buf.at[p], u_sem.at[p])

    def q_copy(p):
        return pltpu.make_async_copy(q_hbm.at[:, :, p], q_buf.at[p], q_sem.at[p])

    for p in range(nx):
        u_copy(p).start()
        q_copy(p).start()
    c0[0] = jnp.zeros((rows, nz), F32)
    c0[nx + 1] = jnp.zeros((rows, nz), F32)

    def products(p, m, dest):
        qm = q_buf[p, pick[m]].reshape(rows, nz)
        u = u_buf[p, m].reshape(rows, nz)
        dest[m] = jnp.dot(lw[...], jnp.concatenate([qm, qm, u], axis=0), preferred_element_type=F32)

    def plane(p, src, dest):
        after = jnp.minimum(p + 1, nx - 1)

        @pl.when(p < nx - 1)
        def _():
            u_copy(after).wait()
            q_copy(after).wait()

        acc[...] = jnp.zeros_like(acc)
        before = jnp.maximum(p - 1, 0)

        def body(step, carry):
            for k in range(GROUP):
                products(after, step * GROUP + k, dest)
            for j in range(nv):
                at = slice(j * ny, (j + 1) * ny)
                sums = [acc[n, at] for n in range(4)]
                for k in range(GROUP):
                    m = step * GROUP + k
                    a = amp[m]
                    w0, w1, w2, dy = (src[m, n * rows + j * ny : n * rows + (j + 1) * ny] for n in range(4))
                    dx = u_buf[after, m, j].astype(F32) - u_buf[before, m, j].astype(F32)
                    uf = u_buf[p, m, j].astype(F32)
                    dz = diff_lanes(uf)
                    uf = uf * a
                    terms = [(dx * w0 + dy * w1 + dz * w2) * a, uf * w0, uf * w1, uf * w2]
                    sums = [v + t for v, t in zip(sums, terms)]
                for n in range(4):
                    acc[n, at] = sums[n]
            return carry

        lax.fori_loop(0, nm // GROUP, body, 0)
        ends = jnp.where(p == 0, 1.0, 0.0) - jnp.where(p == nx - 1, 1.0, 0.0)
        c0[p + 1] = acc[1]
        out[p] = acc[0] - diff_lanes(acc[3]) + ends * acc[1] - diff_rows(acc[2], ny, 0.0, 0.0)

    u_copy(0).wait()
    q_copy(0).wait()

    def first(m, carry):
        products(0, m, even)
        return carry

    lax.fori_loop(0, nm, first, 0, unroll=GROUP)

    def pair(i, carry):
        plane(2 * i, even, odd)
        plane(2 * i + 1, odd, even)
        return carry

    lax.fori_loop(0, nx // 2, pair, 0)

    def finish(p, carry):
        out[p] = out[p] - c0[p + 2] + c0[p]
        return carry

    lax.fori_loop(0, nx, finish, 0)


def main(pick, amp, lw, direct, adjoint):
    nm, nv, nx, ny, nz = direct.shape
    rows = nv * ny
    buf = pltpu.VMEM((nx, nm, nv, ny, nz), BF16)
    return pl.pallas_call(
        main_kernel,
        in_specs=[in_smem(), in_smem(), in_vmem(), in_hbm(), in_hbm()],
        out_specs=in_vmem(),
        out_shape=sds((nx, rows, nz), F32),
        scratch_shapes=[
            buf,
            buf,
            pltpu.VMEM((nm, 4 * rows, nz), F32),
            pltpu.VMEM((nm, 4 * rows, nz), F32),
            pltpu.VMEM((4, rows, nz), F32),
            pltpu.VMEM((nx + 2, rows, nz), F32),
            pltpu.SemaphoreType.DMA((nx,)),
            pltpu.SemaphoreType.DMA((nx,)),
        ],
        compiler_params=params(56),
        cost_estimate=pl.CostEstimate(flops=10**6, bytes_accessed=10**5, transcendentals=0),
        name="main",
    )(pick, amp, lw, direct, adjoint)


def weight_of(cells):
    return jnp.where(cells == 0, 1.0, jnp.where(cells == 1, 0.5, 0.0)).astype(F32)


def spread(ref, x, n):
    nv, _, nz = ref.shape
    return jnp.concatenate([jnp.broadcast_to(ref[j, pl.ds(x, 1), :], (n, nz)) for j in range(nv)], axis=0)


def write_lines(values, x, n, lo, hi):
    for j in range(lo.shape[0]):
        lo[j, pl.ds(x, 1), :] = values[j * n : j * n + 1]
        hi[j, pl.ds(x, 1), :] = values[(j + 1) * n - 1 : (j + 1) * n]


def boundary_kernel(scale, pick, amp, local, cell, *refs):
    w = refs[0:4]
    parts, tailed = by_face(refs[4:10])
    field, xlo, xhi, ylo, yhi = refs[10:15]
    add = refs[15:19]
    nx, rows, nz = local.shape
    nv = add[0].shape[0]
    ny = rows // nv
    for f in range(4):
        add[f][...] = whole_of(tailed[f], 0)

    def face(j, carry):
        for f in range(4):
            add[f][j] -= summed(pick, amp, parts[f], w[f], j)
        return carry

    lax.fori_loop(0, nv, face, 0)

    row = row_of((rows, nz), ny)

    def plane(x, carry):
        lo, hi = spread(add[2], x, ny), spread(add[3], x, ny)
        field[x] = local[x] + jnp.where(row == 0, lo, 0.0) - jnp.where(row == ny - 1, hi, 0.0)
        return carry

    lax.fori_loop(0, nx, plane, 0)
    field[0] += add[0][...].reshape(rows, nz)
    field[nx - 1] -= add[1][...].reshape(rows, nz)

    def weigh(x, carry):
        weight = weight_of(cell[x]) * scale
        g = field[x] * jnp.concatenate([weight] * nv, axis=0)
        field[x] = g
        write_lines(g, x, ny, ylo, yhi)
        return carry

    lax.fori_loop(0, nx, weigh, 0)
    xlo[...] = field[0].reshape(xlo.shape)
    xhi[...] = field[nx - 1].reshape(xhi.shape)


def boundary(scale, pick, amp, local, cell, w_faces, halo):
    nx, rows, nz = local.shape
    face = [sds(halo[f].shape[1:], F32) for f in range(4)]
    return pl.pallas_call(
        lambda *refs: boundary_kernel(scale, *refs),
        in_specs=[in_smem()] * 2 + [in_vmem()] * 12,
        out_specs=[in_vmem()] * 5,
        out_shape=[sds(local.shape, F32)] + face,
        scratch_shapes=[pltpu.VMEM(f.shape, F32) for f in face],
        compiler_params=params(28),
        name="boundary",
    )(pick, amp, local, cell, *w_faces, *halo)


def mix_rows(lw, values):
    hi = values.astype(BF16)
    lo = (values - hi.astype(F32)).astype(BF16)
    return jnp.dot(lw, jnp.concatenate([hi, lo, hi], axis=0), preferred_element_type=F32)


def step_kernel(last, lw, lw_y, base, cell, field, *refs):
    got_base = refs[0:4]
    got = refs[4:8]
    out = refs[8]
    faces = refs[9:13]
    b_pad, c0, bh_lo, bh_hi, ch_lo, ch_hi = refs[-6:]
    nv, nx, ny, nz = base.shape
    rows = nv * ny
    for f, at in ((0, 0), (1, nx + 1)):
        b = whole_of(got_base[f], 1).reshape(rows, nz)
        b_pad[at] = b
        c0[at] = b * mix_rows(lw[:rows], got[f][...].reshape(rows, nz))
    for f, bh, ch in ((2, bh_lo, ch_lo), (3, bh_hi, ch_hi)):
        b = whole_of(got_base[f], 1)
        bh[...] = b
        ch[...] = b * mix_rows(lw_y[...], got[f][...].reshape(nv * nx, nz)).reshape(nv, nx, nz)

    def fill(x, carry):
        b_pad[x + 1] = base[:, x].reshape(rows, nz)
        return carry

    lax.fori_loop(0, nx, fill, 0)

    def plane(x, carry):
        w = mix_rows(lw[...], field[x])
        w0, w1, w2 = (w[n * rows : (n + 1) * rows] for n in range(3))
        b = b_pad[x + 1]
        c0[x + 1] = b * w0
        h = (b_pad[x + 2] - b_pad[x]) * w0
        h = h + diff_rows(b, ny, spread(bh_lo, x, ny), spread(bh_hi, x, ny)) * w1
        h = h - diff_rows(b * w1, ny, spread(ch_lo, x, ny), spread(ch_hi, x, ny))
        h = h + diff_lanes(b) * w2 - diff_lanes(b * w2)
        if last:
            out[:, x] = h.reshape(nv, ny, nz)
        else:
            out[x] = h
        return carry

    lax.fori_loop(0, nx, plane, 0)

    def finish(x, carry):
        change = c0[x] - c0[x + 2]
        if last:
            out[:, x] = out[:, x] + change.reshape(nv, ny, nz)
        else:
            g = (out[x] + change) * jnp.concatenate([weight_of(cell[x])] * nv, axis=0)
            out[x] = g
            write_lines(g, x, ny, faces[2], faces[3])
        return carry

    lax.fori_loop(0, nx, finish, 0)
    if not last:
        faces[0][...] = out[0].reshape(nv, ny, nz)
        faces[1][...] = out[nx - 1].reshape(nv, ny, nz)


def apply_step(last, lw, lw_y, base, cell, field, got_base, got):
    nv, nx, ny, nz = base.shape
    rows = nv * ny
    face = [] if last else [sds((nv, n, nz), F32) for n in (ny, ny, nx, nx)]
    line = pltpu.VMEM((nv, nx, nz), F32)
    padded = pltpu.VMEM((nx + 2, rows, nz), F32)
    return pl.pallas_call(
        lambda *refs: step_kernel(last, *refs),
        in_specs=[in_vmem()] * 13,
        out_specs=[in_vmem()] * (1 + len(face)),
        out_shape=[sds(base.shape if last else field.shape, F32)] + face,
        scratch_shapes=[padded, padded, line, line, line, line],
        compiler_params=params(28),
        name="step_two" if last else "step_one",
    )(lw, lw_y, base, cell, field, *got_base, *got)


def exchange_axis(axis, lo, hi):
    count = lax.axis_size(axis)
    up = [(i, i + 1) for i in range(count - 1)]
    down = [(i + 1, i) for i in range(count - 1)]
    return [lax.ppermute(hi, axis, up), lax.ppermute(lo, axis, down)]


def exchange(arrays):
    return exchange_axis("chord", *arrays[:2]) + exchange_axis("normal", *arrays[2:])


def sum_over(axis, values):
    count = lax.axis_size(axis)
    if count & (count - 1):
        return lax.psum(values, axis)
    bit = 1
    while bit < count:
        values = values + lax.ppermute(values, axis, [(i, i ^ bit) for i in range(count)])
        bit *= 2
    return values


def kron_rows(mix, n):
    nv = mix.shape[1]
    hi = lax.reduce_precision(mix, 8, 7)
    lo = lax.reduce_precision(mix - hi, 8, 7)
    small = jnp.concatenate([hi.transpose(0, 2, 1), lo.transpose(0, 2, 1)], axis=2)
    rows, cols = np.arange(nv * n), np.arange(2 * nv * n)
    left = jnp.asarray((rows[:, None] // n == np.arange(nv)[None]).astype(np.float32))
    right = jnp.asarray((cols[None] // n == np.arange(2 * nv)[:, None]).astype(np.float32))
    mask = jnp.asarray((rows[:, None] % n == cols[None] % n).astype(np.float32))
    wide = jnp.einsum("rj,djc,ck->drk", left, small, right, precision=lax.Precision.HIGHEST)
    return (wide * mask).astype(BF16)


def main_rows(lw, nv, ny):
    dy = np.kron(np.eye(nv, dtype=np.float32), np.eye(ny, k=1, dtype=np.float32) - np.eye(ny, k=-1, dtype=np.float32))
    rows = nv * ny
    top = jnp.pad(lw.reshape(3 * rows, 2 * rows), ((0, 0), (0, rows)))
    return jnp.concatenate([top, jnp.pad(jnp.asarray(dy, BF16), ((0, 0), (2 * rows, 0)))], axis=0)


def step_rows(lw):
    half = lw.shape[-1] // 2
    return jnp.concatenate([lw[..., :half], lw[..., :half], lw[..., half:]], axis=-1)


def per_device(direct, adjoint, base, cell, pick, mix):
    nm, nv, nx, ny, nz = direct.shape
    cells_all = nv * nx * ny * nz * lax.axis_size("chord") * lax.axis_size("normal")
    *own, sums = pack(direct)
    early = exchange_axis("normal", *own[2:4])
    sums = sum_over("chord", jnp.sum(sums, axis=1))
    lw_y = kron_rows(mix, ny)
    lw_x = lw_y if nx == ny else kron_rows(mix, nx)
    w_faces = [*mix_chord(lw_y[0], adjoint), *mix_normal(lw_x[1], adjoint)]
    *early, sums = lax.optimization_barrier((*early, sums, *w_faces))[:3]
    sums = sum_over("normal", sums)
    amp = lax.rsqrt(sums / cells_all + 1e-06)
    late = exchange(faces(pick, amp, base, own, w_faces))
    halo = late[:2] + early + late[2:]
    local = main(pick, amp, main_rows(lw_y, nv, ny), direct, adjoint)
    field, *sides = boundary(1.0 / nm, pick, amp, local, cell, w_faces, halo)
    lw_step = step_rows(lw_y.reshape(3 * nv * ny, -1))
    lw_line = step_rows(lw_x[1])
    field, *sides = apply_step(False, lw_step, lw_line, base, cell, field, late, exchange(sides))
    return apply_step(True, lw_step, lw_line, base, cell, field, late, exchange(sides))[0]


def solution(mesh):
    return jax.shard_map(
        per_device,
        mesh=mesh,
        in_specs=(
            P(None, None, "chord", "normal", None),
            P(None, None, "chord", "normal", None),
            P(None, "chord", "normal", None),
            P("chord", "normal", None),
            P(),
            P(),
        ),
        out_specs=P(None, "chord", "normal", None),
        check_vma=False,
    )
```

time: 184 us -> 149 us (0.81)
  the two profiles are of different devices: /device:TPU:5 before, /device:TPU:18 now
where the time goes in v4:
time: 149 us; the launch traced here: 148 us
  Pallas kernels  72.7 us (49%)
  starting transfers between devices  45.6 us (31%)
  waiting for transfers between devices  16.9 us (11%)
  local copies, waits for them, and re-layouts  9.58 us (6%)
  other arithmetic  1.72 us (1%)
    ppermute x14, starting transfers between devices, exchange_axis(): return [lax.ppermute(hi, axis, up), lax.ppermute(lo, axis, down)]  42.7 us
    pallas_call x1, Pallas kernels, main(): pl.pallas_call(main_kernel, in_specs=[in_smem(), in_smem(), in_vmem(), in...  33.3 us
    pallas_call x2, Pallas kernels, apply_step(): pl.pallas_call(lambda *refs: step_kernel(last, *refs), in_specs=[in_vmem(...  14 us
    ppermute x5, waiting for transfers between devices, sum_over(): lax.ppermute(values, axis, [(i, i ^ bit) for i in range(count)])  9.34 us
    unnamed x54, local copies, waits for them, and re-layouts  8.33 us
    pallas_call x1, Pallas kernels, mix_normal(): pl.pallas_call(mix_normal_kernel, grid=(nm // GROUP,), in_specs=[pl.Block...  8.28 us
    ppermute x14, waiting for transfers between devices, exchange_axis(): return [lax.ppermute(hi, axis, up), lax.ppermute(lo, axis, down)]  7.61 us
    pallas_call x1, Pallas kernels, pack(): pl.pallas_call(lambda *refs: direct_kernel(half, *refs), grid=(steps,), i...  7.23 us
  transfers between devices with their start and end apart: 19, of which 7 were waited for; matrix products, arithmetic and copies ran while one was open for 2% of the time, Pallas kernels for 31%

profile of v4, /device:TPU:18, one launch (start us, length us, event | category | flops | bytes accessed | tf_op | source)
XLA Modules:
  0.0 147.7 jit_solution(4036699893898223913)
XLA Ops:
  0.0 7.2 %pack_direct.1 = (bf16[20,5,16,256]{3,2,1,0:T(8,128)(2,1)}, bf16[20,5,16,256]{3,2,1,0:T(8,128)(2,1)}, bf16[8,5,16,256]{3,2,1,0:T(8,128)(2,1)}, bf16[8,5,16,256]{...) custom-call(bf16[16,5,16,16,256]{4,3,2,1,0:T(8,128)(2,1)} %u_hbm.1), custom_call_target="tpu_custom_call" | custom-call | flops 15728640 | bytes 10485760 | tf_op jit(solution)/shard_map/pack_direct/pallas_call | solution.py:87
  7.3 0.8 reduce_sum.9
  8.1 0.1 collective-permute-start.2
  8.1 3.4 %collective-permute-start = (bf16[8,5,16,256]{3,2,1,0:T(8,128)(2,1)}, bf16[8,5,16,256]{3,2,1,0:T(8,128)(2,1)S(1)}, u32[]{:S(2)}, u32[]{:S(2)}) collective-permute-start(bf16[8,5,16,256]{3,2,1,0:T(8,128)(2,1)} %get-tuple-element.33.refs_3_), channel_id=1, source_target_pairs={{0,1},{1,2},{2,3},{3,4},{4,5},{5,6},{6,7},{8,9},{9,10},{10,11},{11... | collective-permute-start | bytes 983048 | tf_op jit(solution)/shard_map/ppermute | solution.py:502
  11.6 3.3 %collective-permute-start.1 = (bf16[8,5,16,256]{3,2,1,0:T(8,128)(2,1)}, bf16[8,5,16,256]{3,2,1,0:T(8,128)(2,1)S(1)}, u32[]{:S(2)}, u32[]{:S(2)}) collective-permute-start(bf16[8,5,16,256]{3,2,1,0:T(8,128)(2,1)} %get-tuple-element.34.refs_2_), channel_id=1, source_target_pairs={{1,0},{2,1},{3,2},{4,3},{5,4},{6,5},{7,6},{9,8},{10,9},{11,10},{12... | collective-permute-start | bytes 983048 | tf_op jit(solution)/shard_map/ppermute | solution.py:502
  14.9 0.2 fusion.4
  15.2 0.4 fusion.1
  15.6 0.6 slice_bitcast_fusion
  16.2 3.8 %mix_chord.1 = (f32[16,80,256]{2,1,0:T(8,128)}, f32[16,80,256]{2,1,0:T(8,128)}) custom-call(bf16[80,160]{1,0:T(8,128)(2,1)} %get-tuple-element.61.lw, bf16[16,5,16,16,256]{4,3,2,1,0:T(8,128)(2,1)} %q_hbm.1, bf16[16,5,16,16,256]{4,3,2,1,0:T(8,128)(2,1)} %q_hbm.1), custom_call_target="tpu_custom_call" | custom-call | flops 100000000 | bytes 6000000 | tf_op jit(solution)/shard_map/mix_chord/pallas_call | solution.py:118
  20.0 0.0 collective-permute-done.2
  20.1 0.6 collective-permute-start.3
  20.7 0.0 copy-start.15
  20.7 8.3 %mix_normal.1 = (f32[16,80,256]{2,1,0:T(8,128)}, f32[16,80,256]{2,1,0:T(8,128)}) custom-call(bf16[80,160]{1,0:T(8,128)(2,1)} %get-tuple-element.62.lw, bf16[16,5,16,16,256]{4,3,2,1,0:T(8,128)(2,1)} %q_hbm.1), custom_call_target="tpu_custom_call" | custom-call | flops 15728640 | bytes 15728640 | tf_op jit(solution)/shard_map/mix_normal/pallas_call | solution.py:151
  29.0 0.0 collective-permute-done.3
  29.0 0.0 collective-permute-done.refs_10_
  29.0 0.7 copy-done.11
  29.7 0.0 collective-permute-done.1.refs_11_
  29.7 0.7 copy-done.13
  30.4 0.6 collective-permute-start.4
  31.0 2.9 %collective-permute-done.4 = f32[16]{0:T(128)S(1)} collective-permute-done((f32[16]{0:T(128)S(1)}, f32[16]{0:T(128)S(1)}, u32[]{:S(2)}, u32[]{:S(2)}) %collective-permute-start.4) | collective-permute-done | bytes 96 | tf_op jit(solution)/shard_map/ppermute | solution.py:515
  34.0 1.6 %collective-permute-start.5 = (f32[16]{0:T(128)S(1)}, f32[16]{0:T(128)S(1)}, u32[]{:S(2)}, u32[]{:S(2)}) collective-permute-start(f32[16]{0:T(128)S(1)} %add.24), channel_id=1, source_target_pairs={{0,2},{1,3},{2,0},{3,1},{4,6},{5,7},{6,4},{7,5},{8,10},{9,11},{10,... | collective-permute-start | bytes 200 | tf_op jit(solution)/shard_map/ppermute | solution.py:515
  35.5 2.0 %collective-permute-done.5 = f32[16]{0:T(128)S(1)} collective-permute-done((f32[16]{0:T(128)S(1)}, f32[16]{0:T(128)S(1)}, u32[]{:S(2)}, u32[]{:S(2)}) %collective-permute-start.5) | collective-permute-done | bytes 96 | tf_op jit(solution)/shard_map/ppermute | solution.py:515
  37.5 0.0 collective-permute-start.6
  37.5 4.4 %collective-permute-done.6 = f32[16]{0:T(128)S(1)} collective-permute-done((f32[16]{0:T(128)S(1)}, f32[16]{0:T(128)S(1)}, u32[]{:S(2)}, u32[]{:S(2)}) %collective-permute-start.6) | collective-permute-done | bytes 96 | tf_op jit(solution)/shard_map/ppermute | solution.py:515
  42.0 1.3 copy-done.4
  43.3 1.3 copy-done.6
  44.7 3.5 %faces.1 = (bf16[20,5,16,256]{3,2,1,0:T(8,128)(2,1)}, bf16[20,5,16,256]{3,2,1,0:T(8,128)(2,1)}, bf16[12,5,16,256]{3,2,1,0:T(8,128)(2,1)}, bf16[12,5,16,256]{3,2,1,0:T(8,128)(2,1)}) custom-call(s32[16]{0:T(128)S(1)} %copy-done.15, f32[16]{0:T(128)S(1)} %add_rsqrt_fusion.amp.refs_1_, ...), custom_call_target="tpu_custom_call", output_to_operand_aliasing={{0}: (3, {}), {1}: (4, {}), {2}: (7, {}), {3}: (8, {})} | custom-call | tf_op jit(solution)/shard_map/faces/pallas_call | solution.py:216
  48.1 1.9 %collective-permute-start.7 = (bf16[20,5,16,256]{3,2,1,0:T(8,128)(2,1)}, bf16[20,5,16,256]{3,2,1,0:T(8,128)(2,1)S(1)}, u32[]{:S(2)}, u32[]{:S(2)}) collective-permute-start(bf16[20,5,16,256]{3,2,1,0:T(8,128)(2,1)} %get-tuple-element.45), channel_id=1, source_target_pairs={{0,8},{8,16},{16,24},{1,9},{9,17},{17,25},{2,10},{10,18},{18,26},{... | collective-permute-start | bytes 2457608 | tf_op jit(solution)/shard_map/ppermute | solution.py:502
  50.1 3.6 %collective-permute-start.8 = (bf16[20,5,16,256]{3,2,1,0:T(8,128)(2,1)}, bf16[20,5,16,256]{3,2,1,0:T(8,128)(2,1)S(1)}, u32[]{:S(2)}, u32[]{:S(2)}) collective-permute-start(bf16[20,5,16,256]{3,2,1,0:T(8,128)(2,1)} %get-tuple-element.46), channel_id=1, source_target_pairs={{8,0},{16,8},{24,16},{9,1},{17,9},{25,17},{10,2},{18,10},{26,18},{... | collective-permute-start | bytes 2457608 | tf_op jit(solution)/shard_map/ppermute | solution.py:502
  53.7 2.4 %collective-permute-start.10 = (bf16[12,5,16,256]{3,2,1,0:T(8,128)(2,1)}, bf16[12,5,16,256]{3,2,1,0:T(8,128)(2,1)}, u32[]{:S(2)}, u32[]{:S(2)}) collective-permute-start(bf16[12,5,16,256]{3,2,1,0:T(8,128)(2,1)} %get-tuple-element.50), channel_id=1, source_target_pairs={{1,0},{2,1},{3,2},{4,3},{5,4},{6,5},{7,6},{9,8},{10,9},{11,10},{12... | collective-permute-start | bytes 1474568 | tf_op jit(solution)/shard_map/ppermute | solution.py:502
  56.1 3.4 %collective-permute-start.9 = (bf16[12,5,16,256]{3,2,1,0:T(8,128)(2,1)}, bf16[12,5,16,256]{3,2,1,0:T(8,128)(2,1)}, u32[]{:S(2)}, u32[]{:S(2)}) collective-permute-start(bf16[12,5,16,256]{3,2,1,0:T(8,128)(2,1)} %get-tuple-element.49), channel_id=1, source_target_pairs={{0,1},{1,2},{2,3},{3,4},{4,5},{5,6},{6,7},{8,9},{9,10},{10,11},{11... | collective-permute-start | bytes 1474568 | tf_op jit(solution)/shard_map/ppermute | solution.py:502
  59.6 0.6 slice.25
  60.2 0.1 pad_maximum_fusion.refs_0_
  60.3 0.7 fusion.3.lw
  61.0 33.3 %main.1.refs_2_ = f32[16,80,256]{2,1,0:T(8,128)} custom-call(s32[16]{0:T(128)} %refs_0_.3, f32[16]{0:T(128)} %copy-done.17, bf16[320,240]{1,0:T(8,128)(2,1)} %fusion.3.lw, bf16[16,5,16,16,256]{4,3,2,1,0:T(8,128)(2,1)} %u_hbm.1, bf16[16,5,16,16,256]{4,3,2,1,0:T(8,128)(2,1)} %q_hbm.1), custom_call_target="tpu_custom_call" | custom-call | flops 1000000 | bytes 100000 | tf_op jit(solution)/shard_map/main/pallas_call | solution.py:328
  94.3 0.0 collective-permute-done.10.refs_13_.refs_8_
  94.3 0.0 collective-permute-done.9.refs_12_.refs_7_
  94.3 0.0 collective-permute-done.7.refs_8_.refs_5_
  94.3 0.0 collective-permute-done.8.refs_9_.refs_6_
  94.4 0.0 copy-start.1
  94.4 1.3 copy-done.1
  95.7 0.9 copy-done.8
  96.6 1.0 copy-done.12
  97.6 1.0 copy-done.14
  98.6 2.6 %boundary.1 = (f32[16,80,256]{2,1,0:T(8,128)S(1)}, f32[5,16,256]{2,1,0:T(8,128)S(1)}, f32[5,16,256]{2,1,0:T(8,128)S(1)}, f32[5,16,256]{2,1,0:T(8,128)S(1)}, f32[5,16,256]{2,1,0:T(8,128)S(1)}) custom-call(s32[16]{0:T(128)S(1)} %copy-done.16, f32[16]{0:T(128)S(1)} %copy-done.18, f32[16,80,256]{2,1,0:T(8,128)S(1)} %copy-done.1, s32[16,16,256]{2,1,0:T(8,128)S(1)} %copy-done.8, ...), custom_call_target="tpu_custom_call" | custom-call | tf_op jit(solution)/shard_map/boundary/pallas_call | solution.py:408
  101.2 1.9 %collective-permute-start.11 = (f32[5,16,256]{2,1,0:T(8,128)S(1)}, f32[5,16,256]{2,1,0:T(8,128)S(1)}, u32[]{:S(2)}, u32[]{:S(2)}) collective-permute-start(f32[5,16,256]{2,1,0:T(8,128)S(1)} %get-tuple-element.52), channel_id=1, source_target_pairs={{0,8},{8,16},{16,24},{1,9},{9,17},{17,25},{2,10},{10,18},{18,26},{... | collective-permute-start | bytes 245768 | tf_op jit(solution)/shard_map/ppermute | solution.py:502
  103.1 3.6 %collective-permute-start.12 = (f32[5,16,256]{2,1,0:T(8,128)S(1)}, f32[5,16,256]{2,1,0:T(8,128)S(1)}, u32[]{:S(2)}, u32[]{:S(2)}) collective-permute-start(f32[5,16,256]{2,1,0:T(8,128)S(1)} %get-tuple-element.53), channel_id=1, source_target_pairs={{8,0},{16,8},{24,16},{9,1},{17,9},{25,17},{10,2},{18,10},{26,18},{... | collective-permute-start | bytes 245768 | tf_op jit(solution)/shard_map/ppermute | solution.py:502
  106.8 3.5 %collective-permute-start.13 = (f32[5,16,256]{2,1,0:T(8,128)S(1)}, f32[5,16,256]{2,1,0:T(8,128)S(1)}, u32[]{:S(2)}, u32[]{:S(2)}) collective-permute-start(f32[5,16,256]{2,1,0:T(8,128)S(1)} %get-tuple-element.54), channel_id=1, source_target_pairs={{0,1},{1,2},{2,3},{3,4},{4,5},{5,6},{6,7},{8,9},{9,10},{10,11},{11... | collective-permute-start | bytes 245768 | tf_op jit(solution)/shard_map/ppermute | solution.py:502
  110.2 3.3 %collective-permute-start.14 = (f32[5,16,256]{2,1,0:T(8,128)S(1)}, f32[5,16,256]{2,1,0:T(8,128)S(1)}, u32[]{:S(2)}, u32[]{:S(2)}) collective-permute-start(f32[5,16,256]{2,1,0:T(8,128)S(1)} %get-tuple-element.55), channel_id=1, source_target_pairs={{1,0},{2,1},{3,2},{4,3},{5,4},{6,5},{7,6},{9,8},{10,9},{11,10},{12... | collective-permute-start | bytes 245768 | tf_op jit(solution)/shard_map/ppermute | solution.py:502
  113.6 0.1 pad_maximum_fusion.1.refs_1_
  113.6 0.0 collective-permute-done.11.refs_9_
  113.6 0.0 collective-permute-done.12.refs_10_
  113.7 0.4 collective-permute-done.13.refs_11_
  114.0 2.8 %collective-permute-done.14.refs_12_ = f32[5,16,256]{2,1,0:T(8,128)S(1)} collective-permute-done((f32[5,16,256]{2,1,0:T(8,128)S(1)}, f32[5,16,256]{2,1,0:T(8,128)S(1)}, u32[]{:S(2)}, u32[]{:S(2)}) %collective-permute-start.14) | collective-permute-done | bytes 81952 | tf_op jit(solution)/shard_map/ppermute | solution.py:502
  116.9 6.6 %step_one.1 = (f32[16,80,256]{2,1,0:T(8,128)S(1)}, f32[5,16,256]{2,1,0:T(8,128)S(1)}, f32[5,16,256]{2,1,0:T(8,128)S(1)}, f32[5,16,256]{2,1,0:T(8,128)S(1)}, f32[5,16,256]{2,1,0:T(8,128)S(1)}) custom-call(bf16[240,240]{1,0:T(8,128)(2,1)S(1)} %pad_maximum_fusion.refs_0_, bf16[80,240]{1,0:T(8,128)(2,1)S(1)} %pad_maximum_fusion.1.refs_1_, ...), custom_call_target="tpu_custom_call" | custom-call | tf_op jit(solution)/shard_map/step_one/pallas_call | solution.py:487
  123.4 1.9 %collective-permute-start.15 = (f32[5,16,256]{2,1,0:T(8,128)S(1)}, f32[5,16,256]{2,1,0:T(8,128)S(1)}, u32[]{:S(2)}, u32[]{:S(2)}) collective-permute-start(f32[5,16,256]{2,1,0:T(8,128)S(1)} %get-tuple-element.57), channel_id=1, source_target_pairs={{0,8},{8,16},{16,24},{1,9},{9,17},{17,25},{2,10},{10,18},{18,26},{... | collective-permute-start | bytes 245768 | tf_op jit(solution)/shard_map/ppermute | solution.py:502
  125.3 3.6 %collective-permute-start.16 = (f32[5,16,256]{2,1,0:T(8,128)S(1)}, f32[5,16,256]{2,1,0:T(8,128)S(1)}, u32[]{:S(2)}, u32[]{:S(2)}) collective-permute-start(f32[5,16,256]{2,1,0:T(8,128)S(1)} %get-tuple-element.58), channel_id=1, source_target_pairs={{8,0},{16,8},{24,16},{9,1},{17,9},{25,17},{10,2},{18,10},{26,18},{... | collective-permute-start | bytes 245768 | tf_op jit(solution)/shard_map/ppermute | solution.py:502
  129.0 4.8 %collective-permute-start.17 = (f32[5,16,256]{2,1,0:T(8,128)S(1)}, f32[5,16,256]{2,1,0:T(8,128)S(1)}, u32[]{:S(2)}, u32[]{:S(2)}) collective-permute-start(f32[5,16,256]{2,1,0:T(8,128)S(1)} %get-tuple-element.59), channel_id=1, source_target_pairs={{0,1},{1,2},{2,3},{3,4},{4,5},{5,6},{6,7},{8,9},{9,10},{10,11},{11... | collective-permute-start | bytes 245768 | tf_op jit(solution)/shard_map/ppermute | solution.py:502
  133.8 1.9 %collective-permute-start.18 = (f32[5,16,256]{2,1,0:T(8,128)S(1)}, f32[5,16,256]{2,1,0:T(8,128)S(1)}, u32[]{:S(2)}, u32[]{:S(2)}) collective-permute-start(f32[5,16,256]{2,1,0:T(8,128)S(1)} %get-tuple-element.60), channel_id=1, source_target_pairs={{1,0},{2,1},{3,2},{4,3},{5,4},{6,5},{7,6},{9,8},{10,9},{11,10},{12... | collective-permute-start | bytes 245768 | tf_op jit(solution)/shard_map/ppermute | solution.py:502
  135.8 0.0 collective-permute-done.15.refs_9_
  135.8 0.0 collective-permute-done.16.refs_10_
  135.8 0.5 collective-permute-done.17.refs_11_
  136.2 3.9 %collective-permute-done.18.refs_12_ = f32[5,16,256]{2,1,0:T(8,128)S(1)} collective-permute-done((f32[5,16,256]{2,1,0:T(8,128)S(1)}, f32[5,16,256]{2,1,0:T(8,128)S(1)}, u32[]{:S(2)}, u32[]{:S(2)}) %collective-permute-start.18) | collective-permute-done | bytes 81952 | tf_op jit(solution)/shard_map/ppermute | solution.py:502
  140.2 7.5 %step_two.1 = f32[5,16,16,256]{3,2,1,0:T(8,128)} custom-call(bf16[240,240]{1,0:T(8,128)(2,1)S(1)} %pad_maximum_fusion.refs_0_, bf16[80,240]{1,0:T(8,128)(2,1)S(1)} %pad_maximum_fusion.1.refs_1_, f32[5,16,16,256]{3,2,1,0:T(8,128)S(1)} %copy-done, s32[16,16,256]{2,1,0:T(8,128)S(1)} %copy-done.8, f32[16,80,256]{2,1,0:T(8,128)S(1)} %get-tuple-element.56.refs_4_, ...), custom_call_target="tpu_custom_call" | custom-call | tf_op jit(solution)/shard_map/step_two/pallas_call | solution.py:487
  (52 shorter events, 0.1 us)
Async XLA Ops:
  0.0 14.9 %copy-start.24 = (f32[10,160,1]{1,0,2:T(8,128)S(1)}, f32[10,160,1]{1,0,2:T(8,128)}, u32[]{:S(2)}) copy-start(f32[10,160,1]{1,0,2:T(8,128)} %constant.27) | copy-start | bytes 19204
  0.0 15.2 %copy-start.21 = (f32[80,160]{1,0:T(8,128)S(1)}, f32[80,160]{1,0:T(8,128)}, u32[]{:S(2)}) copy-start(f32[80,160]{1,0:T(8,128)} %constant.20.clone) | copy-start | bytes 153604
  0.0 15.2 %copy-start.26 = (f32[80,5,1]{0,1,2:T(8,128)S(1)}, f32[80,5,1]{0,1,2:T(8,128)}, u32[]{:S(2)}) copy-start(f32[80,5,1]{0,1,2:T(8,128)} %constant.28) | copy-start | bytes 4804
  0.0 14.9 %copy-start.25 = (f32[3,5,5]{2,0,1:T(4,128)S(1)}, f32[3,5,5]{2,0,1:T(4,128)}, u32[]{:S(2)}) copy-start(f32[3,5,5]{2,0,1:T(4,128)} %param.15) | copy-start | bytes 904
  8.1 12.0 %collective-permute-start.2 = (f32[16]{0:T(128)S(1)}, f32[16]{0:T(128)S(1)}, u32[]{:S(2)}, u32[]{:S(2)}) collective-permute-start(f32[16]{0:T(128)S(1)} %reduce_sum.9), channel_id=1, source_target_pairs={{0,8},{8,0},{16,24},{24,16},{1,9},{9,1},{17,25},{25,17},{2,10},{10... | collective-permute-start | bytes 200 | tf_op jit(solution)/shard_map/ppermute | solution.py:515
  8.1 20.8 %collective-permute-start = (bf16[8,5,16,256]{3,2,1,0:T(8,128)(2,1)}, bf16[8,5,16,256]{3,2,1,0:T(8,128)(2,1)S(1)}, u32[]{:S(2)}, u32[]{:S(2)}) collective-permute-start(bf16[8,5,16,256]{3,2,1,0:T(8,128)(2,1)} %get-tuple-element.33.refs_3_), channel_id=1, source_target_pairs={{0,1},{1,2},{2,3},{3,4},{4,5},{5,6},{6,7},{8,9},{9,10},{10,11},{11... | collective-permute-start | bytes 983048 | tf_op jit(solution)/shard_map/ppermute | solution.py:502
  11.6 18.1 %collective-permute-start.1 = (bf16[8,5,16,256]{3,2,1,0:T(8,128)(2,1)}, bf16[8,5,16,256]{3,2,1,0:T(8,128)(2,1)S(1)}, u32[]{:S(2)}, u32[]{:S(2)}) collective-permute-start(bf16[8,5,16,256]{3,2,1,0:T(8,128)(2,1)} %get-tuple-element.34.refs_2_), channel_id=1, source_target_pairs={{1,0},{2,1},{3,2},{4,3},{5,4},{6,5},{7,6},{9,8},{10,9},{11,10},{12... | collective-permute-start | bytes 983048 | tf_op jit(solution)/shard_map/ppermute | solution.py:502
  20.1 8.9 %collective-permute-start.3 = (f32[16]{0:T(128)S(1)}, f32[16]{0:T(128)S(1)}, u32[]{:S(2)}, u32[]{:S(2)}) collective-permute-start(f32[16]{0:T(128)S(1)} %add.22), channel_id=1, source_target_pairs={{0,16},{8,24},{16,0},{24,8},{1,17},{9,25},{17,1},{25,9},{2,18},{10... | collective-permute-start | bytes 200 | tf_op jit(solution)/shard_map/ppermute | solution.py:515
  20.7 21.3 %copy-start = (f32[5,16,16,256]{3,2,1,0:T(8,128)S(1)}, f32[5,16,16,256]{3,2,1,0:T(8,128)}, u32[]{:S(2)}) copy-start(f32[5,16,16,256]{3,2,1,0:T(8,128)} %refs_2_.3) | copy-start | bytes 3932164
  20.7 21.3 %copy-start.2 = (f32[16,80,256]{2,1,0:T(8,128)S(1)}, f32[16,80,256]{2,1,0:T(8,128)}, u32[]{:S(2)}) copy-start(f32[16,80,256]{2,1,0:T(8,128)} %get-tuple-element.36.refs_6_.refs_4_) | copy-start | bytes 3932164
  20.7 21.3 %copy-start.3 = (f32[16,80,256]{2,1,0:T(8,128)S(1)}, f32[16,80,256]{2,1,0:T(8,128)}, u32[]{:S(2)}) copy-start(f32[16,80,256]{2,1,0:T(8,128)} %get-tuple-element.37.refs_7_.refs_5_) | copy-start | bytes 3932164
  20.7 21.3 %copy-start.9 = (bf16[8,5,16,256]{3,2,1,0:T(8,128)(2,1)S(1)}, bf16[8,5,16,256]{3,2,1,0:T(8,128)(2,1)}, u32[]{:S(2)}) copy-start(bf16[8,5,16,256]{3,2,1,0:T(8,128)(2,1)} %get-tuple-element.34.refs_2_) | copy-start | bytes 983044
  20.7 21.3 %copy-start.10 = (bf16[8,5,16,256]{3,2,1,0:T(8,128)(2,1)S(1)}, bf16[8,5,16,256]{3,2,1,0:T(8,128)(2,1)}, u32[]{:S(2)}) copy-start(bf16[8,5,16,256]{3,2,1,0:T(8,128)(2,1)} %get-tuple-element.33.refs_3_) | copy-start | bytes 983044
  20.7 21.3 %copy-start.15 = (s32[16]{0:T(128)S(1)}, s32[16]{0:T(128)}, u32[]{:S(2)}) copy-start(s32[16]{0:T(128)} %refs_0_.3) | copy-start | bytes 196
  29.0 0.7 copy-start.11
  29.7 0.7 copy-start.13
  30.4 3.5 %collective-permute-start.4 = (f32[16]{0:T(128)S(1)}, f32[16]{0:T(128)S(1)}, u32[]{:S(2)}, u32[]{:S(2)}) collective-permute-start(f32[16]{0:T(128)S(1)} %add.23), channel_id=1, source_target_pairs={{0,1},{1,0},{2,3},{3,2},{4,5},{5,4},{6,7},{7,6},{8,9},{9,8},{10,11... | collective-permute-start | bytes 200 | tf_op jit(solution)/shard_map/ppermute | solution.py:515
  34.0 3.5 %collective-permute-start.5 = (f32[16]{0:T(128)S(1)}, f32[16]{0:T(128)S(1)}, u32[]{:S(2)}, u32[]{:S(2)}) collective-permute-start(f32[16]{0:T(128)S(1)} %add.24), channel_id=1, source_target_pairs={{0,2},{1,3},{2,0},{3,1},{4,6},{5,7},{6,4},{7,5},{8,10},{9,11},{10,... | collective-permute-start | bytes 200 | tf_op jit(solution)/shard_map/ppermute | solution.py:515
  37.5 4.4 %collective-permute-start.6 = (f32[16]{0:T(128)S(1)}, f32[16]{0:T(128)S(1)}, u32[]{:S(2)}, u32[]{:S(2)}) collective-permute-start(f32[16]{0:T(128)S(1)} %add.25), channel_id=1, source_target_pairs={{0,4},{1,5},{2,6},{3,7},{4,0},{5,1},{6,2},{7,3},{8,12},{9,13},{10,... | collective-permute-start | bytes 200 | tf_op jit(solution)/shard_map/ppermute | solution.py:515
  42.0 6.2 %copy-start.17 = (f32[16]{0:T(128)}, f32[16]{0:T(128)S(1)}, u32[]{:S(2)}) copy-start(f32[16]{0:T(128)S(1)} %add_rsqrt_fusion.amp.refs_1_) | copy-start | bytes 196
  42.0 1.3 copy-start.4
  43.3 1.3 copy-start.6
  44.6 14.9 %copy-start.19 = (bf16[80,160]{1,0:T(8,128)(2,1)S(1)}, bf16[80,160]{1,0:T(8,128)(2,1)}, u32[]{:S(2)}) copy-start(bf16[80,160]{1,0:T(8,128)(2,1)} %get-tuple-element.62.lw) | copy-start | bytes 76804
  44.6 15.7 %copy-start.23 = (bf16[80,240]{1,0:T(8,128)(2,1)S(1)}, bf16[80,240]{1,0:T(8,128)(2,1)}, u32[]{:S(2)}) copy-start(bf16[80,240]{1,0:T(8,128)(2,1)} %constant.26) | copy-start | bytes 115204
  48.1 46.2 %collective-permute-start.7 = (bf16[20,5,16,256]{3,2,1,0:T(8,128)(2,1)}, bf16[20,5,16,256]{3,2,1,0:T(8,128)(2,1)S(1)}, u32[]{:S(2)}, u32[]{:S(2)}) collective-permute-start(bf16[20,5,16,256]{3,2,1,0:T(8,128)(2,1)} %get-tuple-element.45), channel_id=1, source_target_pairs={{0,8},{8,16},{16,24},{1,9},{9,17},{17,25},{2,10},{10,18},{18,26},{... | collective-permute-start | bytes 2457608 | tf_op jit(solution)/shard_map/ppermute | solution.py:502
  50.1 44.3 %collective-permute-start.8 = (bf16[20,5,16,256]{3,2,1,0:T(8,128)(2,1)}, bf16[20,5,16,256]{3,2,1,0:T(8,128)(2,1)S(1)}, u32[]{:S(2)}, u32[]{:S(2)}) collective-permute-start(bf16[20,5,16,256]{3,2,1,0:T(8,128)(2,1)} %get-tuple-element.46), channel_id=1, source_target_pairs={{8,0},{16,8},{24,16},{9,1},{17,9},{25,17},{10,2},{18,10},{26,18},{... | collective-permute-start | bytes 2457608 | tf_op jit(solution)/shard_map/ppermute | solution.py:502
  53.7 40.6 %collective-permute-start.10 = (bf16[12,5,16,256]{3,2,1,0:T(8,128)(2,1)}, bf16[12,5,16,256]{3,2,1,0:T(8,128)(2,1)}, u32[]{:S(2)}, u32[]{:S(2)}) collective-permute-start(bf16[12,5,16,256]{3,2,1,0:T(8,128)(2,1)} %get-tuple-element.50), channel_id=1, source_target_pairs={{1,0},{2,1},{3,2},{4,3},{5,4},{6,5},{7,6},{9,8},{10,9},{11,10},{12... | collective-permute-start | bytes 1474568 | tf_op jit(solution)/shard_map/ppermute | solution.py:502
  56.1 38.2 %collective-permute-start.9 = (bf16[12,5,16,256]{3,2,1,0:T(8,128)(2,1)}, bf16[12,5,16,256]{3,2,1,0:T(8,128)(2,1)}, u32[]{:S(2)}, u32[]{:S(2)}) collective-permute-start(bf16[12,5,16,256]{3,2,1,0:T(8,128)(2,1)} %get-tuple-element.49), channel_id=1, source_target_pairs={{0,1},{1,2},{2,3},{3,4},{4,5},{5,6},{6,7},{8,9},{9,10},{10,11},{11... | collective-permute-start | bytes 1474568 | tf_op jit(solution)/shard_map/ppermute | solution.py:502
  61.0 33.3 %copy-start.5 = (f32[16,80,256]{2,1,0:T(8,128)S(1)}, f32[16,80,256]{2,1,0:T(8,128)}, u32[]{:S(2)}) copy-start(f32[16,80,256]{2,1,0:T(8,128)} %get-tuple-element.38.refs_8_.refs_6_) | copy-start | bytes 3932164
  61.0 33.3 %copy-start.7 = (f32[16,80,256]{2,1,0:T(8,128)S(1)}, f32[16,80,256]{2,1,0:T(8,128)}, u32[]{:S(2)}) copy-start(f32[16,80,256]{2,1,0:T(8,128)} %get-tuple-element.39.refs_9_.refs_7_) | copy-start | bytes 3932164
  61.0 33.4 %copy-start.16 = (s32[16]{0:T(128)S(1)}, s32[16]{0:T(128)}, u32[]{:S(2)}) copy-start(s32[16]{0:T(128)} %refs_0_.3) | copy-start | bytes 196
  61.0 33.4 %copy-start.18 = (f32[16]{0:T(128)S(1)}, f32[16]{0:T(128)}, u32[]{:S(2)}) copy-start(f32[16]{0:T(128)} %copy-done.17) | copy-start | bytes 196
  94.4 1.3 copy-start.1
  95.7 0.9 copy-start.8
  96.6 1.0 copy-start.12
  97.6 1.0 copy-start.14
  98.6 15.0 %copy-start.20 = (bf16[80,160]{1,0:T(8,128)(2,1)S(1)}, bf16[80,160]{1,0:T(8,128)(2,1)}, u32[]{:S(2)}) copy-start(bf16[80,160]{1,0:T(8,128)(2,1)} %get-tuple-element.62.lw) | copy-start | bytes 76804
  98.6 15.0 %copy-start.22 = (bf16[80,80]{1,0:T(8,128)(2,1)S(1)}, bf16[80,80]{1,0:T(8,128)(2,1)}, u32[]{:S(2)}) copy-start(bf16[80,80]{1,0:T(8,128)(2,1)} %slice.25) | copy-start | bytes 38404
  101.2 12.4 %collective-permute-start.11 = (f32[5,16,256]{2,1,0:T(8,128)S(1)}, f32[5,16,256]{2,1,0:T(8,128)S(1)}, u32[]{:S(2)}, u32[]{:S(2)}) collective-permute-start(f32[5,16,256]{2,1,0:T(8,128)S(1)} %get-tuple-element.52), channel_id=1, source_target_pairs={{0,8},{8,16},{16,24},{1,9},{9,17},{17,25},{2,10},{10,18},{18,26},{... | collective-permute-start | bytes 245768 | tf_op jit(solution)/shard_map/ppermute | solution.py:502
  103.1 10.5 %collective-permute-start.12 = (f32[5,16,256]{2,1,0:T(8,128)S(1)}, f32[5,16,256]{2,1,0:T(8,128)S(1)}, u32[]{:S(2)}, u32[]{:S(2)}) collective-permute-start(f32[5,16,256]{2,1,0:T(8,128)S(1)} %get-tuple-element.53), channel_id=1, source_target_pairs={{8,0},{16,8},{24,16},{9,1},{17,9},{25,17},{10,2},{18,10},{26,18},{... | collective-permute-start | bytes 245768 | tf_op jit(solution)/shard_map/ppermute | solution.py:502
  106.8 7.3 %collective-permute-start.13 = (f32[5,16,256]{2,1,0:T(8,128)S(1)}, f32[5,16,256]{2,1,0:T(8,128)S(1)}, u32[]{:S(2)}, u32[]{:S(2)}) collective-permute-start(f32[5,16,256]{2,1,0:T(8,128)S(1)} %get-tuple-element.54), channel_id=1, source_target_pairs={{0,1},{1,2},{2,3},{3,4},{4,5},{5,6},{6,7},{8,9},{9,10},{10,11},{11... | collective-permute-start | bytes 245768 | tf_op jit(solution)/shard_map/ppermute | solution.py:502
  110.2 6.6 %collective-permute-start.14 = (f32[5,16,256]{2,1,0:T(8,128)S(1)}, f32[5,16,256]{2,1,0:T(8,128)S(1)}, u32[]{:S(2)}, u32[]{:S(2)}) collective-permute-start(f32[5,16,256]{2,1,0:T(8,128)S(1)} %get-tuple-element.55), channel_id=1, source_target_pairs={{1,0},{2,1},{3,2},{4,3},{5,4},{6,5},{7,6},{9,8},{10,9},{11,10},{12... | collective-permute-start | bytes 245768 | tf_op jit(solution)/shard_map/ppermute | solution.py:502
  123.4 12.3 %collective-permute-start.15 = (f32[5,16,256]{2,1,0:T(8,128)S(1)}, f32[5,16,256]{2,1,0:T(8,128)S(1)}, u32[]{:S(2)}, u32[]{:S(2)}) collective-permute-start(f32[5,16,256]{2,1,0:T(8,128)S(1)} %get-tuple-element.57), channel_id=1, source_target_pairs={{0,8},{8,16},{16,24},{1,9},{9,17},{17,25},{2,10},{10,18},{18,26},{... | collective-permute-start | bytes 245768 | tf_op jit(solution)/shard_map/ppermute | solution.py:502
  125.3 10.4 %collective-permute-start.16 = (f32[5,16,256]{2,1,0:T(8,128)S(1)}, f32[5,16,256]{2,1,0:T(8,128)S(1)}, u32[]{:S(2)}, u32[]{:S(2)}) collective-permute-start(f32[5,16,256]{2,1,0:T(8,128)S(1)} %get-tuple-element.58), channel_id=1, source_target_pairs={{8,0},{16,8},{24,16},{9,1},{17,9},{25,17},{10,2},{18,10},{26,18},{... | collective-permute-start | bytes 245768 | tf_op jit(solution)/shard_map/ppermute | solution.py:502
  129.0 7.2 %collective-permute-start.17 = (f32[5,16,256]{2,1,0:T(8,128)S(1)}, f32[5,16,256]{2,1,0:T(8,128)S(1)}, u32[]{:S(2)}, u32[]{:S(2)}) collective-permute-start(f32[5,16,256]{2,1,0:T(8,128)S(1)} %get-tuple-element.59), channel_id=1, source_target_pairs={{0,1},{1,2},{2,3},{3,4},{4,5},{5,6},{6,7},{8,9},{9,10},{10,11},{11... | collective-permute-start | bytes 245768 | tf_op jit(solution)/shard_map/ppermute | solution.py:502
  133.8 6.3 %collective-permute-start.18 = (f32[5,16,256]{2,1,0:T(8,128)S(1)}, f32[5,16,256]{2,1,0:T(8,128)S(1)}, u32[]{:S(2)}, u32[]{:S(2)}) collective-permute-start(f32[5,16,256]{2,1,0:T(8,128)S(1)} %get-tuple-element.60), channel_id=1, source_target_pairs={{1,0},{2,1},{3,2},{4,3},{5,4},{6,5},{7,6},{9,8},{10,9},{11,10},{12... | collective-permute-start | bytes 245768 | tf_op jit(solution)/shard_map/ppermute | solution.py:502

commit v5 on v4

--- a/solution.py
+++ b/solution.py
@@ -164,28 +164,34 @@
     )(lw, modes)
 
 
-def summed(pick, amp, parts, w, j):
-    nm = w.shape[0]
-    n, nz = parts[0][0].shape[2:]
+def summed(pick, amp, parts, w):
+    n, nz = w.shape[1:]
     total = jnp.zeros((n, nz), F32)
     m = 0
     for u, count in parts:
         for k in range(count):
-            total = total + amp[m] * (u[k, j].astype(F32) * w[pick[m], pl.ds(pl.multiple_of(j * n, n), n), :])
+            total = total + amp[m] * (u[k, 0].astype(F32) * w[pick[m]])
             m += 1
     return total
 
 
-def by_face(refs):
-    modes = [ref.shape[0] - TAIL for ref in refs]
-    parts = [[(refs[f], modes[f])] for f in range(2)]
-    parts += [[(refs[f], refs[f].shape[0]), (refs[f + 2], modes[f + 2])] for f in (2, 3)]
-    return parts, [refs[0], refs[1], refs[4], refs[5]]
+def by_face(refs, nm):
+    first = refs[2].shape[0]
+    return [[(refs[f], nm)] for f in range(2)] + [[(refs[f], first), (refs[f + 2], nm - first)] for f in (2, 3)]
 
 
 def whole_of(ref, part):
     n = ref.shape[0] - TAIL + 2 * part
     return ref[n].astype(F32) + ref[n + 1].astype(F32)
+
+
+def of_variable(shape, dim):
+    block = tuple(1 if i == dim else size for i, size in enumerate(shape))
+    return pl.BlockSpec(block, lambda j: tuple(j if i == dim else 0 for i in range(len(shape))))
+
+
+def rows_of_variable(shape, nv):
+    return pl.BlockSpec((shape[0], shape[1] // nv, shape[2]), lambda j: (0, j, 0))
 
 
 def faces_kernel(pick, amp, base, *refs):
@@ -193,35 +199,35 @@
     w = refs[6:10]
     tails = refs[10:14]
     scratch = refs[14]
-    nv, nx, ny, nz = base.shape
-    parts, _ = by_face(u)
-
-    def body(j, carry):
-        lines = [base[j, 0], base[j, nx - 1], *edge_lines(base[j], scratch)]
-        for f in range(4):
-            for n, value in enumerate((summed(pick, amp, parts[f], w[f], j), lines[f])):
-                hi = value.astype(BF16)
-                tails[f][2 * n, j] = hi
-                tails[f][2 * n + 1, j] = (value - hi.astype(F32)).astype(BF16)
-        return carry
-
-    lax.fori_loop(0, nv, body, 0)
+    nx = base.shape[1]
+    parts = by_face(u, w[0].shape[0])
+    lines = [base[0, 0], base[0, nx - 1], *edge_lines(base[0], scratch)]
+    for f in range(4):
+        for n, value in enumerate((summed(pick, amp, parts[f], w[f]), lines[f])):
+            hi = value.astype(BF16)
+            tails[f][2 * n, 0] = hi
+            tails[f][2 * n + 1, 0] = (value - hi.astype(F32)).astype(BF16)
 
 
 def faces(pick, amp, base, u_faces, w_faces):
     nv, nx, ny, nz = base.shape
-    whole = lambda a: pl.BlockSpec(a.shape, lambda s: (0,) * a.ndim)
+    first = u_faces[2].shape[0]
+    nm = w_faces[0].shape[0]
+    counts = [nm, nm, first, first, nm - first, nm - first]
     tailed = [u_faces[f] for f in (0, 1, 4, 5)]
     at = [a.shape[0] // TAIL - 1 for a in tailed]
     return pl.pallas_call(
         faces_kernel,
-        grid=(1,),
-        in_specs=[in_smem()] * 2 + [whole(a) for a in (base, *u_faces, *w_faces)],
-        out_specs=[pl.BlockSpec((TAIL,) + a.shape[1:], lambda s, n=n: (n, 0, 0, 0)) for a, n in zip(tailed, at)],
+        grid=(nv,),
+        in_specs=[in_smem()] * 2
+        + [of_variable(base.shape, 0)]
+        + [of_variable((count,) + a.shape[1:], 1) for a, count in zip(u_faces, counts)]
+        + [rows_of_variable(a.shape, nv) for a in w_faces],
+        out_specs=[pl.BlockSpec((TAIL, 1) + a.shape[2:], lambda j, n=n: (n, j, 0, 0)) for a, n in zip(tailed, at)],
         out_shape=[sds(a.shape, BF16) for a in tailed],
         input_output_aliases={3: 0, 4: 1, 7: 2, 8: 3},
         scratch_shapes=[pltpu.VMEM((nz // LANES, nx * ny, LANES), F32)],
-        compiler_params=params(40),
+        compiler_params=params(56),
         name="faces",
     )(pick, amp, base, *u_faces, *w_faces)
 
@@ -241,7 +247,7 @@
     return jnp.where(row == n - 1, hi, pltpu.roll(a, rows - 1, 0)) - jnp.where(row == 0, lo, pltpu.roll(a, 1, 0))
 
 
-def main_kernel(pick, amp, lw, u_hbm, q_hbm, out, u_buf, q_buf, even, odd, acc, c0, u_sem, q_sem):
+def main_kernel(pick, amp, lw, u_hbm, q_hbm, out, u_buf, q_buf, even, odd, u_even, u_odd, acc, c0, u_sem, q_sem):
     nx, nm, nv, ny, nz = u_buf.shape
     rows = nv * ny
 
@@ -259,10 +265,9 @@
 
     def products(p, m, dest):
         qm = q_buf[p, pick[m]].reshape(rows, nz)
-        u = u_buf[p, m].reshape(rows, nz)
-        dest[m] = jnp.dot(lw[...], jnp.concatenate([qm, qm, u], axis=0), preferred_element_type=F32)
-
-    def plane(p, src, dest):
+        dest[m] = jnp.dot(lw[...], jnp.concatenate([qm, qm], axis=0), preferred_element_type=F32)
+
+    def plane(p, src, dest, u_src, u_dest):
         after = jnp.minimum(p + 1, nx - 1)
 
         @pl.when(p < nx - 1)
@@ -271,45 +276,48 @@
             q_copy(after).wait()
 
         acc[...] = jnp.zeros_like(acc)
-        before = jnp.maximum(p - 1, 0)
 
         def body(step, carry):
             for k in range(GROUP):
                 products(after, step * GROUP + k, dest)
             for j in range(nv):
                 at = slice(j * ny, (j + 1) * ny)
-                sums = [acc[n, at] for n in range(4)]
+                sums = [acc[n, at] for n in range(5)]
                 for k in range(GROUP):
                     m = step * GROUP + k
-                    a = amp[m]
-                    w0, w1, w2, dy = (src[m, n * rows + j * ny : n * rows + (j + 1) * ny] for n in range(4))
-                    dx = u_buf[after, m, j].astype(F32) - u_buf[before, m, j].astype(F32)
-                    uf = u_buf[p, m, j].astype(F32)
-                    dz = diff_lanes(uf)
-                    uf = uf * a
-                    terms = [(dx * w0 + dy * w1 + dz * w2) * a, uf * w0, uf * w1, uf * w2]
+                    w0, down, up, w2 = (src[m, n * rows + j * ny : n * rows + (j + 1) * ny] for n in range(4))
+                    u = u_src[m, at]
+                    following = u_buf[after, m, j].astype(F32) * amp[m]
+                    dx = following - u_dest[m, at]
+                    u_dest[m, at] = following
+                    terms = [dx * w0 + diff_lanes(u) * w2, u * w0, u * down, u * up, u * w2]
                     sums = [v + t for v, t in zip(sums, terms)]
-                for n in range(4):
+                for n in range(5):
                     acc[n, at] = sums[n]
             return carry
 
         lax.fori_loop(0, nm // GROUP, body, 0)
-        ends = jnp.where(p == 0, 1.0, 0.0) - jnp.where(p == nx - 1, 1.0, 0.0)
+        last = jnp.where(p == nx - 1, 1.0, 0.0)
         c0[p + 1] = acc[1]
-        out[p] = acc[0] - diff_lanes(acc[3]) + ends * acc[1] - diff_rows(acc[2], ny, 0.0, 0.0)
+        row = row_of((rows, nz), ny)
+        h = acc[0] - diff_lanes(acc[4]) - last * acc[1]
+        h = h + jnp.where(row == ny - 1, 0.0, pltpu.roll(acc[2], rows - 1, 0))
+        out[p] = h + jnp.where(row == 0, 0.0, pltpu.roll(acc[3], 1, 0))
 
     u_copy(0).wait()
     q_copy(0).wait()
+    u_odd[...] = jnp.zeros_like(u_odd)
 
     def first(m, carry):
         products(0, m, even)
+        u_even[m] = u_buf[0, m].reshape(rows, nz).astype(F32) * amp[m]
         return carry
 
     lax.fori_loop(0, nm, first, 0, unroll=GROUP)
 
     def pair(i, carry):
-        plane(2 * i, even, odd)
-        plane(2 * i + 1, odd, even)
+        plane(2 * i, even, odd, u_even, u_odd)
+        plane(2 * i + 1, odd, even, u_odd, u_even)
         return carry
 
     lax.fori_loop(0, nx // 2, pair, 0)
@@ -318,7 +326,7 @@
         out[p] = out[p] - c0[p + 2] + c0[p]
         return carry
 
-    lax.fori_loop(0, nx, finish, 0)
+    lax.fori_loop(0, nx, finish, 0, unroll=4)
 
 
 def main(pick, amp, lw, direct, adjoint):
@@ -335,7 +343,9 @@
             buf,
             pltpu.VMEM((nm, 4 * rows, nz), F32),
             pltpu.VMEM((nm, 4 * rows, nz), F32),
-            pltpu.VMEM((4, rows, nz), F32),
+            pltpu.VMEM((nm, rows, nz), F32),
+            pltpu.VMEM((nm, rows, nz), F32),
+            pltpu.VMEM((5, rows, nz), F32),
             pltpu.VMEM((nx + 2, rows, nz), F32),
             pltpu.SemaphoreType.DMA((nx,)),
             pltpu.SemaphoreType.DMA((nx,)),
@@ -363,57 +373,51 @@
 
 def boundary_kernel(scale, pick, amp, local, cell, *refs):
     w = refs[0:4]
-    parts, tailed = by_face(refs[4:10])
+    halo = [refs[4 + f] for f in (4, 5, 2, 3, 0, 1)]
     field, xlo, xhi, ylo, yhi = refs[10:15]
-    add = refs[15:19]
-    nx, rows, nz = local.shape
-    nv = add[0].shape[0]
-    ny = rows // nv
+    base_halo = refs[15:19]
+    add = refs[19:23]
+    nx, ny, nz = local.shape
+    parts = by_face(halo, w[0].shape[0])
+    tailed = [halo[f] for f in (0, 1, 4, 5)]
     for f in range(4):
-        add[f][...] = whole_of(tailed[f], 0)
-
-    def face(j, carry):
-        for f in range(4):
-            add[f][j] -= summed(pick, amp, parts[f], w[f], j)
-        return carry
-
-    lax.fori_loop(0, nv, face, 0)
-
-    row = row_of((rows, nz), ny)
+        sign = 1.0 if f % 2 == 0 else -1.0
+        add[f][...] = sign * (whole_of(tailed[f], 0)[0] - summed(pick, amp, parts[f], w[f]))
+        base_halo[f][...] = whole_of(tailed[f], 1)
+    row = lax.broadcasted_iota(jnp.int32, (ny, nz), 0)
 
     def plane(x, carry):
-        lo, hi = spread(add[2], x, ny), spread(add[3], x, ny)
-        field[x] = local[x] + jnp.where(row == 0, lo, 0.0) - jnp.where(row == ny - 1, hi, 0.0)
-        return carry
-
-    lax.fori_loop(0, nx, plane, 0)
-    field[0] += add[0][...].reshape(rows, nz)
-    field[nx - 1] -= add[1][...].reshape(rows, nz)
-
-    def weigh(x, carry):
-        weight = weight_of(cell[x]) * scale
-        g = field[x] * jnp.concatenate([weight] * nv, axis=0)
+        lo, hi = add[2][pl.ds(x, 1), :], add[3][pl.ds(x, 1), :]
+        g = local[x] + jnp.where(row == 0, lo, 0.0) + jnp.where(row == ny - 1, hi, 0.0)
+        g = g + jnp.where(x == 0, 1.0, 0.0) * add[0][...] + jnp.where(x == nx - 1, 1.0, 0.0) * add[1][...]
+        g = g * (weight_of(cell[x]) * scale)
         field[x] = g
         write_lines(g, x, ny, ylo, yhi)
         return carry
 
-    lax.fori_loop(0, nx, weigh, 0)
-    xlo[...] = field[0].reshape(xlo.shape)
-    xhi[...] = field[nx - 1].reshape(xhi.shape)
+    lax.fori_loop(0, nx, plane, 0, unroll=4)
+    xlo[0] = field[0]
+    xhi[0] = field[nx - 1]
 
 
 def boundary(scale, pick, amp, local, cell, w_faces, halo):
     nx, rows, nz = local.shape
+    nv = halo[0].shape[1]
     face = [sds(halo[f].shape[1:], F32) for f in range(4)]
+    ordered = [halo[f] for f in (4, 5, 2, 3, 0, 1)]
     return pl.pallas_call(
         lambda *refs: boundary_kernel(scale, *refs),
-        in_specs=[in_smem()] * 2 + [in_vmem()] * 12,
-        out_specs=[in_vmem()] * 5,
-        out_shape=[sds(local.shape, F32)] + face,
-        scratch_shapes=[pltpu.VMEM(f.shape, F32) for f in face],
-        compiler_params=params(28),
+        grid=(nv,),
+        in_specs=[in_smem()] * 2
+        + [rows_of_variable(local.shape, nv), pl.BlockSpec(cell.shape, lambda j: (0, 0, 0))]
+        + [rows_of_variable(a.shape, nv) for a in w_faces]
+        + [of_variable(a.shape, 1) for a in ordered],
+        out_specs=[rows_of_variable(local.shape, nv)] + [of_variable(f.shape, 0) for f in face * 2],
+        out_shape=[sds(local.shape, F32)] + face * 2,
+        scratch_shapes=[pltpu.VMEM(f.shape[1:], F32) for f in face],
+        compiler_params=params(56),
         name="boundary",
-    )(pick, amp, local, cell, *w_faces, *halo)
+    )(pick, amp, local, cell, *w_faces, *ordered)
 
 
 def mix_rows(lw, values):
@@ -423,19 +427,19 @@
 
 
 def step_kernel(last, lw, lw_y, base, cell, field, *refs):
-    got_base = refs[0:4]
-    got = refs[4:8]
+    got = [refs[f] for f in (2, 3, 0, 1)]
+    got_base = refs[4:8]
     out = refs[8]
     faces = refs[9:13]
     b_pad, c0, bh_lo, bh_hi, ch_lo, ch_hi = refs[-6:]
     nv, nx, ny, nz = base.shape
     rows = nv * ny
     for f, at in ((0, 0), (1, nx + 1)):
-        b = whole_of(got_base[f], 1).reshape(rows, nz)
+        b = got_base[f][...].reshape(rows, nz)
         b_pad[at] = b
         c0[at] = b * mix_rows(lw[:rows], got[f][...].reshape(rows, nz))
     for f, bh, ch in ((2, bh_lo, ch_lo), (3, bh_hi, ch_hi)):
-        b = whole_of(got_base[f], 1)
+        b = got_base[f][...]
         bh[...] = b
         ch[...] = b * mix_rows(lw_y[...], got[f][...].reshape(nv * nx, nz)).reshape(nv, nx, nz)
 
@@ -443,7 +447,7 @@
         b_pad[x + 1] = base[:, x].reshape(rows, nz)
         return carry
 
-    lax.fori_loop(0, nx, fill, 0)
+    lax.fori_loop(0, nx, fill, 0, unroll=4)
 
     def plane(x, carry):
         w = mix_rows(lw[...], field[x])
@@ -460,7 +464,7 @@
             out[x] = h
         return carry
 
-    lax.fori_loop(0, nx, plane, 0)
+    lax.fori_loop(0, nx, plane, 0, unroll=4)
 
     def finish(x, carry):
         change = c0[x] - c0[x + 2]
@@ -472,7 +476,7 @@
             write_lines(g, x, ny, faces[2], faces[3])
         return carry
 
-    lax.fori_loop(0, nx, finish, 0)
+    lax.fori_loop(0, nx, finish, 0, unroll=4)
     if not last:
         faces[0][...] = out[0].reshape(nv, ny, nz)
         faces[1][...] = out[nx - 1].reshape(nv, ny, nz)
@@ -492,7 +496,7 @@
         scratch_shapes=[padded, padded, line, line, line, line],
         compiler_params=params(28),
         name="step_two" if last else "step_one",
-    )(lw, lw_y, base, cell, field, *got_base, *got)
+    )(lw, lw_y, base, cell, field, *got[2:], *got[:2], *got_base)
 
 
 def exchange_axis(axis, lo, hi):
@@ -503,7 +507,8 @@
 
 
 def exchange(arrays):
-    return exchange_axis("chord", *arrays[:2]) + exchange_axis("normal", *arrays[2:])
+    normal = exchange_axis("normal", *arrays[2:])
+    return exchange_axis("chord", *arrays[:2]) + normal
 
 
 def sum_over(axis, values):
@@ -525,16 +530,16 @@
     rows, cols = np.arange(nv * n), np.arange(2 * nv * n)
     left = jnp.asarray((rows[:, None] // n == np.arange(nv)[None]).astype(np.float32))
     right = jnp.asarray((cols[None] // n == np.arange(2 * nv)[:, None]).astype(np.float32))
-    mask = jnp.asarray((rows[:, None] % n == cols[None] % n).astype(np.float32))
-    wide = jnp.einsum("rj,djc,ck->drk", left, small, right, precision=lax.Precision.HIGHEST)
-    return (wide * mask).astype(BF16)
-
-
-def main_rows(lw, nv, ny):
-    dy = np.kron(np.eye(nv, dtype=np.float32), np.eye(ny, k=1, dtype=np.float32) - np.eye(ny, k=-1, dtype=np.float32))
-    rows = nv * ny
-    top = jnp.pad(lw.reshape(3 * rows, 2 * rows), ((0, 0), (0, rows)))
-    return jnp.concatenate([top, jnp.pad(jnp.asarray(dy, BF16), ((0, 0), (2 * rows, 0)))], axis=0)
+    return jnp.einsum("rj,djc,ck->drk", left, small, right, precision=lax.Precision.HIGHEST)
+
+
+def within(wide, n, cells):
+    return (wide * jnp.asarray(np.tile(cells, (wide.shape[-2] // n, wide.shape[-1] // n)))).astype(BF16)
+
+
+def main_rows(wide, n):
+    eye, below, above = (np.eye(n, k=k, dtype=np.float32) for k in (0, -1, 1))
+    return jnp.concatenate([within(wide[d], n, c) for d, c in ((0, eye), (1, below - eye), (1, eye - above), (2, eye))], axis=0)
 
 
 def step_rows(lw):
@@ -548,20 +553,22 @@
     *own, sums = pack(direct)
     early = exchange_axis("normal", *own[2:4])
     sums = sum_over("chord", jnp.sum(sums, axis=1))
-    lw_y = kron_rows(mix, ny)
-    lw_x = lw_y if nx == ny else kron_rows(mix, nx)
+    wide = kron_rows(mix, ny)
+    lw_y = within(wide, ny, np.eye(ny, dtype=np.float32))
+    lw_x = lw_y if nx == ny else within(kron_rows(mix, nx), nx, np.eye(nx, dtype=np.float32))
     w_faces = [*mix_chord(lw_y[0], adjoint), *mix_normal(lw_x[1], adjoint)]
     *early, sums = lax.optimization_barrier((*early, sums, *w_faces))[:3]
     sums = sum_over("normal", sums)
     amp = lax.rsqrt(sums / cells_all + 1e-06)
     late = exchange(faces(pick, amp, base, own, w_faces))
     halo = late[:2] + early + late[2:]
-    local = main(pick, amp, main_rows(lw_y, nv, ny), direct, adjoint)
+    local = main(pick, amp, main_rows(wide, ny), direct, adjoint)
     field, *sides = boundary(1.0 / nm, pick, amp, local, cell, w_faces, halo)
+    sides, base_halo = sides[:4], sides[4:]
     lw_step = step_rows(lw_y.reshape(3 * nv * ny, -1))
     lw_line = step_rows(lw_x[1])
-    field, *sides = apply_step(False, lw_step, lw_line, base, cell, field, late, exchange(sides))
-    return apply_step(True, lw_step, lw_line, base, cell, field, late, exchange(sides))[0]
+    field, *sides = apply_step(False, lw_step, lw_line, base, cell, field, base_halo, exchange(sides))
+    return apply_step(True, lw_step, lw_line, base, cell, field, base_halo, exchange(sides))[0]
 
 
 def solution(mesh):

time: 149 us -> 143 us (0.960)
  the two profiles are of different devices: /device:TPU:18 before, /device:TPU:5 now
where the time goes in v5:
time: 143 us; the launch traced here: 141 us
  Pallas kernels  69.1 us (48%)
  starting transfers between devices  48.5 us (34%)
  waiting for transfers between devices  12.1 us (8%)
  local copies, waits for them, and re-layouts  7.66 us (5%)
  other arithmetic  2.31 us (2%)
    ppermute x14, starting transfers between devices, exchange_axis(): return [lax.ppermute(hi, axis, up), lax.ppermute(lo, axis, down)]  42.9 us
    pallas_call x1, Pallas kernels, main(): pl.pallas_call(main_kernel, in_specs=[in_smem(), in_smem(), in_vmem(), in...  29.7 us
    pallas_call x1, Pallas kernels, mix_normal(): pl.pallas_call(mix_normal_kernel, grid=(nm // GROUP,), in_specs=[pl.Block...  8.15 us
    ppermute x14, waiting for transfers between devices, exchange_axis(): return [lax.ppermute(hi, axis, up), lax.ppermute(lo, axis, down)]  7.59 us
    pallas_call x1, Pallas kernels, pack(): pl.pallas_call(lambda *refs: direct_kernel(half, *refs), grid=(steps,), i...  7.24 us
    pallas_call x2, Pallas kernels, apply_step(): pl.pallas_call(lambda *refs: step_kernel(last, *refs), in_specs=[in_vmem(...  7.17 us
    pallas_call x1, Pallas kernels, boundary(): pl.pallas_call(lambda *refs: boundary_kernel(scale, *refs), grid=(nv,), i...  7.04 us
    unnamed x42, local copies, waits for them, and re-layouts  7.01 us
  transfers between devices with their start and end apart: 19, of which 5 were waited for; matrix products, arithmetic and copies ran while one was open for 2% of the time, Pallas kernels for 30%

profile of v5, /device:TPU:5, one launch (start us, length us, event | category | flops | bytes accessed | tf_op | source)
XLA Modules:
  0.0 140.8 jit_solution(11206416803250752866)
XLA Ops:
  0.0 7.2 %pack_direct.1 = (bf16[20,5,16,256]{3,2,1,0:T(8,128)(2,1)}, bf16[20,5,16,256]{3,2,1,0:T(8,128)(2,1)}, bf16[8,5,16,256]{3,2,1,0:T(8,128)(2,1)}, bf16[8,5,16,256]{...) custom-call(bf16[16,5,16,16,256]{4,3,2,1,0:T(8,128)(2,1)} %u_hbm.1), custom_call_target="tpu_custom_call" | custom-call | flops 15728640 | bytes 10485760 | tf_op jit(solution)/shard_map/pack_direct/pallas_call | solution.py:87
  7.3 0.8 reduce_sum.9
  8.1 0.7 collective-permute-start.2
  8.8 3.1 %collective-permute-start = (bf16[8,5,16,256]{3,2,1,0:T(8,128)(2,1)}, bf16[8,5,16,256]{3,2,1,0:T(8,128)(2,1)S(1)}, u32[]{:S(2)}, u32[]{:S(2)}) collective-permute-start(bf16[8,5,16,256]{3,2,1,0:T(8,128)(2,1)} %get-tuple-element.37.refs_3_), channel_id=1, source_target_pairs={{0,1},{1,2},{2,3},{3,4},{4,5},{5,6},{6,7},{8,9},{9,10},{10,11},{11... | collective-permute-start | bytes 983048 | tf_op jit(solution)/shard_map/ppermute | solution.py:506
  11.9 2.1 %collective-permute-start.1 = (bf16[8,5,16,256]{3,2,1,0:T(8,128)(2,1)}, bf16[8,5,16,256]{3,2,1,0:T(8,128)(2,1)S(1)}, u32[]{:S(2)}, u32[]{:S(2)}) collective-permute-start(bf16[8,5,16,256]{3,2,1,0:T(8,128)(2,1)} %get-tuple-element.38.refs_2_), channel_id=1, source_target_pairs={{1,0},{2,1},{3,2},{4,3},{5,4},{6,5},{7,6},{9,8},{10,9},{11,10},{12... | collective-permute-start | bytes 983048 | tf_op jit(solution)/shard_map/ppermute | solution.py:506
  14.2 0.2 fusion.6
  14.4 0.4 multiply_convert_fusion
  14.8 0.6 slice_bitcast_fusion
  15.5 3.8 %mix_chord.1 = (f32[16,80,256]{2,1,0:T(8,128)}, f32[16,80,256]{2,1,0:T(8,128)}) custom-call(bf16[80,160]{1,0:T(8,128)(2,1)} %get-tuple-element.73.lw, bf16[16,5,16,16,256]{4,3,2,1,0:T(8,128)(2,1)} %q_hbm.1, bf16[16,5,16,16,256]{4,3,2,1,0:T(8,128)(2,1)} %q_hbm.1), custom_call_target="tpu_custom_call" | custom-call | flops 100000000 | bytes 6000000 | tf_op jit(solution)/shard_map/mix_chord/pallas_call | solution.py:118
  19.3 0.0 collective-permute-done.2
  19.3 1.3 collective-permute-start.3
  20.5 8.1 %mix_normal.1 = (f32[16,80,256]{2,1,0:T(8,128)}, f32[16,80,256]{2,1,0:T(8,128)}) custom-call(bf16[80,160]{1,0:T(8,128)(2,1)} %get-tuple-element.74.lw, bf16[16,5,16,16,256]{4,3,2,1,0:T(8,128)(2,1)} %q_hbm.1), custom_call_target="tpu_custom_call" | custom-call | flops 15728640 | bytes 15728640 | tf_op jit(solution)/shard_map/mix_normal/pallas_call | solution.py:151
  28.7 0.0 collective-permute-done.3
  28.7 0.0 collective-permute-done.refs_10_
  28.7 0.0 collective-permute-done.1.refs_11_
  28.7 0.1 collective-permute-start.4
  28.8 2.4 %collective-permute-done.4 = f32[16]{0:T(128)S(1)} collective-permute-done((f32[16]{0:T(128)S(1)}, f32[16]{0:T(128)S(1)}, u32[]{:S(2)}, u32[]{:S(2)}) %collective-permute-start.4) | collective-permute-done | bytes 96 | tf_op jit(solution)/shard_map/ppermute | solution.py:520
  31.2 1.3 collective-permute-start.5
  32.5 1.1 collective-permute-done.5
  33.6 2.3 %collective-permute-start.6 = (f32[16]{0:T(128)S(1)}, f32[16]{0:T(128)S(1)}, u32[]{:S(2)}, u32[]{:S(2)}) collective-permute-start(f32[16]{0:T(128)S(1)} %add.21), channel_id=1, source_target_pairs={{0,4},{1,5},{2,6},{3,7},{4,0},{5,1},{6,2},{7,3},{8,12},{9,13},{10,... | collective-permute-start | bytes 200 | tf_op jit(solution)/shard_map/ppermute | solution.py:520
  35.9 1.0 collective-permute-done.6
  36.9 0.5 add_rsqrt_fusion.amp.refs_1_
  37.4 6.0 %faces.1 = (bf16[20,5,16,256]{3,2,1,0:T(8,128)(2,1)}, bf16[20,5,16,256]{3,2,1,0:T(8,128)(2,1)}, bf16[12,5,16,256]{3,2,1,0:T(8,128)(2,1)}, bf16[12,5,16,256]{3,2,1,0:T(8,128)(2,1)}) custom-call(s32[16]{0:T(128)} %refs_0_.3, f32[16]{0:T(128)} %add_rsqrt_fusion.amp.refs_1_, ...), custom_call_target="tpu_custom_call", output_to_operand_aliasing={{0}: (3, {}), {1}: (4, {}), {2}: (7, {}), {3}: (8, {})} | custom-call | tf_op jit(solution)/shard_map/faces/pallas_call | solution.py:219
  43.5 6.4 %collective-permute-start.9 = (bf16[20,5,16,256]{3,2,1,0:T(8,128)(2,1)}, bf16[20,5,16,256]{3,2,1,0:T(8,128)(2,1)S(1)}, u32[]{:S(2)}, u32[]{:S(2)}) collective-permute-start(bf16[20,5,16,256]{3,2,1,0:T(8,128)(2,1)} %get-tuple-element.53), channel_id=1, source_target_pairs={{0,8},{8,16},{16,24},{1,9},{9,17},{17,25},{2,10},{10,18},{18,26},{... | collective-permute-start | bytes 2457608 | tf_op jit(solution)/shard_map/ppermute | solution.py:506
  49.9 1.9 %collective-permute-start.10 = (bf16[20,5,16,256]{3,2,1,0:T(8,128)(2,1)}, bf16[20,5,16,256]{3,2,1,0:T(8,128)(2,1)S(1)}, u32[]{:S(2)}, u32[]{:S(2)}) collective-permute-start(bf16[20,5,16,256]{3,2,1,0:T(8,128)(2,1)} %get-tuple-element.54), channel_id=1, source_target_pairs={{8,0},{16,8},{24,16},{9,1},{17,9},{25,17},{10,2},{18,10},{26,18},{... | collective-permute-start | bytes 2457608 | tf_op jit(solution)/shard_map/ppermute | solution.py:506
  51.8 4.0 %collective-permute-start.7 = (bf16[12,5,16,256]{3,2,1,0:T(8,128)(2,1)}, bf16[12,5,16,256]{3,2,1,0:T(8,128)(2,1)S(1)}, u32[]{:S(2)}, u32[]{:S(2)}) collective-permute-start(bf16[12,5,16,256]{3,2,1,0:T(8,128)(2,1)} %get-tuple-element.49), channel_id=1, source_target_pairs={{0,1},{1,2},{2,3},{3,4},{4,5},{5,6},{6,7},{8,9},{9,10},{10,11},{11... | collective-permute-start | bytes 1474568 | tf_op jit(solution)/shard_map/ppermute | solution.py:506
  55.8 1.9 %collective-permute-start.8 = (bf16[12,5,16,256]{3,2,1,0:T(8,128)(2,1)}, bf16[12,5,16,256]{3,2,1,0:T(8,128)(2,1)S(1)}, u32[]{:S(2)}, u32[]{:S(2)}) collective-permute-start(bf16[12,5,16,256]{3,2,1,0:T(8,128)(2,1)} %get-tuple-element.50), channel_id=1, source_target_pairs={{1,0},{2,1},{3,2},{4,3},{5,4},{6,5},{7,6},{9,8},{10,9},{11,10},{12... | collective-permute-start | bytes 1474568 | tf_op jit(solution)/shard_map/ppermute | solution.py:506
  57.8 0.1 pad_maximum_fusion.1.refs_0_
  58.0 0.7 pad_maximum_fusion.lw
  58.7 29.7 %main.1.refs_2_ = f32[16,80,256]{2,1,0:T(8,128)} custom-call(s32[16]{0:T(128)} %refs_0_.3, f32[16]{0:T(128)} %add_rsqrt_fusion.amp.refs_1_, bf16[320,160]{1,0:T(8,128)(2,1)} %pad_maximum_fusion.lw, bf16[16,5,16,16,256]{4,3,2,1,0:T(8,128)(2,1)} %u_hbm.1, bf16[16,5,16,16,256]{4,3,2,1,0:T(8,128)(2,1)} %q_hbm.1), custom_call_target="tpu_custom_call" | custom-call | flops 1000000 | bytes 100000 | tf_op jit(solution)/shard_map/main/pallas_call | solution.py:336
  88.3 0.0 copy-start
  88.4 0.0 copy-start.1
  88.4 0.0 collective-permute-done.7.refs_8_
  88.4 0.0 collective-permute-done.8.refs_9_
  88.4 0.0 collective-permute-done.9.refs_12_
  88.4 0.0 collective-permute-done.10.refs_13_
  88.4 0.8 copy-done.10
  89.2 0.2 copy-done.11
  89.4 0.2 copy-done.7
  89.6 1.0 copy-done.8
  90.5 7.0 %boundary.1 = (f32[16,80,256]{2,1,0:T(8,128)}, f32[5,16,256]{2,1,0:T(8,128)}, f32[5,16,256]{2,1,0:T(8,128)}, f32[5,16,256]{2,1,0:T(8,128)}, f32[5,16,256]{2,1,0:...) custom-call(s32[16]{0:T(128)} %refs_0_.3, ...), custom_call_target="tpu_custom_call" | custom-call | tf_op jit(solution)/shard_map/boundary/pallas_call | solution.py:408
  97.6 4.2 %collective-permute-start.11 = (f32[5,16,256]{2,1,0:T(8,128)}, f32[5,16,256]{2,1,0:T(8,128)S(1)}, u32[]{:S(2)}, u32[]{:S(2)}) collective-permute-start(f32[5,16,256]{2,1,0:T(8,128)} %get-tuple-element.56), channel_id=1, source_target_pairs={{0,1},{1,2},{2,3},{3,4},{4,5},{5,6},{6,7},{8,9},{9,10},{10,11},{11... | collective-permute-start | bytes 245768 | tf_op jit(solution)/shard_map/ppermute | solution.py:506
  101.8 1.9 %collective-permute-start.12 = (f32[5,16,256]{2,1,0:T(8,128)}, f32[5,16,256]{2,1,0:T(8,128)S(1)}, u32[]{:S(2)}, u32[]{:S(2)}) collective-permute-start(f32[5,16,256]{2,1,0:T(8,128)} %get-tuple-element.57), channel_id=1, source_target_pairs={{1,0},{2,1},{3,2},{4,3},{5,4},{6,5},{7,6},{9,8},{10,9},{11,10},{12... | collective-permute-start | bytes 245768 | tf_op jit(solution)/shard_map/ppermute | solution.py:506
  103.8 4.5 %collective-permute-start.13 = (f32[5,16,256]{2,1,0:T(8,128)}, f32[5,16,256]{2,1,0:T(8,128)S(1)}, u32[]{:S(2)}, u32[]{:S(2)}) collective-permute-start(f32[5,16,256]{2,1,0:T(8,128)} %get-tuple-element.58), channel_id=1, source_target_pairs={{0,8},{8,16},{16,24},{1,9},{9,17},{17,25},{2,10},{10,18},{18,26},{... | collective-permute-start | bytes 245768 | tf_op jit(solution)/shard_map/ppermute | solution.py:506
  108.3 1.9 %collective-permute-start.14 = (f32[5,16,256]{2,1,0:T(8,128)}, f32[5,16,256]{2,1,0:T(8,128)S(1)}, u32[]{:S(2)}, u32[]{:S(2)}) collective-permute-start(f32[5,16,256]{2,1,0:T(8,128)} %get-tuple-element.59), channel_id=1, source_target_pairs={{8,0},{16,8},{24,16},{9,1},{17,9},{25,17},{10,2},{18,10},{26,18},{... | collective-permute-start | bytes 245768 | tf_op jit(solution)/shard_map/ppermute | solution.py:506
  110.2 0.1 pad_maximum_fusion.2.refs_1_
  110.3 0.0 collective-permute-done.11.refs_5_
  110.3 0.0 collective-permute-done.12.refs_6_
  110.3 0.0 collective-permute-done.13.refs_7_
  110.3 3.9 %collective-permute-done.14.refs_8_ = f32[5,16,256]{2,1,0:T(8,128)S(1)} collective-permute-done((f32[5,16,256]{2,1,0:T(8,128)}, f32[5,16,256]{2,1,0:T(8,128)S(1)}, u32[]{:S(2)}, u32[]{:S(2)}) %collective-permute-start.14) | collective-permute-done | bytes 81952 | tf_op jit(solution)/shard_map/ppermute | solution.py:506
  114.2 1.3 copy-done.2
  115.6 0.9 copy-done.3
  116.4 0.9 copy-done.4
  117.3 0.9 copy-done.5
  118.2 0.9 copy-done.6
  119.1 3.1 %step_one.1 = (f32[16,80,256]{2,1,0:T(8,128)S(1)}, f32[5,16,256]{2,1,0:T(8,128)S(1)}, f32[5,16,256]{2,1,0:T(8,128)S(1)}, f32[5,16,256]{2,1,0:T(8,128)S(1)}, f32[5,16,256]{2,1,0:T(8,128)S(1)}) custom-call(bf16[240,240]{1,0:T(8,128)(2,1)S(1)} %pad_maximum_fusion.1.refs_0_, bf16[80,240]{1,0:T(8,128)(2,1)S(1)} %pad_maximum_fusion.2.refs_1_, ...), custom_call_target="tpu_custom_call" | custom-call | tf_op jit(solution)/shard_map/step_one/pallas_call | solution.py:491
  122.2 4.5 %collective-permute-start.15 = (f32[5,16,256]{2,1,0:T(8,128)S(1)}, f32[5,16,256]{2,1,0:T(8,128)S(1)}, u32[]{:S(2)}, u32[]{:S(2)}) collective-permute-start(f32[5,16,256]{2,1,0:T(8,128)S(1)} %get-tuple-element.65), channel_id=1, source_target_pairs={{0,1},{1,2},{2,3},{3,4},{4,5},{5,6},{6,7},{8,9},{9,10},{10,11},{11... | collective-permute-start | bytes 245768 | tf_op jit(solution)/shard_map/ppermute | solution.py:506
  126.8 1.9 %collective-permute-start.16 = (f32[5,16,256]{2,1,0:T(8,128)S(1)}, f32[5,16,256]{2,1,0:T(8,128)S(1)}, u32[]{:S(2)}, u32[]{:S(2)}) collective-permute-start(f32[5,16,256]{2,1,0:T(8,128)S(1)} %get-tuple-element.66), channel_id=1, source_target_pairs={{1,0},{2,1},{3,2},{4,3},{5,4},{6,5},{7,6},{9,8},{10,9},{11,10},{12... | collective-permute-start | bytes 245768 | tf_op jit(solution)/shard_map/ppermute | solution.py:506
  128.7 2.2 %collective-permute-start.17 = (f32[5,16,256]{2,1,0:T(8,128)S(1)}, f32[5,16,256]{2,1,0:T(8,128)S(1)}, u32[]{:S(2)}, u32[]{:S(2)}) collective-permute-start(f32[5,16,256]{2,1,0:T(8,128)S(1)} %get-tuple-element.67), channel_id=1, source_target_pairs={{0,8},{8,16},{16,24},{1,9},{9,17},{17,25},{2,10},{10,18},{18,26},{... | collective-permute-start | bytes 245768 | tf_op jit(solution)/shard_map/ppermute | solution.py:506
  131.0 2.1 %collective-permute-start.18 = (f32[5,16,256]{2,1,0:T(8,128)S(1)}, f32[5,16,256]{2,1,0:T(8,128)S(1)}, u32[]{:S(2)}, u32[]{:S(2)}) collective-permute-start(f32[5,16,256]{2,1,0:T(8,128)S(1)} %get-tuple-element.68), channel_id=1, source_target_pairs={{8,0},{16,8},{24,16},{9,1},{17,9},{25,17},{10,2},{18,10},{26,18},{... | collective-permute-start | bytes 245768 | tf_op jit(solution)/shard_map/ppermute | solution.py:506
  133.1 0.0 collective-permute-done.16.refs_6_
  133.1 0.0 collective-permute-done.17.refs_7_
  133.1 3.6 %collective-permute-done.18.refs_8_ = f32[5,16,256]{2,1,0:T(8,128)S(1)} collective-permute-done((f32[5,16,256]{2,1,0:T(8,128)S(1)}, f32[5,16,256]{2,1,0:T(8,128)S(1)}, u32[]{:S(2)}, u32[]{:S(2)}) %collective-permute-start.18) | collective-permute-done | bytes 81952 | tf_op jit(solution)/shard_map/ppermute | solution.py:506
  136.7 4.0 %step_two.1 = f32[5,16,16,256]{3,2,1,0:T(8,128)} custom-call(bf16[240,240]{1,0:T(8,128)(2,1)S(1)} %pad_maximum_fusion.1.refs_0_, bf16[80,240]{1,0:T(8,128)(2,1)S(1)} %pad_maximum_fusion.2.refs_1_, f32[5,16,16,256]{3,2,1,0:T(8,128)S(1)} %copy-done, s32[16,16,256]{2,1,0:T(8,128)S(1)} %copy-done.1, f32[16,80,256]{2,1,0:T(8,128)S(1)} %get-tuple-element.64.refs_4_, ...), custom_call_target="tpu_custom_call" | custom-call | tf_op jit(solution)/shard_map/step_two/pallas_call | solution.py:491
  (41 shorter events, 0.1 us)
Async XLA Ops:
  0.0 14.1 %copy-start.18 = (f32[10,160,1]{1,0,2:T(8,128)S(1)}, f32[10,160,1]{1,0,2:T(8,128)}, u32[]{:S(2)}) copy-start(f32[10,160,1]{1,0,2:T(8,128)} %constant.26) | copy-start | bytes 19204
  0.0 14.4 %copy-start.17 = (f32[80,160]{1,0:T(8,128)S(1)}, f32[80,160]{1,0:T(8,128)}, u32[]{:S(2)}) copy-start(f32[80,160]{1,0:T(8,128)} %constant.19.clone) | copy-start | bytes 153604
  0.0 14.4 %copy-start.20 = (f32[80,5,1]{0,1,2:T(8,128)S(1)}, f32[80,5,1]{0,1,2:T(8,128)}, u32[]{:S(2)}) copy-start(f32[80,5,1]{0,1,2:T(8,128)} %constant.27) | copy-start | bytes 4804
  0.0 14.1 %copy-start.19 = (f32[3,5,5]{2,0,1:T(4,128)S(1)}, f32[3,5,5]{2,0,1:T(4,128)}, u32[]{:S(2)}) copy-start(f32[3,5,5]{2,0,1:T(4,128)} %param.18) | copy-start | bytes 904
  8.1 11.2 %collective-permute-start.2 = (f32[16]{0:T(128)S(1)}, f32[16]{0:T(128)S(1)}, u32[]{:S(2)}, u32[]{:S(2)}) collective-permute-start(f32[16]{0:T(128)S(1)} %reduce_sum.9), channel_id=1, source_target_pairs={{0,8},{8,0},{16,24},{24,16},{1,9},{9,1},{17,25},{25,17},{2,10},{10... | collective-permute-start | bytes 200 | tf_op jit(solution)/shard_map/ppermute | solution.py:520
  8.8 19.9 %collective-permute-start = (bf16[8,5,16,256]{3,2,1,0:T(8,128)(2,1)}, bf16[8,5,16,256]{3,2,1,0:T(8,128)(2,1)S(1)}, u32[]{:S(2)}, u32[]{:S(2)}) collective-permute-start(bf16[8,5,16,256]{3,2,1,0:T(8,128)(2,1)} %get-tuple-element.37.refs_3_), channel_id=1, source_target_pairs={{0,1},{1,2},{2,3},{3,4},{4,5},{5,6},{6,7},{8,9},{9,10},{10,11},{11... | collective-permute-start | bytes 983048 | tf_op jit(solution)/shard_map/ppermute | solution.py:506
  11.9 16.8 %collective-permute-start.1 = (bf16[8,5,16,256]{3,2,1,0:T(8,128)(2,1)}, bf16[8,5,16,256]{3,2,1,0:T(8,128)(2,1)S(1)}, u32[]{:S(2)}, u32[]{:S(2)}) collective-permute-start(bf16[8,5,16,256]{3,2,1,0:T(8,128)(2,1)} %get-tuple-element.38.refs_2_), channel_id=1, source_target_pairs={{1,0},{2,1},{3,2},{4,3},{5,4},{6,5},{7,6},{9,8},{10,9},{11,10},{12... | collective-permute-start | bytes 983048 | tf_op jit(solution)/shard_map/ppermute | solution.py:506
  19.3 9.4 %collective-permute-start.3 = (f32[16]{0:T(128)S(1)}, f32[16]{0:T(128)S(1)}, u32[]{:S(2)}, u32[]{:S(2)}) collective-permute-start(f32[16]{0:T(128)S(1)} %add.18), channel_id=1, source_target_pairs={{0,16},{8,24},{16,0},{24,8},{1,17},{9,25},{17,1},{25,9},{2,18},{10... | collective-permute-start | bytes 200 | tf_op jit(solution)/shard_map/ppermute | solution.py:520
  28.7 14.8 %copy-start.12 = (bf16[8,5,16,256]{3,2,1,0:T(8,128)(2,1)}, bf16[8,5,16,256]{3,2,1,0:T(8,128)(2,1)S(1)}, u32[]{:S(2)}) copy-start(bf16[8,5,16,256]{3,2,1,0:T(8,128)(2,1)S(1)} %collective-permute-done.refs_10_) | copy-start | bytes 983044
  28.7 14.8 %copy-start.13 = (bf16[8,5,16,256]{3,2,1,0:T(8,128)(2,1)}, bf16[8,5,16,256]{3,2,1,0:T(8,128)(2,1)S(1)}, u32[]{:S(2)}) copy-start(bf16[8,5,16,256]{3,2,1,0:T(8,128)(2,1)S(1)} %collective-permute-done.1.refs_11_) | copy-start | bytes 983044
  28.7 2.5 %collective-permute-start.4 = (f32[16]{0:T(128)S(1)}, f32[16]{0:T(128)S(1)}, u32[]{:S(2)}, u32[]{:S(2)}) collective-permute-start(f32[16]{0:T(128)S(1)} %add.19), channel_id=1, source_target_pairs={{0,1},{1,0},{2,3},{3,2},{4,5},{5,4},{6,7},{7,6},{8,9},{9,8},{10,11... | collective-permute-start | bytes 200 | tf_op jit(solution)/shard_map/ppermute | solution.py:520
  31.2 2.4 %collective-permute-start.5 = (f32[16]{0:T(128)S(1)}, f32[16]{0:T(128)S(1)}, u32[]{:S(2)}, u32[]{:S(2)}) collective-permute-start(f32[16]{0:T(128)S(1)} %add.20), channel_id=1, source_target_pairs={{0,2},{1,3},{2,0},{3,1},{4,6},{5,7},{6,4},{7,5},{8,10},{9,11},{10,... | collective-permute-start | bytes 200 | tf_op jit(solution)/shard_map/ppermute | solution.py:520
  33.6 3.3 %collective-permute-start.6 = (f32[16]{0:T(128)S(1)}, f32[16]{0:T(128)S(1)}, u32[]{:S(2)}, u32[]{:S(2)}) collective-permute-start(f32[16]{0:T(128)S(1)} %add.21), channel_id=1, source_target_pairs={{0,4},{1,5},{2,6},{3,7},{4,0},{5,1},{6,2},{7,3},{8,12},{9,13},{10,... | collective-permute-start | bytes 200 | tf_op jit(solution)/shard_map/ppermute | solution.py:520
  37.4 20.3 %copy-start.9 = (bf16[80,160]{1,0:T(8,128)(2,1)S(1)}, bf16[80,160]{1,0:T(8,128)(2,1)}, u32[]{:S(2)}) copy-start(bf16[80,160]{1,0:T(8,128)(2,1)} %get-tuple-element.74.lw) | copy-start | bytes 76804
  37.4 20.5 %copy-start.14 = (f32[1,80,160]{2,1,0:T(8,128)S(1)}, f32[1,80,160]{2,1,0:T(8,128)}, u32[]{:S(2)}) copy-start(f32[1,80,160]{2,1,0:T(8,128)} %constant.24) | copy-start | bytes 153604
  37.4 20.5 %copy-start.15 = (f32[1,80,160]{2,1,0:T(8,128)S(1)}, f32[1,80,160]{2,1,0:T(8,128)}, u32[]{:S(2)}) copy-start(f32[1,80,160]{2,1,0:T(8,128)} %constant.23) | copy-start | bytes 153604
  37.4 20.5 %copy-start.16 = (f32[1,80,160]{2,1,0:T(8,128)S(1)}, f32[1,80,160]{2,1,0:T(8,128)}, u32[]{:S(2)}) copy-start(f32[1,80,160]{2,1,0:T(8,128)} %constant.22) | copy-start | bytes 153604
  43.5 44.9 %collective-permute-start.9 = (bf16[20,5,16,256]{3,2,1,0:T(8,128)(2,1)}, bf16[20,5,16,256]{3,2,1,0:T(8,128)(2,1)S(1)}, u32[]{:S(2)}, u32[]{:S(2)}) collective-permute-start(bf16[20,5,16,256]{3,2,1,0:T(8,128)(2,1)} %get-tuple-element.53), channel_id=1, source_target_pairs={{0,8},{8,16},{16,24},{1,9},{9,17},{17,25},{2,10},{10,18},{18,26},{... | collective-permute-start | bytes 2457608 | tf_op jit(solution)/shard_map/ppermute | solution.py:506
  49.9 38.6 %collective-permute-start.10 = (bf16[20,5,16,256]{3,2,1,0:T(8,128)(2,1)}, bf16[20,5,16,256]{3,2,1,0:T(8,128)(2,1)S(1)}, u32[]{:S(2)}, u32[]{:S(2)}) collective-permute-start(bf16[20,5,16,256]{3,2,1,0:T(8,128)(2,1)} %get-tuple-element.54), channel_id=1, source_target_pairs={{8,0},{16,8},{24,16},{9,1},{17,9},{25,17},{10,2},{18,10},{26,18},{... | collective-permute-start | bytes 2457608 | tf_op jit(solution)/shard_map/ppermute | solution.py:506
  51.8 36.6 %collective-permute-start.7 = (bf16[12,5,16,256]{3,2,1,0:T(8,128)(2,1)}, bf16[12,5,16,256]{3,2,1,0:T(8,128)(2,1)S(1)}, u32[]{:S(2)}, u32[]{:S(2)}) collective-permute-start(bf16[12,5,16,256]{3,2,1,0:T(8,128)(2,1)} %get-tuple-element.49), channel_id=1, source_target_pairs={{0,1},{1,2},{2,3},{3,4},{4,5},{5,6},{6,7},{8,9},{9,10},{10,11},{11... | collective-permute-start | bytes 1474568 | tf_op jit(solution)/shard_map/ppermute | solution.py:506
  55.8 32.6 %collective-permute-start.8 = (bf16[12,5,16,256]{3,2,1,0:T(8,128)(2,1)}, bf16[12,5,16,256]{3,2,1,0:T(8,128)(2,1)S(1)}, u32[]{:S(2)}, u32[]{:S(2)}) collective-permute-start(bf16[12,5,16,256]{3,2,1,0:T(8,128)(2,1)} %get-tuple-element.50), channel_id=1, source_target_pairs={{1,0},{2,1},{3,2},{4,3},{5,4},{6,5},{7,6},{9,8},{10,9},{11,10},{12... | collective-permute-start | bytes 1474568 | tf_op jit(solution)/shard_map/ppermute | solution.py:506
  88.3 25.9 %copy-start = (f32[5,16,16,256]{3,2,1,0:T(8,128)S(1)}, f32[5,16,16,256]{3,2,1,0:T(8,128)}, u32[]{:S(2)}) copy-start(f32[5,16,16,256]{3,2,1,0:T(8,128)} %refs_2_.3) | copy-start | bytes 3932164
  88.4 25.9 %copy-start.1 = (s32[16,16,256]{2,1,0:T(8,128)S(1)}, s32[16,16,256]{2,1,0:T(8,128)}, u32[]{:S(2)}) copy-start(s32[16,16,256]{2,1,0:T(8,128)} %refs_3_.5) | copy-start | bytes 786436
  88.4 0.8 copy-start.10
  88.4 1.0 copy-start.11
  88.4 1.2 copy-start.7
  89.6 1.0 copy-start.8
  97.6 12.7 %collective-permute-start.11 = (f32[5,16,256]{2,1,0:T(8,128)}, f32[5,16,256]{2,1,0:T(8,128)S(1)}, u32[]{:S(2)}, u32[]{:S(2)}) collective-permute-start(f32[5,16,256]{2,1,0:T(8,128)} %get-tuple-element.56), channel_id=1, source_target_pairs={{0,1},{1,2},{2,3},{3,4},{4,5},{5,6},{6,7},{8,9},{9,10},{10,11},{11... | collective-permute-start | bytes 245768 | tf_op jit(solution)/shard_map/ppermute | solution.py:506
  101.8 8.4 %collective-permute-start.12 = (f32[5,16,256]{2,1,0:T(8,128)}, f32[5,16,256]{2,1,0:T(8,128)S(1)}, u32[]{:S(2)}, u32[]{:S(2)}) collective-permute-start(f32[5,16,256]{2,1,0:T(8,128)} %get-tuple-element.57), channel_id=1, source_target_pairs={{1,0},{2,1},{3,2},{4,3},{5,4},{6,5},{7,6},{9,8},{10,9},{11,10},{12... | collective-permute-start | bytes 245768 | tf_op jit(solution)/shard_map/ppermute | solution.py:506
  103.8 6.5 %collective-permute-start.13 = (f32[5,16,256]{2,1,0:T(8,128)}, f32[5,16,256]{2,1,0:T(8,128)S(1)}, u32[]{:S(2)}, u32[]{:S(2)}) collective-permute-start(f32[5,16,256]{2,1,0:T(8,128)} %get-tuple-element.58), channel_id=1, source_target_pairs={{0,8},{8,16},{16,24},{1,9},{9,17},{17,25},{2,10},{10,18},{18,26},{... | collective-permute-start | bytes 245768 | tf_op jit(solution)/shard_map/ppermute | solution.py:506
  108.3 6.0 %collective-permute-start.14 = (f32[5,16,256]{2,1,0:T(8,128)}, f32[5,16,256]{2,1,0:T(8,128)S(1)}, u32[]{:S(2)}, u32[]{:S(2)}) collective-permute-start(f32[5,16,256]{2,1,0:T(8,128)} %get-tuple-element.59), channel_id=1, source_target_pairs={{8,0},{16,8},{24,16},{9,1},{17,9},{25,17},{10,2},{18,10},{26,18},{... | collective-permute-start | bytes 245768 | tf_op jit(solution)/shard_map/ppermute | solution.py:506
  114.2 1.3 copy-start.2
  115.6 0.9 copy-start.3
  116.4 0.9 copy-start.4
  117.3 0.9 copy-start.5
  118.2 0.9 copy-start.6
  122.2 10.8 %collective-permute-start.15 = (f32[5,16,256]{2,1,0:T(8,128)S(1)}, f32[5,16,256]{2,1,0:T(8,128)S(1)}, u32[]{:S(2)}, u32[]{:S(2)}) collective-permute-start(f32[5,16,256]{2,1,0:T(8,128)S(1)} %get-tuple-element.65), channel_id=1, source_target_pairs={{0,1},{1,2},{2,3},{3,4},{4,5},{5,6},{6,7},{8,9},{9,10},{10,11},{11... | collective-permute-start | bytes 245768 | tf_op jit(solution)/shard_map/ppermute | solution.py:506
  126.8 6.3 %collective-permute-start.16 = (f32[5,16,256]{2,1,0:T(8,128)S(1)}, f32[5,16,256]{2,1,0:T(8,128)S(1)}, u32[]{:S(2)}, u32[]{:S(2)}) collective-permute-start(f32[5,16,256]{2,1,0:T(8,128)S(1)} %get-tuple-element.66), channel_id=1, source_target_pairs={{1,0},{2,1},{3,2},{4,3},{5,4},{6,5},{7,6},{9,8},{10,9},{11,10},{12... | collective-permute-start | bytes 245768 | tf_op jit(solution)/shard_map/ppermute | solution.py:506
  128.7 4.4 %collective-permute-start.17 = (f32[5,16,256]{2,1,0:T(8,128)S(1)}, f32[5,16,256]{2,1,0:T(8,128)S(1)}, u32[]{:S(2)}, u32[]{:S(2)}) collective-permute-start(f32[5,16,256]{2,1,0:T(8,128)S(1)} %get-tuple-element.67), channel_id=1, source_target_pairs={{0,8},{8,16},{16,24},{1,9},{9,17},{17,25},{2,10},{10,18},{18,26},{... | collective-permute-start | bytes 245768 | tf_op jit(solution)/shard_map/ppermute | solution.py:506
  131.0 5.8 %collective-permute-start.18 = (f32[5,16,256]{2,1,0:T(8,128)S(1)}, f32[5,16,256]{2,1,0:T(8,128)S(1)}, u32[]{:S(2)}, u32[]{:S(2)}) collective-permute-start(f32[5,16,256]{2,1,0:T(8,128)S(1)} %get-tuple-element.68), channel_id=1, source_target_pairs={{8,0},{16,8},{24,16},{9,1},{17,9},{25,17},{10,2},{18,10},{26,18},{... | collective-permute-start | bytes 245768 | tf_op jit(solution)/shard_map/ppermute | solution.py:506

commit v6 on v5

--- a/solution.py
+++ b/solution.py
@@ -12,6 +12,7 @@
 MIB = 1024 * 1024
 GROUP = 4
 TAIL = 4
+LARGE = 51
 
 
 def in_vmem():
@@ -45,9 +46,8 @@
     return [jnp.concatenate(o, axis=1) for o in out]
 
 
-def direct_kernel(half, src, xlo, xhi, ylo_a, yhi_a, ylo_b, yhi_b, energy, scratch):
+def direct_kernel(src, xlo, xhi, ylo, yhi, energy, scratch):
     group, nv, nx, ny, nz = src.shape
-    step = pl.program_id(0)
 
     def body(m, carry):
         xlo[m] = src[m, :, 0]
@@ -55,43 +55,30 @@
         total = jnp.zeros((ny, nz), F32)
         for i in range(nv):
             cells = src[m, i].astype(F32)
-            lo, hi = (line.astype(BF16) for line in edge_lines(cells, scratch.at[i]))
-
-            @pl.when(step < half)
-            def _():
-                ylo_a[m, i] = lo
-                yhi_a[m, i] = hi
-
-            @pl.when(step >= half)
-            def _():
-                ylo_b[m, i] = lo
-                yhi_b[m, i] = hi
-
+            lo, hi = edge_lines(cells, scratch.at[i])
+            ylo[m, i] = lo.astype(BF16)
+            yhi[m, i] = hi.astype(BF16)
             total = total + jnp.sum(cells * cells, axis=0)
         line = jnp.sum(total, axis=0, keepdims=True)
         line = sum(line[:, h : h + LANES] for h in range(0, nz, LANES))
-        energy[pl.ds(step * group + m, 1), :] = line
-        return carry
-
-    lax.fori_loop(0, group, body, 0)
+        energy[pl.ds(pl.program_id(0) * group + m, 1), :] = line
+        return carry
+
+    lax.fori_loop(0, group, body, 0, unroll=2)
 
 
 def pack(direct):
     nm, nv, nx, ny, nz = direct.shape
-    steps = nm // GROUP
-    half = steps // 2
-    kinds = [(ny, nm + TAIL, lambda s: s)] * 2
-    kinds += [(nx, half * GROUP, lambda s: jnp.minimum(s, half - 1))] * 2
-    kinds += [(nx, nm - half * GROUP + TAIL, lambda s: jnp.maximum(s - half, 0))] * 2
-    face_spec = lambda n, at: pl.BlockSpec((GROUP, nv, n, nz), lambda s: (at(s), 0, 0, 0))
-    return pl.pallas_call(
-        lambda *refs: direct_kernel(half, *refs),
-        grid=(steps,),
+    sizes = (ny, ny, nx, nx)
+    return pl.pallas_call(
+        direct_kernel,
+        grid=(nm // GROUP,),
         in_specs=[pl.BlockSpec((GROUP, nv, nx, ny, nz), lambda s: (s, 0, 0, 0, 0))],
-        out_specs=[face_spec(n, at) for n, _, at in kinds] + [pl.BlockSpec((nm, LANES), lambda s: (0, 0))],
-        out_shape=[sds((count, nv, n, nz), BF16) for n, count, _ in kinds] + [sds((nm, LANES), F32)],
+        out_specs=[pl.BlockSpec((GROUP, nv, n, nz), lambda s: (s, 0, 0, 0)) for n in sizes]
+        + [pl.BlockSpec((nm, LANES), lambda s: (0, 0))],
+        out_shape=[sds((nm + TAIL, nv, n, nz), BF16) for n in sizes] + [sds((nm, LANES), F32)],
         scratch_shapes=[pltpu.VMEM((nv, nz // LANES, nx * ny, LANES), F32)],
-        compiler_params=params(56),
+        compiler_params=params(LARGE),
         cost_estimate=pl.CostEstimate(flops=3 * direct.size, bytes_accessed=2 * direct.size, transcendentals=0),
         name="pack_direct",
     )(direct)
@@ -125,7 +112,7 @@
         ],
         out_specs=[whole, whole],
         out_shape=[w, w],
-        compiler_params=params(56),
+        compiler_params=params(LARGE),
         cost_estimate=pl.CostEstimate(flops=10**8, bytes_accessed=6 * 10**6, transcendentals=0),
         name="mix_chord",
     )(lw, modes, modes)
@@ -141,7 +128,7 @@
             out[m] = jnp.dot(lw[...], jnp.concatenate([face, face], axis=0), preferred_element_type=F32)
         return carry
 
-    lax.fori_loop(0, group, body, 0)
+    lax.fori_loop(0, group, body, 0, unroll=2)
 
 
 def mix_normal(lw, modes):
@@ -158,26 +145,19 @@
         out_specs=[out, out],
         out_shape=[w, w],
         scratch_shapes=[pltpu.VMEM((nv, nz // LANES, nx * ny, LANES), F32)],
-        compiler_params=params(56),
+        compiler_params=params(LARGE),
         cost_estimate=pl.CostEstimate(flops=3 * modes.size, bytes_accessed=3 * modes.size, transcendentals=0),
         name="mix_normal",
     )(lw, modes)
 
 
-def summed(pick, amp, parts, w):
-    n, nz = w.shape[1:]
+def summed(pick, amp, u, w, j):
+    nm = w.shape[0]
+    n, nz = u.shape[2:]
     total = jnp.zeros((n, nz), F32)
-    m = 0
-    for u, count in parts:
-        for k in range(count):
-            total = total + amp[m] * (u[k, 0].astype(F32) * w[pick[m]])
-            m += 1
+    for m in range(nm):
+        total = total + amp[m] * (u[m, j].astype(F32) * w[pick[m], pl.ds(pl.multiple_of(j * n, n), n), :])
     return total
-
-
-def by_face(refs, nm):
-    first = refs[2].shape[0]
-    return [[(refs[f], nm)] for f in range(2)] + [[(refs[f], first), (refs[f + 2], nm - first)] for f in (2, 3)]
 
 
 def whole_of(ref, part):
@@ -185,49 +165,37 @@
     return ref[n].astype(F32) + ref[n + 1].astype(F32)
 
 
-def of_variable(shape, dim):
-    block = tuple(1 if i == dim else size for i, size in enumerate(shape))
-    return pl.BlockSpec(block, lambda j: tuple(j if i == dim else 0 for i in range(len(shape))))
-
-
-def rows_of_variable(shape, nv):
-    return pl.BlockSpec((shape[0], shape[1] // nv, shape[2]), lambda j: (0, j, 0))
-
-
 def faces_kernel(pick, amp, base, *refs):
-    u = refs[0:6]
-    w = refs[6:10]
-    tails = refs[10:14]
-    scratch = refs[14]
-    nx = base.shape[1]
-    parts = by_face(u, w[0].shape[0])
-    lines = [base[0, 0], base[0, nx - 1], *edge_lines(base[0], scratch)]
-    for f in range(4):
-        for n, value in enumerate((summed(pick, amp, parts[f], w[f]), lines[f])):
-            hi = value.astype(BF16)
-            tails[f][2 * n, 0] = hi
-            tails[f][2 * n + 1, 0] = (value - hi.astype(F32)).astype(BF16)
+    u = refs[0:4]
+    w = refs[4:8]
+    tails = refs[8:12]
+    scratch = refs[12]
+    nv, nx, ny, nz = base.shape
+
+    def body(j, carry):
+        lines = [base[j, 0], base[j, nx - 1], *edge_lines(base[j], scratch)]
+        for f in range(4):
+            for n, value in enumerate((summed(pick, amp, u[f], w[f], j), lines[f])):
+                hi = value.astype(BF16)
+                tails[f][2 * n, j] = hi
+                tails[f][2 * n + 1, j] = (value - hi.astype(F32)).astype(BF16)
+        return carry
+
+    lax.fori_loop(0, nv, body, 0)
 
 
 def faces(pick, amp, base, u_faces, w_faces):
     nv, nx, ny, nz = base.shape
-    first = u_faces[2].shape[0]
-    nm = w_faces[0].shape[0]
-    counts = [nm, nm, first, first, nm - first, nm - first]
-    tailed = [u_faces[f] for f in (0, 1, 4, 5)]
-    at = [a.shape[0] // TAIL - 1 for a in tailed]
+    whole = lambda a: pl.BlockSpec(a.shape, lambda s: (0,) * a.ndim)
     return pl.pallas_call(
         faces_kernel,
-        grid=(nv,),
-        in_specs=[in_smem()] * 2
-        + [of_variable(base.shape, 0)]
-        + [of_variable((count,) + a.shape[1:], 1) for a, count in zip(u_faces, counts)]
-        + [rows_of_variable(a.shape, nv) for a in w_faces],
-        out_specs=[pl.BlockSpec((TAIL, 1) + a.shape[2:], lambda j, n=n: (n, j, 0, 0)) for a, n in zip(tailed, at)],
-        out_shape=[sds(a.shape, BF16) for a in tailed],
-        input_output_aliases={3: 0, 4: 1, 7: 2, 8: 3},
+        grid=(1,),
+        in_specs=[in_smem()] * 2 + [whole(a) for a in (base, *u_faces, *w_faces)],
+        out_specs=[pl.BlockSpec((TAIL,) + a.shape[1:], lambda s: (a.shape[0] // TAIL - 1, 0, 0, 0)) for a in u_faces],
+        out_shape=[sds(a.shape, BF16) for a in u_faces],
+        input_output_aliases={3: 0, 4: 1, 5: 2, 6: 3},
         scratch_shapes=[pltpu.VMEM((nz // LANES, nx * ny, LANES), F32)],
-        compiler_params=params(56),
+        compiler_params=params(36),
         name="faces",
     )(pick, amp, base, *u_faces, *w_faces)
 
@@ -247,7 +215,7 @@
     return jnp.where(row == n - 1, hi, pltpu.roll(a, rows - 1, 0)) - jnp.where(row == 0, lo, pltpu.roll(a, 1, 0))
 
 
-def main_kernel(pick, amp, lw, u_hbm, q_hbm, out, u_buf, q_buf, even, odd, u_even, u_odd, acc, c0, u_sem, q_sem):
+def main_kernel(pick, amp, lw, rz, u_hbm, q_hbm, out, u_buf, q_buf, even, odd, dz_even, dz_odd, u_even, u_odd, acc, c0, u_sem, q_sem):
     nx, nm, nv, ny, nz = u_buf.shape
     rows = nv * ny
 
@@ -267,7 +235,12 @@
         qm = q_buf[p, pick[m]].reshape(rows, nz)
         dest[m] = jnp.dot(lw[...], jnp.concatenate([qm, qm], axis=0), preferred_element_type=F32)
 
-    def plane(p, src, dest, u_src, u_dest):
+    def span_differences(p, step, dest):
+        u = u_buf[p, pl.ds(step * GROUP, GROUP)].reshape(GROUP * rows, nz)
+        dz = jnp.dot(u, rz[...], preferred_element_type=F32)
+        dest[pl.ds(step * GROUP, GROUP)] = dz.reshape(GROUP, rows, nz)
+
+    def plane(p, src, dest, dz_src, dz_dest, u_src, u_dest):
         after = jnp.minimum(p + 1, nx - 1)
 
         @pl.when(p < nx - 1)
@@ -280,6 +253,7 @@
         def body(step, carry):
             for k in range(GROUP):
                 products(after, step * GROUP + k, dest)
+            span_differences(after, step, dz_dest)
             for j in range(nv):
                 at = slice(j * ny, (j + 1) * ny)
                 sums = [acc[n, at] for n in range(5)]
@@ -287,10 +261,11 @@
                     m = step * GROUP + k
                     w0, down, up, w2 = (src[m, n * rows + j * ny : n * rows + (j + 1) * ny] for n in range(4))
                     u = u_src[m, at]
-                    following = u_buf[after, m, j].astype(F32) * amp[m]
+                    a = amp[m]
+                    following = u_buf[after, m, j].astype(F32) * a
                     dx = following - u_dest[m, at]
                     u_dest[m, at] = following
-                    terms = [dx * w0 + diff_lanes(u) * w2, u * w0, u * down, u * up, u * w2]
+                    terms = [dx * w0 + (dz_src[m, at] * a) * w2, u * w0, u * down, u * up, u * w2]
                     sums = [v + t for v, t in zip(sums, terms)]
                 for n in range(5):
                     acc[n, at] = sums[n]
@@ -314,10 +289,12 @@
         return carry
 
     lax.fori_loop(0, nm, first, 0, unroll=GROUP)
+    for step in range(nm // GROUP):
+        span_differences(0, step, dz_even)
 
     def pair(i, carry):
-        plane(2 * i, even, odd, u_even, u_odd)
-        plane(2 * i + 1, odd, even, u_odd, u_even)
+        plane(2 * i, even, odd, dz_even, dz_odd, u_even, u_odd)
+        plane(2 * i + 1, odd, even, dz_odd, dz_even, u_odd, u_even)
         return carry
 
     lax.fori_loop(0, nx // 2, pair, 0)
@@ -329,13 +306,13 @@
     lax.fori_loop(0, nx, finish, 0, unroll=4)
 
 
-def main(pick, amp, lw, direct, adjoint):
+def main(pick, amp, lw, rz, direct, adjoint):
     nm, nv, nx, ny, nz = direct.shape
     rows = nv * ny
     buf = pltpu.VMEM((nx, nm, nv, ny, nz), BF16)
     return pl.pallas_call(
         main_kernel,
-        in_specs=[in_smem(), in_smem(), in_vmem(), in_hbm(), in_hbm()],
+        in_specs=[in_smem(), in_smem(), in_vmem(), in_vmem(), in_hbm(), in_hbm()],
         out_specs=in_vmem(),
         out_shape=sds((nx, rows, nz), F32),
         scratch_shapes=[
@@ -345,15 +322,17 @@
             pltpu.VMEM((nm, 4 * rows, nz), F32),
             pltpu.VMEM((nm, rows, nz), F32),
             pltpu.VMEM((nm, rows, nz), F32),
+            pltpu.VMEM((nm, rows, nz), F32),
+            pltpu.VMEM((nm, rows, nz), F32),
             pltpu.VMEM((5, rows, nz), F32),
             pltpu.VMEM((nx + 2, rows, nz), F32),
             pltpu.SemaphoreType.DMA((nx,)),
             pltpu.SemaphoreType.DMA((nx,)),
         ],
-        compiler_params=params(56),
+        compiler_params=params(LARGE),
         cost_estimate=pl.CostEstimate(flops=10**6, bytes_accessed=10**5, transcendentals=0),
         name="main",
-    )(pick, amp, lw, direct, adjoint)
+    )(pick, amp, lw, rz, direct, adjoint)
 
 
 def weight_of(cells):
@@ -373,51 +352,52 @@
 
 def boundary_kernel(scale, pick, amp, local, cell, *refs):
     w = refs[0:4]
-    halo = [refs[4 + f] for f in (4, 5, 2, 3, 0, 1)]
-    field, xlo, xhi, ylo, yhi = refs[10:15]
-    base_halo = refs[15:19]
-    add = refs[19:23]
-    nx, ny, nz = local.shape
-    parts = by_face(halo, w[0].shape[0])
-    tailed = [halo[f] for f in (0, 1, 4, 5)]
+    halo = refs[4:8]
+    field, xlo, xhi, ylo, yhi = refs[8:13]
+    base_halo = refs[13:17]
+    add = refs[17:21]
+    nx, rows, nz = local.shape
+    nv = add[0].shape[0]
+    ny = rows // nv
     for f in range(4):
-        sign = 1.0 if f % 2 == 0 else -1.0
-        add[f][...] = sign * (whole_of(tailed[f], 0)[0] - summed(pick, amp, parts[f], w[f]))
-        base_halo[f][...] = whole_of(tailed[f], 1)
-    row = lax.broadcasted_iota(jnp.int32, (ny, nz), 0)
+        add[f][...] = whole_of(halo[f], 0)
+        base_halo[f][...] = whole_of(halo[f], 1)
+
+    def face(j, carry):
+        for f in range(4):
+            add[f][j] -= summed(pick, amp, halo[f], w[f], j)
+        return carry
+
+    lax.fori_loop(0, nv, face, 0)
+    row = row_of((rows, nz), ny)
 
     def plane(x, carry):
-        lo, hi = add[2][pl.ds(x, 1), :], add[3][pl.ds(x, 1), :]
-        g = local[x] + jnp.where(row == 0, lo, 0.0) + jnp.where(row == ny - 1, hi, 0.0)
-        g = g + jnp.where(x == 0, 1.0, 0.0) * add[0][...] + jnp.where(x == nx - 1, 1.0, 0.0) * add[1][...]
-        g = g * (weight_of(cell[x]) * scale)
+        lo, hi = spread(add[2], x, ny), spread(add[3], x, ny)
+        g = local[x] + jnp.where(row == 0, lo, 0.0) - jnp.where(row == ny - 1, hi, 0.0)
+        g = g + jnp.where(x == 0, 1.0, 0.0) * add[0][...].reshape(rows, nz)
+        g = g - jnp.where(x == nx - 1, 1.0, 0.0) * add[1][...].reshape(rows, nz)
+        g = g * jnp.concatenate([weight_of(cell[x]) * scale] * nv, axis=0)
         field[x] = g
         write_lines(g, x, ny, ylo, yhi)
         return carry
 
-    lax.fori_loop(0, nx, plane, 0, unroll=4)
-    xlo[0] = field[0]
-    xhi[0] = field[nx - 1]
+    lax.fori_loop(0, nx, plane, 0, unroll=2)
+    xlo[...] = field[0].reshape(xlo.shape)
+    xhi[...] = field[nx - 1].reshape(xhi.shape)
 
 
 def boundary(scale, pick, amp, local, cell, w_faces, halo):
     nx, rows, nz = local.shape
-    nv = halo[0].shape[1]
-    face = [sds(halo[f].shape[1:], F32) for f in range(4)]
-    ordered = [halo[f] for f in (4, 5, 2, 3, 0, 1)]
+    face = [sds(a.shape[1:], F32) for a in halo]
     return pl.pallas_call(
         lambda *refs: boundary_kernel(scale, *refs),
-        grid=(nv,),
-        in_specs=[in_smem()] * 2
-        + [rows_of_variable(local.shape, nv), pl.BlockSpec(cell.shape, lambda j: (0, 0, 0))]
-        + [rows_of_variable(a.shape, nv) for a in w_faces]
-        + [of_variable(a.shape, 1) for a in ordered],
-        out_specs=[rows_of_variable(local.shape, nv)] + [of_variable(f.shape, 0) for f in face * 2],
+        in_specs=[in_smem()] * 2 + [in_vmem()] * 10,
+        out_specs=[in_vmem()] * 9,
         out_shape=[sds(local.shape, F32)] + face * 2,
-        scratch_shapes=[pltpu.VMEM(f.shape[1:], F32) for f in face],
-        compiler_params=params(56),
+        scratch_shapes=[pltpu.VMEM(f.shape, F32) for f in face],
+        compiler_params=params(28),
         name="boundary",
-    )(pick, amp, local, cell, *w_faces, *ordered)
+    )(pick, amp, local, cell, *w_faces, *halo)
 
 
 def mix_rows(lw, values):
@@ -542,6 +522,11 @@
     return jnp.concatenate([within(wide[d], n, c) for d, c in ((0, eye), (1, below - eye), (1, eye - above), (2, eye))], axis=0)
 
 
+def span_difference(nz):
+    eye = np.eye(nz, dtype=np.float32)
+    return jnp.asarray(np.roll(eye, -1, 1) - np.roll(eye, 1, 1), BF16)
+
+
 def step_rows(lw):
     half = lw.shape[-1] // 2
     return jnp.concatenate([lw[..., :half], lw[..., :half], lw[..., half:]], axis=-1)
@@ -551,18 +536,14 @@
     nm, nv, nx, ny, nz = direct.shape
     cells_all = nv * nx * ny * nz * lax.axis_size("chord") * lax.axis_size("normal")
     *own, sums = pack(direct)
-    early = exchange_axis("normal", *own[2:4])
-    sums = sum_over("chord", jnp.sum(sums, axis=1))
+    sums = sum_over("chord", sum_over("normal", jnp.sum(sums, axis=1)))
+    amp = lax.rsqrt(sums / cells_all + 1e-06)
     wide = kron_rows(mix, ny)
     lw_y = within(wide, ny, np.eye(ny, dtype=np.float32))
     lw_x = lw_y if nx == ny else within(kron_rows(mix, nx), nx, np.eye(nx, dtype=np.float32))
     w_faces = [*mix_chord(lw_y[0], adjoint), *mix_normal(lw_x[1], adjoint)]
-    *early, sums = lax.optimization_barrier((*early, sums, *w_faces))[:3]
-    sums = sum_over("normal", sums)
-    amp = lax.rsqrt(sums / cells_all + 1e-06)
-    late = exchange(faces(pick, amp, base, own, w_faces))
-    halo = late[:2] + early + late[2:]
-    local = main(pick, amp, main_rows(wide, ny), direct, adjoint)
+    halo = exchange(faces(pick, amp, base, own, w_faces))
+    local = main(pick, amp, main_rows(wide, ny), span_difference(nz), direct, adjoint)
     field, *sides = boundary(1.0 / nm, pick, amp, local, cell, w_faces, halo)
     sides, base_halo = sides[:4], sides[4:]
     lw_step = step_rows(lw_y.reshape(3 * nv * ny, -1))

time: 143 us -> 123 us (0.86)
  local copies, waits for them, and re-layouts: 7.66 us -> 0.08 us
  starting transfers between devices: 48.5 us -> 41.9 us
  Pallas kernels: 69.1 us -> 66.5 us
  other arithmetic: 2.31 us -> 0.41 us
    ppermute x14 -> x12, starting transfers between devices: 42.9 us -> 32.8 us  [exchange_axis(): return [lax.ppermute(hi, axis, up), lax.ppermute(lo, axis, down)]]
    pallas_call x1, Pallas kernels: 29.7 us -> 39.1 us  [main(): pl.pallas_call(main_kernel, in_specs=[in_smem(), in_smem(), in_vmem(), in...]
    pallas_call x3, Pallas kernels: 20.3 us -> 11.2 us  [the longest x1 6.32 us: pack(): pl.pallas_call(direct_kernel, grid=(nm // GROUP,), in_specs=[pl.BlockSpec...]
    unnamed x42 -> x24, local copies, waits for them, and re-layouts: 7.01 us -> 0.06 us
    ppermute x5, starting transfers between devices: 5.65 us -> 9.07 us  [sum_over(): lax.ppermute(values, axis, [(i, i ^ bit) for i in range(count)])]
    pallas_call x1, Pallas kernels: 3.8 us -> 2.28 us  [mix_chord(): pl.pallas_call(mix_chord_kernel, grid=(1,), in_specs=[pl.BlockSpec(lw.sha...]
    pallas_call x1, Pallas kernels: 8.15 us -> 6.65 us  [mix_normal(): pl.pallas_call(mix_normal_kernel, grid=(nm // GROUP,), in_specs=[pl.Block...]
    ppermute x14 -> x12, waiting for transfers between devices: 7.59 us -> 7.27 us  [exchange_axis(): return [lax.ppermute(hi, axis, up), lax.ppermute(lo, axis, down)]]
  transfers between devices with their start and end apart: 19 -> 17, of which waited for: 5 -> 5; matrix products, arithmetic and copies ran while one was open for 2% -> 1% of each run, Pallas kernels for 30% -> 40%
where the time goes in v6:
time: 123 us; the launch traced here: 121 us
  Pallas kernels  66.5 us (54%)
  starting transfers between devices  41.9 us (34%)
  waiting for transfers between devices  11 us (9%)
    pallas_call x1, Pallas kernels, main(): pl.pallas_call(main_kernel, in_specs=[in_smem(), in_smem(), in_vmem(), in...  39.1 us
    ppermute x12, starting transfers between devices, exchange_axis(): return [lax.ppermute(hi, axis, up), lax.ppermute(lo, axis, down)]  32.8 us
    ppermute x5, starting transfers between devices, sum_over(): lax.ppermute(values, axis, [(i, i ^ bit) for i in range(count)])  9.07 us
    pallas_call x2, Pallas kernels, apply_step(): pl.pallas_call(lambda *refs: step_kernel(last, *refs), in_specs=[in_vmem(...  7.27 us
    ppermute x12, waiting for transfers between devices, exchange_axis(): return [lax.ppermute(hi, axis, up), lax.ppermute(lo, axis, down)]  7.27 us
    pallas_call x1, Pallas kernels, mix_normal(): pl.pallas_call(mix_normal_kernel, grid=(nm // GROUP,), in_specs=[pl.Block...  6.65 us
    pallas_call x1, Pallas kernels, pack(): pl.pallas_call(direct_kernel, grid=(nm // GROUP,), in_specs=[pl.BlockSpec...  6.32 us
    ppermute x5, waiting for transfers between devices, sum_over(): lax.ppermute(values, axis, [(i, i ^ bit) for i in range(count)])  3.76 us
  transfers between devices with their start and end apart: 17, of which 5 were waited for; matrix products, arithmetic and copies ran while one was open for 1% of the time, Pallas kernels for 40%

profile of v6, /device:TPU:5, one launch (start us, length us, event | category | flops | bytes accessed | tf_op | source)
XLA Modules:
  0.0 120.9 jit_solution(11602589647194885536)
XLA Ops:
  0.0 0.0 copy-start.10
  0.0 6.3 %pack_direct.1 = (bf16[20,5,16,256]{3,2,1,0:T(8,128)(2,1)S(1)}, bf16[20,5,16,256]{3,2,1,0:T(8,128)(2,1)S(1)}, bf16[20,5,16,256]{3,2,1,0:T(8,128)(2,1)S(1)}, bf16...) custom-call(bf16[16,5,16,16,256]{4,3,2,1,0:T(8,128)(2,1)} %u_hbm.1), custom_call_target="tpu_custom_call" | custom-call | flops 15728640 | bytes 10485760 | tf_op jit(solution)/shard_map/pack_direct/pallas_call | solution.py:73
  6.3 0.1 reduce_sum.9
  6.5 0.1 collective-permute-start
  6.5 0.0 copy-done.10
  6.6 0.0 copy-done.9
  6.6 0.2 fusion.6
  6.8 2.1 %collective-permute-done = f32[16]{0:T(128)S(1)} collective-permute-done((f32[16]{0:T(128)S(1)}, f32[16]{0:T(128)S(1)}, u32[]{:S(2)}, u32[]{:S(2)}) %collective-permute-start) | collective-permute-done | bytes 96 | tf_op jit(solution)/shard_map/ppermute | solution.py:500
  8.9 1.3 %collective-permute-start.1 = (f32[16]{0:T(128)S(1)}, f32[16]{0:T(128)S(1)}, u32[]{:S(2)}, u32[]{:S(2)}) collective-permute-start(f32[16]{0:T(128)S(1)} %add.18), channel_id=1, source_target_pairs={{0,2},{1,3},{2,0},{3,1},{4,6},{5,7},{6,4},{7,5},{8,10},{9,11},{10,... | collective-permute-start | bytes 200 | tf_op jit(solution)/shard_map/ppermute | solution.py:500
  10.2 0.0 copy-done.8
  10.2 0.0 copy-done.11
  10.2 0.4 multiply_convert_fusion
  10.6 0.7 collective-permute-done.1
  11.3 2.3 %collective-permute-start.2 = (f32[16]{0:T(128)S(1)}, f32[16]{0:T(128)S(1)}, u32[]{:S(2)}, u32[]{:S(2)}) collective-permute-start(f32[16]{0:T(128)S(1)} %add.19), channel_id=1, source_target_pairs={{0,4},{1,5},{2,6},{3,7},{4,0},{5,1},{6,2},{7,3},{8,12},{9,13},{10,... | collective-permute-start | bytes 200 | tf_op jit(solution)/shard_map/ppermute | solution.py:500
  13.6 1.0 collective-permute-done.2
  14.6 4.1 %collective-permute-start.3 = (f32[16]{0:T(128)S(1)}, f32[16]{0:T(128)S(1)}, u32[]{:S(2)}, u32[]{:S(2)}) collective-permute-start(f32[16]{0:T(128)S(1)} %add.20), channel_id=1, source_target_pairs={{0,8},{8,0},{16,24},{24,16},{1,9},{9,1},{17,25},{25,17},{2,10},{10... | collective-permute-start | bytes 200 | tf_op jit(solution)/shard_map/ppermute | solution.py:500
  18.7 2.3 %mix_chord.1 = (f32[16,80,256]{2,1,0:T(8,128)S(1)}, f32[16,80,256]{2,1,0:T(8,128)S(1)}) custom-call(bf16[80,160]{1,0:T(8,128)(2,1)S(1)} %get-tuple-element.63.lw, bf16[16,5,16,16,256]{4,3,2,1,0:T(8,128)(2,1)} %src.3, bf16[16,5,16,16,256]{4,3,2,1,0:T(8,128)(2,1)} %src.3), custom_call_target="tpu_custom_call" | custom-call | flops 100000000 | bytes 6000000 | tf_op jit(solution)/shard_map/mix_chord/pallas_call | solution.py:105
  21.0 0.0 collective-permute-done.3
  21.0 1.3 %collective-permute-start.4 = (f32[16]{0:T(128)S(1)}, f32[16]{0:T(128)S(1)}, u32[]{:S(2)}, u32[]{:S(2)}) collective-permute-start(f32[16]{0:T(128)S(1)} %add.21), channel_id=1, source_target_pairs={{0,16},{8,24},{16,0},{24,8},{1,17},{9,25},{17,1},{25,9},{2,18},{10... | collective-permute-start | bytes 200 | tf_op jit(solution)/shard_map/ppermute | solution.py:500
  22.3 6.6 %mix_normal.1 = (f32[16,80,256]{2,1,0:T(8,128)S(1)}, f32[16,80,256]{2,1,0:T(8,128)S(1)}) custom-call(bf16[80,160]{1,0:T(8,128)(2,1)S(1)} %get-tuple-element.64.lw, bf16[16,5,16,16,256]{4,3,2,1,0:T(8,128)(2,1)} %src.3), custom_call_target="tpu_custom_call" | custom-call | flops 15728640 | bytes 15728640 | tf_op jit(solution)/shard_map/mix_normal/pallas_call | solution.py:138
  29.0 0.0 collective-permute-done.4
  29.0 0.0 copy-done
  29.0 0.0 copy-done.2
  29.0 0.0 copy-done.4
  29.0 0.0 copy-start.5
  29.0 0.0 copy-start.6
  29.0 0.0 copy-start.7
  29.1 1.5 %faces.1 = (bf16[20,5,16,256]{3,2,1,0:T(8,128)(2,1)S(1)}, bf16[20,5,16,256]{3,2,1,0:T(8,128)(2,1)S(1)}, bf16[20,5,16,256]{3,2,1,0:T(8,128)(2,1)S(1)}, bf16[20,5,16,256]{3,2,1,0:T(8,128)(2,1)S(1)}) custom-call(s32[16]{0:T(128)S(1)} %copy-done.4, ...), custom_call_target="tpu_custom_call", output_to_operand_aliasing={{0}: (3, {}), {1}: (4, {}), {2}: (5, {}), {3}: (6, {})} | custom-call | tf_op jit(solution)/shard_map/faces/pallas_call | solution.py:190
  30.6 0.0 copy-start.3
  30.6 2.5 %collective-permute-start.5 = (bf16[20,5,16,256]{3,2,1,0:T(8,128)(2,1)S(1)}, bf16[20,5,16,256]{3,2,1,0:T(8,128)(2,1)}, u32[]{:S(2)}, u32[]{:S(2)}) collective-permute-start(bf16[20,5,16,256]{3,2,1,0:T(8,128)(2,1)S(1)} %get-tuple-element.41), channel_id=1, source_target_pairs={{0,8},{8,16},{16,24},{1,9},{9,17},{17,25},{2,10},{10,18},{18,26},{... | collective-permute-start | bytes 2457608 | tf_op jit(solution)/shard_map/ppermute | solution.py:486
  33.1 2.9 %collective-permute-start.6 = (bf16[20,5,16,256]{3,2,1,0:T(8,128)(2,1)S(1)}, bf16[20,5,16,256]{3,2,1,0:T(8,128)(2,1)}, u32[]{:S(2)}, u32[]{:S(2)}) collective-permute-start(bf16[20,5,16,256]{3,2,1,0:T(8,128)(2,1)S(1)} %get-tuple-element.42), channel_id=1, source_target_pairs={{8,0},{16,8},{24,16},{9,1},{17,9},{25,17},{10,2},{18,10},{26,18},{... | collective-permute-start | bytes 2457608 | tf_op jit(solution)/shard_map/ppermute | solution.py:486
  35.9 3.1 %collective-permute-start.7 = (bf16[20,5,16,256]{3,2,1,0:T(8,128)(2,1)S(1)}, bf16[20,5,16,256]{3,2,1,0:T(8,128)(2,1)}, u32[]{:S(2)}, u32[]{:S(2)}) collective-permute-start(bf16[20,5,16,256]{3,2,1,0:T(8,128)(2,1)S(1)} %get-tuple-element.43), channel_id=1, source_target_pairs={{0,1},{1,2},{2,3},{3,4},{4,5},{5,6},{6,7},{8,9},{9,10},{10,11},{11... | collective-permute-start | bytes 2457608 | tf_op jit(solution)/shard_map/ppermute | solution.py:486
  39.1 3.0 %collective-permute-start.8 = (bf16[20,5,16,256]{3,2,1,0:T(8,128)(2,1)S(1)}, bf16[20,5,16,256]{3,2,1,0:T(8,128)(2,1)}, u32[]{:S(2)}, u32[]{:S(2)}) collective-permute-start(bf16[20,5,16,256]{3,2,1,0:T(8,128)(2,1)S(1)} %get-tuple-element.44), channel_id=1, source_target_pairs={{1,0},{2,1},{3,2},{4,3},{5,4},{6,5},{7,6},{9,8},{10,9},{11,10},{12... | collective-permute-start | bytes 2457608 | tf_op jit(solution)/shard_map/ppermute | solution.py:486
  42.1 0.1 pad_maximum_fusion.1.refs_0_
  42.3 0.0 copy-done.5
  42.3 0.0 copy-done.6
  42.3 0.0 copy-done.7
  42.4 0.0 copy-start.1
  42.4 39.1 %main.1.refs_2_ = f32[16,80,256]{2,1,0:T(8,128)S(1)} custom-call(s32[16]{0:T(128)S(1)} %copy-done.4, f32[16]{0:T(128)S(1)} %add_rsqrt_fusion.amp.refs_1_, bf16[320,160]{1,0:T(8,128)(2,1)S(1)} %pad_maximum_fusion.lw, bf16[256,256]{1,0:T(8,128)(2,1)S(1)} %copy-done.3, bf16[16,5,16,16,256]{4,3,2,1,0:T(8,128)(2,1)} %u_hbm.1, bf16[16,5,16,16,256]{4,3,2,1,0:T(8,128)(2,1)} %src.3), custom_call_target="tpu_custom_call" | custom-call | flops 1000000 | bytes 100000 | tf_op jit(solution)/shard_map/main/pallas_call | solution.py:313
  81.5 0.0 collective-permute-done.5.refs_8_
  81.5 0.0 collective-permute-done.6.refs_9_
  81.5 0.0 collective-permute-done.7.refs_10_
  81.5 0.0 collective-permute-done.8.refs_11_
  81.5 0.0 copy-done.1
  81.5 3.4 %boundary.1 = (f32[16,80,256]{2,1,0:T(8,128)S(1)}, f32[5,16,256]{2,1,0:T(8,128)S(1)}, f32[5,16,256]{2,1,0:T(8,128)S(1)}, f32[5,16,256]{2,1,0:T(8,128)S(1)}, f32[...) custom-call(s32[16]{0:T(128)S(1)} %copy-done.4, ...), custom_call_target="tpu_custom_call" | custom-call | tf_op jit(solution)/shard_map/boundary/pallas_call | solution.py:392
  84.9 3.2 %collective-permute-start.9 = (f32[5,16,256]{2,1,0:T(8,128)S(1)}, f32[5,16,256]{2,1,0:T(8,128)S(1)}, u32[]{:S(2)}, u32[]{:S(2)}) collective-permute-start(f32[5,16,256]{2,1,0:T(8,128)S(1)} %get-tuple-element.46), channel_id=1, source_target_pairs={{0,1},{1,2},{2,3},{3,4},{4,5},{5,6},{6,7},{8,9},{9,10},{10,11},{11... | collective-permute-start | bytes 245768 | tf_op jit(solution)/shard_map/ppermute | solution.py:486
  88.1 2.1 %collective-permute-start.10 = (f32[5,16,256]{2,1,0:T(8,128)S(1)}, f32[5,16,256]{2,1,0:T(8,128)S(1)}, u32[]{:S(2)}, u32[]{:S(2)}) collective-permute-start(f32[5,16,256]{2,1,0:T(8,128)S(1)} %get-tuple-element.47), channel_id=1, source_target_pairs={{1,0},{2,1},{3,2},{4,3},{5,4},{6,5},{7,6},{9,8},{10,9},{11,10},{12... | collective-permute-start | bytes 245768 | tf_op jit(solution)/shard_map/ppermute | solution.py:486
  90.2 3.8 %collective-permute-start.11 = (f32[5,16,256]{2,1,0:T(8,128)S(1)}, f32[5,16,256]{2,1,0:T(8,128)S(1)}, u32[]{:S(2)}, u32[]{:S(2)}) collective-permute-start(f32[5,16,256]{2,1,0:T(8,128)S(1)} %get-tuple-element.48), channel_id=1, source_target_pairs={{0,8},{8,16},{16,24},{1,9},{9,17},{17,25},{2,10},{10,18},{18,26},{... | collective-permute-start | bytes 245768 | tf_op jit(solution)/shard_map/ppermute | solution.py:486
  94.0 1.9 %collective-permute-start.12 = (f32[5,16,256]{2,1,0:T(8,128)S(1)}, f32[5,16,256]{2,1,0:T(8,128)S(1)}, u32[]{:S(2)}, u32[]{:S(2)}) collective-permute-start(f32[5,16,256]{2,1,0:T(8,128)S(1)} %get-tuple-element.49), channel_id=1, source_target_pairs={{8,0},{16,8},{24,16},{9,1},{17,9},{25,17},{10,2},{18,10},{26,18},{... | collective-permute-start | bytes 245768 | tf_op jit(solution)/shard_map/ppermute | solution.py:486
  95.9 0.1 pad_maximum_fusion.2.refs_1_
  96.0 0.0 collective-permute-done.9.refs_5_
  96.0 0.0 collective-permute-done.10.refs_6_
  96.0 0.0 collective-permute-done.11.refs_7_
  96.0 3.7 %collective-permute-done.12.refs_8_ = f32[5,16,256]{2,1,0:T(8,128)S(1)} collective-permute-done((f32[5,16,256]{2,1,0:T(8,128)S(1)}, f32[5,16,256]{2,1,0:T(8,128)S(1)}, u32[]{:S(2)}, u32[]{:S(2)}) %collective-permute-start.12) | collective-permute-done | bytes 81952 | tf_op jit(solution)/shard_map/ppermute | solution.py:486
  99.8 3.2 %step_one.1 = (f32[16,80,256]{2,1,0:T(8,128)S(1)}, f32[5,16,256]{2,1,0:T(8,128)S(1)}, f32[5,16,256]{2,1,0:T(8,128)S(1)}, f32[5,16,256]{2,1,0:T(8,128)S(1)}, f32[5,16,256]{2,1,0:T(8,128)S(1)}) custom-call(bf16[240,240]{1,0:T(8,128)(2,1)S(1)} %pad_maximum_fusion.1.refs_0_, bf16[80,240]{1,0:T(8,128)(2,1)S(1)} %pad_maximum_fusion.2.refs_1_, ...), custom_call_target="tpu_custom_call" | custom-call | tf_op jit(solution)/shard_map/step_one/pallas_call | solution.py:471
  103.0 4.1 %collective-permute-start.13 = (f32[5,16,256]{2,1,0:T(8,128)S(1)}, f32[5,16,256]{2,1,0:T(8,128)S(1)}, u32[]{:S(2)}, u32[]{:S(2)}) collective-permute-start(f32[5,16,256]{2,1,0:T(8,128)S(1)} %get-tuple-element.55), channel_id=1, source_target_pairs={{0,1},{1,2},{2,3},{3,4},{4,5},{5,6},{6,7},{8,9},{9,10},{10,11},{11... | collective-permute-start | bytes 245768 | tf_op jit(solution)/shard_map/ppermute | solution.py:486
  107.0 1.9 %collective-permute-start.14 = (f32[5,16,256]{2,1,0:T(8,128)S(1)}, f32[5,16,256]{2,1,0:T(8,128)S(1)}, u32[]{:S(2)}, u32[]{:S(2)}) collective-permute-start(f32[5,16,256]{2,1,0:T(8,128)S(1)} %get-tuple-element.56), channel_id=1, source_target_pairs={{1,0},{2,1},{3,2},{4,3},{5,4},{6,5},{7,6},{9,8},{10,9},{11,10},{12... | collective-permute-start | bytes 245768 | tf_op jit(solution)/shard_map/ppermute | solution.py:486
  109.0 2.1 %collective-permute-start.15 = (f32[5,16,256]{2,1,0:T(8,128)S(1)}, f32[5,16,256]{2,1,0:T(8,128)S(1)}, u32[]{:S(2)}, u32[]{:S(2)}) collective-permute-start(f32[5,16,256]{2,1,0:T(8,128)S(1)} %get-tuple-element.57), channel_id=1, source_target_pairs={{0,8},{8,16},{16,24},{1,9},{9,17},{17,25},{2,10},{10,18},{18,26},{... | collective-permute-start | bytes 245768 | tf_op jit(solution)/shard_map/ppermute | solution.py:486
  111.1 2.2 %collective-permute-start.16 = (f32[5,16,256]{2,1,0:T(8,128)S(1)}, f32[5,16,256]{2,1,0:T(8,128)S(1)}, u32[]{:S(2)}, u32[]{:S(2)}) collective-permute-start(f32[5,16,256]{2,1,0:T(8,128)S(1)} %get-tuple-element.58), channel_id=1, source_target_pairs={{8,0},{16,8},{24,16},{9,1},{17,9},{25,17},{10,2},{18,10},{26,18},{... | collective-permute-start | bytes 245768 | tf_op jit(solution)/shard_map/ppermute | solution.py:486
  113.3 0.0 collective-permute-done.13.refs_5_
  113.3 0.0 collective-permute-done.14.refs_6_
  113.3 0.0 collective-permute-done.15.refs_7_
  113.3 3.5 %collective-permute-done.16.refs_8_ = f32[5,16,256]{2,1,0:T(8,128)S(1)} collective-permute-done((f32[5,16,256]{2,1,0:T(8,128)S(1)}, f32[5,16,256]{2,1,0:T(8,128)S(1)}, u32[]{:S(2)}, u32[]{:S(2)}) %collective-permute-start.16) | collective-permute-done | bytes 81952 | tf_op jit(solution)/shard_map/ppermute | solution.py:486
  116.9 4.1 %step_two.1 = f32[5,16,16,256]{3,2,1,0:T(8,128)} custom-call(bf16[240,240]{1,0:T(8,128)(2,1)S(1)} %pad_maximum_fusion.1.refs_0_, bf16[80,240]{1,0:T(8,128)(2,1)S(1)} %pad_maximum_fusion.2.refs_1_, f32[5,16,16,256]{3,2,1,0:T(8,128)S(1)} %copy-done, s32[16,16,256]{2,1,0:T(8,128)S(1)} %copy-done.1, f32[16,80,256]{2,1,0:T(8,128)S(1)} %get-tuple-element.54.refs_4_, ...), custom_call_target="tpu_custom_call" | custom-call | tf_op jit(solution)/shard_map/step_two/pallas_call | solution.py:471
  (19 shorter events, 0.1 us)
Async XLA Ops:
  0.0 6.6 %copy-start.9 = (f32[10,160,1]{1,0,2:T(8,128)S(1)}, f32[10,160,1]{1,0,2:T(8,128)}, u32[]{:S(2)}) copy-start(f32[10,160,1]{1,0,2:T(8,128)} %constant.29) | copy-start | bytes 19204
  0.0 10.2 %copy-start.8 = (f32[80,160]{1,0:T(8,128)S(1)}, f32[80,160]{1,0:T(8,128)}, u32[]{:S(2)}) copy-start(f32[80,160]{1,0:T(8,128)} %constant.21.clone) | copy-start | bytes 153604
  0.0 10.2 %copy-start.11 = (f32[80,5,1]{0,1,2:T(8,128)S(1)}, f32[80,5,1]{0,1,2:T(8,128)}, u32[]{:S(2)}) copy-start(f32[80,5,1]{0,1,2:T(8,128)} %constant.30) | copy-start | bytes 4804
  0.0 6.5 %copy-start.10 = (f32[3,5,5]{2,0,1:T(4,128)S(1)}, f32[3,5,5]{2,0,1:T(4,128)}, u32[]{:S(2)}) copy-start(f32[3,5,5]{2,0,1:T(4,128)} %param.19) | copy-start | bytes 904
  6.5 2.4 %collective-permute-start = (f32[16]{0:T(128)S(1)}, f32[16]{0:T(128)S(1)}, u32[]{:S(2)}, u32[]{:S(2)}) collective-permute-start(f32[16]{0:T(128)S(1)} %reduce_sum.9), channel_id=1, source_target_pairs={{0,1},{1,0},{2,3},{3,2},{4,5},{5,4},{6,7},{7,6},{8,9},{9,8},{10,11... | collective-permute-start | bytes 200 | tf_op jit(solution)/shard_map/ppermute | solution.py:500
  8.9 2.4 %collective-permute-start.1 = (f32[16]{0:T(128)S(1)}, f32[16]{0:T(128)S(1)}, u32[]{:S(2)}, u32[]{:S(2)}) collective-permute-start(f32[16]{0:T(128)S(1)} %add.18), channel_id=1, source_target_pairs={{0,2},{1,3},{2,0},{3,1},{4,6},{5,7},{6,4},{7,5},{8,10},{9,11},{10,... | collective-permute-start | bytes 200 | tf_op jit(solution)/shard_map/ppermute | solution.py:500
  11.3 3.3 %collective-permute-start.2 = (f32[16]{0:T(128)S(1)}, f32[16]{0:T(128)S(1)}, u32[]{:S(2)}, u32[]{:S(2)}) collective-permute-start(f32[16]{0:T(128)S(1)} %add.19), channel_id=1, source_target_pairs={{0,4},{1,5},{2,6},{3,7},{4,0},{5,1},{6,2},{7,3},{8,12},{9,13},{10,... | collective-permute-start | bytes 200 | tf_op jit(solution)/shard_map/ppermute | solution.py:500
  14.6 6.4 %collective-permute-start.3 = (f32[16]{0:T(128)S(1)}, f32[16]{0:T(128)S(1)}, u32[]{:S(2)}, u32[]{:S(2)}) collective-permute-start(f32[16]{0:T(128)S(1)} %add.20), channel_id=1, source_target_pairs={{0,8},{8,0},{16,24},{24,16},{1,9},{9,1},{17,25},{25,17},{2,10},{10... | collective-permute-start | bytes 200 | tf_op jit(solution)/shard_map/ppermute | solution.py:500
  21.0 7.9 %collective-permute-start.4 = (f32[16]{0:T(128)S(1)}, f32[16]{0:T(128)S(1)}, u32[]{:S(2)}, u32[]{:S(2)}) collective-permute-start(f32[16]{0:T(128)S(1)} %add.21), channel_id=1, source_target_pairs={{0,16},{8,24},{16,0},{24,8},{1,17},{9,25},{17,1},{25,9},{2,18},{10... | collective-permute-start | bytes 200 | tf_op jit(solution)/shard_map/ppermute | solution.py:500
  22.3 6.7 %copy-start = (f32[5,16,16,256]{3,2,1,0:T(8,128)S(1)}, f32[5,16,16,256]{3,2,1,0:T(8,128)}, u32[]{:S(2)}) copy-start(f32[5,16,16,256]{3,2,1,0:T(8,128)} %refs_2_.3) | copy-start | bytes 3932164
  22.3 6.7 %copy-start.2 = (bf16[20,5,16,256]{3,2,1,0:T(8,128)(2,1)S(1)}, bf16[20,5,16,256]{3,2,1,0:T(8,128)(2,1)}, u32[]{:S(2)}) copy-start(bf16[20,5,16,256]{3,2,1,0:T(8,128)(2,1)} %get-tuple-element.40.refs_3_) | copy-start | bytes 2457604
  22.3 6.7 %copy-start.4 = (s32[16]{0:T(128)S(1)}, s32[16]{0:T(128)}, u32[]{:S(2)}) copy-start(s32[16]{0:T(128)} %refs_0_.1) | copy-start | bytes 196
  29.0 13.2 %copy-start.5 = (f32[1,80,160]{2,1,0:T(8,128)S(1)}, f32[1,80,160]{2,1,0:T(8,128)}, u32[]{:S(2)}) copy-start(f32[1,80,160]{2,1,0:T(8,128)} %constant.27) | copy-start | bytes 153604
  29.0 13.2 %copy-start.6 = (f32[1,80,160]{2,1,0:T(8,128)S(1)}, f32[1,80,160]{2,1,0:T(8,128)}, u32[]{:S(2)}) copy-start(f32[1,80,160]{2,1,0:T(8,128)} %constant.26) | copy-start | bytes 153604
  29.0 13.2 %copy-start.7 = (f32[1,80,160]{2,1,0:T(8,128)S(1)}, f32[1,80,160]{2,1,0:T(8,128)}, u32[]{:S(2)}) copy-start(f32[1,80,160]{2,1,0:T(8,128)} %constant.25) | copy-start | bytes 153604
  30.6 11.8 %copy-start.3 = (bf16[256,256]{1,0:T(8,128)(2,1)S(1)}, bf16[256,256]{1,0:T(8,128)(2,1)}, u32[]{:S(2)}) copy-start(bf16[256,256]{1,0:T(8,128)(2,1)} %constant.24.clone.rz) | copy-start | bytes 393220
  30.6 50.9 %collective-permute-start.5 = (bf16[20,5,16,256]{3,2,1,0:T(8,128)(2,1)S(1)}, bf16[20,5,16,256]{3,2,1,0:T(8,128)(2,1)}, u32[]{:S(2)}, u32[]{:S(2)}) collective-permute-start(bf16[20,5,16,256]{3,2,1,0:T(8,128)(2,1)S(1)} %get-tuple-element.41), channel_id=1, source_target_pairs={{0,8},{8,16},{16,24},{1,9},{9,17},{17,25},{2,10},{10,18},{18,26},{... | collective-permute-start | bytes 2457608 | tf_op jit(solution)/shard_map/ppermute | solution.py:486
  33.1 48.4 %collective-permute-start.6 = (bf16[20,5,16,256]{3,2,1,0:T(8,128)(2,1)S(1)}, bf16[20,5,16,256]{3,2,1,0:T(8,128)(2,1)}, u32[]{:S(2)}, u32[]{:S(2)}) collective-permute-start(bf16[20,5,16,256]{3,2,1,0:T(8,128)(2,1)S(1)} %get-tuple-element.42), channel_id=1, source_target_pairs={{8,0},{16,8},{24,16},{9,1},{17,9},{25,17},{10,2},{18,10},{26,18},{... | collective-permute-start | bytes 2457608 | tf_op jit(solution)/shard_map/ppermute | solution.py:486
  35.9 45.5 %collective-permute-start.7 = (bf16[20,5,16,256]{3,2,1,0:T(8,128)(2,1)S(1)}, bf16[20,5,16,256]{3,2,1,0:T(8,128)(2,1)}, u32[]{:S(2)}, u32[]{:S(2)}) collective-permute-start(bf16[20,5,16,256]{3,2,1,0:T(8,128)(2,1)S(1)} %get-tuple-element.43), channel_id=1, source_target_pairs={{0,1},{1,2},{2,3},{3,4},{4,5},{5,6},{6,7},{8,9},{9,10},{10,11},{11... | collective-permute-start | bytes 2457608 | tf_op jit(solution)/shard_map/ppermute | solution.py:486
  39.1 42.4 %collective-permute-start.8 = (bf16[20,5,16,256]{3,2,1,0:T(8,128)(2,1)S(1)}, bf16[20,5,16,256]{3,2,1,0:T(8,128)(2,1)}, u32[]{:S(2)}, u32[]{:S(2)}) collective-permute-start(bf16[20,5,16,256]{3,2,1,0:T(8,128)(2,1)S(1)} %get-tuple-element.44), channel_id=1, source_target_pairs={{1,0},{2,1},{3,2},{4,3},{5,4},{6,5},{7,6},{9,8},{10,9},{11,10},{12... | collective-permute-start | bytes 2457608 | tf_op jit(solution)/shard_map/ppermute | solution.py:486
  42.4 39.1 %copy-start.1 = (s32[16,16,256]{2,1,0:T(8,128)S(1)}, s32[16,16,256]{2,1,0:T(8,128)}, u32[]{:S(2)}) copy-start(s32[16,16,256]{2,1,0:T(8,128)} %refs_3_.5) | copy-start | bytes 786436
  84.9 11.1 %collective-permute-start.9 = (f32[5,16,256]{2,1,0:T(8,128)S(1)}, f32[5,16,256]{2,1,0:T(8,128)S(1)}, u32[]{:S(2)}, u32[]{:S(2)}) collective-permute-start(f32[5,16,256]{2,1,0:T(8,128)S(1)} %get-tuple-element.46), channel_id=1, source_target_pairs={{0,1},{1,2},{2,3},{3,4},{4,5},{5,6},{6,7},{8,9},{9,10},{10,11},{11... | collective-permute-start | bytes 245768 | tf_op jit(solution)/shard_map/ppermute | solution.py:486
  88.1 8.0 %collective-permute-start.10 = (f32[5,16,256]{2,1,0:T(8,128)S(1)}, f32[5,16,256]{2,1,0:T(8,128)S(1)}, u32[]{:S(2)}, u32[]{:S(2)}) collective-permute-start(f32[5,16,256]{2,1,0:T(8,128)S(1)} %get-tuple-element.47), channel_id=1, source_target_pairs={{1,0},{2,1},{3,2},{4,3},{5,4},{6,5},{7,6},{9,8},{10,9},{11,10},{12... | collective-permute-start | bytes 245768 | tf_op jit(solution)/shard_map/ppermute | solution.py:486
  90.2 5.8 %collective-permute-start.11 = (f32[5,16,256]{2,1,0:T(8,128)S(1)}, f32[5,16,256]{2,1,0:T(8,128)S(1)}, u32[]{:S(2)}, u32[]{:S(2)}) collective-permute-start(f32[5,16,256]{2,1,0:T(8,128)S(1)} %get-tuple-element.48), channel_id=1, source_target_pairs={{0,8},{8,16},{16,24},{1,9},{9,17},{17,25},{2,10},{10,18},{18,26},{... | collective-permute-start | bytes 245768 | tf_op jit(solution)/shard_map/ppermute | solution.py:486
  94.0 5.8 %collective-permute-start.12 = (f32[5,16,256]{2,1,0:T(8,128)S(1)}, f32[5,16,256]{2,1,0:T(8,128)S(1)}, u32[]{:S(2)}, u32[]{:S(2)}) collective-permute-start(f32[5,16,256]{2,1,0:T(8,128)S(1)} %get-tuple-element.49), channel_id=1, source_target_pairs={{8,0},{16,8},{24,16},{9,1},{17,9},{25,17},{10,2},{18,10},{26,18},{... | collective-permute-start | bytes 245768 | tf_op jit(solution)/shard_map/ppermute | solution.py:486
  103.0 10.3 %collective-permute-start.13 = (f32[5,16,256]{2,1,0:T(8,128)S(1)}, f32[5,16,256]{2,1,0:T(8,128)S(1)}, u32[]{:S(2)}, u32[]{:S(2)}) collective-permute-start(f32[5,16,256]{2,1,0:T(8,128)S(1)} %get-tuple-element.55), channel_id=1, source_target_pairs={{0,1},{1,2},{2,3},{3,4},{4,5},{5,6},{6,7},{8,9},{9,10},{10,11},{11... | collective-permute-start | bytes 245768 | tf_op jit(solution)/shard_map/ppermute | solution.py:486
  107.0 6.3 %collective-permute-start.14 = (f32[5,16,256]{2,1,0:T(8,128)S(1)}, f32[5,16,256]{2,1,0:T(8,128)S(1)}, u32[]{:S(2)}, u32[]{:S(2)}) collective-permute-start(f32[5,16,256]{2,1,0:T(8,128)S(1)} %get-tuple-element.56), channel_id=1, source_target_pairs={{1,0},{2,1},{3,2},{4,3},{5,4},{6,5},{7,6},{9,8},{10,9},{11,10},{12... | collective-permute-start | bytes 245768 | tf_op jit(solution)/shard_map/ppermute | solution.py:486
  109.0 4.4 %collective-permute-start.15 = (f32[5,16,256]{2,1,0:T(8,128)S(1)}, f32[5,16,256]{2,1,0:T(8,128)S(1)}, u32[]{:S(2)}, u32[]{:S(2)}) collective-permute-start(f32[5,16,256]{2,1,0:T(8,128)S(1)} %get-tuple-element.57), channel_id=1, source_target_pairs={{0,8},{8,16},{16,24},{1,9},{9,17},{17,25},{2,10},{10,18},{18,26},{... | collective-permute-start | bytes 245768 | tf_op jit(solution)/shard_map/ppermute | solution.py:486
  111.1 5.8 %collective-permute-start.16 = (f32[5,16,256]{2,1,0:T(8,128)S(1)}, f32[5,16,256]{2,1,0:T(8,128)S(1)}, u32[]{:S(2)}, u32[]{:S(2)}) collective-permute-start(f32[5,16,256]{2,1,0:T(8,128)S(1)} %get-tuple-element.58), channel_id=1, source_target_pairs={{8,0},{16,8},{24,16},{9,1},{17,9},{25,17},{10,2},{18,10},{26,18},{... | collective-permute-start | bytes 245768 | tf_op jit(solution)/shard_map/ppermute | solution.py:486

commit v7 on v6

--- a/solution.py
+++ b/solution.py
@@ -215,7 +215,7 @@
     return jnp.where(row == n - 1, hi, pltpu.roll(a, rows - 1, 0)) - jnp.where(row == 0, lo, pltpu.roll(a, 1, 0))
 
 
-def main_kernel(pick, amp, lw, rz, u_hbm, q_hbm, out, u_buf, q_buf, even, odd, dz_even, dz_odd, u_even, u_odd, acc, c0, u_sem, q_sem):
+def main_kernel(pick, amp, lw, u_hbm, q_hbm, out, u_buf, q_buf, even, odd, u_even, u_odd, acc, c0, u_sem, q_sem):
     nx, nm, nv, ny, nz = u_buf.shape
     rows = nv * ny
 
@@ -235,12 +235,7 @@
         qm = q_buf[p, pick[m]].reshape(rows, nz)
         dest[m] = jnp.dot(lw[...], jnp.concatenate([qm, qm], axis=0), preferred_element_type=F32)
 
-    def span_differences(p, step, dest):
-        u = u_buf[p, pl.ds(step * GROUP, GROUP)].reshape(GROUP * rows, nz)
-        dz = jnp.dot(u, rz[...], preferred_element_type=F32)
-        dest[pl.ds(step * GROUP, GROUP)] = dz.reshape(GROUP, rows, nz)
-
-    def plane(p, src, dest, dz_src, dz_dest, u_src, u_dest):
+    def plane(p, src, dest, u_src, u_dest):
         after = jnp.minimum(p + 1, nx - 1)
 
         @pl.when(p < nx - 1)
@@ -253,21 +248,23 @@
         def body(step, carry):
             for k in range(GROUP):
                 products(after, step * GROUP + k, dest)
-            span_differences(after, step, dz_dest)
             for j in range(nv):
                 at = slice(j * ny, (j + 1) * ny)
-                sums = [acc[n, at] for n in range(5)]
+                sums = [acc[n, at] for n in range(6)]
                 for k in range(GROUP):
                     m = step * GROUP + k
-                    w0, down, up, w2 = (src[m, n * rows + j * ny : n * rows + (j + 1) * ny] for n in range(4))
+                    w0, w1, w2 = (src[m, n * rows + j * ny : n * rows + (j + 1) * ny] for n in range(3))
                     u = u_src[m, at]
-                    a = amp[m]
-                    following = u_buf[after, m, j].astype(F32) * a
+                    following = u_buf[after, m, j].astype(F32) * amp[m]
                     dx = following - u_dest[m, at]
                     u_dest[m, at] = following
-                    terms = [dx * w0 + (dz_src[m, at] * a) * w2, u * w0, u * down, u * up, u * w2]
+                    down1 = pltpu.roll(w1, 1, 0) - w1
+                    down2 = pltpu.roll(w2, 1, 1) - w2
+                    up1 = pltpu.roll(down1, ny - 1, 0)
+                    up2 = pltpu.roll(down2, nz - 1, 1)
+                    terms = [dx * w0, u * w0, u * down1, u * up1, u * down2, u * up2]
                     sums = [v + t for v, t in zip(sums, terms)]
-                for n in range(5):
+                for n in range(6):
                     acc[n, at] = sums[n]
             return carry
 
@@ -275,7 +272,7 @@
         last = jnp.where(p == nx - 1, 1.0, 0.0)
         c0[p + 1] = acc[1]
         row = row_of((rows, nz), ny)
-        h = acc[0] - diff_lanes(acc[4]) - last * acc[1]
+        h = acc[0] - last * acc[1] + pltpu.roll(acc[4], nz - 1, 1) + pltpu.roll(acc[5], 1, 1)
         h = h + jnp.where(row == ny - 1, 0.0, pltpu.roll(acc[2], rows - 1, 0))
         out[p] = h + jnp.where(row == 0, 0.0, pltpu.roll(acc[3], 1, 0))
 
@@ -289,12 +286,10 @@
         return carry
 
     lax.fori_loop(0, nm, first, 0, unroll=GROUP)
-    for step in range(nm // GROUP):
-        span_differences(0, step, dz_even)
 
     def pair(i, carry):
-        plane(2 * i, even, odd, dz_even, dz_odd, u_even, u_odd)
-        plane(2 * i + 1, odd, even, dz_odd, dz_even, u_odd, u_even)
+        plane(2 * i, even, odd, u_even, u_odd)
+        plane(2 * i + 1, odd, even, u_odd, u_even)
         return carry
 
     lax.fori_loop(0, nx // 2, pair, 0)
@@ -306,25 +301,23 @@
     lax.fori_loop(0, nx, finish, 0, unroll=4)
 
 
-def main(pick, amp, lw, rz, direct, adjoint):
+def main(pick, amp, lw, direct, adjoint):
     nm, nv, nx, ny, nz = direct.shape
     rows = nv * ny
     buf = pltpu.VMEM((nx, nm, nv, ny, nz), BF16)
     return pl.pallas_call(
         main_kernel,
-        in_specs=[in_smem(), in_smem(), in_vmem(), in_vmem(), in_hbm(), in_hbm()],
+        in_specs=[in_smem(), in_smem(), in_vmem(), in_hbm(), in_hbm()],
         out_specs=in_vmem(),
         out_shape=sds((nx, rows, nz), F32),
         scratch_shapes=[
             buf,
             buf,
-            pltpu.VMEM((nm, 4 * rows, nz), F32),
-            pltpu.VMEM((nm, 4 * rows, nz), F32),
+            pltpu.VMEM((nm, 3 * rows, nz), F32),
+            pltpu.VMEM((nm, 3 * rows, nz), F32),
             pltpu.VMEM((nm, rows, nz), F32),
             pltpu.VMEM((nm, rows, nz), F32),
-            pltpu.VMEM((nm, rows, nz), F32),
-            pltpu.VMEM((nm, rows, nz), F32),
-            pltpu.VMEM((5, rows, nz), F32),
+            pltpu.VMEM((6, rows, nz), F32),
             pltpu.VMEM((nx + 2, rows, nz), F32),
             pltpu.SemaphoreType.DMA((nx,)),
             pltpu.SemaphoreType.DMA((nx,)),
@@ -332,7 +325,7 @@
         compiler_params=params(LARGE),
         cost_estimate=pl.CostEstimate(flops=10**6, bytes_accessed=10**5, transcendentals=0),
         name="main",
-    )(pick, amp, lw, rz, direct, adjoint)
+    )(pick, amp, lw, direct, adjoint)
 
 
 def weight_of(cells):
@@ -352,7 +345,7 @@
 
 def boundary_kernel(scale, pick, amp, local, cell, *refs):
     w = refs[0:4]
-    halo = refs[4:8]
+    halo = [refs[4 + f] for f in (2, 3, 0, 1)]
     field, xlo, xhi, ylo, yhi = refs[8:13]
     base_halo = refs[13:17]
     add = refs[17:21]
@@ -397,7 +390,7 @@
         scratch_shapes=[pltpu.VMEM(f.shape, F32) for f in face],
         compiler_params=params(28),
         name="boundary",
-    )(pick, amp, local, cell, *w_faces, *halo)
+    )(pick, amp, local, cell, *w_faces, *halo[2:], *halo[:2])
 
 
 def mix_rows(lw, values):
@@ -517,16 +510,6 @@
     return (wide * jnp.asarray(np.tile(cells, (wide.shape[-2] // n, wide.shape[-1] // n)))).astype(BF16)
 
 
-def main_rows(wide, n):
-    eye, below, above = (np.eye(n, k=k, dtype=np.float32) for k in (0, -1, 1))
-    return jnp.concatenate([within(wide[d], n, c) for d, c in ((0, eye), (1, below - eye), (1, eye - above), (2, eye))], axis=0)
-
-
-def span_difference(nz):
-    eye = np.eye(nz, dtype=np.float32)
-    return jnp.asarray(np.roll(eye, -1, 1) - np.roll(eye, 1, 1), BF16)
-
-
 def step_rows(lw):
     half = lw.shape[-1] // 2
     return jnp.concatenate([lw[..., :half], lw[..., :half], lw[..., half:]], axis=-1)
@@ -543,7 +526,7 @@
     lw_x = lw_y if nx == ny else within(kron_rows(mix, nx), nx, np.eye(nx, dtype=np.float32))
     w_faces = [*mix_chord(lw_y[0], adjoint), *mix_normal(lw_x[1], adjoint)]
     halo = exchange(faces(pick, amp, base, own, w_faces))
-    local = main(pick, amp, main_rows(wide, ny), span_difference(nz), direct, adjoint)
+    local = main(pick, amp, lw_y.reshape(3 * nv * ny, -1), direct, adjoint)
     field, *sides = boundary(1.0 / nm, pick, amp, local, cell, w_faces, halo)
     sides, base_halo = sides[:4], sides[4:]
     lw_step = step_rows(lw_y.reshape(3 * nv * ny, -1))

time: 123 us -> 121 us (0.984)
  Pallas kernels: 66.5 us -> 63.6 us
  starting transfers between devices: 41.9 us -> 44.8 us
  waiting for transfers between devices: 11 us -> 8.94 us
    ppermute x12, starting transfers between devices: 32.8 us -> 35.7 us  [exchange_axis(): return [lax.ppermute(hi, axis, up), lax.ppermute(lo, axis, down)]]
    pallas_call x1, Pallas kernels: 39.1 us -> 36.5 us  [main(): pl.pallas_call(main_kernel, in_specs=[in_smem(), in_smem(), in_vmem(), in...]
    ppermute x12, waiting for transfers between devices: 7.27 us -> 5.18 us  [exchange_axis(): return [lax.ppermute(hi, axis, up), lax.ppermute(lo, axis, down)]]
  transfers between devices with their start and end apart: 17 -> 17, of which waited for: 5 -> 5; matrix products, arithmetic and copies ran while one was open for 1% -> 1% of each run, Pallas kernels for 40% -> 38%
where the time goes in v7:
time: 121 us; the launch traced here: 119 us
  Pallas kernels  63.6 us (53%)
  starting transfers between devices  44.8 us (37%)
  waiting for transfers between devices  8.94 us (7%)
    pallas_call x1, Pallas kernels, main(): pl.pallas_call(main_kernel, in_specs=[in_smem(), in_smem(), in_vmem(), in...  36.5 us
    ppermute x12, starting transfers between devices, exchange_axis(): return [lax.ppermute(hi, axis, up), lax.ppermute(lo, axis, down)]  35.7 us
    ppermute x5, starting transfers between devices, sum_over(): lax.ppermute(values, axis, [(i, i ^ bit) for i in range(count)])  9.07 us
    pallas_call x2, Pallas kernels, apply_step(): pl.pallas_call(lambda *refs: step_kernel(last, *refs), in_specs=[in_vmem(...  7.27 us
    pallas_call x1, Pallas kernels, mix_normal(): pl.pallas_call(mix_normal_kernel, grid=(nm // GROUP,), in_specs=[pl.Block...  6.65 us
    pallas_call x1, Pallas kernels, pack(): pl.pallas_call(direct_kernel, grid=(nm // GROUP,), in_specs=[pl.BlockSpec...  6.32 us
    ppermute x12, waiting for transfers between devices, exchange_axis(): return [lax.ppermute(hi, axis, up), lax.ppermute(lo, axis, down)]  5.18 us
    ppermute x5, waiting for transfers between devices, sum_over(): lax.ppermute(values, axis, [(i, i ^ bit) for i in range(count)])  3.76 us
  transfers between devices with their start and end apart: 17, of which 5 were waited for; matrix products, arithmetic and copies ran while one was open for 1% of the time, Pallas kernels for 38%

profile of v7, /device:TPU:5, one launch (start us, length us, event | category | flops | bytes accessed | tf_op | source)
XLA Modules:
  0.0 118.7 jit_solution(6618809193281992905)
XLA Ops:
  0.0 0.0 copy-start.5
  0.0 0.0 copy-start.4
  0.0 0.0 copy-start.7
  0.0 0.0 copy-start.6
  0.0 6.3 %pack_direct.1 = (bf16[20,5,16,256]{3,2,1,0:T(8,128)(2,1)S(1)}, bf16[20,5,16,256]{3,2,1,0:T(8,128)(2,1)S(1)}, bf16[20,5,16,256]{3,2,1,0:T(8,128)(2,1)S(1)}, bf16...) custom-call(bf16[16,5,16,16,256]{4,3,2,1,0:T(8,128)(2,1)} %u_hbm.1), custom_call_target="tpu_custom_call" | custom-call | flops 15728640 | bytes 10485760 | tf_op jit(solution)/shard_map/pack_direct/pallas_call | solution.py:73
  6.3 0.1 reduce_sum.9
  6.5 0.1 collective-permute-start
  6.5 0.0 copy-done.6
  6.6 0.0 copy-done.5
  6.6 0.2 fusion.2
  6.8 2.1 %collective-permute-done = f32[16]{0:T(128)S(1)} collective-permute-done((f32[16]{0:T(128)S(1)}, f32[16]{0:T(128)S(1)}, u32[]{:S(2)}, u32[]{:S(2)}) %collective-permute-start) | collective-permute-done | bytes 96 | tf_op jit(solution)/shard_map/ppermute | solution.py:493
  8.9 1.3 %collective-permute-start.1 = (f32[16]{0:T(128)S(1)}, f32[16]{0:T(128)S(1)}, u32[]{:S(2)}, u32[]{:S(2)}) collective-permute-start(f32[16]{0:T(128)S(1)} %add.18), channel_id=1, source_target_pairs={{0,2},{1,3},{2,0},{3,1},{4,6},{5,7},{6,4},{7,5},{8,10},{9,11},{10,... | collective-permute-start | bytes 200 | tf_op jit(solution)/shard_map/ppermute | solution.py:493
  10.2 0.0 copy-done.4
  10.2 0.0 copy-done.7
  10.2 0.4 fusion.1
  10.6 0.7 collective-permute-done.1
  11.3 2.3 %collective-permute-start.2 = (f32[16]{0:T(128)S(1)}, f32[16]{0:T(128)S(1)}, u32[]{:S(2)}, u32[]{:S(2)}) collective-permute-start(f32[16]{0:T(128)S(1)} %add.19), channel_id=1, source_target_pairs={{0,4},{1,5},{2,6},{3,7},{4,0},{5,1},{6,2},{7,3},{8,12},{9,13},{10,... | collective-permute-start | bytes 200 | tf_op jit(solution)/shard_map/ppermute | solution.py:493
  13.6 1.0 collective-permute-done.2
  14.6 4.1 %collective-permute-start.3 = (f32[16]{0:T(128)S(1)}, f32[16]{0:T(128)S(1)}, u32[]{:S(2)}, u32[]{:S(2)}) collective-permute-start(f32[16]{0:T(128)S(1)} %add.20), channel_id=1, source_target_pairs={{0,8},{8,0},{16,24},{24,16},{1,9},{9,1},{17,25},{25,17},{2,10},{10... | collective-permute-start | bytes 200 | tf_op jit(solution)/shard_map/ppermute | solution.py:493
  18.7 2.3 %mix_chord.1 = (f32[16,80,256]{2,1,0:T(8,128)S(1)}, f32[16,80,256]{2,1,0:T(8,128)S(1)}) custom-call(bf16[80,160]{1,0:T(8,128)(2,1)S(1)} %get-tuple-element.59.lw, bf16[16,5,16,16,256]{4,3,2,1,0:T(8,128)(2,1)} %src.3, bf16[16,5,16,16,256]{4,3,2,1,0:T(8,128)(2,1)} %src.3), custom_call_target="tpu_custom_call" | custom-call | flops 100000000 | bytes 6000000 | tf_op jit(solution)/shard_map/mix_chord/pallas_call | solution.py:105
  21.0 0.0 collective-permute-done.3
  21.0 1.3 %collective-permute-start.4 = (f32[16]{0:T(128)S(1)}, f32[16]{0:T(128)S(1)}, u32[]{:S(2)}, u32[]{:S(2)}) collective-permute-start(f32[16]{0:T(128)S(1)} %add.21), channel_id=1, source_target_pairs={{0,16},{8,24},{16,0},{24,8},{1,17},{9,25},{17,1},{25,9},{2,18},{10... | collective-permute-start | bytes 200 | tf_op jit(solution)/shard_map/ppermute | solution.py:493
  22.3 0.0 copy-start
  22.3 0.0 copy-start.2
  22.3 0.0 copy-start.3
  22.3 6.7 %mix_normal.1 = (f32[16,80,256]{2,1,0:T(8,128)S(1)}, f32[16,80,256]{2,1,0:T(8,128)S(1)}) custom-call(bf16[80,160]{1,0:T(8,128)(2,1)S(1)} %get-tuple-element.60.lw, bf16[16,5,16,16,256]{4,3,2,1,0:T(8,128)(2,1)} %src.3), custom_call_target="tpu_custom_call" | custom-call | flops 15728640 | bytes 15728640 | tf_op jit(solution)/shard_map/mix_normal/pallas_call | solution.py:138
  29.0 0.0 collective-permute-done.4
  29.0 0.0 copy-done
  29.0 0.0 copy-done.2
  29.0 0.0 copy-done.3
  29.0 1.5 %faces.1 = (bf16[20,5,16,256]{3,2,1,0:T(8,128)(2,1)S(1)}, bf16[20,5,16,256]{3,2,1,0:T(8,128)(2,1)S(1)}, bf16[20,5,16,256]{3,2,1,0:T(8,128)(2,1)S(1)}, bf16[20,5,16,256]{3,2,1,0:T(8,128)(2,1)S(1)}) custom-call(s32[16]{0:T(128)S(1)} %copy-done.3, ...), custom_call_target="tpu_custom_call", output_to_operand_aliasing={{0}: (3, {}), {1}: (4, {}), {2}: (5, {}), {3}: (6, {})} | custom-call | tf_op jit(solution)/shard_map/faces/pallas_call | solution.py:190
  30.5 3.1 %collective-permute-start.5 = (bf16[20,5,16,256]{3,2,1,0:T(8,128)(2,1)S(1)}, bf16[20,5,16,256]{3,2,1,0:T(8,128)(2,1)S(1)}, u32[]{:S(2)}, u32[]{:S(2)}) collective-permute-start(bf16[20,5,16,256]{3,2,1,0:T(8,128)(2,1)S(1)} %get-tuple-element.41), channel_id=1, source_target_pairs={{0,1},{1,2},{2,3},{3,4},{4,5},{5,6},{6,7},{8,9},{9,10},{10,11},{11... | collective-permute-start | bytes 2457608 | tf_op jit(solution)/shard_map/ppermute | solution.py:479
  33.7 2.2 %collective-permute-start.6 = (bf16[20,5,16,256]{3,2,1,0:T(8,128)(2,1)S(1)}, bf16[20,5,16,256]{3,2,1,0:T(8,128)(2,1)}, u32[]{:S(2)}, u32[]{:S(2)}) collective-permute-start(bf16[20,5,16,256]{3,2,1,0:T(8,128)(2,1)S(1)} %get-tuple-element.42), channel_id=1, source_target_pairs={{1,0},{2,1},{3,2},{4,3},{5,4},{6,5},{7,6},{9,8},{10,9},{11,10},{12... | collective-permute-start | bytes 2457608 | tf_op jit(solution)/shard_map/ppermute | solution.py:479
  35.9 2.9 %collective-permute-start.7 = (bf16[20,5,16,256]{3,2,1,0:T(8,128)(2,1)S(1)}, bf16[20,5,16,256]{3,2,1,0:T(8,128)(2,1)}, u32[]{:S(2)}, u32[]{:S(2)}) collective-permute-start(bf16[20,5,16,256]{3,2,1,0:T(8,128)(2,1)S(1)} %get-tuple-element.43), channel_id=1, source_target_pairs={{0,8},{8,16},{16,24},{1,9},{9,17},{17,25},{2,10},{10,18},{18,26},{... | collective-permute-start | bytes 2457608 | tf_op jit(solution)/shard_map/ppermute | solution.py:479
  38.8 2.4 %collective-permute-start.8 = (bf16[20,5,16,256]{3,2,1,0:T(8,128)(2,1)S(1)}, bf16[20,5,16,256]{3,2,1,0:T(8,128)(2,1)}, u32[]{:S(2)}, u32[]{:S(2)}) collective-permute-start(bf16[20,5,16,256]{3,2,1,0:T(8,128)(2,1)S(1)} %get-tuple-element.44), channel_id=1, source_target_pairs={{8,0},{16,8},{24,16},{9,1},{17,9},{25,17},{10,2},{18,10},{26,18},{... | collective-permute-start | bytes 2457608 | tf_op jit(solution)/shard_map/ppermute | solution.py:479
  41.2 0.1 pad_maximum_fusion.refs_0_
  41.3 0.0 copy-start.1
  41.3 36.5 %main.1.refs_2_ = f32[16,80,256]{2,1,0:T(8,128)S(1)} custom-call(s32[16]{0:T(128)S(1)} %copy-done.3, f32[16]{0:T(128)S(1)} %add_rsqrt_fusion.amp.refs_1_, bf16[240,160]{1,0:T(8,128)(2,1)S(1)} %bitcast.22, bf16[16,5,16,16,256]{4,3,2,1,0:T(8,128)(2,1)} %u_hbm.1, bf16[16,5,16,16,256]{4,3,2,1,0:T(8,128)(2,1)} %src.3), custom_call_target="tpu_custom_call" | custom-call | flops 1000000 | bytes 100000 | tf_op jit(solution)/shard_map/main/pallas_call | solution.py:308
  77.7 0.0 collective-permute-done.5.refs_8_
  77.8 0.0 collective-permute-done.6.refs_9_
  77.8 0.0 collective-permute-done.7.refs_10_
  77.8 0.0 collective-permute-done.8.refs_11_
  77.8 0.0 copy-done.1
  77.8 3.1 %boundary.1 = (f32[16,80,256]{2,1,0:T(8,128)S(1)}, f32[5,16,256]{2,1,0:T(8,128)S(1)}, f32[5,16,256]{2,1,0:T(8,128)S(1)}, f32[5,16,256]{2,1,0:T(8,128)S(1)}, f32[...) custom-call(s32[16]{0:T(128)S(1)} %copy-done.3, ...), custom_call_target="tpu_custom_call" | custom-call | tf_op jit(solution)/shard_map/boundary/pallas_call | solution.py:385
  80.9 1.9 %collective-permute-start.10 = (f32[5,16,256]{2,1,0:T(8,128)S(1)}, f32[5,16,256]{2,1,0:T(8,128)S(1)}, u32[]{:S(2)}, u32[]{:S(2)}) collective-permute-start(f32[5,16,256]{2,1,0:T(8,128)S(1)} %get-tuple-element.47), channel_id=1, source_target_pairs={{1,0},{2,1},{3,2},{4,3},{5,4},{6,5},{7,6},{9,8},{10,9},{11,10},{12... | collective-permute-start | bytes 245768 | tf_op jit(solution)/shard_map/ppermute | solution.py:479
  82.8 3.2 %collective-permute-start.11 = (f32[5,16,256]{2,1,0:T(8,128)S(1)}, f32[5,16,256]{2,1,0:T(8,128)S(1)}, u32[]{:S(2)}, u32[]{:S(2)}) collective-permute-start(f32[5,16,256]{2,1,0:T(8,128)S(1)} %get-tuple-element.48), channel_id=1, source_target_pairs={{0,8},{8,16},{16,24},{1,9},{9,17},{17,25},{2,10},{10,18},{18,26},{... | collective-permute-start | bytes 245768 | tf_op jit(solution)/shard_map/ppermute | solution.py:479
  86.1 1.9 %collective-permute-start.12 = (f32[5,16,256]{2,1,0:T(8,128)S(1)}, f32[5,16,256]{2,1,0:T(8,128)S(1)}, u32[]{:S(2)}, u32[]{:S(2)}) collective-permute-start(f32[5,16,256]{2,1,0:T(8,128)S(1)} %get-tuple-element.49), channel_id=1, source_target_pairs={{8,0},{16,8},{24,16},{9,1},{17,9},{25,17},{10,2},{18,10},{26,18},{... | collective-permute-start | bytes 245768 | tf_op jit(solution)/shard_map/ppermute | solution.py:479
  88.0 4.5 %collective-permute-start.9 = (f32[5,16,256]{2,1,0:T(8,128)S(1)}, f32[5,16,256]{2,1,0:T(8,128)S(1)}, u32[]{:S(2)}, u32[]{:S(2)}) collective-permute-start(f32[5,16,256]{2,1,0:T(8,128)S(1)} %get-tuple-element.46), channel_id=1, source_target_pairs={{0,1},{1,2},{2,3},{3,4},{4,5},{5,6},{6,7},{8,9},{9,10},{10,11},{11... | collective-permute-start | bytes 245768 | tf_op jit(solution)/shard_map/ppermute | solution.py:479
  92.5 0.1 pad_maximum_fusion.1.refs_1_
  92.6 0.0 collective-permute-done.10.refs_6_
  92.6 0.0 collective-permute-done.11.refs_7_
  92.6 0.0 collective-permute-done.12.refs_8_
  92.7 1.4 %collective-permute-done.9.refs_5_ = f32[5,16,256]{2,1,0:T(8,128)S(1)} collective-permute-done((f32[5,16,256]{2,1,0:T(8,128)S(1)}, f32[5,16,256]{2,1,0:T(8,128)S(1)}, u32[]{:S(2)}, u32[]{:S(2)}) %collective-permute-start.9) | collective-permute-done | bytes 81952 | tf_op jit(solution)/shard_map/ppermute | solution.py:479
  94.0 3.2 %step_one.1 = (f32[16,80,256]{2,1,0:T(8,128)S(1)}, f32[5,16,256]{2,1,0:T(8,128)S(1)}, f32[5,16,256]{2,1,0:T(8,128)S(1)}, f32[5,16,256]{2,1,0:T(8,128)S(1)}, f32[5,16,256]{2,1,0:T(8,128)S(1)}) custom-call(bf16[240,240]{1,0:T(8,128)(2,1)S(1)} %pad_maximum_fusion.refs_0_, bf16[80,240]{1,0:T(8,128)(2,1)S(1)} %pad_maximum_fusion.1.refs_1_, ...), custom_call_target="tpu_custom_call" | custom-call | tf_op jit(solution)/shard_map/step_one/pallas_call | solution.py:464
  97.2 4.6 %collective-permute-start.13 = (f32[5,16,256]{2,1,0:T(8,128)S(1)}, f32[5,16,256]{2,1,0:T(8,128)S(1)}, u32[]{:S(2)}, u32[]{:S(2)}) collective-permute-start(f32[5,16,256]{2,1,0:T(8,128)S(1)} %get-tuple-element.55), channel_id=1, source_target_pairs={{0,1},{1,2},{2,3},{3,4},{4,5},{5,6},{6,7},{8,9},{9,10},{10,11},{11... | collective-permute-start | bytes 245768 | tf_op jit(solution)/shard_map/ppermute | solution.py:479
  101.8 1.9 %collective-permute-start.14 = (f32[5,16,256]{2,1,0:T(8,128)S(1)}, f32[5,16,256]{2,1,0:T(8,128)S(1)}, u32[]{:S(2)}, u32[]{:S(2)}) collective-permute-start(f32[5,16,256]{2,1,0:T(8,128)S(1)} %get-tuple-element.56), channel_id=1, source_target_pairs={{1,0},{2,1},{3,2},{4,3},{5,4},{6,5},{7,6},{9,8},{10,9},{11,10},{12... | collective-permute-start | bytes 245768 | tf_op jit(solution)/shard_map/ppermute | solution.py:479
  103.7 5.1 %collective-permute-start.15 = (f32[5,16,256]{2,1,0:T(8,128)S(1)}, f32[5,16,256]{2,1,0:T(8,128)S(1)}, u32[]{:S(2)}, u32[]{:S(2)}) collective-permute-start(f32[5,16,256]{2,1,0:T(8,128)S(1)} %get-tuple-element.57), channel_id=1, source_target_pairs={{0,8},{8,16},{16,24},{1,9},{9,17},{17,25},{2,10},{10,18},{18,26},{... | collective-permute-start | bytes 245768 | tf_op jit(solution)/shard_map/ppermute | solution.py:479
  108.8 1.9 %collective-permute-start.16 = (f32[5,16,256]{2,1,0:T(8,128)S(1)}, f32[5,16,256]{2,1,0:T(8,128)S(1)}, u32[]{:S(2)}, u32[]{:S(2)}) collective-permute-start(f32[5,16,256]{2,1,0:T(8,128)S(1)} %get-tuple-element.58), channel_id=1, source_target_pairs={{8,0},{16,8},{24,16},{9,1},{17,9},{25,17},{10,2},{18,10},{26,18},{... | collective-permute-start | bytes 245768 | tf_op jit(solution)/shard_map/ppermute | solution.py:479
  110.8 0.0 collective-permute-done.13.refs_5_
  110.8 0.0 collective-permute-done.14.refs_6_
  110.8 0.0 collective-permute-done.15.refs_7_
  110.8 3.8 %collective-permute-done.16.refs_8_ = f32[5,16,256]{2,1,0:T(8,128)S(1)} collective-permute-done((f32[5,16,256]{2,1,0:T(8,128)S(1)}, f32[5,16,256]{2,1,0:T(8,128)S(1)}, u32[]{:S(2)}, u32[]{:S(2)}) %collective-permute-start.16) | collective-permute-done | bytes 81952 | tf_op jit(solution)/shard_map/ppermute | solution.py:479
  114.6 4.1 %step_two.1 = f32[5,16,16,256]{3,2,1,0:T(8,128)} custom-call(bf16[240,240]{1,0:T(8,128)(2,1)S(1)} %pad_maximum_fusion.refs_0_, bf16[80,240]{1,0:T(8,128)(2,1)S(1)} %pad_maximum_fusion.1.refs_1_, f32[5,16,16,256]{3,2,1,0:T(8,128)S(1)} %copy-done, s32[16,16,256]{2,1,0:T(8,128)S(1)} %copy-done.1, f32[16,80,256]{2,1,0:T(8,128)S(1)} %get-tuple-element.54.refs_4_, ...), custom_call_target="tpu_custom_call" | custom-call | tf_op jit(solution)/shard_map/step_two/pallas_call | solution.py:464
  (10 shorter events, 0.1 us)
Async XLA Ops:
  0.0 6.6 %copy-start.5 = (f32[10,160,1]{1,0,2:T(8,128)S(1)}, f32[10,160,1]{1,0,2:T(8,128)}, u32[]{:S(2)}) copy-start(f32[10,160,1]{1,0,2:T(8,128)} %constant.16) | copy-start | bytes 19204
  0.0 10.2 %copy-start.4 = (f32[80,160]{1,0:T(8,128)S(1)}, f32[80,160]{1,0:T(8,128)}, u32[]{:S(2)}) copy-start(f32[80,160]{1,0:T(8,128)} %constant.15.clone) | copy-start | bytes 153604
  0.0 10.2 %copy-start.7 = (f32[80,5,1]{0,1,2:T(8,128)S(1)}, f32[80,5,1]{0,1,2:T(8,128)}, u32[]{:S(2)}) copy-start(f32[80,5,1]{0,1,2:T(8,128)} %constant.17) | copy-start | bytes 4804
  0.0 6.5 %copy-start.6 = (f32[3,5,5]{2,0,1:T(4,128)S(1)}, f32[3,5,5]{2,0,1:T(4,128)}, u32[]{:S(2)}) copy-start(f32[3,5,5]{2,0,1:T(4,128)} %param.14) | copy-start | bytes 904
  6.5 2.4 %collective-permute-start = (f32[16]{0:T(128)S(1)}, f32[16]{0:T(128)S(1)}, u32[]{:S(2)}, u32[]{:S(2)}) collective-permute-start(f32[16]{0:T(128)S(1)} %reduce_sum.9), channel_id=1, source_target_pairs={{0,1},{1,0},{2,3},{3,2},{4,5},{5,4},{6,7},{7,6},{8,9},{9,8},{10,11... | collective-permute-start | bytes 200 | tf_op jit(solution)/shard_map/ppermute | solution.py:493
  8.9 2.4 %collective-permute-start.1 = (f32[16]{0:T(128)S(1)}, f32[16]{0:T(128)S(1)}, u32[]{:S(2)}, u32[]{:S(2)}) collective-permute-start(f32[16]{0:T(128)S(1)} %add.18), channel_id=1, source_target_pairs={{0,2},{1,3},{2,0},{3,1},{4,6},{5,7},{6,4},{7,5},{8,10},{9,11},{10,... | collective-permute-start | bytes 200 | tf_op jit(solution)/shard_map/ppermute | solution.py:493
  11.3 3.3 %collective-permute-start.2 = (f32[16]{0:T(128)S(1)}, f32[16]{0:T(128)S(1)}, u32[]{:S(2)}, u32[]{:S(2)}) collective-permute-start(f32[16]{0:T(128)S(1)} %add.19), channel_id=1, source_target_pairs={{0,4},{1,5},{2,6},{3,7},{4,0},{5,1},{6,2},{7,3},{8,12},{9,13},{10,... | collective-permute-start | bytes 200 | tf_op jit(solution)/shard_map/ppermute | solution.py:493
  14.6 6.4 %collective-permute-start.3 = (f32[16]{0:T(128)S(1)}, f32[16]{0:T(128)S(1)}, u32[]{:S(2)}, u32[]{:S(2)}) collective-permute-start(f32[16]{0:T(128)S(1)} %add.20), channel_id=1, source_target_pairs={{0,8},{8,0},{16,24},{24,16},{1,9},{9,1},{17,25},{25,17},{2,10},{10... | collective-permute-start | bytes 200 | tf_op jit(solution)/shard_map/ppermute | solution.py:493
  21.0 7.9 %collective-permute-start.4 = (f32[16]{0:T(128)S(1)}, f32[16]{0:T(128)S(1)}, u32[]{:S(2)}, u32[]{:S(2)}) collective-permute-start(f32[16]{0:T(128)S(1)} %add.21), channel_id=1, source_target_pairs={{0,16},{8,24},{16,0},{24,8},{1,17},{9,25},{17,1},{25,9},{2,18},{10... | collective-permute-start | bytes 200 | tf_op jit(solution)/shard_map/ppermute | solution.py:493
  22.3 6.7 %copy-start = (f32[5,16,16,256]{3,2,1,0:T(8,128)S(1)}, f32[5,16,16,256]{3,2,1,0:T(8,128)}, u32[]{:S(2)}) copy-start(f32[5,16,16,256]{3,2,1,0:T(8,128)} %refs_2_.3) | copy-start | bytes 3932164
  22.3 6.7 %copy-start.2 = (bf16[20,5,16,256]{3,2,1,0:T(8,128)(2,1)S(1)}, bf16[20,5,16,256]{3,2,1,0:T(8,128)(2,1)}, u32[]{:S(2)}) copy-start(bf16[20,5,16,256]{3,2,1,0:T(8,128)(2,1)} %get-tuple-element.40.refs_3_) | copy-start | bytes 2457604
  22.3 6.7 %copy-start.3 = (s32[16]{0:T(128)S(1)}, s32[16]{0:T(128)}, u32[]{:S(2)}) copy-start(s32[16]{0:T(128)} %refs_0_.1) | copy-start | bytes 196
  30.5 47.2 %collective-permute-start.5 = (bf16[20,5,16,256]{3,2,1,0:T(8,128)(2,1)S(1)}, bf16[20,5,16,256]{3,2,1,0:T(8,128)(2,1)S(1)}, u32[]{:S(2)}, u32[]{:S(2)}) collective-permute-start(bf16[20,5,16,256]{3,2,1,0:T(8,128)(2,1)S(1)} %get-tuple-element.41), channel_id=1, source_target_pairs={{0,1},{1,2},{2,3},{3,4},{4,5},{5,6},{6,7},{8,9},{9,10},{10,11},{11... | collective-permute-start | bytes 2457608 | tf_op jit(solution)/shard_map/ppermute | solution.py:479
  33.7 44.1 %collective-permute-start.6 = (bf16[20,5,16,256]{3,2,1,0:T(8,128)(2,1)S(1)}, bf16[20,5,16,256]{3,2,1,0:T(8,128)(2,1)}, u32[]{:S(2)}, u32[]{:S(2)}) collective-permute-start(bf16[20,5,16,256]{3,2,1,0:T(8,128)(2,1)S(1)} %get-tuple-element.42), channel_id=1, source_target_pairs={{1,0},{2,1},{3,2},{4,3},{5,4},{6,5},{7,6},{9,8},{10,9},{11,10},{12... | collective-permute-start | bytes 2457608 | tf_op jit(solution)/shard_map/ppermute | solution.py:479
  35.9 41.9 %collective-permute-start.7 = (bf16[20,5,16,256]{3,2,1,0:T(8,128)(2,1)S(1)}, bf16[20,5,16,256]{3,2,1,0:T(8,128)(2,1)}, u32[]{:S(2)}, u32[]{:S(2)}) collective-permute-start(bf16[20,5,16,256]{3,2,1,0:T(8,128)(2,1)S(1)} %get-tuple-element.43), channel_id=1, source_target_pairs={{0,8},{8,16},{16,24},{1,9},{9,17},{17,25},{2,10},{10,18},{18,26},{... | collective-permute-start | bytes 2457608 | tf_op jit(solution)/shard_map/ppermute | solution.py:479
  38.8 39.0 %collective-permute-start.8 = (bf16[20,5,16,256]{3,2,1,0:T(8,128)(2,1)S(1)}, bf16[20,5,16,256]{3,2,1,0:T(8,128)(2,1)}, u32[]{:S(2)}, u32[]{:S(2)}) collective-permute-start(bf16[20,5,16,256]{3,2,1,0:T(8,128)(2,1)S(1)} %get-tuple-element.44), channel_id=1, source_target_pairs={{8,0},{16,8},{24,16},{9,1},{17,9},{25,17},{10,2},{18,10},{26,18},{... | collective-permute-start | bytes 2457608 | tf_op jit(solution)/shard_map/ppermute | solution.py:479
  41.3 36.5 %copy-start.1 = (s32[16,16,256]{2,1,0:T(8,128)S(1)}, s32[16,16,256]{2,1,0:T(8,128)}, u32[]{:S(2)}) copy-start(s32[16,16,256]{2,1,0:T(8,128)} %refs_3_.5) | copy-start | bytes 786436
  80.9 11.7 %collective-permute-start.10 = (f32[5,16,256]{2,1,0:T(8,128)S(1)}, f32[5,16,256]{2,1,0:T(8,128)S(1)}, u32[]{:S(2)}, u32[]{:S(2)}) collective-permute-start(f32[5,16,256]{2,1,0:T(8,128)S(1)} %get-tuple-element.47), channel_id=1, source_target_pairs={{1,0},{2,1},{3,2},{4,3},{5,4},{6,5},{7,6},{9,8},{10,9},{11,10},{12... | collective-permute-start | bytes 245768 | tf_op jit(solution)/shard_map/ppermute | solution.py:479
  82.8 9.8 %collective-permute-start.11 = (f32[5,16,256]{2,1,0:T(8,128)S(1)}, f32[5,16,256]{2,1,0:T(8,128)S(1)}, u32[]{:S(2)}, u32[]{:S(2)}) collective-permute-start(f32[5,16,256]{2,1,0:T(8,128)S(1)} %get-tuple-element.48), channel_id=1, source_target_pairs={{0,8},{8,16},{16,24},{1,9},{9,17},{17,25},{2,10},{10,18},{18,26},{... | collective-permute-start | bytes 245768 | tf_op jit(solution)/shard_map/ppermute | solution.py:479
  86.1 6.6 %collective-permute-start.12 = (f32[5,16,256]{2,1,0:T(8,128)S(1)}, f32[5,16,256]{2,1,0:T(8,128)S(1)}, u32[]{:S(2)}, u32[]{:S(2)}) collective-permute-start(f32[5,16,256]{2,1,0:T(8,128)S(1)} %get-tuple-element.49), channel_id=1, source_target_pairs={{8,0},{16,8},{24,16},{9,1},{17,9},{25,17},{10,2},{18,10},{26,18},{... | collective-permute-start | bytes 245768 | tf_op jit(solution)/shard_map/ppermute | solution.py:479
  88.0 6.0 %collective-permute-start.9 = (f32[5,16,256]{2,1,0:T(8,128)S(1)}, f32[5,16,256]{2,1,0:T(8,128)S(1)}, u32[]{:S(2)}, u32[]{:S(2)}) collective-permute-start(f32[5,16,256]{2,1,0:T(8,128)S(1)} %get-tuple-element.46), channel_id=1, source_target_pairs={{0,1},{1,2},{2,3},{3,4},{4,5},{5,6},{6,7},{8,9},{9,10},{10,11},{11... | collective-permute-start | bytes 245768 | tf_op jit(solution)/shard_map/ppermute | solution.py:479
  97.2 13.6 %collective-permute-start.13 = (f32[5,16,256]{2,1,0:T(8,128)S(1)}, f32[5,16,256]{2,1,0:T(8,128)S(1)}, u32[]{:S(2)}, u32[]{:S(2)}) collective-permute-start(f32[5,16,256]{2,1,0:T(8,128)S(1)} %get-tuple-element.55), channel_id=1, source_target_pairs={{0,1},{1,2},{2,3},{3,4},{4,5},{5,6},{6,7},{8,9},{9,10},{10,11},{11... | collective-permute-start | bytes 245768 | tf_op jit(solution)/shard_map/ppermute | solution.py:479
  101.8 8.9 %collective-permute-start.14 = (f32[5,16,256]{2,1,0:T(8,128)S(1)}, f32[5,16,256]{2,1,0:T(8,128)S(1)}, u32[]{:S(2)}, u32[]{:S(2)}) collective-permute-start(f32[5,16,256]{2,1,0:T(8,128)S(1)} %get-tuple-element.56), channel_id=1, source_target_pairs={{1,0},{2,1},{3,2},{4,3},{5,4},{6,5},{7,6},{9,8},{10,9},{11,10},{12... | collective-permute-start | bytes 245768 | tf_op jit(solution)/shard_map/ppermute | solution.py:479
  103.7 7.0 %collective-permute-start.15 = (f32[5,16,256]{2,1,0:T(8,128)S(1)}, f32[5,16,256]{2,1,0:T(8,128)S(1)}, u32[]{:S(2)}, u32[]{:S(2)}) collective-permute-start(f32[5,16,256]{2,1,0:T(8,128)S(1)} %get-tuple-element.57), channel_id=1, source_target_pairs={{0,8},{8,16},{16,24},{1,9},{9,17},{17,25},{2,10},{10,18},{18,26},{... | collective-permute-start | bytes 245768 | tf_op jit(solution)/shard_map/ppermute | solution.py:479
  108.8 5.8 %collective-permute-start.16 = (f32[5,16,256]{2,1,0:T(8,128)S(1)}, f32[5,16,256]{2,1,0:T(8,128)S(1)}, u32[]{:S(2)}, u32[]{:S(2)}) collective-permute-start(f32[5,16,256]{2,1,0:T(8,128)S(1)} %get-tuple-element.58), channel_id=1, source_target_pairs={{8,0},{16,8},{24,16},{9,1},{17,9},{25,17},{10,2},{18,10},{26,18},{... | collective-permute-start | bytes 245768 | tf_op jit(solution)/shard_map/ppermute | solution.py:479

commit v8 on v7

--- a/solution.py
+++ b/solution.py
@@ -246,33 +246,31 @@
         acc[...] = jnp.zeros_like(acc)
 
         def body(step, carry):
-            for k in range(GROUP):
-                products(after, step * GROUP + k, dest)
             for j in range(nv):
+                if j < GROUP:
+                    products(after, step * GROUP + j, dest)
                 at = slice(j * ny, (j + 1) * ny)
-                sums = [acc[n, at] for n in range(6)]
+                sums = [acc[n, at] for n in range(5)]
                 for k in range(GROUP):
                     m = step * GROUP + k
-                    w0, w1, w2 = (src[m, n * rows + j * ny : n * rows + (j + 1) * ny] for n in range(3))
+                    w0, down, up, w2 = (src[m, n * rows + j * ny : n * rows + (j + 1) * ny] for n in range(4))
                     u = u_src[m, at]
                     following = u_buf[after, m, j].astype(F32) * amp[m]
                     dx = following - u_dest[m, at]
                     u_dest[m, at] = following
-                    down1 = pltpu.roll(w1, 1, 0) - w1
-                    down2 = pltpu.roll(w2, 1, 1) - w2
-                    up1 = pltpu.roll(down1, ny - 1, 0)
-                    up2 = pltpu.roll(down2, nz - 1, 1)
-                    terms = [dx * w0, u * w0, u * down1, u * up1, u * down2, u * up2]
+                    terms = [dx * w0 + diff_lanes(u) * w2, u * w0, u * down, u * up, u * w2]
                     sums = [v + t for v, t in zip(sums, terms)]
-                for n in range(6):
+                for n in range(5):
                     acc[n, at] = sums[n]
+            for k in range(nv, GROUP):
+                products(after, step * GROUP + k, dest)
             return carry
 
         lax.fori_loop(0, nm // GROUP, body, 0)
         last = jnp.where(p == nx - 1, 1.0, 0.0)
         c0[p + 1] = acc[1]
         row = row_of((rows, nz), ny)
-        h = acc[0] - last * acc[1] + pltpu.roll(acc[4], nz - 1, 1) + pltpu.roll(acc[5], 1, 1)
+        h = acc[0] - diff_lanes(acc[4]) - last * acc[1]
         h = h + jnp.where(row == ny - 1, 0.0, pltpu.roll(acc[2], rows - 1, 0))
         out[p] = h + jnp.where(row == 0, 0.0, pltpu.roll(acc[3], 1, 0))
 
@@ -313,11 +311,11 @@
         scratch_shapes=[
             buf,
             buf,
-            pltpu.VMEM((nm, 3 * rows, nz), F32),
-            pltpu.VMEM((nm, 3 * rows, nz), F32),
+            pltpu.VMEM((nm, 4 * rows, nz), F32),
+            pltpu.VMEM((nm, 4 * rows, nz), F32),
             pltpu.VMEM((nm, rows, nz), F32),
             pltpu.VMEM((nm, rows, nz), F32),
-            pltpu.VMEM((6, rows, nz), F32),
+            pltpu.VMEM((5, rows, nz), F32),
             pltpu.VMEM((nx + 2, rows, nz), F32),
             pltpu.SemaphoreType.DMA((nx,)),
             pltpu.SemaphoreType.DMA((nx,)),
@@ -510,6 +508,11 @@
     return (wide * jnp.asarray(np.tile(cells, (wide.shape[-2] // n, wide.shape[-1] // n)))).astype(BF16)
 
 
+def main_rows(wide, n):
+    eye, below, above = (np.eye(n, k=k, dtype=np.float32) for k in (0, -1, 1))
+    return jnp.concatenate([within(wide[d], n, c) for d, c in ((0, eye), (1, below - eye), (1, eye - above), (2, eye))], axis=0)
+
+
 def step_rows(lw):
     half = lw.shape[-1] // 2
     return jnp.concatenate([lw[..., :half], lw[..., :half], lw[..., half:]], axis=-1)
@@ -526,7 +529,7 @@
     lw_x = lw_y if nx == ny else within(kron_rows(mix, nx), nx, np.eye(nx, dtype=np.float32))
     w_faces = [*mix_chord(lw_y[0], adjoint), *mix_normal(lw_x[1], adjoint)]
     halo = exchange(faces(pick, amp, base, own, w_faces))
-    local = main(pick, amp, lw_y.reshape(3 * nv * ny, -1), direct, adjoint)
+    local = main(pick, amp, main_rows(wide, ny), direct, adjoint)
     field, *sides = boundary(1.0 / nm, pick, amp, local, cell, w_faces, halo)
     sides, base_halo = sides[:4], sides[4:]
     lw_step = step_rows(lw_y.reshape(3 * nv * ny, -1))

time: 121 us -> 114 us (0.942)
  Pallas kernels: 63.6 us -> 57.6 us
  starting transfers between devices: 44.8 us -> 41.8 us
  waiting for transfers between devices: 8.94 us -> 11 us
    pallas_call x1, Pallas kernels: 36.5 us -> 30.2 us  [main(): pl.pallas_call(main_kernel, in_specs=[in_smem(), in_smem(), in_vmem(), in...]
    ppermute x12, starting transfers between devices: 35.7 us -> 32.7 us  [exchange_axis(): return [lax.ppermute(hi, axis, up), lax.ppermute(lo, axis, down)]]
    ppermute x12, waiting for transfers between devices: 5.18 us -> 7.27 us  [exchange_axis(): return [lax.ppermute(hi, axis, up), lax.ppermute(lo, axis, down)]]
  transfers between devices with their start and end apart: 17 -> 17, of which waited for: 5 -> 5; matrix products, arithmetic and copies ran while one was open for 1% -> 1% of each run, Pallas kernels for 38% -> 35%
where the time goes in v8:
time: 114 us; the launch traced here: 112 us
  Pallas kernels  57.6 us (51%)
  starting transfers between devices  41.8 us (37%)
  waiting for transfers between devices  11 us (10%)
    ppermute x12, starting transfers between devices, exchange_axis(): return [lax.ppermute(hi, axis, up), lax.ppermute(lo, axis, down)]  32.7 us
    pallas_call x1, Pallas kernels, main(): pl.pallas_call(main_kernel, in_specs=[in_smem(), in_smem(), in_vmem(), in...  30.2 us
    ppermute x5, starting transfers between devices, sum_over(): lax.ppermute(values, axis, [(i, i ^ bit) for i in range(count)])  9.07 us
    pallas_call x2, Pallas kernels, apply_step(): pl.pallas_call(lambda *refs: step_kernel(last, *refs), in_specs=[in_vmem(...  7.27 us
    ppermute x12, waiting for transfers between devices, exchange_axis(): return [lax.ppermute(hi, axis, up), lax.ppermute(lo, axis, down)]  7.27 us
    pallas_call x1, Pallas kernels, mix_normal(): pl.pallas_call(mix_normal_kernel, grid=(nm // GROUP,), in_specs=[pl.Block...  6.65 us
    pallas_call x1, Pallas kernels, pack(): pl.pallas_call(direct_kernel, grid=(nm // GROUP,), in_specs=[pl.BlockSpec...  6.32 us
    ppermute x5, waiting for transfers between devices, sum_over(): lax.ppermute(values, axis, [(i, i ^ bit) for i in range(count)])  3.76 us
  transfers between devices with their start and end apart: 17, of which 5 were waited for; matrix products, arithmetic and copies ran while one was open for 1% of the time, Pallas kernels for 35%

profile of v8, /device:TPU:5, one launch (start us, length us, event | category | flops | bytes accessed | tf_op | source)
XLA Modules:
  0.0 111.9 jit_solution(11144186645441256804)
XLA Ops:
  0.0 0.0 copy-start.7
  0.0 0.0 copy-start.9
  0.0 6.3 %pack_direct.1 = (bf16[20,5,16,256]{3,2,1,0:T(8,128)(2,1)S(1)}, bf16[20,5,16,256]{3,2,1,0:T(8,128)(2,1)S(1)}, bf16[20,5,16,256]{3,2,1,0:T(8,128)(2,1)S(1)}, bf16...) custom-call(bf16[16,5,16,16,256]{4,3,2,1,0:T(8,128)(2,1)} %u_hbm.1), custom_call_target="tpu_custom_call" | custom-call | flops 15728640 | bytes 10485760 | tf_op jit(solution)/shard_map/pack_direct/pallas_call | solution.py:73
  6.3 0.1 reduce_sum.9
  6.5 0.1 collective-permute-start
  6.5 0.0 copy-done.9
  6.6 0.0 copy-done.8
  6.6 0.2 fusion.6
  6.8 2.1 %collective-permute-done = f32[16]{0:T(128)S(1)} collective-permute-done((f32[16]{0:T(128)S(1)}, f32[16]{0:T(128)S(1)}, u32[]{:S(2)}, u32[]{:S(2)}) %collective-permute-start) | collective-permute-done | bytes 96 | tf_op jit(solution)/shard_map/ppermute | solution.py:491
  8.9 1.3 %collective-permute-start.1 = (f32[16]{0:T(128)S(1)}, f32[16]{0:T(128)S(1)}, u32[]{:S(2)}, u32[]{:S(2)}) collective-permute-start(f32[16]{0:T(128)S(1)} %add.18), channel_id=1, source_target_pairs={{0,2},{1,3},{2,0},{3,1},{4,6},{5,7},{6,4},{7,5},{8,10},{9,11},{10,... | collective-permute-start | bytes 200 | tf_op jit(solution)/shard_map/ppermute | solution.py:491
  10.2 0.0 copy-done.7
  10.2 0.0 copy-done.10
  10.2 0.4 multiply_convert_fusion
  10.6 0.7 collective-permute-done.1
  11.3 2.3 %collective-permute-start.2 = (f32[16]{0:T(128)S(1)}, f32[16]{0:T(128)S(1)}, u32[]{:S(2)}, u32[]{:S(2)}) collective-permute-start(f32[16]{0:T(128)S(1)} %add.19), channel_id=1, source_target_pairs={{0,4},{1,5},{2,6},{3,7},{4,0},{5,1},{6,2},{7,3},{8,12},{9,13},{10,... | collective-permute-start | bytes 200 | tf_op jit(solution)/shard_map/ppermute | solution.py:491
  13.6 1.0 collective-permute-done.2
  14.6 4.1 %collective-permute-start.3 = (f32[16]{0:T(128)S(1)}, f32[16]{0:T(128)S(1)}, u32[]{:S(2)}, u32[]{:S(2)}) collective-permute-start(f32[16]{0:T(128)S(1)} %add.20), channel_id=1, source_target_pairs={{0,8},{8,0},{16,24},{24,16},{1,9},{9,1},{17,25},{25,17},{2,10},{10... | collective-permute-start | bytes 200 | tf_op jit(solution)/shard_map/ppermute | solution.py:491
  18.7 2.3 %mix_chord.1 = (f32[16,80,256]{2,1,0:T(8,128)S(1)}, f32[16,80,256]{2,1,0:T(8,128)S(1)}) custom-call(bf16[80,160]{1,0:T(8,128)(2,1)S(1)} %get-tuple-element.63.lw, bf16[16,5,16,16,256]{4,3,2,1,0:T(8,128)(2,1)} %src.3, bf16[16,5,16,16,256]{4,3,2,1,0:T(8,128)(2,1)} %src.3), custom_call_target="tpu_custom_call" | custom-call | flops 100000000 | bytes 6000000 | tf_op jit(solution)/shard_map/mix_chord/pallas_call | solution.py:105
  21.0 0.0 collective-permute-done.3
  21.0 1.3 %collective-permute-start.4 = (f32[16]{0:T(128)S(1)}, f32[16]{0:T(128)S(1)}, u32[]{:S(2)}, u32[]{:S(2)}) collective-permute-start(f32[16]{0:T(128)S(1)} %add.21), channel_id=1, source_target_pairs={{0,16},{8,24},{16,0},{24,8},{1,17},{9,25},{17,1},{25,9},{2,18},{10... | collective-permute-start | bytes 200 | tf_op jit(solution)/shard_map/ppermute | solution.py:491
  22.3 6.6 %mix_normal.1 = (f32[16,80,256]{2,1,0:T(8,128)S(1)}, f32[16,80,256]{2,1,0:T(8,128)S(1)}) custom-call(bf16[80,160]{1,0:T(8,128)(2,1)S(1)} %get-tuple-element.64.lw, bf16[16,5,16,16,256]{4,3,2,1,0:T(8,128)(2,1)} %src.3), custom_call_target="tpu_custom_call" | custom-call | flops 15728640 | bytes 15728640 | tf_op jit(solution)/shard_map/mix_normal/pallas_call | solution.py:138
  29.0 0.0 collective-permute-done.4
  29.0 0.0 copy-done
  29.0 0.0 copy-done.2
  29.0 0.0 copy-done.3
  29.0 0.0 copy-start.4
  29.0 0.0 copy-start.5
  29.0 0.0 copy-start.6
  29.0 1.5 %faces.1 = (bf16[20,5,16,256]{3,2,1,0:T(8,128)(2,1)S(1)}, bf16[20,5,16,256]{3,2,1,0:T(8,128)(2,1)S(1)}, bf16[20,5,16,256]{3,2,1,0:T(8,128)(2,1)S(1)}, bf16[20,5,16,256]{3,2,1,0:T(8,128)(2,1)S(1)}) custom-call(s32[16]{0:T(128)S(1)} %copy-done.3, ...), custom_call_target="tpu_custom_call", output_to_operand_aliasing={{0}: (3, {}), {1}: (4, {}), {2}: (5, {}), {3}: (6, {})} | custom-call | tf_op jit(solution)/shard_map/faces/pallas_call | solution.py:190
  30.6 3.2 %collective-permute-start.5 = (bf16[20,5,16,256]{3,2,1,0:T(8,128)(2,1)S(1)}, bf16[20,5,16,256]{3,2,1,0:T(8,128)(2,1)}, u32[]{:S(2)}, u32[]{:S(2)}) collective-permute-start(bf16[20,5,16,256]{3,2,1,0:T(8,128)(2,1)S(1)} %get-tuple-element.41), channel_id=1, source_target_pairs={{0,1},{1,2},{2,3},{3,4},{4,5},{5,6},{6,7},{8,9},{9,10},{10,11},{11... | collective-permute-start | bytes 2457608 | tf_op jit(solution)/shard_map/ppermute | solution.py:477
  33.7 3.0 %collective-permute-start.6 = (bf16[20,5,16,256]{3,2,1,0:T(8,128)(2,1)S(1)}, bf16[20,5,16,256]{3,2,1,0:T(8,128)(2,1)}, u32[]{:S(2)}, u32[]{:S(2)}) collective-permute-start(bf16[20,5,16,256]{3,2,1,0:T(8,128)(2,1)S(1)} %get-tuple-element.42), channel_id=1, source_target_pairs={{1,0},{2,1},{3,2},{4,3},{5,4},{6,5},{7,6},{9,8},{10,9},{11,10},{12... | collective-permute-start | bytes 2457608 | tf_op jit(solution)/shard_map/ppermute | solution.py:477
  36.7 2.9 %collective-permute-start.7 = (bf16[20,5,16,256]{3,2,1,0:T(8,128)(2,1)S(1)}, bf16[20,5,16,256]{3,2,1,0:T(8,128)(2,1)}, u32[]{:S(2)}, u32[]{:S(2)}) collective-permute-start(bf16[20,5,16,256]{3,2,1,0:T(8,128)(2,1)S(1)} %get-tuple-element.43), channel_id=1, source_target_pairs={{0,8},{8,16},{16,24},{1,9},{9,17},{17,25},{2,10},{10,18},{18,26},{... | collective-permute-start | bytes 2457608 | tf_op jit(solution)/shard_map/ppermute | solution.py:477
  39.6 2.3 %collective-permute-start.8 = (bf16[20,5,16,256]{3,2,1,0:T(8,128)(2,1)S(1)}, bf16[20,5,16,256]{3,2,1,0:T(8,128)(2,1)}, u32[]{:S(2)}, u32[]{:S(2)}) collective-permute-start(bf16[20,5,16,256]{3,2,1,0:T(8,128)(2,1)S(1)} %get-tuple-element.44), channel_id=1, source_target_pairs={{8,0},{16,8},{24,16},{9,1},{17,9},{25,17},{10,2},{18,10},{26,18},{... | collective-permute-start | bytes 2457608 | tf_op jit(solution)/shard_map/ppermute | solution.py:477
  42.0 0.1 pad_maximum_fusion.1.refs_0_
  42.1 0.0 copy-done.4
  42.1 0.0 copy-done.5
  42.1 0.0 copy-done.6
  42.2 0.0 copy-start.1
  42.2 30.2 %main.1.refs_2_ = f32[16,80,256]{2,1,0:T(8,128)S(1)} custom-call(s32[16]{0:T(128)S(1)} %copy-done.3, f32[16]{0:T(128)S(1)} %add_rsqrt_fusion.amp.refs_1_, bf16[320,160]{1,0:T(8,128)(2,1)S(1)} %pad_maximum_fusion.lw, bf16[16,5,16,16,256]{4,3,2,1,0:T(8,128)(2,1)} %u_hbm.1, bf16[16,5,16,16,256]{4,3,2,1,0:T(8,128)(2,1)} %src.3), custom_call_target="tpu_custom_call" | custom-call | flops 1000000 | bytes 100000 | tf_op jit(solution)/shard_map/main/pallas_call | solution.py:306
  72.4 0.0 collective-permute-done.5.refs_8_
  72.4 0.0 collective-permute-done.6.refs_9_
  72.5 0.0 collective-permute-done.7.refs_10_
  72.5 0.0 collective-permute-done.8.refs_11_
  72.5 0.0 copy-done.1
  72.5 3.4 %boundary.1 = (f32[16,80,256]{2,1,0:T(8,128)S(1)}, f32[5,16,256]{2,1,0:T(8,128)S(1)}, f32[5,16,256]{2,1,0:T(8,128)S(1)}, f32[5,16,256]{2,1,0:T(8,128)S(1)}, f32[...) custom-call(s32[16]{0:T(128)S(1)} %copy-done.3, ...), custom_call_target="tpu_custom_call" | custom-call | tf_op jit(solution)/shard_map/boundary/pallas_call | solution.py:383
  75.9 3.2 %collective-permute-start.9 = (f32[5,16,256]{2,1,0:T(8,128)S(1)}, f32[5,16,256]{2,1,0:T(8,128)S(1)}, u32[]{:S(2)}, u32[]{:S(2)}) collective-permute-start(f32[5,16,256]{2,1,0:T(8,128)S(1)} %get-tuple-element.46), channel_id=1, source_target_pairs={{0,1},{1,2},{2,3},{3,4},{4,5},{5,6},{6,7},{8,9},{9,10},{10,11},{11... | collective-permute-start | bytes 245768 | tf_op jit(solution)/shard_map/ppermute | solution.py:477
  79.0 2.1 %collective-permute-start.10 = (f32[5,16,256]{2,1,0:T(8,128)S(1)}, f32[5,16,256]{2,1,0:T(8,128)S(1)}, u32[]{:S(2)}, u32[]{:S(2)}) collective-permute-start(f32[5,16,256]{2,1,0:T(8,128)S(1)} %get-tuple-element.47), channel_id=1, source_target_pairs={{1,0},{2,1},{3,2},{4,3},{5,4},{6,5},{7,6},{9,8},{10,9},{11,10},{12... | collective-permute-start | bytes 245768 | tf_op jit(solution)/shard_map/ppermute | solution.py:477
  81.2 3.8 %collective-permute-start.11 = (f32[5,16,256]{2,1,0:T(8,128)S(1)}, f32[5,16,256]{2,1,0:T(8,128)S(1)}, u32[]{:S(2)}, u32[]{:S(2)}) collective-permute-start(f32[5,16,256]{2,1,0:T(8,128)S(1)} %get-tuple-element.48), channel_id=1, source_target_pairs={{0,8},{8,16},{16,24},{1,9},{9,17},{17,25},{2,10},{10,18},{18,26},{... | collective-permute-start | bytes 245768 | tf_op jit(solution)/shard_map/ppermute | solution.py:477
  85.0 1.9 %collective-permute-start.12 = (f32[5,16,256]{2,1,0:T(8,128)S(1)}, f32[5,16,256]{2,1,0:T(8,128)S(1)}, u32[]{:S(2)}, u32[]{:S(2)}) collective-permute-start(f32[5,16,256]{2,1,0:T(8,128)S(1)} %get-tuple-element.49), channel_id=1, source_target_pairs={{8,0},{16,8},{24,16},{9,1},{17,9},{25,17},{10,2},{18,10},{26,18},{... | collective-permute-start | bytes 245768 | tf_op jit(solution)/shard_map/ppermute | solution.py:477
  86.9 0.1 pad_maximum_fusion.2.refs_1_
  87.0 0.0 collective-permute-done.9.refs_5_
  87.0 0.0 collective-permute-done.10.refs_6_
  87.0 0.0 collective-permute-done.11.refs_7_
  87.0 3.7 %collective-permute-done.12.refs_8_ = f32[5,16,256]{2,1,0:T(8,128)S(1)} collective-permute-done((f32[5,16,256]{2,1,0:T(8,128)S(1)}, f32[5,16,256]{2,1,0:T(8,128)S(1)}, u32[]{:S(2)}, u32[]{:S(2)}) %collective-permute-start.12) | collective-permute-done | bytes 81952 | tf_op jit(solution)/shard_map/ppermute | solution.py:477
  90.7 3.2 %step_one.1 = (f32[16,80,256]{2,1,0:T(8,128)S(1)}, f32[5,16,256]{2,1,0:T(8,128)S(1)}, f32[5,16,256]{2,1,0:T(8,128)S(1)}, f32[5,16,256]{2,1,0:T(8,128)S(1)}, f32[5,16,256]{2,1,0:T(8,128)S(1)}) custom-call(bf16[240,240]{1,0:T(8,128)(2,1)S(1)} %pad_maximum_fusion.1.refs_0_, bf16[80,240]{1,0:T(8,128)(2,1)S(1)} %pad_maximum_fusion.2.refs_1_, ...), custom_call_target="tpu_custom_call" | custom-call | tf_op jit(solution)/shard_map/step_one/pallas_call | solution.py:462
  93.9 4.1 %collective-permute-start.13 = (f32[5,16,256]{2,1,0:T(8,128)S(1)}, f32[5,16,256]{2,1,0:T(8,128)S(1)}, u32[]{:S(2)}, u32[]{:S(2)}) collective-permute-start(f32[5,16,256]{2,1,0:T(8,128)S(1)} %get-tuple-element.55), channel_id=1, source_target_pairs={{0,1},{1,2},{2,3},{3,4},{4,5},{5,6},{6,7},{8,9},{9,10},{10,11},{11... | collective-permute-start | bytes 245768 | tf_op jit(solution)/shard_map/ppermute | solution.py:477
  98.0 1.9 %collective-permute-start.14 = (f32[5,16,256]{2,1,0:T(8,128)S(1)}, f32[5,16,256]{2,1,0:T(8,128)S(1)}, u32[]{:S(2)}, u32[]{:S(2)}) collective-permute-start(f32[5,16,256]{2,1,0:T(8,128)S(1)} %get-tuple-element.56), channel_id=1, source_target_pairs={{1,0},{2,1},{3,2},{4,3},{5,4},{6,5},{7,6},{9,8},{10,9},{11,10},{12... | collective-permute-start | bytes 245768 | tf_op jit(solution)/shard_map/ppermute | solution.py:477
  99.9 2.1 %collective-permute-start.15 = (f32[5,16,256]{2,1,0:T(8,128)S(1)}, f32[5,16,256]{2,1,0:T(8,128)S(1)}, u32[]{:S(2)}, u32[]{:S(2)}) collective-permute-start(f32[5,16,256]{2,1,0:T(8,128)S(1)} %get-tuple-element.57), channel_id=1, source_target_pairs={{0,8},{8,16},{16,24},{1,9},{9,17},{17,25},{2,10},{10,18},{18,26},{... | collective-permute-start | bytes 245768 | tf_op jit(solution)/shard_map/ppermute | solution.py:477
  102.1 2.2 %collective-permute-start.16 = (f32[5,16,256]{2,1,0:T(8,128)S(1)}, f32[5,16,256]{2,1,0:T(8,128)S(1)}, u32[]{:S(2)}, u32[]{:S(2)}) collective-permute-start(f32[5,16,256]{2,1,0:T(8,128)S(1)} %get-tuple-element.58), channel_id=1, source_target_pairs={{8,0},{16,8},{24,16},{9,1},{17,9},{25,17},{10,2},{18,10},{26,18},{... | collective-permute-start | bytes 245768 | tf_op jit(solution)/shard_map/ppermute | solution.py:477
  104.3 0.0 collective-permute-done.13.refs_5_
  104.3 0.0 collective-permute-done.14.refs_6_
  104.3 0.0 collective-permute-done.15.refs_7_
  104.3 3.5 %collective-permute-done.16.refs_8_ = f32[5,16,256]{2,1,0:T(8,128)S(1)} collective-permute-done((f32[5,16,256]{2,1,0:T(8,128)S(1)}, f32[5,16,256]{2,1,0:T(8,128)S(1)}, u32[]{:S(2)}, u32[]{:S(2)}) %collective-permute-start.16) | collective-permute-done | bytes 81952 | tf_op jit(solution)/shard_map/ppermute | solution.py:477
  107.8 4.1 %step_two.1 = f32[5,16,16,256]{3,2,1,0:T(8,128)} custom-call(bf16[240,240]{1,0:T(8,128)(2,1)S(1)} %pad_maximum_fusion.1.refs_0_, bf16[80,240]{1,0:T(8,128)(2,1)S(1)} %pad_maximum_fusion.2.refs_1_, f32[5,16,16,256]{3,2,1,0:T(8,128)S(1)} %copy-done, s32[16,16,256]{2,1,0:T(8,128)S(1)} %copy-done.1, f32[16,80,256]{2,1,0:T(8,128)S(1)} %get-tuple-element.54.refs_4_, ...), custom_call_target="tpu_custom_call" | custom-call | tf_op jit(solution)/shard_map/step_two/pallas_call | solution.py:462
  (17 shorter events, 0.1 us)
Async XLA Ops:
  0.0 6.6 %copy-start.8 = (f32[10,160,1]{1,0,2:T(8,128)S(1)}, f32[10,160,1]{1,0,2:T(8,128)}, u32[]{:S(2)}) copy-start(f32[10,160,1]{1,0,2:T(8,128)} %constant.26) | copy-start | bytes 19204
  0.0 10.2 %copy-start.7 = (f32[80,160]{1,0:T(8,128)S(1)}, f32[80,160]{1,0:T(8,128)}, u32[]{:S(2)}) copy-start(f32[80,160]{1,0:T(8,128)} %constant.19.clone) | copy-start | bytes 153604
  0.0 10.2 %copy-start.10 = (f32[80,5,1]{0,1,2:T(8,128)S(1)}, f32[80,5,1]{0,1,2:T(8,128)}, u32[]{:S(2)}) copy-start(f32[80,5,1]{0,1,2:T(8,128)} %constant.27) | copy-start | bytes 4804
  0.0 6.5 %copy-start.9 = (f32[3,5,5]{2,0,1:T(4,128)S(1)}, f32[3,5,5]{2,0,1:T(4,128)}, u32[]{:S(2)}) copy-start(f32[3,5,5]{2,0,1:T(4,128)} %param.18) | copy-start | bytes 904
  6.5 2.4 %collective-permute-start = (f32[16]{0:T(128)S(1)}, f32[16]{0:T(128)S(1)}, u32[]{:S(2)}, u32[]{:S(2)}) collective-permute-start(f32[16]{0:T(128)S(1)} %reduce_sum.9), channel_id=1, source_target_pairs={{0,1},{1,0},{2,3},{3,2},{4,5},{5,4},{6,7},{7,6},{8,9},{9,8},{10,11... | collective-permute-start | bytes 200 | tf_op jit(solution)/shard_map/ppermute | solution.py:491
  8.9 2.4 %collective-permute-start.1 = (f32[16]{0:T(128)S(1)}, f32[16]{0:T(128)S(1)}, u32[]{:S(2)}, u32[]{:S(2)}) collective-permute-start(f32[16]{0:T(128)S(1)} %add.18), channel_id=1, source_target_pairs={{0,2},{1,3},{2,0},{3,1},{4,6},{5,7},{6,4},{7,5},{8,10},{9,11},{10,... | collective-permute-start | bytes 200 | tf_op jit(solution)/shard_map/ppermute | solution.py:491
  11.3 3.3 %collective-permute-start.2 = (f32[16]{0:T(128)S(1)}, f32[16]{0:T(128)S(1)}, u32[]{:S(2)}, u32[]{:S(2)}) collective-permute-start(f32[16]{0:T(128)S(1)} %add.19), channel_id=1, source_target_pairs={{0,4},{1,5},{2,6},{3,7},{4,0},{5,1},{6,2},{7,3},{8,12},{9,13},{10,... | collective-permute-start | bytes 200 | tf_op jit(solution)/shard_map/ppermute | solution.py:491
  14.6 6.4 %collective-permute-start.3 = (f32[16]{0:T(128)S(1)}, f32[16]{0:T(128)S(1)}, u32[]{:S(2)}, u32[]{:S(2)}) collective-permute-start(f32[16]{0:T(128)S(1)} %add.20), channel_id=1, source_target_pairs={{0,8},{8,0},{16,24},{24,16},{1,9},{9,1},{17,25},{25,17},{2,10},{10... | collective-permute-start | bytes 200 | tf_op jit(solution)/shard_map/ppermute | solution.py:491
  21.0 7.9 %collective-permute-start.4 = (f32[16]{0:T(128)S(1)}, f32[16]{0:T(128)S(1)}, u32[]{:S(2)}, u32[]{:S(2)}) collective-permute-start(f32[16]{0:T(128)S(1)} %add.21), channel_id=1, source_target_pairs={{0,16},{8,24},{16,0},{24,8},{1,17},{9,25},{17,1},{25,9},{2,18},{10... | collective-permute-start | bytes 200 | tf_op jit(solution)/shard_map/ppermute | solution.py:491
  22.3 6.7 %copy-start = (f32[5,16,16,256]{3,2,1,0:T(8,128)S(1)}, f32[5,16,16,256]{3,2,1,0:T(8,128)}, u32[]{:S(2)}) copy-start(f32[5,16,16,256]{3,2,1,0:T(8,128)} %refs_2_.3) | copy-start | bytes 3932164
  22.3 6.7 %copy-start.2 = (bf16[20,5,16,256]{3,2,1,0:T(8,128)(2,1)S(1)}, bf16[20,5,16,256]{3,2,1,0:T(8,128)(2,1)}, u32[]{:S(2)}) copy-start(bf16[20,5,16,256]{3,2,1,0:T(8,128)(2,1)} %get-tuple-element.40.refs_3_) | copy-start | bytes 2457604
  22.3 6.7 %copy-start.3 = (s32[16]{0:T(128)S(1)}, s32[16]{0:T(128)}, u32[]{:S(2)}) copy-start(s32[16]{0:T(128)} %refs_0_.1) | copy-start | bytes 196
  29.0 13.1 %copy-start.4 = (f32[1,80,160]{2,1,0:T(8,128)S(1)}, f32[1,80,160]{2,1,0:T(8,128)}, u32[]{:S(2)}) copy-start(f32[1,80,160]{2,1,0:T(8,128)} %constant.24) | copy-start | bytes 153604
  29.0 13.1 %copy-start.5 = (f32[1,80,160]{2,1,0:T(8,128)S(1)}, f32[1,80,160]{2,1,0:T(8,128)}, u32[]{:S(2)}) copy-start(f32[1,80,160]{2,1,0:T(8,128)} %constant.23) | copy-start | bytes 153604
  29.0 13.1 %copy-start.6 = (f32[1,80,160]{2,1,0:T(8,128)S(1)}, f32[1,80,160]{2,1,0:T(8,128)}, u32[]{:S(2)}) copy-start(f32[1,80,160]{2,1,0:T(8,128)} %constant.22) | copy-start | bytes 153604
  30.6 41.9 %collective-permute-start.5 = (bf16[20,5,16,256]{3,2,1,0:T(8,128)(2,1)S(1)}, bf16[20,5,16,256]{3,2,1,0:T(8,128)(2,1)}, u32[]{:S(2)}, u32[]{:S(2)}) collective-permute-start(bf16[20,5,16,256]{3,2,1,0:T(8,128)(2,1)S(1)} %get-tuple-element.41), channel_id=1, source_target_pairs={{0,1},{1,2},{2,3},{3,4},{4,5},{5,6},{6,7},{8,9},{9,10},{10,11},{11... | collective-permute-start | bytes 2457608 | tf_op jit(solution)/shard_map/ppermute | solution.py:477
  33.7 38.7 %collective-permute-start.6 = (bf16[20,5,16,256]{3,2,1,0:T(8,128)(2,1)S(1)}, bf16[20,5,16,256]{3,2,1,0:T(8,128)(2,1)}, u32[]{:S(2)}, u32[]{:S(2)}) collective-permute-start(bf16[20,5,16,256]{3,2,1,0:T(8,128)(2,1)S(1)} %get-tuple-element.42), channel_id=1, source_target_pairs={{1,0},{2,1},{3,2},{4,3},{5,4},{6,5},{7,6},{9,8},{10,9},{11,10},{12... | collective-permute-start | bytes 2457608 | tf_op jit(solution)/shard_map/ppermute | solution.py:477
  36.7 35.7 %collective-permute-start.7 = (bf16[20,5,16,256]{3,2,1,0:T(8,128)(2,1)S(1)}, bf16[20,5,16,256]{3,2,1,0:T(8,128)(2,1)}, u32[]{:S(2)}, u32[]{:S(2)}) collective-permute-start(bf16[20,5,16,256]{3,2,1,0:T(8,128)(2,1)S(1)} %get-tuple-element.43), channel_id=1, source_target_pairs={{0,8},{8,16},{16,24},{1,9},{9,17},{17,25},{2,10},{10,18},{18,26},{... | collective-permute-start | bytes 2457608 | tf_op jit(solution)/shard_map/ppermute | solution.py:477
  39.6 32.8 %collective-permute-start.8 = (bf16[20,5,16,256]{3,2,1,0:T(8,128)(2,1)S(1)}, bf16[20,5,16,256]{3,2,1,0:T(8,128)(2,1)}, u32[]{:S(2)}, u32[]{:S(2)}) collective-permute-start(bf16[20,5,16,256]{3,2,1,0:T(8,128)(2,1)S(1)} %get-tuple-element.44), channel_id=1, source_target_pairs={{8,0},{16,8},{24,16},{9,1},{17,9},{25,17},{10,2},{18,10},{26,18},{... | collective-permute-start | bytes 2457608 | tf_op jit(solution)/shard_map/ppermute | solution.py:477
  42.2 30.3 %copy-start.1 = (s32[16,16,256]{2,1,0:T(8,128)S(1)}, s32[16,16,256]{2,1,0:T(8,128)}, u32[]{:S(2)}) copy-start(s32[16,16,256]{2,1,0:T(8,128)} %refs_3_.5) | copy-start | bytes 786436
  75.9 11.1 %collective-permute-start.9 = (f32[5,16,256]{2,1,0:T(8,128)S(1)}, f32[5,16,256]{2,1,0:T(8,128)S(1)}, u32[]{:S(2)}, u32[]{:S(2)}) collective-permute-start(f32[5,16,256]{2,1,0:T(8,128)S(1)} %get-tuple-element.46), channel_id=1, source_target_pairs={{0,1},{1,2},{2,3},{3,4},{4,5},{5,6},{6,7},{8,9},{9,10},{10,11},{11... | collective-permute-start | bytes 245768 | tf_op jit(solution)/shard_map/ppermute | solution.py:477
  79.0 8.0 %collective-permute-start.10 = (f32[5,16,256]{2,1,0:T(8,128)S(1)}, f32[5,16,256]{2,1,0:T(8,128)S(1)}, u32[]{:S(2)}, u32[]{:S(2)}) collective-permute-start(f32[5,16,256]{2,1,0:T(8,128)S(1)} %get-tuple-element.47), channel_id=1, source_target_pairs={{1,0},{2,1},{3,2},{4,3},{5,4},{6,5},{7,6},{9,8},{10,9},{11,10},{12... | collective-permute-start | bytes 245768 | tf_op jit(solution)/shard_map/ppermute | solution.py:477
  81.2 5.9 %collective-permute-start.11 = (f32[5,16,256]{2,1,0:T(8,128)S(1)}, f32[5,16,256]{2,1,0:T(8,128)S(1)}, u32[]{:S(2)}, u32[]{:S(2)}) collective-permute-start(f32[5,16,256]{2,1,0:T(8,128)S(1)} %get-tuple-element.48), channel_id=1, source_target_pairs={{0,8},{8,16},{16,24},{1,9},{9,17},{17,25},{2,10},{10,18},{18,26},{... | collective-permute-start | bytes 245768 | tf_op jit(solution)/shard_map/ppermute | solution.py:477
  85.0 5.8 %collective-permute-start.12 = (f32[5,16,256]{2,1,0:T(8,128)S(1)}, f32[5,16,256]{2,1,0:T(8,128)S(1)}, u32[]{:S(2)}, u32[]{:S(2)}) collective-permute-start(f32[5,16,256]{2,1,0:T(8,128)S(1)} %get-tuple-element.49), channel_id=1, source_target_pairs={{8,0},{16,8},{24,16},{9,1},{17,9},{25,17},{10,2},{18,10},{26,18},{... | collective-permute-start | bytes 245768 | tf_op jit(solution)/shard_map/ppermute | solution.py:477
  93.9 10.3 %collective-permute-start.13 = (f32[5,16,256]{2,1,0:T(8,128)S(1)}, f32[5,16,256]{2,1,0:T(8,128)S(1)}, u32[]{:S(2)}, u32[]{:S(2)}) collective-permute-start(f32[5,16,256]{2,1,0:T(8,128)S(1)} %get-tuple-element.55), channel_id=1, source_target_pairs={{0,1},{1,2},{2,3},{3,4},{4,5},{5,6},{6,7},{8,9},{9,10},{10,11},{11... | collective-permute-start | bytes 245768 | tf_op jit(solution)/shard_map/ppermute | solution.py:477
  98.0 6.3 %collective-permute-start.14 = (f32[5,16,256]{2,1,0:T(8,128)S(1)}, f32[5,16,256]{2,1,0:T(8,128)S(1)}, u32[]{:S(2)}, u32[]{:S(2)}) collective-permute-start(f32[5,16,256]{2,1,0:T(8,128)S(1)} %get-tuple-element.56), channel_id=1, source_target_pairs={{1,0},{2,1},{3,2},{4,3},{5,4},{6,5},{7,6},{9,8},{10,9},{11,10},{12... | collective-permute-start | bytes 245768 | tf_op jit(solution)/shard_map/ppermute | solution.py:477
  99.9 4.4 %collective-permute-start.15 = (f32[5,16,256]{2,1,0:T(8,128)S(1)}, f32[5,16,256]{2,1,0:T(8,128)S(1)}, u32[]{:S(2)}, u32[]{:S(2)}) collective-permute-start(f32[5,16,256]{2,1,0:T(8,128)S(1)} %get-tuple-element.57), channel_id=1, source_target_pairs={{0,8},{8,16},{16,24},{1,9},{9,17},{17,25},{2,10},{10,18},{18,26},{... | collective-permute-start | bytes 245768 | tf_op jit(solution)/shard_map/ppermute | solution.py:477
  102.1 5.8 %collective-permute-start.16 = (f32[5,16,256]{2,1,0:T(8,128)S(1)}, f32[5,16,256]{2,1,0:T(8,128)S(1)}, u32[]{:S(2)}, u32[]{:S(2)}) collective-permute-start(f32[5,16,256]{2,1,0:T(8,128)S(1)} %get-tuple-element.58), channel_id=1, source_target_pairs={{8,0},{16,8},{24,16},{9,1},{17,9},{25,17},{10,2},{18,10},{26,18},{... | collective-permute-start | bytes 245768 | tf_op jit(solution)/shard_map/ppermute | solution.py:477

commit v9 on v8

--- a/solution.py
+++ b/solution.py
@@ -12,6 +12,7 @@
 MIB = 1024 * 1024
 GROUP = 4
 TAIL = 4
+TURN = 8
 LARGE = 51
 
 
@@ -247,12 +248,12 @@
 
         def body(step, carry):
             for j in range(nv):
-                if j < GROUP:
-                    products(after, step * GROUP + j, dest)
+                for k in range(2 * j, min(2 * j + 2, TURN)):
+                    products(after, step * TURN + k, dest)
                 at = slice(j * ny, (j + 1) * ny)
                 sums = [acc[n, at] for n in range(5)]
-                for k in range(GROUP):
-                    m = step * GROUP + k
+                for k in range(TURN):
+                    m = step * TURN + k
                     w0, down, up, w2 = (src[m, n * rows + j * ny : n * rows + (j + 1) * ny] for n in range(4))
                     u = u_src[m, at]
                     following = u_buf[after, m, j].astype(F32) * amp[m]
@@ -262,11 +263,11 @@
                     sums = [v + t for v, t in zip(sums, terms)]
                 for n in range(5):
                     acc[n, at] = sums[n]
-            for k in range(nv, GROUP):
-                products(after, step * GROUP + k, dest)
+            for k in range(2 * nv, TURN):
+                products(after, step * TURN + k, dest)
             return carry
 
-        lax.fori_loop(0, nm // GROUP, body, 0)
+        lax.fori_loop(0, nm // TURN, body, 0)
         last = jnp.where(p == nx - 1, 1.0, 0.0)
         c0[p + 1] = acc[1]
         row = row_of((rows, nz), ny)
@@ -283,7 +284,7 @@
         u_even[m] = u_buf[0, m].reshape(rows, nz).astype(F32) * amp[m]
         return carry
 
-    lax.fori_loop(0, nm, first, 0, unroll=GROUP)
+    lax.fori_loop(0, nm, first, 0, unroll=4)
 
     def pair(i, carry):
         plane(2 * i, even, odd, u_even, u_odd)

time: 114 us -> 112 us (0.982)
  Pallas kernels: 57.6 us -> 52.8 us
  waiting for transfers between devices: 11 us -> 13 us
    pallas_call x1, Pallas kernels: 30.2 us -> 25.4 us  [main(): pl.pallas_call(main_kernel, in_specs=[in_smem(), in_smem(), in_vmem(), in...]
    ppermute x12, waiting for transfers between devices: 7.27 us -> 9.28 us  [exchange_axis(): return [lax.ppermute(hi, axis, up), lax.ppermute(lo, axis, down)]]
  transfers between devices with their start and end apart: 17 -> 17, of which waited for: 5 -> 6; matrix products, arithmetic and copies ran while one was open for 1% -> 1% of each run, Pallas kernels for 35% -> 31%
where the time goes in v9:
time: 112 us; the launch traced here: 110 us
  Pallas kernels  52.8 us (47%)
  starting transfers between devices  42.5 us (38%)
  waiting for transfers between devices  13 us (12%)
    ppermute x12, starting transfers between devices, exchange_axis(): return [lax.ppermute(hi, axis, up), lax.ppermute(lo, axis, down)]  33.5 us
    pallas_call x1, Pallas kernels, main(): pl.pallas_call(main_kernel, in_specs=[in_smem(), in_smem(), in_vmem(), in...  25.4 us
    ppermute x12, waiting for transfers between devices, exchange_axis(): return [lax.ppermute(hi, axis, up), lax.ppermute(lo, axis, down)]  9.28 us
    ppermute x5, starting transfers between devices, sum_over(): lax.ppermute(values, axis, [(i, i ^ bit) for i in range(count)])  9.07 us
    pallas_call x2, Pallas kernels, apply_step(): pl.pallas_call(lambda *refs: step_kernel(last, *refs), in_specs=[in_vmem(...  7.27 us
    pallas_call x1, Pallas kernels, mix_normal(): pl.pallas_call(mix_normal_kernel, grid=(nm // GROUP,), in_specs=[pl.Block...  6.65 us
    pallas_call x1, Pallas kernels, pack(): pl.pallas_call(direct_kernel, grid=(nm // GROUP,), in_specs=[pl.BlockSpec...  6.32 us
    ppermute x5, waiting for transfers between devices, sum_over(): lax.ppermute(values, axis, [(i, i ^ bit) for i in range(count)])  3.76 us
  transfers between devices with their start and end apart: 17, of which 6 were waited for; matrix products, arithmetic and copies ran while one was open for 1% of the time, Pallas kernels for 31%

profile of v9, /device:TPU:5, one launch (start us, length us, event | category | flops | bytes accessed | tf_op | source)
XLA Modules:
  0.0 109.9 jit_solution(9425514521655995267)
XLA Ops:
  0.0 0.0 copy-start.8
  0.0 0.0 copy-start.9
  0.0 6.3 %pack_direct.1 = (bf16[20,5,16,256]{3,2,1,0:T(8,128)(2,1)S(1)}, bf16[20,5,16,256]{3,2,1,0:T(8,128)(2,1)S(1)}, bf16[20,5,16,256]{3,2,1,0:T(8,128)(2,1)S(1)}, bf16...) custom-call(bf16[16,5,16,16,256]{4,3,2,1,0:T(8,128)(2,1)} %u_hbm.1), custom_call_target="tpu_custom_call" | custom-call | flops 15728640 | bytes 10485760 | tf_op jit(solution)/shard_map/pack_direct/pallas_call | solution.py:74
  6.3 0.1 reduce_sum.9
  6.5 0.1 collective-permute-start
  6.5 0.0 copy-done.9
  6.6 0.0 copy-done.8
  6.6 0.2 fusion.6
  6.8 2.1 %collective-permute-done = f32[16]{0:T(128)S(1)} collective-permute-done((f32[16]{0:T(128)S(1)}, f32[16]{0:T(128)S(1)}, u32[]{:S(2)}, u32[]{:S(2)}) %collective-permute-start) | collective-permute-done | bytes 96 | tf_op jit(solution)/shard_map/ppermute | solution.py:492
  8.9 1.3 %collective-permute-start.1 = (f32[16]{0:T(128)S(1)}, f32[16]{0:T(128)S(1)}, u32[]{:S(2)}, u32[]{:S(2)}) collective-permute-start(f32[16]{0:T(128)S(1)} %add.18), channel_id=1, source_target_pairs={{0,2},{1,3},{2,0},{3,1},{4,6},{5,7},{6,4},{7,5},{8,10},{9,11},{10,... | collective-permute-start | bytes 200 | tf_op jit(solution)/shard_map/ppermute | solution.py:492
  10.2 0.0 copy-done.7
  10.2 0.0 copy-done.10
  10.2 0.4 multiply_convert_fusion
  10.6 0.7 collective-permute-done.1
  11.3 2.3 %collective-permute-start.2 = (f32[16]{0:T(128)S(1)}, f32[16]{0:T(128)S(1)}, u32[]{:S(2)}, u32[]{:S(2)}) collective-permute-start(f32[16]{0:T(128)S(1)} %add.19), channel_id=1, source_target_pairs={{0,4},{1,5},{2,6},{3,7},{4,0},{5,1},{6,2},{7,3},{8,12},{9,13},{10,... | collective-permute-start | bytes 200 | tf_op jit(solution)/shard_map/ppermute | solution.py:492
  13.6 1.0 collective-permute-done.2
  14.6 4.1 %collective-permute-start.3 = (f32[16]{0:T(128)S(1)}, f32[16]{0:T(128)S(1)}, u32[]{:S(2)}, u32[]{:S(2)}) collective-permute-start(f32[16]{0:T(128)S(1)} %add.20), channel_id=1, source_target_pairs={{0,8},{8,0},{16,24},{24,16},{1,9},{9,1},{17,25},{25,17},{2,10},{10... | collective-permute-start | bytes 200 | tf_op jit(solution)/shard_map/ppermute | solution.py:492
  18.7 2.3 %mix_chord.1 = (f32[16,80,256]{2,1,0:T(8,128)S(1)}, f32[16,80,256]{2,1,0:T(8,128)S(1)}) custom-call(bf16[80,160]{1,0:T(8,128)(2,1)S(1)} %get-tuple-element.63.lw, bf16[16,5,16,16,256]{4,3,2,1,0:T(8,128)(2,1)} %src.3, bf16[16,5,16,16,256]{4,3,2,1,0:T(8,128)(2,1)} %src.3), custom_call_target="tpu_custom_call" | custom-call | flops 100000000 | bytes 6000000 | tf_op jit(solution)/shard_map/mix_chord/pallas_call | solution.py:106
  21.0 0.0 collective-permute-done.3
  21.0 1.3 %collective-permute-start.4 = (f32[16]{0:T(128)S(1)}, f32[16]{0:T(128)S(1)}, u32[]{:S(2)}, u32[]{:S(2)}) collective-permute-start(f32[16]{0:T(128)S(1)} %add.21), channel_id=1, source_target_pairs={{0,16},{8,24},{16,0},{24,8},{1,17},{9,25},{17,1},{25,9},{2,18},{10... | collective-permute-start | bytes 200 | tf_op jit(solution)/shard_map/ppermute | solution.py:492
  22.3 6.6 %mix_normal.1 = (f32[16,80,256]{2,1,0:T(8,128)S(1)}, f32[16,80,256]{2,1,0:T(8,128)S(1)}) custom-call(bf16[80,160]{1,0:T(8,128)(2,1)S(1)} %get-tuple-element.64.lw, bf16[16,5,16,16,256]{4,3,2,1,0:T(8,128)(2,1)} %src.3), custom_call_target="tpu_custom_call" | custom-call | flops 15728640 | bytes 15728640 | tf_op jit(solution)/shard_map/mix_normal/pallas_call | solution.py:139
  29.0 0.0 collective-permute-done.4
  29.0 0.0 copy-done
  29.0 0.0 copy-done.2
  29.0 0.0 copy-done.3
  29.0 0.0 copy-start.4
  29.0 0.0 copy-start.5
  29.0 0.0 copy-start.6
  29.0 1.5 %faces.1 = (bf16[20,5,16,256]{3,2,1,0:T(8,128)(2,1)S(1)}, bf16[20,5,16,256]{3,2,1,0:T(8,128)(2,1)S(1)}, bf16[20,5,16,256]{3,2,1,0:T(8,128)(2,1)S(1)}, bf16[20,5,16,256]{3,2,1,0:T(8,128)(2,1)S(1)}) custom-call(s32[16]{0:T(128)S(1)} %copy-done.3, ...), custom_call_target="tpu_custom_call", output_to_operand_aliasing={{0}: (3, {}), {1}: (4, {}), {2}: (5, {}), {3}: (6, {})} | custom-call | tf_op jit(solution)/shard_map/faces/pallas_call | solution.py:191
  30.6 3.2 %collective-permute-start.5 = (bf16[20,5,16,256]{3,2,1,0:T(8,128)(2,1)S(1)}, bf16[20,5,16,256]{3,2,1,0:T(8,128)(2,1)}, u32[]{:S(2)}, u32[]{:S(2)}) collective-permute-start(bf16[20,5,16,256]{3,2,1,0:T(8,128)(2,1)S(1)} %get-tuple-element.41), channel_id=1, source_target_pairs={{0,1},{1,2},{2,3},{3,4},{4,5},{5,6},{6,7},{8,9},{9,10},{10,11},{11... | collective-permute-start | bytes 2457608 | tf_op jit(solution)/shard_map/ppermute | solution.py:478
  33.7 3.0 %collective-permute-start.6 = (bf16[20,5,16,256]{3,2,1,0:T(8,128)(2,1)S(1)}, bf16[20,5,16,256]{3,2,1,0:T(8,128)(2,1)}, u32[]{:S(2)}, u32[]{:S(2)}) collective-permute-start(bf16[20,5,16,256]{3,2,1,0:T(8,128)(2,1)S(1)} %get-tuple-element.42), channel_id=1, source_target_pairs={{1,0},{2,1},{3,2},{4,3},{5,4},{6,5},{7,6},{9,8},{10,9},{11,10},{12... | collective-permute-start | bytes 2457608 | tf_op jit(solution)/shard_map/ppermute | solution.py:478
  36.7 2.9 %collective-permute-start.7 = (bf16[20,5,16,256]{3,2,1,0:T(8,128)(2,1)S(1)}, bf16[20,5,16,256]{3,2,1,0:T(8,128)(2,1)}, u32[]{:S(2)}, u32[]{:S(2)}) collective-permute-start(bf16[20,5,16,256]{3,2,1,0:T(8,128)(2,1)S(1)} %get-tuple-element.43), channel_id=1, source_target_pairs={{0,8},{8,16},{16,24},{1,9},{9,17},{17,25},{2,10},{10,18},{18,26},{... | collective-permute-start | bytes 2457608 | tf_op jit(solution)/shard_map/ppermute | solution.py:478
  39.6 2.3 %collective-permute-start.8 = (bf16[20,5,16,256]{3,2,1,0:T(8,128)(2,1)S(1)}, bf16[20,5,16,256]{3,2,1,0:T(8,128)(2,1)}, u32[]{:S(2)}, u32[]{:S(2)}) collective-permute-start(bf16[20,5,16,256]{3,2,1,0:T(8,128)(2,1)S(1)} %get-tuple-element.44), channel_id=1, source_target_pairs={{8,0},{16,8},{24,16},{9,1},{17,9},{25,17},{10,2},{18,10},{26,18},{... | collective-permute-start | bytes 2457608 | tf_op jit(solution)/shard_map/ppermute | solution.py:478
  42.0 0.1 pad_maximum_fusion.1.refs_0_
  42.1 0.0 copy-done.4
  42.1 0.0 copy-done.5
  42.1 0.0 copy-done.6
  42.2 0.0 copy-start.1
  42.2 25.4 %main.1.refs_2_ = f32[16,80,256]{2,1,0:T(8,128)S(1)} custom-call(s32[16]{0:T(128)S(1)} %copy-done.3, f32[16]{0:T(128)S(1)} %add_rsqrt_fusion.amp.refs_1_, bf16[320,160]{1,0:T(8,128)(2,1)S(1)} %pad_maximum_fusion.lw, bf16[16,5,16,16,256]{4,3,2,1,0:T(8,128)(2,1)} %u_hbm.1, bf16[16,5,16,16,256]{4,3,2,1,0:T(8,128)(2,1)} %src.3), custom_call_target="tpu_custom_call" | custom-call | flops 1000000 | bytes 100000 | tf_op jit(solution)/shard_map/main/pallas_call | solution.py:307
  67.7 2.0 %collective-permute-done.5.refs_8_ = bf16[20,5,16,256]{3,2,1,0:T(8,128)(2,1)} collective-permute-done((bf16[20,5,16,256]{3,2,1,0:T(8,128)(2,1)S(1)}, bf16[20,5,16,256]{3,2,1,0:T(8,128)(2,1)}, u32[]{:S(2)}, u32[]{:S(2)}) %collective-permute-start.5) | collective-permute-done | bytes 819232 | tf_op jit(solution)/shard_map/ppermute | solution.py:478
  69.7 0.0 collective-permute-done.6.refs_9_
  69.7 0.0 collective-permute-done.7.refs_10_
  69.7 0.0 collective-permute-done.8.refs_11_
  69.7 0.0 copy-done.1
  69.7 3.4 %boundary.1 = (f32[16,80,256]{2,1,0:T(8,128)S(1)}, f32[5,16,256]{2,1,0:T(8,128)S(1)}, f32[5,16,256]{2,1,0:T(8,128)S(1)}, f32[5,16,256]{2,1,0:T(8,128)S(1)}, f32[...) custom-call(s32[16]{0:T(128)S(1)} %copy-done.3, ...), custom_call_target="tpu_custom_call" | custom-call | tf_op jit(solution)/shard_map/boundary/pallas_call | solution.py:384
  73.1 4.7 %collective-permute-start.9 = (f32[5,16,256]{2,1,0:T(8,128)S(1)}, f32[5,16,256]{2,1,0:T(8,128)S(1)}, u32[]{:S(2)}, u32[]{:S(2)}) collective-permute-start(f32[5,16,256]{2,1,0:T(8,128)S(1)} %get-tuple-element.46), channel_id=1, source_target_pairs={{0,1},{1,2},{2,3},{3,4},{4,5},{5,6},{6,7},{8,9},{9,10},{10,11},{11... | collective-permute-start | bytes 245768 | tf_op jit(solution)/shard_map/ppermute | solution.py:478
  77.7 1.9 %collective-permute-start.10 = (f32[5,16,256]{2,1,0:T(8,128)S(1)}, f32[5,16,256]{2,1,0:T(8,128)S(1)}, u32[]{:S(2)}, u32[]{:S(2)}) collective-permute-start(f32[5,16,256]{2,1,0:T(8,128)S(1)} %get-tuple-element.47), channel_id=1, source_target_pairs={{1,0},{2,1},{3,2},{4,3},{5,4},{6,5},{7,6},{9,8},{10,9},{11,10},{12... | collective-permute-start | bytes 245768 | tf_op jit(solution)/shard_map/ppermute | solution.py:478
  79.7 2.8 %collective-permute-start.11 = (f32[5,16,256]{2,1,0:T(8,128)S(1)}, f32[5,16,256]{2,1,0:T(8,128)S(1)}, u32[]{:S(2)}, u32[]{:S(2)}) collective-permute-start(f32[5,16,256]{2,1,0:T(8,128)S(1)} %get-tuple-element.48), channel_id=1, source_target_pairs={{0,8},{8,16},{16,24},{1,9},{9,17},{17,25},{2,10},{10,18},{18,26},{... | collective-permute-start | bytes 245768 | tf_op jit(solution)/shard_map/ppermute | solution.py:478
  82.5 1.9 %collective-permute-start.12 = (f32[5,16,256]{2,1,0:T(8,128)S(1)}, f32[5,16,256]{2,1,0:T(8,128)S(1)}, u32[]{:S(2)}, u32[]{:S(2)}) collective-permute-start(f32[5,16,256]{2,1,0:T(8,128)S(1)} %get-tuple-element.49), channel_id=1, source_target_pairs={{8,0},{16,8},{24,16},{9,1},{17,9},{25,17},{10,2},{18,10},{26,18},{... | collective-permute-start | bytes 245768 | tf_op jit(solution)/shard_map/ppermute | solution.py:478
  84.4 0.1 pad_maximum_fusion.2.refs_1_
  84.5 0.0 collective-permute-done.9.refs_5_
  84.5 0.0 collective-permute-done.10.refs_6_
  84.5 0.0 collective-permute-done.11.refs_7_
  84.5 3.7 %collective-permute-done.12.refs_8_ = f32[5,16,256]{2,1,0:T(8,128)S(1)} collective-permute-done((f32[5,16,256]{2,1,0:T(8,128)S(1)}, f32[5,16,256]{2,1,0:T(8,128)S(1)}, u32[]{:S(2)}, u32[]{:S(2)}) %collective-permute-start.12) | collective-permute-done | bytes 81952 | tf_op jit(solution)/shard_map/ppermute | solution.py:478
  88.2 3.2 %step_one.1 = (f32[16,80,256]{2,1,0:T(8,128)S(1)}, f32[5,16,256]{2,1,0:T(8,128)S(1)}, f32[5,16,256]{2,1,0:T(8,128)S(1)}, f32[5,16,256]{2,1,0:T(8,128)S(1)}, f32[5,16,256]{2,1,0:T(8,128)S(1)}) custom-call(bf16[240,240]{1,0:T(8,128)(2,1)S(1)} %pad_maximum_fusion.1.refs_0_, bf16[80,240]{1,0:T(8,128)(2,1)S(1)} %pad_maximum_fusion.2.refs_1_, ...), custom_call_target="tpu_custom_call" | custom-call | tf_op jit(solution)/shard_map/step_one/pallas_call | solution.py:463
  91.4 4.5 %collective-permute-start.13 = (f32[5,16,256]{2,1,0:T(8,128)S(1)}, f32[5,16,256]{2,1,0:T(8,128)S(1)}, u32[]{:S(2)}, u32[]{:S(2)}) collective-permute-start(f32[5,16,256]{2,1,0:T(8,128)S(1)} %get-tuple-element.55), channel_id=1, source_target_pairs={{0,1},{1,2},{2,3},{3,4},{4,5},{5,6},{6,7},{8,9},{9,10},{10,11},{11... | collective-permute-start | bytes 245768 | tf_op jit(solution)/shard_map/ppermute | solution.py:478
  96.0 1.9 %collective-permute-start.14 = (f32[5,16,256]{2,1,0:T(8,128)S(1)}, f32[5,16,256]{2,1,0:T(8,128)S(1)}, u32[]{:S(2)}, u32[]{:S(2)}) collective-permute-start(f32[5,16,256]{2,1,0:T(8,128)S(1)} %get-tuple-element.56), channel_id=1, source_target_pairs={{1,0},{2,1},{3,2},{4,3},{5,4},{6,5},{7,6},{9,8},{10,9},{11,10},{12... | collective-permute-start | bytes 245768 | tf_op jit(solution)/shard_map/ppermute | solution.py:478
  97.9 2.1 %collective-permute-start.15 = (f32[5,16,256]{2,1,0:T(8,128)S(1)}, f32[5,16,256]{2,1,0:T(8,128)S(1)}, u32[]{:S(2)}, u32[]{:S(2)}) collective-permute-start(f32[5,16,256]{2,1,0:T(8,128)S(1)} %get-tuple-element.57), channel_id=1, source_target_pairs={{0,8},{8,16},{16,24},{1,9},{9,17},{17,25},{2,10},{10,18},{18,26},{... | collective-permute-start | bytes 245768 | tf_op jit(solution)/shard_map/ppermute | solution.py:478
  100.1 2.2 %collective-permute-start.16 = (f32[5,16,256]{2,1,0:T(8,128)S(1)}, f32[5,16,256]{2,1,0:T(8,128)S(1)}, u32[]{:S(2)}, u32[]{:S(2)}) collective-permute-start(f32[5,16,256]{2,1,0:T(8,128)S(1)} %get-tuple-element.58), channel_id=1, source_target_pairs={{8,0},{16,8},{24,16},{9,1},{17,9},{25,17},{10,2},{18,10},{26,18},{... | collective-permute-start | bytes 245768 | tf_op jit(solution)/shard_map/ppermute | solution.py:478
  102.3 0.0 collective-permute-done.13.refs_5_
  102.3 0.0 collective-permute-done.14.refs_6_
  102.3 0.0 collective-permute-done.15.refs_7_
  102.3 3.5 %collective-permute-done.16.refs_8_ = f32[5,16,256]{2,1,0:T(8,128)S(1)} collective-permute-done((f32[5,16,256]{2,1,0:T(8,128)S(1)}, f32[5,16,256]{2,1,0:T(8,128)S(1)}, u32[]{:S(2)}, u32[]{:S(2)}) %collective-permute-start.16) | collective-permute-done | bytes 81952 | tf_op jit(solution)/shard_map/ppermute | solution.py:478
  105.8 4.1 %step_two.1 = f32[5,16,16,256]{3,2,1,0:T(8,128)} custom-call(bf16[240,240]{1,0:T(8,128)(2,1)S(1)} %pad_maximum_fusion.1.refs_0_, bf16[80,240]{1,0:T(8,128)(2,1)S(1)} %pad_maximum_fusion.2.refs_1_, f32[5,16,16,256]{3,2,1,0:T(8,128)S(1)} %copy-done, s32[16,16,256]{2,1,0:T(8,128)S(1)} %copy-done.1, f32[16,80,256]{2,1,0:T(8,128)S(1)} %get-tuple-element.54.refs_4_, ...), custom_call_target="tpu_custom_call" | custom-call | tf_op jit(solution)/shard_map/step_two/pallas_call | solution.py:463
  (17 shorter events, 0.1 us)
Async XLA Ops:
  0.0 6.6 %copy-start.8 = (f32[10,160,1]{1,0,2:T(8,128)S(1)}, f32[10,160,1]{1,0,2:T(8,128)}, u32[]{:S(2)}) copy-start(f32[10,160,1]{1,0,2:T(8,128)} %constant.26) | copy-start | bytes 19204
  0.0 10.2 %copy-start.7 = (f32[80,160]{1,0:T(8,128)S(1)}, f32[80,160]{1,0:T(8,128)}, u32[]{:S(2)}) copy-start(f32[80,160]{1,0:T(8,128)} %constant.19.clone) | copy-start | bytes 153604
  0.0 10.2 %copy-start.10 = (f32[80,5,1]{0,1,2:T(8,128)S(1)}, f32[80,5,1]{0,1,2:T(8,128)}, u32[]{:S(2)}) copy-start(f32[80,5,1]{0,1,2:T(8,128)} %constant.27) | copy-start | bytes 4804
  0.0 6.5 %copy-start.9 = (f32[3,5,5]{2,0,1:T(4,128)S(1)}, f32[3,5,5]{2,0,1:T(4,128)}, u32[]{:S(2)}) copy-start(f32[3,5,5]{2,0,1:T(4,128)} %param.18) | copy-start | bytes 904
  6.5 2.4 %collective-permute-start = (f32[16]{0:T(128)S(1)}, f32[16]{0:T(128)S(1)}, u32[]{:S(2)}, u32[]{:S(2)}) collective-permute-start(f32[16]{0:T(128)S(1)} %reduce_sum.9), channel_id=1, source_target_pairs={{0,1},{1,0},{2,3},{3,2},{4,5},{5,4},{6,7},{7,6},{8,9},{9,8},{10,11... | collective-permute-start | bytes 200 | tf_op jit(solution)/shard_map/ppermute | solution.py:492
  8.9 2.4 %collective-permute-start.1 = (f32[16]{0:T(128)S(1)}, f32[16]{0:T(128)S(1)}, u32[]{:S(2)}, u32[]{:S(2)}) collective-permute-start(f32[16]{0:T(128)S(1)} %add.18), channel_id=1, source_target_pairs={{0,2},{1,3},{2,0},{3,1},{4,6},{5,7},{6,4},{7,5},{8,10},{9,11},{10,... | collective-permute-start | bytes 200 | tf_op jit(solution)/shard_map/ppermute | solution.py:492
  11.3 3.3 %collective-permute-start.2 = (f32[16]{0:T(128)S(1)}, f32[16]{0:T(128)S(1)}, u32[]{:S(2)}, u32[]{:S(2)}) collective-permute-start(f32[16]{0:T(128)S(1)} %add.19), channel_id=1, source_target_pairs={{0,4},{1,5},{2,6},{3,7},{4,0},{5,1},{6,2},{7,3},{8,12},{9,13},{10,... | collective-permute-start | bytes 200 | tf_op jit(solution)/shard_map/ppermute | solution.py:492
  14.6 6.4 %collective-permute-start.3 = (f32[16]{0:T(128)S(1)}, f32[16]{0:T(128)S(1)}, u32[]{:S(2)}, u32[]{:S(2)}) collective-permute-start(f32[16]{0:T(128)S(1)} %add.20), channel_id=1, source_target_pairs={{0,8},{8,0},{16,24},{24,16},{1,9},{9,1},{17,25},{25,17},{2,10},{10... | collective-permute-start | bytes 200 | tf_op jit(solution)/shard_map/ppermute | solution.py:492
  21.0 7.9 %collective-permute-start.4 = (f32[16]{0:T(128)S(1)}, f32[16]{0:T(128)S(1)}, u32[]{:S(2)}, u32[]{:S(2)}) collective-permute-start(f32[16]{0:T(128)S(1)} %add.21), channel_id=1, source_target_pairs={{0,16},{8,24},{16,0},{24,8},{1,17},{9,25},{17,1},{25,9},{2,18},{10... | collective-permute-start | bytes 200 | tf_op jit(solution)/shard_map/ppermute | solution.py:492
  22.3 6.7 %copy-start = (f32[5,16,16,256]{3,2,1,0:T(8,128)S(1)}, f32[5,16,16,256]{3,2,1,0:T(8,128)}, u32[]{:S(2)}) copy-start(f32[5,16,16,256]{3,2,1,0:T(8,128)} %refs_2_.3) | copy-start | bytes 3932164
  22.3 6.7 %copy-start.2 = (bf16[20,5,16,256]{3,2,1,0:T(8,128)(2,1)S(1)}, bf16[20,5,16,256]{3,2,1,0:T(8,128)(2,1)}, u32[]{:S(2)}) copy-start(bf16[20,5,16,256]{3,2,1,0:T(8,128)(2,1)} %get-tuple-element.40.refs_3_) | copy-start | bytes 2457604
  22.3 6.7 %copy-start.3 = (s32[16]{0:T(128)S(1)}, s32[16]{0:T(128)}, u32[]{:S(2)}) copy-start(s32[16]{0:T(128)} %refs_0_.1) | copy-start | bytes 196
  29.0 13.1 %copy-start.4 = (f32[1,80,160]{2,1,0:T(8,128)S(1)}, f32[1,80,160]{2,1,0:T(8,128)}, u32[]{:S(2)}) copy-start(f32[1,80,160]{2,1,0:T(8,128)} %constant.24) | copy-start | bytes 153604
  29.0 13.1 %copy-start.5 = (f32[1,80,160]{2,1,0:T(8,128)S(1)}, f32[1,80,160]{2,1,0:T(8,128)}, u32[]{:S(2)}) copy-start(f32[1,80,160]{2,1,0:T(8,128)} %constant.23) | copy-start | bytes 153604
  29.0 13.1 %copy-start.6 = (f32[1,80,160]{2,1,0:T(8,128)S(1)}, f32[1,80,160]{2,1,0:T(8,128)}, u32[]{:S(2)}) copy-start(f32[1,80,160]{2,1,0:T(8,128)} %constant.22) | copy-start | bytes 153604
  30.6 39.1 %collective-permute-start.5 = (bf16[20,5,16,256]{3,2,1,0:T(8,128)(2,1)S(1)}, bf16[20,5,16,256]{3,2,1,0:T(8,128)(2,1)}, u32[]{:S(2)}, u32[]{:S(2)}) collective-permute-start(bf16[20,5,16,256]{3,2,1,0:T(8,128)(2,1)S(1)} %get-tuple-element.41), channel_id=1, source_target_pairs={{0,1},{1,2},{2,3},{3,4},{4,5},{5,6},{6,7},{8,9},{9,10},{10,11},{11... | collective-permute-start | bytes 2457608 | tf_op jit(solution)/shard_map/ppermute | solution.py:478
  33.7 36.0 %collective-permute-start.6 = (bf16[20,5,16,256]{3,2,1,0:T(8,128)(2,1)S(1)}, bf16[20,5,16,256]{3,2,1,0:T(8,128)(2,1)}, u32[]{:S(2)}, u32[]{:S(2)}) collective-permute-start(bf16[20,5,16,256]{3,2,1,0:T(8,128)(2,1)S(1)} %get-tuple-element.42), channel_id=1, source_target_pairs={{1,0},{2,1},{3,2},{4,3},{5,4},{6,5},{7,6},{9,8},{10,9},{11,10},{12... | collective-permute-start | bytes 2457608 | tf_op jit(solution)/shard_map/ppermute | solution.py:478
  36.7 32.9 %collective-permute-start.7 = (bf16[20,5,16,256]{3,2,1,0:T(8,128)(2,1)S(1)}, bf16[20,5,16,256]{3,2,1,0:T(8,128)(2,1)}, u32[]{:S(2)}, u32[]{:S(2)}) collective-permute-start(bf16[20,5,16,256]{3,2,1,0:T(8,128)(2,1)S(1)} %get-tuple-element.43), channel_id=1, source_target_pairs={{0,8},{8,16},{16,24},{1,9},{9,17},{17,25},{2,10},{10,18},{18,26},{... | collective-permute-start | bytes 2457608 | tf_op jit(solution)/shard_map/ppermute | solution.py:478
  39.6 30.0 %collective-permute-start.8 = (bf16[20,5,16,256]{3,2,1,0:T(8,128)(2,1)S(1)}, bf16[20,5,16,256]{3,2,1,0:T(8,128)(2,1)}, u32[]{:S(2)}, u32[]{:S(2)}) collective-permute-start(bf16[20,5,16,256]{3,2,1,0:T(8,128)(2,1)S(1)} %get-tuple-element.44), channel_id=1, source_target_pairs={{8,0},{16,8},{24,16},{9,1},{17,9},{25,17},{10,2},{18,10},{26,18},{... | collective-permute-start | bytes 2457608 | tf_op jit(solution)/shard_map/ppermute | solution.py:478
  42.2 27.5 %copy-start.1 = (s32[16,16,256]{2,1,0:T(8,128)S(1)}, s32[16,16,256]{2,1,0:T(8,128)}, u32[]{:S(2)}) copy-start(s32[16,16,256]{2,1,0:T(8,128)} %refs_3_.5) | copy-start | bytes 786436
  73.1 11.4 %collective-permute-start.9 = (f32[5,16,256]{2,1,0:T(8,128)S(1)}, f32[5,16,256]{2,1,0:T(8,128)S(1)}, u32[]{:S(2)}, u32[]{:S(2)}) collective-permute-start(f32[5,16,256]{2,1,0:T(8,128)S(1)} %get-tuple-element.46), channel_id=1, source_target_pairs={{0,1},{1,2},{2,3},{3,4},{4,5},{5,6},{6,7},{8,9},{9,10},{10,11},{11... | collective-permute-start | bytes 245768 | tf_op jit(solution)/shard_map/ppermute | solution.py:478
  77.7 6.8 %collective-permute-start.10 = (f32[5,16,256]{2,1,0:T(8,128)S(1)}, f32[5,16,256]{2,1,0:T(8,128)S(1)}, u32[]{:S(2)}, u32[]{:S(2)}) collective-permute-start(f32[5,16,256]{2,1,0:T(8,128)S(1)} %get-tuple-element.47), channel_id=1, source_target_pairs={{1,0},{2,1},{3,2},{4,3},{5,4},{6,5},{7,6},{9,8},{10,9},{11,10},{12... | collective-permute-start | bytes 245768 | tf_op jit(solution)/shard_map/ppermute | solution.py:478
  79.7 4.9 %collective-permute-start.11 = (f32[5,16,256]{2,1,0:T(8,128)S(1)}, f32[5,16,256]{2,1,0:T(8,128)S(1)}, u32[]{:S(2)}, u32[]{:S(2)}) collective-permute-start(f32[5,16,256]{2,1,0:T(8,128)S(1)} %get-tuple-element.48), channel_id=1, source_target_pairs={{0,8},{8,16},{16,24},{1,9},{9,17},{17,25},{2,10},{10,18},{18,26},{... | collective-permute-start | bytes 245768 | tf_op jit(solution)/shard_map/ppermute | solution.py:478
  82.5 5.8 %collective-permute-start.12 = (f32[5,16,256]{2,1,0:T(8,128)S(1)}, f32[5,16,256]{2,1,0:T(8,128)S(1)}, u32[]{:S(2)}, u32[]{:S(2)}) collective-permute-start(f32[5,16,256]{2,1,0:T(8,128)S(1)} %get-tuple-element.49), channel_id=1, source_target_pairs={{8,0},{16,8},{24,16},{9,1},{17,9},{25,17},{10,2},{18,10},{26,18},{... | collective-permute-start | bytes 245768 | tf_op jit(solution)/shard_map/ppermute | solution.py:478
  91.4 10.8 %collective-permute-start.13 = (f32[5,16,256]{2,1,0:T(8,128)S(1)}, f32[5,16,256]{2,1,0:T(8,128)S(1)}, u32[]{:S(2)}, u32[]{:S(2)}) collective-permute-start(f32[5,16,256]{2,1,0:T(8,128)S(1)} %get-tuple-element.55), channel_id=1, source_target_pairs={{0,1},{1,2},{2,3},{3,4},{4,5},{5,6},{6,7},{8,9},{9,10},{10,11},{11... | collective-permute-start | bytes 245768 | tf_op jit(solution)/shard_map/ppermute | solution.py:478
  96.0 6.3 %collective-permute-start.14 = (f32[5,16,256]{2,1,0:T(8,128)S(1)}, f32[5,16,256]{2,1,0:T(8,128)S(1)}, u32[]{:S(2)}, u32[]{:S(2)}) collective-permute-start(f32[5,16,256]{2,1,0:T(8,128)S(1)} %get-tuple-element.56), channel_id=1, source_target_pairs={{1,0},{2,1},{3,2},{4,3},{5,4},{6,5},{7,6},{9,8},{10,9},{11,10},{12... | collective-permute-start | bytes 245768 | tf_op jit(solution)/shard_map/ppermute | solution.py:478
  97.9 4.4 %collective-permute-start.15 = (f32[5,16,256]{2,1,0:T(8,128)S(1)}, f32[5,16,256]{2,1,0:T(8,128)S(1)}, u32[]{:S(2)}, u32[]{:S(2)}) collective-permute-start(f32[5,16,256]{2,1,0:T(8,128)S(1)} %get-tuple-element.57), channel_id=1, source_target_pairs={{0,8},{8,16},{16,24},{1,9},{9,17},{17,25},{2,10},{10,18},{18,26},{... | collective-permute-start | bytes 245768 | tf_op jit(solution)/shard_map/ppermute | solution.py:478
  100.1 5.8 %collective-permute-start.16 = (f32[5,16,256]{2,1,0:T(8,128)S(1)}, f32[5,16,256]{2,1,0:T(8,128)S(1)}, u32[]{:S(2)}, u32[]{:S(2)}) collective-permute-start(f32[5,16,256]{2,1,0:T(8,128)S(1)} %get-tuple-element.58), channel_id=1, source_target_pairs={{8,0},{16,8},{24,16},{9,1},{17,9},{25,17},{10,2},{18,10},{26,18},{... | collective-permute-start | bytes 245768 | tf_op jit(solution)/shard_map/ppermute | solution.py:478

commit v10 on v9

--- a/solution.py
+++ b/solution.py
@@ -12,7 +12,8 @@
 MIB = 1024 * 1024
 GROUP = 4
 TAIL = 4
-TURN = 8
+TURN = 16
+PACK = 2
 LARGE = 51
 
 
@@ -73,9 +74,9 @@
     sizes = (ny, ny, nx, nx)
     return pl.pallas_call(
         direct_kernel,
-        grid=(nm // GROUP,),
-        in_specs=[pl.BlockSpec((GROUP, nv, nx, ny, nz), lambda s: (s, 0, 0, 0, 0))],
-        out_specs=[pl.BlockSpec((GROUP, nv, n, nz), lambda s: (s, 0, 0, 0)) for n in sizes]
+        grid=(nm // PACK,),
+        in_specs=[pl.BlockSpec((PACK, nv, nx, ny, nz), lambda s: (s, 0, 0, 0, 0))],
+        out_specs=[pl.BlockSpec((PACK, nv, n, nz), lambda s: (s, 0, 0, 0)) for n in sizes]
         + [pl.BlockSpec((nm, LANES), lambda s: (0, 0))],
         out_shape=[sds((nm + TAIL, nv, n, nz), BF16) for n in sizes] + [sds((nm, LANES), F32)],
         scratch_shapes=[pltpu.VMEM((nv, nz // LANES, nx * ny, LANES), F32)],
@@ -135,13 +136,13 @@
 def mix_normal(lw, modes):
     nm, nv, nx, ny, nz = modes.shape
     w = sds((nm, nv * nx, nz), F32)
-    out = pl.BlockSpec((GROUP, nv * nx, nz), lambda s: (s, 0, 0))
+    out = pl.BlockSpec((PACK, nv * nx, nz), lambda s: (s, 0, 0))
     return pl.pallas_call(
         mix_normal_kernel,
-        grid=(nm // GROUP,),
+        grid=(nm // PACK,),
         in_specs=[
             pl.BlockSpec(lw.shape, lambda s: (0, 0)),
-            pl.BlockSpec((GROUP, nv, nx, ny, nz), lambda s: (s, 0, 0, 0, 0)),
+            pl.BlockSpec((PACK, nv, nx, ny, nz), lambda s: (s, 0, 0, 0, 0)),
         ],
         out_specs=[out, out],
         out_shape=[w, w],
@@ -245,10 +246,11 @@
             q_copy(after).wait()
 
         acc[...] = jnp.zeros_like(acc)
+        each = -(-TURN // nv)
 
         def body(step, carry):
             for j in range(nv):
-                for k in range(2 * j, min(2 * j + 2, TURN)):
+                for k in range(each * j, min(each * (j + 1), TURN)):
                     products(after, step * TURN + k, dest)
                 at = slice(j * ny, (j + 1) * ny)
                 sums = [acc[n, at] for n in range(5)]
@@ -263,8 +265,6 @@
                     sums = [v + t for v, t in zip(sums, terms)]
                 for n in range(5):
                     acc[n, at] = sums[n]
-            for k in range(2 * nv, TURN):
-                products(after, step * TURN + k, dest)
             return carry
 
         lax.fori_loop(0, nm // TURN, body, 0)

time: 112 us -> 115 us (1.027)
  waiting for transfers between devices: 13 us -> 16.1 us
    pallas_call x2, Pallas kernels: 13 us -> 16.1 us  [the longest x1 8.09 us: mix_normal(): pl.pallas_call(mix_normal_kernel, grid=(nm // PACK,), in_specs=[pl.BlockS...]
    ppermute x12, waiting for transfers between devices: 9.28 us -> 12.3 us  [exchange_axis(): return [lax.ppermute(hi, axis, up), lax.ppermute(lo, axis, down)]]
    pallas_call x1, Pallas kernels: 25.4 us -> 22.4 us  [main(): pl.pallas_call(main_kernel, in_specs=[in_smem(), in_smem(), in_vmem(), in...]
  transfers between devices with their start and end apart: 17 -> 17, of which waited for: 6 -> 6; matrix products, arithmetic and copies ran while one was open for 1% -> 1% of each run, Pallas kernels for 31% -> 29%
where the time goes in v10:
time: 115 us; the launch traced here: 113 us
  Pallas kernels  52.9 us (46%)
  starting transfers between devices  42.5 us (37%)
  waiting for transfers between devices  16.1 us (14%)
    ppermute x12, starting transfers between devices, exchange_axis(): return [lax.ppermute(hi, axis, up), lax.ppermute(lo, axis, down)]  33.5 us
    pallas_call x1, Pallas kernels, main(): pl.pallas_call(main_kernel, in_specs=[in_smem(), in_smem(), in_vmem(), in...  22.4 us
    ppermute x12, waiting for transfers between devices, exchange_axis(): return [lax.ppermute(hi, axis, up), lax.ppermute(lo, axis, down)]  12.3 us
    ppermute x5, starting transfers between devices, sum_over(): lax.ppermute(values, axis, [(i, i ^ bit) for i in range(count)])  9.07 us
    pallas_call x1, Pallas kernels, mix_normal(): pl.pallas_call(mix_normal_kernel, grid=(nm // PACK,), in_specs=[pl.BlockS...  8.09 us
    pallas_call x1, Pallas kernels, pack(): pl.pallas_call(direct_kernel, grid=(nm // PACK,), in_specs=[pl.BlockSpec(...  7.99 us
    pallas_call x2, Pallas kernels, apply_step(): pl.pallas_call(lambda *refs: step_kernel(last, *refs), in_specs=[in_vmem(...  7.27 us
    ppermute x5, waiting for transfers between devices, sum_over(): lax.ppermute(values, axis, [(i, i ^ bit) for i in range(count)])  3.76 us
  transfers between devices with their start and end apart: 17, of which 6 were waited for; matrix products, arithmetic and copies ran while one was open for 1% of the time, Pallas kernels for 29%

profile of v10, /device:TPU:5, one launch (start us, length us, event | category | flops | bytes accessed | tf_op | source)
XLA Modules:
  0.0 113.0 jit_solution(4344571779613182361)
XLA Ops:
  0.0 0.0 copy-start.7
  0.0 0.0 copy-start.9
  0.0 8.0 %pack_direct.1 = (bf16[20,5,16,256]{3,2,1,0:T(8,128)(2,1)S(1)}, bf16[20,5,16,256]{3,2,1,0:T(8,128)(2,1)S(1)}, bf16[20,5,16,256]{3,2,1,0:T(8,128)(2,1)S(1)}, bf16...) custom-call(bf16[16,5,16,16,256]{4,3,2,1,0:T(8,128)(2,1)} %u_hbm.1), custom_call_target="tpu_custom_call" | custom-call | flops 15728640 | bytes 10485760 | tf_op jit(solution)/shard_map/pack_direct/pallas_call | solution.py:75
  8.0 0.1 reduce_sum.9
  8.1 0.1 collective-permute-start
  8.2 0.0 copy-done.9
  8.2 0.0 copy-done.8
  8.3 0.2 fusion.6
  8.5 2.1 %collective-permute-done = f32[16]{0:T(128)S(1)} collective-permute-done((f32[16]{0:T(128)S(1)}, f32[16]{0:T(128)S(1)}, u32[]{:S(2)}, u32[]{:S(2)}) %collective-permute-start) | collective-permute-done | bytes 96 | tf_op jit(solution)/shard_map/ppermute | solution.py:492
  10.6 1.3 %collective-permute-start.1 = (f32[16]{0:T(128)S(1)}, f32[16]{0:T(128)S(1)}, u32[]{:S(2)}, u32[]{:S(2)}) collective-permute-start(f32[16]{0:T(128)S(1)} %add.18), channel_id=1, source_target_pairs={{0,2},{1,3},{2,0},{3,1},{4,6},{5,7},{6,4},{7,5},{8,10},{9,11},{10,... | collective-permute-start | bytes 200 | tf_op jit(solution)/shard_map/ppermute | solution.py:492
  11.9 0.0 copy-done.7
  11.9 0.0 copy-done.10
  11.9 0.4 multiply_convert_fusion
  12.3 0.7 collective-permute-done.1
  13.0 2.3 %collective-permute-start.2 = (f32[16]{0:T(128)S(1)}, f32[16]{0:T(128)S(1)}, u32[]{:S(2)}, u32[]{:S(2)}) collective-permute-start(f32[16]{0:T(128)S(1)} %add.19), channel_id=1, source_target_pairs={{0,4},{1,5},{2,6},{3,7},{4,0},{5,1},{6,2},{7,3},{8,12},{9,13},{10,... | collective-permute-start | bytes 200 | tf_op jit(solution)/shard_map/ppermute | solution.py:492
  15.3 1.0 collective-permute-done.2
  16.3 4.1 %collective-permute-start.3 = (f32[16]{0:T(128)S(1)}, f32[16]{0:T(128)S(1)}, u32[]{:S(2)}, u32[]{:S(2)}) collective-permute-start(f32[16]{0:T(128)S(1)} %add.20), channel_id=1, source_target_pairs={{0,8},{8,0},{16,24},{24,16},{1,9},{9,1},{17,25},{25,17},{2,10},{10... | collective-permute-start | bytes 200 | tf_op jit(solution)/shard_map/ppermute | solution.py:492
  20.4 2.3 %mix_chord.1 = (f32[16,80,256]{2,1,0:T(8,128)S(1)}, f32[16,80,256]{2,1,0:T(8,128)S(1)}) custom-call(bf16[80,160]{1,0:T(8,128)(2,1)S(1)} %get-tuple-element.63.lw, bf16[16,5,16,16,256]{4,3,2,1,0:T(8,128)(2,1)} %src.3, bf16[16,5,16,16,256]{4,3,2,1,0:T(8,128)(2,1)} %src.3), custom_call_target="tpu_custom_call" | custom-call | flops 100000000 | bytes 6000000 | tf_op jit(solution)/shard_map/mix_chord/pallas_call | solution.py:107
  22.7 0.0 collective-permute-done.3
  22.7 1.3 %collective-permute-start.4 = (f32[16]{0:T(128)S(1)}, f32[16]{0:T(128)S(1)}, u32[]{:S(2)}, u32[]{:S(2)}) collective-permute-start(f32[16]{0:T(128)S(1)} %add.21), channel_id=1, source_target_pairs={{0,16},{8,24},{16,0},{24,8},{1,17},{9,25},{17,1},{25,9},{2,18},{10... | collective-permute-start | bytes 200 | tf_op jit(solution)/shard_map/ppermute | solution.py:492
  24.0 8.1 %mix_normal.1 = (f32[16,80,256]{2,1,0:T(8,128)S(1)}, f32[16,80,256]{2,1,0:T(8,128)S(1)}) custom-call(bf16[80,160]{1,0:T(8,128)(2,1)S(1)} %get-tuple-element.64.lw, bf16[16,5,16,16,256]{4,3,2,1,0:T(8,128)(2,1)} %src.3), custom_call_target="tpu_custom_call" | custom-call | flops 15728640 | bytes 15728640 | tf_op jit(solution)/shard_map/mix_normal/pallas_call | solution.py:140
  32.1 0.0 collective-permute-done.4
  32.1 0.0 copy-done
  32.1 0.0 copy-done.2
  32.1 0.0 copy-done.3
  32.1 0.0 copy-start.4
  32.1 0.0 copy-start.5
  32.2 0.0 copy-start.6
  32.2 1.5 %faces.1 = (bf16[20,5,16,256]{3,2,1,0:T(8,128)(2,1)S(1)}, bf16[20,5,16,256]{3,2,1,0:T(8,128)(2,1)S(1)}, bf16[20,5,16,256]{3,2,1,0:T(8,128)(2,1)S(1)}, bf16[20,5,16,256]{3,2,1,0:T(8,128)(2,1)S(1)}) custom-call(s32[16]{0:T(128)S(1)} %copy-done.3, ...), custom_call_target="tpu_custom_call", output_to_operand_aliasing={{0}: (3, {}), {1}: (4, {}), {2}: (5, {}), {3}: (6, {})} | custom-call | tf_op jit(solution)/shard_map/faces/pallas_call | solution.py:192
  33.7 3.1 %collective-permute-start.5 = (bf16[20,5,16,256]{3,2,1,0:T(8,128)(2,1)S(1)}, bf16[20,5,16,256]{3,2,1,0:T(8,128)(2,1)}, u32[]{:S(2)}, u32[]{:S(2)}) collective-permute-start(bf16[20,5,16,256]{3,2,1,0:T(8,128)(2,1)S(1)} %get-tuple-element.41), channel_id=1, source_target_pairs={{0,1},{1,2},{2,3},{3,4},{4,5},{5,6},{6,7},{8,9},{9,10},{10,11},{11... | collective-permute-start | bytes 2457608 | tf_op jit(solution)/shard_map/ppermute | solution.py:478
  36.8 3.0 %collective-permute-start.6 = (bf16[20,5,16,256]{3,2,1,0:T(8,128)(2,1)S(1)}, bf16[20,5,16,256]{3,2,1,0:T(8,128)(2,1)}, u32[]{:S(2)}, u32[]{:S(2)}) collective-permute-start(bf16[20,5,16,256]{3,2,1,0:T(8,128)(2,1)S(1)} %get-tuple-element.42), channel_id=1, source_target_pairs={{1,0},{2,1},{3,2},{4,3},{5,4},{6,5},{7,6},{9,8},{10,9},{11,10},{12... | collective-permute-start | bytes 2457608 | tf_op jit(solution)/shard_map/ppermute | solution.py:478
  39.9 2.9 %collective-permute-start.7 = (bf16[20,5,16,256]{3,2,1,0:T(8,128)(2,1)S(1)}, bf16[20,5,16,256]{3,2,1,0:T(8,128)(2,1)}, u32[]{:S(2)}, u32[]{:S(2)}) collective-permute-start(bf16[20,5,16,256]{3,2,1,0:T(8,128)(2,1)S(1)} %get-tuple-element.43), channel_id=1, source_target_pairs={{0,8},{8,16},{16,24},{1,9},{9,17},{17,25},{2,10},{10,18},{18,26},{... | collective-permute-start | bytes 2457608 | tf_op jit(solution)/shard_map/ppermute | solution.py:478
  42.8 2.3 %collective-permute-start.8 = (bf16[20,5,16,256]{3,2,1,0:T(8,128)(2,1)S(1)}, bf16[20,5,16,256]{3,2,1,0:T(8,128)(2,1)}, u32[]{:S(2)}, u32[]{:S(2)}) collective-permute-start(bf16[20,5,16,256]{3,2,1,0:T(8,128)(2,1)S(1)} %get-tuple-element.44), channel_id=1, source_target_pairs={{8,0},{16,8},{24,16},{9,1},{17,9},{25,17},{10,2},{18,10},{26,18},{... | collective-permute-start | bytes 2457608 | tf_op jit(solution)/shard_map/ppermute | solution.py:478
  45.1 0.1 pad_maximum_fusion.1.refs_0_
  45.2 0.0 copy-done.4
  45.2 0.0 copy-done.5
  45.2 0.0 copy-done.6
  45.3 0.0 copy-start.1
  45.3 22.4 %main.1.refs_2_ = f32[16,80,256]{2,1,0:T(8,128)S(1)} custom-call(s32[16]{0:T(128)S(1)} %copy-done.3, f32[16]{0:T(128)S(1)} %add_rsqrt_fusion.amp.refs_1_, bf16[320,160]{1,0:T(8,128)(2,1)S(1)} %pad_maximum_fusion.lw, bf16[16,5,16,16,256]{4,3,2,1,0:T(8,128)(2,1)} %u_hbm.1, bf16[16,5,16,16,256]{4,3,2,1,0:T(8,128)(2,1)} %src.3), custom_call_target="tpu_custom_call" | custom-call | flops 1000000 | bytes 100000 | tf_op jit(solution)/shard_map/main/pallas_call | solution.py:307
  67.7 5.1 %collective-permute-done.5.refs_8_ = bf16[20,5,16,256]{3,2,1,0:T(8,128)(2,1)} collective-permute-done((bf16[20,5,16,256]{3,2,1,0:T(8,128)(2,1)S(1)}, bf16[20,5,16,256]{3,2,1,0:T(8,128)(2,1)}, u32[]{:S(2)}, u32[]{:S(2)}) %collective-permute-start.5) | collective-permute-done | bytes 819232 | tf_op jit(solution)/shard_map/ppermute | solution.py:478
  72.8 0.0 collective-permute-done.6.refs_9_
  72.8 0.0 collective-permute-done.7.refs_10_
  72.8 0.0 collective-permute-done.8.refs_11_
  72.8 0.0 copy-done.1
  72.8 3.4 %boundary.1 = (f32[16,80,256]{2,1,0:T(8,128)S(1)}, f32[5,16,256]{2,1,0:T(8,128)S(1)}, f32[5,16,256]{2,1,0:T(8,128)S(1)}, f32[5,16,256]{2,1,0:T(8,128)S(1)}, f32[...) custom-call(s32[16]{0:T(128)S(1)} %copy-done.3, ...), custom_call_target="tpu_custom_call" | custom-call | tf_op jit(solution)/shard_map/boundary/pallas_call | solution.py:384
  76.2 4.6 %collective-permute-start.9 = (f32[5,16,256]{2,1,0:T(8,128)S(1)}, f32[5,16,256]{2,1,0:T(8,128)S(1)}, u32[]{:S(2)}, u32[]{:S(2)}) collective-permute-start(f32[5,16,256]{2,1,0:T(8,128)S(1)} %get-tuple-element.46), channel_id=1, source_target_pairs={{0,1},{1,2},{2,3},{3,4},{4,5},{5,6},{6,7},{8,9},{9,10},{10,11},{11... | collective-permute-start | bytes 245768 | tf_op jit(solution)/shard_map/ppermute | solution.py:478
  80.8 1.9 %collective-permute-start.10 = (f32[5,16,256]{2,1,0:T(8,128)S(1)}, f32[5,16,256]{2,1,0:T(8,128)S(1)}, u32[]{:S(2)}, u32[]{:S(2)}) collective-permute-start(f32[5,16,256]{2,1,0:T(8,128)S(1)} %get-tuple-element.47), channel_id=1, source_target_pairs={{1,0},{2,1},{3,2},{4,3},{5,4},{6,5},{7,6},{9,8},{10,9},{11,10},{12... | collective-permute-start | bytes 245768 | tf_op jit(solution)/shard_map/ppermute | solution.py:478
  82.8 2.8 %collective-permute-start.11 = (f32[5,16,256]{2,1,0:T(8,128)S(1)}, f32[5,16,256]{2,1,0:T(8,128)S(1)}, u32[]{:S(2)}, u32[]{:S(2)}) collective-permute-start(f32[5,16,256]{2,1,0:T(8,128)S(1)} %get-tuple-element.48), channel_id=1, source_target_pairs={{0,8},{8,16},{16,24},{1,9},{9,17},{17,25},{2,10},{10,18},{18,26},{... | collective-permute-start | bytes 245768 | tf_op jit(solution)/shard_map/ppermute | solution.py:478
  85.6 1.9 %collective-permute-start.12 = (f32[5,16,256]{2,1,0:T(8,128)S(1)}, f32[5,16,256]{2,1,0:T(8,128)S(1)}, u32[]{:S(2)}, u32[]{:S(2)}) collective-permute-start(f32[5,16,256]{2,1,0:T(8,128)S(1)} %get-tuple-element.49), channel_id=1, source_target_pairs={{8,0},{16,8},{24,16},{9,1},{17,9},{25,17},{10,2},{18,10},{26,18},{... | collective-permute-start | bytes 245768 | tf_op jit(solution)/shard_map/ppermute | solution.py:478
  87.5 0.1 pad_maximum_fusion.2.refs_1_
  87.6 0.0 collective-permute-done.9.refs_5_
  87.6 0.0 collective-permute-done.10.refs_6_
  87.6 0.0 collective-permute-done.11.refs_7_
  87.6 3.7 %collective-permute-done.12.refs_8_ = f32[5,16,256]{2,1,0:T(8,128)S(1)} collective-permute-done((f32[5,16,256]{2,1,0:T(8,128)S(1)}, f32[5,16,256]{2,1,0:T(8,128)S(1)}, u32[]{:S(2)}, u32[]{:S(2)}) %collective-permute-start.12) | collective-permute-done | bytes 81952 | tf_op jit(solution)/shard_map/ppermute | solution.py:478
  91.4 3.2 %step_one.1 = (f32[16,80,256]{2,1,0:T(8,128)S(1)}, f32[5,16,256]{2,1,0:T(8,128)S(1)}, f32[5,16,256]{2,1,0:T(8,128)S(1)}, f32[5,16,256]{2,1,0:T(8,128)S(1)}, f32[5,16,256]{2,1,0:T(8,128)S(1)}) custom-call(bf16[240,240]{1,0:T(8,128)(2,1)S(1)} %pad_maximum_fusion.1.refs_0_, bf16[80,240]{1,0:T(8,128)(2,1)S(1)} %pad_maximum_fusion.2.refs_1_, ...), custom_call_target="tpu_custom_call" | custom-call | tf_op jit(solution)/shard_map/step_one/pallas_call | solution.py:463
  94.6 4.5 %collective-permute-start.13 = (f32[5,16,256]{2,1,0:T(8,128)S(1)}, f32[5,16,256]{2,1,0:T(8,128)S(1)}, u32[]{:S(2)}, u32[]{:S(2)}) collective-permute-start(f32[5,16,256]{2,1,0:T(8,128)S(1)} %get-tuple-element.55), channel_id=1, source_target_pairs={{0,1},{1,2},{2,3},{3,4},{4,5},{5,6},{6,7},{8,9},{9,10},{10,11},{11... | collective-permute-start | bytes 245768 | tf_op jit(solution)/shard_map/ppermute | solution.py:478
  99.1 1.9 %collective-permute-start.14 = (f32[5,16,256]{2,1,0:T(8,128)S(1)}, f32[5,16,256]{2,1,0:T(8,128)S(1)}, u32[]{:S(2)}, u32[]{:S(2)}) collective-permute-start(f32[5,16,256]{2,1,0:T(8,128)S(1)} %get-tuple-element.56), channel_id=1, source_target_pairs={{1,0},{2,1},{3,2},{4,3},{5,4},{6,5},{7,6},{9,8},{10,9},{11,10},{12... | collective-permute-start | bytes 245768 | tf_op jit(solution)/shard_map/ppermute | solution.py:478
  101.0 2.1 %collective-permute-start.15 = (f32[5,16,256]{2,1,0:T(8,128)S(1)}, f32[5,16,256]{2,1,0:T(8,128)S(1)}, u32[]{:S(2)}, u32[]{:S(2)}) collective-permute-start(f32[5,16,256]{2,1,0:T(8,128)S(1)} %get-tuple-element.57), channel_id=1, source_target_pairs={{0,8},{8,16},{16,24},{1,9},{9,17},{17,25},{2,10},{10,18},{18,26},{... | collective-permute-start | bytes 245768 | tf_op jit(solution)/shard_map/ppermute | solution.py:478
  103.2 2.2 %collective-permute-start.16 = (f32[5,16,256]{2,1,0:T(8,128)S(1)}, f32[5,16,256]{2,1,0:T(8,128)S(1)}, u32[]{:S(2)}, u32[]{:S(2)}) collective-permute-start(f32[5,16,256]{2,1,0:T(8,128)S(1)} %get-tuple-element.58), channel_id=1, source_target_pairs={{8,0},{16,8},{24,16},{9,1},{17,9},{25,17},{10,2},{18,10},{26,18},{... | collective-permute-start | bytes 245768 | tf_op jit(solution)/shard_map/ppermute | solution.py:478
  105.4 0.0 collective-permute-done.13.refs_5_
  105.4 0.0 collective-permute-done.14.refs_6_
  105.4 0.0 collective-permute-done.15.refs_7_
  105.4 3.5 %collective-permute-done.16.refs_8_ = f32[5,16,256]{2,1,0:T(8,128)S(1)} collective-permute-done((f32[5,16,256]{2,1,0:T(8,128)S(1)}, f32[5,16,256]{2,1,0:T(8,128)S(1)}, u32[]{:S(2)}, u32[]{:S(2)}) %collective-permute-start.16) | collective-permute-done | bytes 81952 | tf_op jit(solution)/shard_map/ppermute | solution.py:478
  108.9 4.1 %step_two.1 = f32[5,16,16,256]{3,2,1,0:T(8,128)} custom-call(bf16[240,240]{1,0:T(8,128)(2,1)S(1)} %pad_maximum_fusion.1.refs_0_, bf16[80,240]{1,0:T(8,128)(2,1)S(1)} %pad_maximum_fusion.2.refs_1_, f32[5,16,16,256]{3,2,1,0:T(8,128)S(1)} %copy-done, s32[16,16,256]{2,1,0:T(8,128)S(1)} %copy-done.1, f32[16,80,256]{2,1,0:T(8,128)S(1)} %get-tuple-element.54.refs_4_, ...), custom_call_target="tpu_custom_call" | custom-call | tf_op jit(solution)/shard_map/step_two/pallas_call | solution.py:463
  (17 shorter events, 0.1 us)
Async XLA Ops:
  0.0 8.2 %copy-start.8 = (f32[10,160,1]{1,0,2:T(8,128)S(1)}, f32[10,160,1]{1,0,2:T(8,128)}, u32[]{:S(2)}) copy-start(f32[10,160,1]{1,0,2:T(8,128)} %constant.26) | copy-start | bytes 19204
  0.0 11.9 %copy-start.7 = (f32[80,160]{1,0:T(8,128)S(1)}, f32[80,160]{1,0:T(8,128)}, u32[]{:S(2)}) copy-start(f32[80,160]{1,0:T(8,128)} %constant.19.clone) | copy-start | bytes 153604
  0.0 11.9 %copy-start.10 = (f32[80,5,1]{0,1,2:T(8,128)S(1)}, f32[80,5,1]{0,1,2:T(8,128)}, u32[]{:S(2)}) copy-start(f32[80,5,1]{0,1,2:T(8,128)} %constant.27) | copy-start | bytes 4804
  0.0 8.2 %copy-start.9 = (f32[3,5,5]{2,0,1:T(4,128)S(1)}, f32[3,5,5]{2,0,1:T(4,128)}, u32[]{:S(2)}) copy-start(f32[3,5,5]{2,0,1:T(4,128)} %param.18) | copy-start | bytes 904
  8.1 2.4 %collective-permute-start = (f32[16]{0:T(128)S(1)}, f32[16]{0:T(128)S(1)}, u32[]{:S(2)}, u32[]{:S(2)}) collective-permute-start(f32[16]{0:T(128)S(1)} %reduce_sum.9), channel_id=1, source_target_pairs={{0,1},{1,0},{2,3},{3,2},{4,5},{5,4},{6,7},{7,6},{8,9},{9,8},{10,11... | collective-permute-start | bytes 200 | tf_op jit(solution)/shard_map/ppermute | solution.py:492
  10.6 2.4 %collective-permute-start.1 = (f32[16]{0:T(128)S(1)}, f32[16]{0:T(128)S(1)}, u32[]{:S(2)}, u32[]{:S(2)}) collective-permute-start(f32[16]{0:T(128)S(1)} %add.18), channel_id=1, source_target_pairs={{0,2},{1,3},{2,0},{3,1},{4,6},{5,7},{6,4},{7,5},{8,10},{9,11},{10,... | collective-permute-start | bytes 200 | tf_op jit(solution)/shard_map/ppermute | solution.py:492
  13.0 3.3 %collective-permute-start.2 = (f32[16]{0:T(128)S(1)}, f32[16]{0:T(128)S(1)}, u32[]{:S(2)}, u32[]{:S(2)}) collective-permute-start(f32[16]{0:T(128)S(1)} %add.19), channel_id=1, source_target_pairs={{0,4},{1,5},{2,6},{3,7},{4,0},{5,1},{6,2},{7,3},{8,12},{9,13},{10,... | collective-permute-start | bytes 200 | tf_op jit(solution)/shard_map/ppermute | solution.py:492
  16.3 6.4 %collective-permute-start.3 = (f32[16]{0:T(128)S(1)}, f32[16]{0:T(128)S(1)}, u32[]{:S(2)}, u32[]{:S(2)}) collective-permute-start(f32[16]{0:T(128)S(1)} %add.20), channel_id=1, source_target_pairs={{0,8},{8,0},{16,24},{24,16},{1,9},{9,1},{17,25},{25,17},{2,10},{10... | collective-permute-start | bytes 200 | tf_op jit(solution)/shard_map/ppermute | solution.py:492
  22.7 9.4 %collective-permute-start.4 = (f32[16]{0:T(128)S(1)}, f32[16]{0:T(128)S(1)}, u32[]{:S(2)}, u32[]{:S(2)}) collective-permute-start(f32[16]{0:T(128)S(1)} %add.21), channel_id=1, source_target_pairs={{0,16},{8,24},{16,0},{24,8},{1,17},{9,25},{17,1},{25,9},{2,18},{10... | collective-permute-start | bytes 200 | tf_op jit(solution)/shard_map/ppermute | solution.py:492
  24.0 8.1 %copy-start = (f32[5,16,16,256]{3,2,1,0:T(8,128)S(1)}, f32[5,16,16,256]{3,2,1,0:T(8,128)}, u32[]{:S(2)}) copy-start(f32[5,16,16,256]{3,2,1,0:T(8,128)} %refs_2_.3) | copy-start | bytes 3932164
  24.0 8.1 %copy-start.2 = (bf16[20,5,16,256]{3,2,1,0:T(8,128)(2,1)S(1)}, bf16[20,5,16,256]{3,2,1,0:T(8,128)(2,1)}, u32[]{:S(2)}) copy-start(bf16[20,5,16,256]{3,2,1,0:T(8,128)(2,1)} %get-tuple-element.40.refs_3_) | copy-start | bytes 2457604
  24.0 8.1 %copy-start.3 = (s32[16]{0:T(128)S(1)}, s32[16]{0:T(128)}, u32[]{:S(2)}) copy-start(s32[16]{0:T(128)} %refs_0_.1) | copy-start | bytes 196
  32.1 13.1 %copy-start.4 = (f32[1,80,160]{2,1,0:T(8,128)S(1)}, f32[1,80,160]{2,1,0:T(8,128)}, u32[]{:S(2)}) copy-start(f32[1,80,160]{2,1,0:T(8,128)} %constant.24) | copy-start | bytes 153604
  32.1 13.1 %copy-start.5 = (f32[1,80,160]{2,1,0:T(8,128)S(1)}, f32[1,80,160]{2,1,0:T(8,128)}, u32[]{:S(2)}) copy-start(f32[1,80,160]{2,1,0:T(8,128)} %constant.23) | copy-start | bytes 153604
  32.2 13.1 %copy-start.6 = (f32[1,80,160]{2,1,0:T(8,128)S(1)}, f32[1,80,160]{2,1,0:T(8,128)}, u32[]{:S(2)}) copy-start(f32[1,80,160]{2,1,0:T(8,128)} %constant.22) | copy-start | bytes 153604
  33.7 39.1 %collective-permute-start.5 = (bf16[20,5,16,256]{3,2,1,0:T(8,128)(2,1)S(1)}, bf16[20,5,16,256]{3,2,1,0:T(8,128)(2,1)}, u32[]{:S(2)}, u32[]{:S(2)}) collective-permute-start(bf16[20,5,16,256]{3,2,1,0:T(8,128)(2,1)S(1)} %get-tuple-element.41), channel_id=1, source_target_pairs={{0,1},{1,2},{2,3},{3,4},{4,5},{5,6},{6,7},{8,9},{9,10},{10,11},{11... | collective-permute-start | bytes 2457608 | tf_op jit(solution)/shard_map/ppermute | solution.py:478
  36.8 36.0 %collective-permute-start.6 = (bf16[20,5,16,256]{3,2,1,0:T(8,128)(2,1)S(1)}, bf16[20,5,16,256]{3,2,1,0:T(8,128)(2,1)}, u32[]{:S(2)}, u32[]{:S(2)}) collective-permute-start(bf16[20,5,16,256]{3,2,1,0:T(8,128)(2,1)S(1)} %get-tuple-element.42), channel_id=1, source_target_pairs={{1,0},{2,1},{3,2},{4,3},{5,4},{6,5},{7,6},{9,8},{10,9},{11,10},{12... | collective-permute-start | bytes 2457608 | tf_op jit(solution)/shard_map/ppermute | solution.py:478
  39.9 32.9 %collective-permute-start.7 = (bf16[20,5,16,256]{3,2,1,0:T(8,128)(2,1)S(1)}, bf16[20,5,16,256]{3,2,1,0:T(8,128)(2,1)}, u32[]{:S(2)}, u32[]{:S(2)}) collective-permute-start(bf16[20,5,16,256]{3,2,1,0:T(8,128)(2,1)S(1)} %get-tuple-element.43), channel_id=1, source_target_pairs={{0,8},{8,16},{16,24},{1,9},{9,17},{17,25},{2,10},{10,18},{18,26},{... | collective-permute-start | bytes 2457608 | tf_op jit(solution)/shard_map/ppermute | solution.py:478
  42.8 30.1 %collective-permute-start.8 = (bf16[20,5,16,256]{3,2,1,0:T(8,128)(2,1)S(1)}, bf16[20,5,16,256]{3,2,1,0:T(8,128)(2,1)}, u32[]{:S(2)}, u32[]{:S(2)}) collective-permute-start(bf16[20,5,16,256]{3,2,1,0:T(8,128)(2,1)S(1)} %get-tuple-element.44), channel_id=1, source_target_pairs={{8,0},{16,8},{24,16},{9,1},{17,9},{25,17},{10,2},{18,10},{26,18},{... | collective-permute-start | bytes 2457608 | tf_op jit(solution)/shard_map/ppermute | solution.py:478
  45.3 27.5 %copy-start.1 = (s32[16,16,256]{2,1,0:T(8,128)S(1)}, s32[16,16,256]{2,1,0:T(8,128)}, u32[]{:S(2)}) copy-start(s32[16,16,256]{2,1,0:T(8,128)} %refs_3_.5) | copy-start | bytes 786436
  76.2 11.4 %collective-permute-start.9 = (f32[5,16,256]{2,1,0:T(8,128)S(1)}, f32[5,16,256]{2,1,0:T(8,128)S(1)}, u32[]{:S(2)}, u32[]{:S(2)}) collective-permute-start(f32[5,16,256]{2,1,0:T(8,128)S(1)} %get-tuple-element.46), channel_id=1, source_target_pairs={{0,1},{1,2},{2,3},{3,4},{4,5},{5,6},{6,7},{8,9},{9,10},{10,11},{11... | collective-permute-start | bytes 245768 | tf_op jit(solution)/shard_map/ppermute | solution.py:478
  80.8 6.8 %collective-permute-start.10 = (f32[5,16,256]{2,1,0:T(8,128)S(1)}, f32[5,16,256]{2,1,0:T(8,128)S(1)}, u32[]{:S(2)}, u32[]{:S(2)}) collective-permute-start(f32[5,16,256]{2,1,0:T(8,128)S(1)} %get-tuple-element.47), channel_id=1, source_target_pairs={{1,0},{2,1},{3,2},{4,3},{5,4},{6,5},{7,6},{9,8},{10,9},{11,10},{12... | collective-permute-start | bytes 245768 | tf_op jit(solution)/shard_map/ppermute | solution.py:478
  82.8 4.9 %collective-permute-start.11 = (f32[5,16,256]{2,1,0:T(8,128)S(1)}, f32[5,16,256]{2,1,0:T(8,128)S(1)}, u32[]{:S(2)}, u32[]{:S(2)}) collective-permute-start(f32[5,16,256]{2,1,0:T(8,128)S(1)} %get-tuple-element.48), channel_id=1, source_target_pairs={{0,8},{8,16},{16,24},{1,9},{9,17},{17,25},{2,10},{10,18},{18,26},{... | collective-permute-start | bytes 245768 | tf_op jit(solution)/shard_map/ppermute | solution.py:478
  85.6 5.8 %collective-permute-start.12 = (f32[5,16,256]{2,1,0:T(8,128)S(1)}, f32[5,16,256]{2,1,0:T(8,128)S(1)}, u32[]{:S(2)}, u32[]{:S(2)}) collective-permute-start(f32[5,16,256]{2,1,0:T(8,128)S(1)} %get-tuple-element.49), channel_id=1, source_target_pairs={{8,0},{16,8},{24,16},{9,1},{17,9},{25,17},{10,2},{18,10},{26,18},{... | collective-permute-start | bytes 245768 | tf_op jit(solution)/shard_map/ppermute | solution.py:478
  94.6 10.8 %collective-permute-start.13 = (f32[5,16,256]{2,1,0:T(8,128)S(1)}, f32[5,16,256]{2,1,0:T(8,128)S(1)}, u32[]{:S(2)}, u32[]{:S(2)}) collective-permute-start(f32[5,16,256]{2,1,0:T(8,128)S(1)} %get-tuple-element.55), channel_id=1, source_target_pairs={{0,1},{1,2},{2,3},{3,4},{4,5},{5,6},{6,7},{8,9},{9,10},{10,11},{11... | collective-permute-start | bytes 245768 | tf_op jit(solution)/shard_map/ppermute | solution.py:478
  99.1 6.3 %collective-permute-start.14 = (f32[5,16,256]{2,1,0:T(8,128)S(1)}, f32[5,16,256]{2,1,0:T(8,128)S(1)}, u32[]{:S(2)}, u32[]{:S(2)}) collective-permute-start(f32[5,16,256]{2,1,0:T(8,128)S(1)} %get-tuple-element.56), channel_id=1, source_target_pairs={{1,0},{2,1},{3,2},{4,3},{5,4},{6,5},{7,6},{9,8},{10,9},{11,10},{12... | collective-permute-start | bytes 245768 | tf_op jit(solution)/shard_map/ppermute | solution.py:478
  101.0 4.4 %collective-permute-start.15 = (f32[5,16,256]{2,1,0:T(8,128)S(1)}, f32[5,16,256]{2,1,0:T(8,128)S(1)}, u32[]{:S(2)}, u32[]{:S(2)}) collective-permute-start(f32[5,16,256]{2,1,0:T(8,128)S(1)} %get-tuple-element.57), channel_id=1, source_target_pairs={{0,8},{8,16},{16,24},{1,9},{9,17},{17,25},{2,10},{10,18},{18,26},{... | collective-permute-start | bytes 245768 | tf_op jit(solution)/shard_map/ppermute | solution.py:478
  103.2 5.8 %collective-permute-start.16 = (f32[5,16,256]{2,1,0:T(8,128)S(1)}, f32[5,16,256]{2,1,0:T(8,128)S(1)}, u32[]{:S(2)}, u32[]{:S(2)}) collective-permute-start(f32[5,16,256]{2,1,0:T(8,128)S(1)} %get-tuple-element.58), channel_id=1, source_target_pairs={{8,0},{16,8},{24,16},{9,1},{17,9},{25,17},{10,2},{18,10},{26,18},{... | collective-permute-start | bytes 245768 | tf_op jit(solution)/shard_map/ppermute | solution.py:478

commit v11 on v10

--- a/solution.py
+++ b/solution.py
@@ -13,7 +13,6 @@
 GROUP = 4
 TAIL = 4
 TURN = 16
-PACK = 2
 LARGE = 51
 
 
@@ -48,38 +47,50 @@
     return [jnp.concatenate(o, axis=1) for o in out]
 
 
-def direct_kernel(src, xlo, xhi, ylo, yhi, energy, scratch):
-    group, nv, nx, ny, nz = src.shape
+def mode_copy(modes, buf, sem, m):
+    return pltpu.make_async_copy(modes.at[m], buf.at[m], sem.at[m])
+
+
+def direct_kernel(modes, xlo, xhi, ylo, yhi, energy, buf, scratch, sem):
+    nm, nv, nx, ny, nz = buf.shape
+    for m in range(nm):
+        mode_copy(modes, buf, sem, m).start()
 
     def body(m, carry):
-        xlo[m] = src[m, :, 0]
-        xhi[m] = src[m, :, nx - 1]
+        mode_copy(modes, buf, sem, m).wait()
+        xlo[m] = buf[m, :, 0]
+        xhi[m] = buf[m, :, nx - 1]
         total = jnp.zeros((ny, nz), F32)
         for i in range(nv):
-            cells = src[m, i].astype(F32)
+            cells = buf[m, i].astype(F32)
             lo, hi = edge_lines(cells, scratch.at[i])
             ylo[m, i] = lo.astype(BF16)
             yhi[m, i] = hi.astype(BF16)
             total = total + jnp.sum(cells * cells, axis=0)
         line = jnp.sum(total, axis=0, keepdims=True)
-        line = sum(line[:, h : h + LANES] for h in range(0, nz, LANES))
-        energy[pl.ds(pl.program_id(0) * group + m, 1), :] = line
-        return carry
-
-    lax.fori_loop(0, group, body, 0, unroll=2)
+        energy[pl.ds(m, 1), :] = sum(line[:, h : h + LANES] for h in range(0, nz, LANES))
+        return carry
+
+    lax.fori_loop(0, nm, body, 0)
+
+
+def mode_buffers(modes):
+    nm, nv, nx, ny, nz = modes.shape
+    return [
+        pltpu.VMEM(modes.shape, BF16),
+        pltpu.VMEM((nv, nz // LANES, nx * ny, LANES), F32),
+        pltpu.SemaphoreType.DMA((nm,)),
+    ]
 
 
 def pack(direct):
     nm, nv, nx, ny, nz = direct.shape
-    sizes = (ny, ny, nx, nx)
     return pl.pallas_call(
         direct_kernel,
-        grid=(nm // PACK,),
-        in_specs=[pl.BlockSpec((PACK, nv, nx, ny, nz), lambda s: (s, 0, 0, 0, 0))],
-        out_specs=[pl.BlockSpec((PACK, nv, n, nz), lambda s: (s, 0, 0, 0)) for n in sizes]
-        + [pl.BlockSpec((nm, LANES), lambda s: (0, 0))],
-        out_shape=[sds((nm + TAIL, nv, n, nz), BF16) for n in sizes] + [sds((nm, LANES), F32)],
-        scratch_shapes=[pltpu.VMEM((nv, nz // LANES, nx * ny, LANES), F32)],
+        in_specs=[in_hbm()],
+        out_specs=[in_vmem()] * 5,
+        out_shape=[sds((nm + TAIL, nv, n, nz), BF16) for n in (ny, ny, nx, nx)] + [sds((nm, LANES), F32)],
+        scratch_shapes=mode_buffers(direct),
         compiler_params=params(LARGE),
         cost_estimate=pl.CostEstimate(flops=3 * direct.size, bytes_accessed=2 * direct.size, transcendentals=0),
         name="pack_direct",
@@ -120,33 +131,31 @@
     )(lw, modes, modes)
 
 
-def mix_normal_kernel(lw, src, w_lo, w_hi, scratch):
-    group, nv, nx, ny, nz = src.shape
+def mix_normal_kernel(lw, modes, w_lo, w_hi, buf, scratch, sem):
+    nm, nv, nx, ny, nz = buf.shape
+    for m in range(nm):
+        mode_copy(modes, buf, sem, m).start()
 
     def body(m, carry):
-        lines = [edge_lines(src[m, i].astype(F32), scratch.at[i]) for i in range(nv)]
+        mode_copy(modes, buf, sem, m).wait()
+        lines = [edge_lines(buf[m, i].astype(F32), scratch.at[i]) for i in range(nv)]
         for side, out in enumerate((w_lo, w_hi)):
             face = jnp.concatenate([line[side] for line in lines], axis=0).astype(BF16)
             out[m] = jnp.dot(lw[...], jnp.concatenate([face, face], axis=0), preferred_element_type=F32)
         return carry
 
-    lax.fori_loop(0, group, body, 0, unroll=2)
+    lax.fori_loop(0, nm, body, 0)
 
 
 def mix_normal(lw, modes):
     nm, nv, nx, ny, nz = modes.shape
     w = sds((nm, nv * nx, nz), F32)
-    out = pl.BlockSpec((PACK, nv * nx, nz), lambda s: (s, 0, 0))
     return pl.pallas_call(
         mix_normal_kernel,
-        grid=(nm // PACK,),
-        in_specs=[
-            pl.BlockSpec(lw.shape, lambda s: (0, 0)),
-            pl.BlockSpec((PACK, nv, nx, ny, nz), lambda s: (s, 0, 0, 0, 0)),
-        ],
-        out_specs=[out, out],
+        in_specs=[in_vmem(), in_hbm()],
+        out_specs=[in_vmem()] * 2,
         out_shape=[w, w],
-        scratch_shapes=[pltpu.VMEM((nv, nz // LANES, nx * ny, LANES), F32)],
+        scratch_shapes=mode_buffers(modes),
         compiler_params=params(LARGE),
         cost_estimate=pl.CostEstimate(flops=3 * modes.size, bytes_accessed=3 * modes.size, transcendentals=0),
         name="mix_normal",

time: 115 us -> 110 us (0.957)
  Pallas kernels: 52.9 us -> 47.9 us
    pallas_call x2, Pallas kernels: 16.1 us -> 11 us  [the longest x1 5.79 us: mix_normal(): pl.pallas_call(mix_normal_kernel, in_specs=[in_vmem(), in_hbm()], out_spe...]
  transfers between devices with their start and end apart: 17 -> 17, of which waited for: 6 -> 6; matrix products, arithmetic and copies ran while one was open for 1% -> 1% of each run, Pallas kernels for 29% -> 28%
where the time goes in v11:
time: 110 us; the launch traced here: 108 us
  Pallas kernels  47.9 us (44%)
  starting transfers between devices  42.5 us (39%)
  waiting for transfers between devices  15.9 us (14%)
    ppermute x12, starting transfers between devices, exchange_axis(): return [lax.ppermute(hi, axis, up), lax.ppermute(lo, axis, down)]  33.5 us
    pallas_call x1, Pallas kernels, main(): pl.pallas_call(main_kernel, in_specs=[in_smem(), in_smem(), in_vmem(), in...  22.5 us
    ppermute x12, waiting for transfers between devices, exchange_axis(): return [lax.ppermute(hi, axis, up), lax.ppermute(lo, axis, down)]  12.2 us
    ppermute x5, starting transfers between devices, sum_over(): lax.ppermute(values, axis, [(i, i ^ bit) for i in range(count)])  9.07 us
    pallas_call x2, Pallas kernels, apply_step(): pl.pallas_call(lambda *refs: step_kernel(last, *refs), in_specs=[in_vmem(...  7.27 us
    pallas_call x1, Pallas kernels, mix_normal(): pl.pallas_call(mix_normal_kernel, in_specs=[in_vmem(), in_hbm()], out_spe...  5.79 us
    pallas_call x1, Pallas kernels, pack(): pl.pallas_call(direct_kernel, in_specs=[in_hbm()], out_specs=[in_vmem()]...  5.19 us
    ppermute x5, waiting for transfers between devices, sum_over(): lax.ppermute(values, axis, [(i, i ^ bit) for i in range(count)])  3.76 us
  transfers between devices with their start and end apart: 17, of which 6 were waited for; matrix products, arithmetic and copies ran while one was open for 1% of the time, Pallas kernels for 28%

profile of v11, /device:TPU:5, one launch (start us, length us, event | category | flops | bytes accessed | tf_op | source)
XLA Modules:
  0.0 107.9 jit_solution(17177891394021855874)
XLA Ops:
  0.0 0.0 copy-start.7
  0.0 0.0 copy-start.9
  0.0 5.2 %pack_direct.1 = (bf16[20,5,16,256]{3,2,1,0:T(8,128)(2,1)S(1)}, bf16[20,5,16,256]{3,2,1,0:T(8,128)(2,1)S(1)}, bf16[20,5,16,256]{3,2,1,0:T(8,128)(2,1)S(1)}, bf16...) custom-call(bf16[16,5,16,16,256]{4,3,2,1,0:T(8,128)(2,1)} %u_hbm.1), custom_call_target="tpu_custom_call" | custom-call | flops 15728640 | bytes 10485760 | tf_op jit(solution)/shard_map/pack_direct/pallas_call | solution.py:88
  5.2 0.1 reduce_sum.9
  5.3 0.1 collective-permute-start
  5.4 0.0 copy-done.9
  5.4 0.0 copy-done.8
  5.5 0.2 fusion.6
  5.7 2.1 %collective-permute-done = f32[16]{0:T(128)S(1)} collective-permute-done((f32[16]{0:T(128)S(1)}, f32[16]{0:T(128)S(1)}, u32[]{:S(2)}, u32[]{:S(2)}) %collective-permute-start) | collective-permute-done | bytes 96 | tf_op jit(solution)/shard_map/ppermute | solution.py:501
  7.8 1.3 %collective-permute-start.1 = (f32[16]{0:T(128)S(1)}, f32[16]{0:T(128)S(1)}, u32[]{:S(2)}, u32[]{:S(2)}) collective-permute-start(f32[16]{0:T(128)S(1)} %add.18), channel_id=1, source_target_pairs={{0,2},{1,3},{2,0},{3,1},{4,6},{5,7},{6,4},{7,5},{8,10},{9,11},{10,... | collective-permute-start | bytes 200 | tf_op jit(solution)/shard_map/ppermute | solution.py:501
  9.1 0.0 copy-done.7
  9.1 0.0 copy-done.10
  9.1 0.4 multiply_convert_fusion
  9.5 0.7 collective-permute-done.1
  10.2 2.3 %collective-permute-start.2 = (f32[16]{0:T(128)S(1)}, f32[16]{0:T(128)S(1)}, u32[]{:S(2)}, u32[]{:S(2)}) collective-permute-start(f32[16]{0:T(128)S(1)} %add.19), channel_id=1, source_target_pairs={{0,4},{1,5},{2,6},{3,7},{4,0},{5,1},{6,2},{7,3},{8,12},{9,13},{10,... | collective-permute-start | bytes 200 | tf_op jit(solution)/shard_map/ppermute | solution.py:501
  12.5 1.0 collective-permute-done.2
  13.5 4.1 %collective-permute-start.3 = (f32[16]{0:T(128)S(1)}, f32[16]{0:T(128)S(1)}, u32[]{:S(2)}, u32[]{:S(2)}) collective-permute-start(f32[16]{0:T(128)S(1)} %add.20), channel_id=1, source_target_pairs={{0,8},{8,0},{16,24},{24,16},{1,9},{9,1},{17,25},{25,17},{2,10},{10... | collective-permute-start | bytes 200 | tf_op jit(solution)/shard_map/ppermute | solution.py:501
  17.6 2.3 %mix_chord.1 = (f32[16,80,256]{2,1,0:T(8,128)S(1)}, f32[16,80,256]{2,1,0:T(8,128)S(1)}) custom-call(bf16[80,160]{1,0:T(8,128)(2,1)S(1)} %get-tuple-element.63.lw, bf16[16,5,16,16,256]{4,3,2,1,0:T(8,128)(2,1)} %modes.3, bf16[16,5,16,16,256]{4,3,2,1,0:T(8,128)(2,1)} %modes.3), custom_call_target="tpu_custom_call" | custom-call | flops 100000000 | bytes 6000000 | tf_op jit(solution)/shard_map/mix_chord/pallas_call | solution.py:118
  19.9 0.0 collective-permute-done.3
  19.9 1.3 %collective-permute-start.4 = (f32[16]{0:T(128)S(1)}, f32[16]{0:T(128)S(1)}, u32[]{:S(2)}, u32[]{:S(2)}) collective-permute-start(f32[16]{0:T(128)S(1)} %add.21), channel_id=1, source_target_pairs={{0,16},{8,24},{16,0},{24,8},{1,17},{9,25},{17,1},{25,9},{2,18},{10... | collective-permute-start | bytes 200 | tf_op jit(solution)/shard_map/ppermute | solution.py:501
  21.2 5.8 %mix_normal.1 = (f32[16,80,256]{2,1,0:T(8,128)S(1)}, f32[16,80,256]{2,1,0:T(8,128)S(1)}) custom-call(bf16[80,160]{1,0:T(8,128)(2,1)S(1)} %get-tuple-element.64.lw, bf16[16,5,16,16,256]{4,3,2,1,0:T(8,128)(2,1)} %modes.3), custom_call_target="tpu_custom_call" | custom-call | flops 15728640 | bytes 15728640 | tf_op jit(solution)/shard_map/mix_normal/pallas_call | solution.py:153
  27.0 0.0 collective-permute-done.4
  27.0 0.0 copy-done
  27.0 0.0 copy-done.2
  27.0 0.0 copy-done.3
  27.0 0.0 copy-start.4
  27.1 0.0 copy-start.5
  27.1 0.0 copy-start.6
  27.1 1.5 %faces.1 = (bf16[20,5,16,256]{3,2,1,0:T(8,128)(2,1)S(1)}, bf16[20,5,16,256]{3,2,1,0:T(8,128)(2,1)S(1)}, bf16[20,5,16,256]{3,2,1,0:T(8,128)(2,1)S(1)}, bf16[20,5,16,256]{3,2,1,0:T(8,128)(2,1)S(1)}) custom-call(s32[16]{0:T(128)S(1)} %copy-done.3, ...), custom_call_target="tpu_custom_call", output_to_operand_aliasing={{0}: (3, {}), {1}: (4, {}), {2}: (5, {}), {3}: (6, {})} | custom-call | tf_op jit(solution)/shard_map/faces/pallas_call | solution.py:201
  28.6 3.1 %collective-permute-start.5 = (bf16[20,5,16,256]{3,2,1,0:T(8,128)(2,1)S(1)}, bf16[20,5,16,256]{3,2,1,0:T(8,128)(2,1)}, u32[]{:S(2)}, u32[]{:S(2)}) collective-permute-start(bf16[20,5,16,256]{3,2,1,0:T(8,128)(2,1)S(1)} %get-tuple-element.41), channel_id=1, source_target_pairs={{0,1},{1,2},{2,3},{3,4},{4,5},{5,6},{6,7},{8,9},{9,10},{10,11},{11... | collective-permute-start | bytes 2457608 | tf_op jit(solution)/shard_map/ppermute | solution.py:487
  31.7 3.0 %collective-permute-start.6 = (bf16[20,5,16,256]{3,2,1,0:T(8,128)(2,1)S(1)}, bf16[20,5,16,256]{3,2,1,0:T(8,128)(2,1)}, u32[]{:S(2)}, u32[]{:S(2)}) collective-permute-start(bf16[20,5,16,256]{3,2,1,0:T(8,128)(2,1)S(1)} %get-tuple-element.42), channel_id=1, source_target_pairs={{1,0},{2,1},{3,2},{4,3},{5,4},{6,5},{7,6},{9,8},{10,9},{11,10},{12... | collective-permute-start | bytes 2457608 | tf_op jit(solution)/shard_map/ppermute | solution.py:487
  34.8 2.9 %collective-permute-start.7 = (bf16[20,5,16,256]{3,2,1,0:T(8,128)(2,1)S(1)}, bf16[20,5,16,256]{3,2,1,0:T(8,128)(2,1)}, u32[]{:S(2)}, u32[]{:S(2)}) collective-permute-start(bf16[20,5,16,256]{3,2,1,0:T(8,128)(2,1)S(1)} %get-tuple-element.43), channel_id=1, source_target_pairs={{0,8},{8,16},{16,24},{1,9},{9,17},{17,25},{2,10},{10,18},{18,26},{... | collective-permute-start | bytes 2457608 | tf_op jit(solution)/shard_map/ppermute | solution.py:487
  37.7 2.3 %collective-permute-start.8 = (bf16[20,5,16,256]{3,2,1,0:T(8,128)(2,1)S(1)}, bf16[20,5,16,256]{3,2,1,0:T(8,128)(2,1)}, u32[]{:S(2)}, u32[]{:S(2)}) collective-permute-start(bf16[20,5,16,256]{3,2,1,0:T(8,128)(2,1)S(1)} %get-tuple-element.44), channel_id=1, source_target_pairs={{8,0},{16,8},{24,16},{9,1},{17,9},{25,17},{10,2},{18,10},{26,18},{... | collective-permute-start | bytes 2457608 | tf_op jit(solution)/shard_map/ppermute | solution.py:487
  40.0 0.1 pad_maximum_fusion.1.refs_0_
  40.1 0.0 copy-done.4
  40.1 0.0 copy-done.5
  40.1 0.0 copy-done.6
  40.2 0.0 copy-start.1
  40.2 22.5 %main.1.refs_2_ = f32[16,80,256]{2,1,0:T(8,128)S(1)} custom-call(s32[16]{0:T(128)S(1)} %copy-done.3, f32[16]{0:T(128)S(1)} %add_rsqrt_fusion.amp.refs_1_, bf16[320,160]{1,0:T(8,128)(2,1)S(1)} %pad_maximum_fusion.lw, bf16[16,5,16,16,256]{4,3,2,1,0:T(8,128)(2,1)} %u_hbm.1, bf16[16,5,16,16,256]{4,3,2,1,0:T(8,128)(2,1)} %modes.3), custom_call_target="tpu_custom_call" | custom-call | flops 1000000 | bytes 100000 | tf_op jit(solution)/shard_map/main/pallas_call | solution.py:316
  62.8 4.9 %collective-permute-done.5.refs_8_ = bf16[20,5,16,256]{3,2,1,0:T(8,128)(2,1)} collective-permute-done((bf16[20,5,16,256]{3,2,1,0:T(8,128)(2,1)S(1)}, bf16[20,5,16,256]{3,2,1,0:T(8,128)(2,1)}, u32[]{:S(2)}, u32[]{:S(2)}) %collective-permute-start.5) | collective-permute-done | bytes 819232 | tf_op jit(solution)/shard_map/ppermute | solution.py:487
  67.7 0.0 collective-permute-done.6.refs_9_
  67.7 0.0 collective-permute-done.7.refs_10_
  67.7 0.0 collective-permute-done.8.refs_11_
  67.7 0.0 copy-done.1
  67.7 3.4 %boundary.1 = (f32[16,80,256]{2,1,0:T(8,128)S(1)}, f32[5,16,256]{2,1,0:T(8,128)S(1)}, f32[5,16,256]{2,1,0:T(8,128)S(1)}, f32[5,16,256]{2,1,0:T(8,128)S(1)}, f32[...) custom-call(s32[16]{0:T(128)S(1)} %copy-done.3, ...), custom_call_target="tpu_custom_call" | custom-call | tf_op jit(solution)/shard_map/boundary/pallas_call | solution.py:393
  71.1 4.6 %collective-permute-start.9 = (f32[5,16,256]{2,1,0:T(8,128)S(1)}, f32[5,16,256]{2,1,0:T(8,128)S(1)}, u32[]{:S(2)}, u32[]{:S(2)}) collective-permute-start(f32[5,16,256]{2,1,0:T(8,128)S(1)} %get-tuple-element.46), channel_id=1, source_target_pairs={{0,1},{1,2},{2,3},{3,4},{4,5},{5,6},{6,7},{8,9},{9,10},{10,11},{11... | collective-permute-start | bytes 245768 | tf_op jit(solution)/shard_map/ppermute | solution.py:487
  75.8 1.9 %collective-permute-start.10 = (f32[5,16,256]{2,1,0:T(8,128)S(1)}, f32[5,16,256]{2,1,0:T(8,128)S(1)}, u32[]{:S(2)}, u32[]{:S(2)}) collective-permute-start(f32[5,16,256]{2,1,0:T(8,128)S(1)} %get-tuple-element.47), channel_id=1, source_target_pairs={{1,0},{2,1},{3,2},{4,3},{5,4},{6,5},{7,6},{9,8},{10,9},{11,10},{12... | collective-permute-start | bytes 245768 | tf_op jit(solution)/shard_map/ppermute | solution.py:487
  77.7 2.8 %collective-permute-start.11 = (f32[5,16,256]{2,1,0:T(8,128)S(1)}, f32[5,16,256]{2,1,0:T(8,128)S(1)}, u32[]{:S(2)}, u32[]{:S(2)}) collective-permute-start(f32[5,16,256]{2,1,0:T(8,128)S(1)} %get-tuple-element.48), channel_id=1, source_target_pairs={{0,8},{8,16},{16,24},{1,9},{9,17},{17,25},{2,10},{10,18},{18,26},{... | collective-permute-start | bytes 245768 | tf_op jit(solution)/shard_map/ppermute | solution.py:487
  80.5 1.9 %collective-permute-start.12 = (f32[5,16,256]{2,1,0:T(8,128)S(1)}, f32[5,16,256]{2,1,0:T(8,128)S(1)}, u32[]{:S(2)}, u32[]{:S(2)}) collective-permute-start(f32[5,16,256]{2,1,0:T(8,128)S(1)} %get-tuple-element.49), channel_id=1, source_target_pairs={{8,0},{16,8},{24,16},{9,1},{17,9},{25,17},{10,2},{18,10},{26,18},{... | collective-permute-start | bytes 245768 | tf_op jit(solution)/shard_map/ppermute | solution.py:487
  82.4 0.1 pad_maximum_fusion.2.refs_1_
  82.5 0.0 collective-permute-done.9.refs_5_
  82.5 0.0 collective-permute-done.10.refs_6_
  82.5 0.0 collective-permute-done.11.refs_7_
  82.6 3.7 %collective-permute-done.12.refs_8_ = f32[5,16,256]{2,1,0:T(8,128)S(1)} collective-permute-done((f32[5,16,256]{2,1,0:T(8,128)S(1)}, f32[5,16,256]{2,1,0:T(8,128)S(1)}, u32[]{:S(2)}, u32[]{:S(2)}) %collective-permute-start.12) | collective-permute-done | bytes 81952 | tf_op jit(solution)/shard_map/ppermute | solution.py:487
  86.3 3.2 %step_one.1 = (f32[16,80,256]{2,1,0:T(8,128)S(1)}, f32[5,16,256]{2,1,0:T(8,128)S(1)}, f32[5,16,256]{2,1,0:T(8,128)S(1)}, f32[5,16,256]{2,1,0:T(8,128)S(1)}, f32[5,16,256]{2,1,0:T(8,128)S(1)}) custom-call(bf16[240,240]{1,0:T(8,128)(2,1)S(1)} %pad_maximum_fusion.1.refs_0_, bf16[80,240]{1,0:T(8,128)(2,1)S(1)} %pad_maximum_fusion.2.refs_1_, ...), custom_call_target="tpu_custom_call" | custom-call | tf_op jit(solution)/shard_map/step_one/pallas_call | solution.py:472
  89.5 4.5 %collective-permute-start.13 = (f32[5,16,256]{2,1,0:T(8,128)S(1)}, f32[5,16,256]{2,1,0:T(8,128)S(1)}, u32[]{:S(2)}, u32[]{:S(2)}) collective-permute-start(f32[5,16,256]{2,1,0:T(8,128)S(1)} %get-tuple-element.55), channel_id=1, source_target_pairs={{0,1},{1,2},{2,3},{3,4},{4,5},{5,6},{6,7},{8,9},{9,10},{10,11},{11... | collective-permute-start | bytes 245768 | tf_op jit(solution)/shard_map/ppermute | solution.py:487
  94.0 1.9 %collective-permute-start.14 = (f32[5,16,256]{2,1,0:T(8,128)S(1)}, f32[5,16,256]{2,1,0:T(8,128)S(1)}, u32[]{:S(2)}, u32[]{:S(2)}) collective-permute-start(f32[5,16,256]{2,1,0:T(8,128)S(1)} %get-tuple-element.56), channel_id=1, source_target_pairs={{1,0},{2,1},{3,2},{4,3},{5,4},{6,5},{7,6},{9,8},{10,9},{11,10},{12... | collective-permute-start | bytes 245768 | tf_op jit(solution)/shard_map/ppermute | solution.py:487
  95.9 2.1 %collective-permute-start.15 = (f32[5,16,256]{2,1,0:T(8,128)S(1)}, f32[5,16,256]{2,1,0:T(8,128)S(1)}, u32[]{:S(2)}, u32[]{:S(2)}) collective-permute-start(f32[5,16,256]{2,1,0:T(8,128)S(1)} %get-tuple-element.57), channel_id=1, source_target_pairs={{0,8},{8,16},{16,24},{1,9},{9,17},{17,25},{2,10},{10,18},{18,26},{... | collective-permute-start | bytes 245768 | tf_op jit(solution)/shard_map/ppermute | solution.py:487
  98.1 2.2 %collective-permute-start.16 = (f32[5,16,256]{2,1,0:T(8,128)S(1)}, f32[5,16,256]{2,1,0:T(8,128)S(1)}, u32[]{:S(2)}, u32[]{:S(2)}) collective-permute-start(f32[5,16,256]{2,1,0:T(8,128)S(1)} %get-tuple-element.58), channel_id=1, source_target_pairs={{8,0},{16,8},{24,16},{9,1},{17,9},{25,17},{10,2},{18,10},{26,18},{... | collective-permute-start | bytes 245768 | tf_op jit(solution)/shard_map/ppermute | solution.py:487
  100.3 0.0 collective-permute-done.13.refs_5_
  100.3 0.0 collective-permute-done.14.refs_6_
  100.3 0.0 collective-permute-done.15.refs_7_
  100.3 3.5 %collective-permute-done.16.refs_8_ = f32[5,16,256]{2,1,0:T(8,128)S(1)} collective-permute-done((f32[5,16,256]{2,1,0:T(8,128)S(1)}, f32[5,16,256]{2,1,0:T(8,128)S(1)}, u32[]{:S(2)}, u32[]{:S(2)}) %collective-permute-start.16) | collective-permute-done | bytes 81952 | tf_op jit(solution)/shard_map/ppermute | solution.py:487
  103.8 4.1 %step_two.1 = f32[5,16,16,256]{3,2,1,0:T(8,128)} custom-call(bf16[240,240]{1,0:T(8,128)(2,1)S(1)} %pad_maximum_fusion.1.refs_0_, bf16[80,240]{1,0:T(8,128)(2,1)S(1)} %pad_maximum_fusion.2.refs_1_, f32[5,16,16,256]{3,2,1,0:T(8,128)S(1)} %copy-done, s32[16,16,256]{2,1,0:T(8,128)S(1)} %copy-done.1, f32[16,80,256]{2,1,0:T(8,128)S(1)} %get-tuple-element.54.refs_4_, ...), custom_call_target="tpu_custom_call" | custom-call | tf_op jit(solution)/shard_map/step_two/pallas_call | solution.py:472
  (17 shorter events, 0.1 us)
Async XLA Ops:
  0.0 5.4 %copy-start.8 = (f32[10,160,1]{1,0,2:T(8,128)S(1)}, f32[10,160,1]{1,0,2:T(8,128)}, u32[]{:S(2)}) copy-start(f32[10,160,1]{1,0,2:T(8,128)} %constant.26) | copy-start | bytes 19204
  0.0 9.1 %copy-start.7 = (f32[80,160]{1,0:T(8,128)S(1)}, f32[80,160]{1,0:T(8,128)}, u32[]{:S(2)}) copy-start(f32[80,160]{1,0:T(8,128)} %constant.19.clone) | copy-start | bytes 153604
  0.0 9.1 %copy-start.10 = (f32[80,5,1]{0,1,2:T(8,128)S(1)}, f32[80,5,1]{0,1,2:T(8,128)}, u32[]{:S(2)}) copy-start(f32[80,5,1]{0,1,2:T(8,128)} %constant.27) | copy-start | bytes 4804
  0.0 5.4 %copy-start.9 = (f32[3,5,5]{2,0,1:T(4,128)S(1)}, f32[3,5,5]{2,0,1:T(4,128)}, u32[]{:S(2)}) copy-start(f32[3,5,5]{2,0,1:T(4,128)} %param.18) | copy-start | bytes 904
  5.3 2.4 %collective-permute-start = (f32[16]{0:T(128)S(1)}, f32[16]{0:T(128)S(1)}, u32[]{:S(2)}, u32[]{:S(2)}) collective-permute-start(f32[16]{0:T(128)S(1)} %reduce_sum.9), channel_id=1, source_target_pairs={{0,1},{1,0},{2,3},{3,2},{4,5},{5,4},{6,7},{7,6},{8,9},{9,8},{10,11... | collective-permute-start | bytes 200 | tf_op jit(solution)/shard_map/ppermute | solution.py:501
  7.8 2.4 %collective-permute-start.1 = (f32[16]{0:T(128)S(1)}, f32[16]{0:T(128)S(1)}, u32[]{:S(2)}, u32[]{:S(2)}) collective-permute-start(f32[16]{0:T(128)S(1)} %add.18), channel_id=1, source_target_pairs={{0,2},{1,3},{2,0},{3,1},{4,6},{5,7},{6,4},{7,5},{8,10},{9,11},{10,... | collective-permute-start | bytes 200 | tf_op jit(solution)/shard_map/ppermute | solution.py:501
  10.2 3.3 %collective-permute-start.2 = (f32[16]{0:T(128)S(1)}, f32[16]{0:T(128)S(1)}, u32[]{:S(2)}, u32[]{:S(2)}) collective-permute-start(f32[16]{0:T(128)S(1)} %add.19), channel_id=1, source_target_pairs={{0,4},{1,5},{2,6},{3,7},{4,0},{5,1},{6,2},{7,3},{8,12},{9,13},{10,... | collective-permute-start | bytes 200 | tf_op jit(solution)/shard_map/ppermute | solution.py:501
  13.5 6.4 %collective-permute-start.3 = (f32[16]{0:T(128)S(1)}, f32[16]{0:T(128)S(1)}, u32[]{:S(2)}, u32[]{:S(2)}) collective-permute-start(f32[16]{0:T(128)S(1)} %add.20), channel_id=1, source_target_pairs={{0,8},{8,0},{16,24},{24,16},{1,9},{9,1},{17,25},{25,17},{2,10},{10... | collective-permute-start | bytes 200 | tf_op jit(solution)/shard_map/ppermute | solution.py:501
  19.9 7.1 %collective-permute-start.4 = (f32[16]{0:T(128)S(1)}, f32[16]{0:T(128)S(1)}, u32[]{:S(2)}, u32[]{:S(2)}) collective-permute-start(f32[16]{0:T(128)S(1)} %add.21), channel_id=1, source_target_pairs={{0,16},{8,24},{16,0},{24,8},{1,17},{9,25},{17,1},{25,9},{2,18},{10... | collective-permute-start | bytes 200 | tf_op jit(solution)/shard_map/ppermute | solution.py:501
  21.2 5.8 %copy-start = (f32[5,16,16,256]{3,2,1,0:T(8,128)S(1)}, f32[5,16,16,256]{3,2,1,0:T(8,128)}, u32[]{:S(2)}) copy-start(f32[5,16,16,256]{3,2,1,0:T(8,128)} %refs_2_.3) | copy-start | bytes 3932164
  21.2 5.8 %copy-start.2 = (bf16[20,5,16,256]{3,2,1,0:T(8,128)(2,1)S(1)}, bf16[20,5,16,256]{3,2,1,0:T(8,128)(2,1)}, u32[]{:S(2)}) copy-start(bf16[20,5,16,256]{3,2,1,0:T(8,128)(2,1)} %get-tuple-element.40.refs_3_) | copy-start | bytes 2457604
  21.2 5.8 %copy-start.3 = (s32[16]{0:T(128)S(1)}, s32[16]{0:T(128)}, u32[]{:S(2)}) copy-start(s32[16]{0:T(128)} %refs_0_.1) | copy-start | bytes 196
  27.0 13.1 %copy-start.4 = (f32[1,80,160]{2,1,0:T(8,128)S(1)}, f32[1,80,160]{2,1,0:T(8,128)}, u32[]{:S(2)}) copy-start(f32[1,80,160]{2,1,0:T(8,128)} %constant.24) | copy-start | bytes 153604
  27.1 13.1 %copy-start.5 = (f32[1,80,160]{2,1,0:T(8,128)S(1)}, f32[1,80,160]{2,1,0:T(8,128)}, u32[]{:S(2)}) copy-start(f32[1,80,160]{2,1,0:T(8,128)} %constant.23) | copy-start | bytes 153604
  27.1 13.1 %copy-start.6 = (f32[1,80,160]{2,1,0:T(8,128)S(1)}, f32[1,80,160]{2,1,0:T(8,128)}, u32[]{:S(2)}) copy-start(f32[1,80,160]{2,1,0:T(8,128)} %constant.22) | copy-start | bytes 153604
  28.6 39.1 %collective-permute-start.5 = (bf16[20,5,16,256]{3,2,1,0:T(8,128)(2,1)S(1)}, bf16[20,5,16,256]{3,2,1,0:T(8,128)(2,1)}, u32[]{:S(2)}, u32[]{:S(2)}) collective-permute-start(bf16[20,5,16,256]{3,2,1,0:T(8,128)(2,1)S(1)} %get-tuple-element.41), channel_id=1, source_target_pairs={{0,1},{1,2},{2,3},{3,4},{4,5},{5,6},{6,7},{8,9},{9,10},{10,11},{11... | collective-permute-start | bytes 2457608 | tf_op jit(solution)/shard_map/ppermute | solution.py:487
  31.7 36.0 %collective-permute-start.6 = (bf16[20,5,16,256]{3,2,1,0:T(8,128)(2,1)S(1)}, bf16[20,5,16,256]{3,2,1,0:T(8,128)(2,1)}, u32[]{:S(2)}, u32[]{:S(2)}) collective-permute-start(bf16[20,5,16,256]{3,2,1,0:T(8,128)(2,1)S(1)} %get-tuple-element.42), channel_id=1, source_target_pairs={{1,0},{2,1},{3,2},{4,3},{5,4},{6,5},{7,6},{9,8},{10,9},{11,10},{12... | collective-permute-start | bytes 2457608 | tf_op jit(solution)/shard_map/ppermute | solution.py:487
  34.8 32.9 %collective-permute-start.7 = (bf16[20,5,16,256]{3,2,1,0:T(8,128)(2,1)S(1)}, bf16[20,5,16,256]{3,2,1,0:T(8,128)(2,1)}, u32[]{:S(2)}, u32[]{:S(2)}) collective-permute-start(bf16[20,5,16,256]{3,2,1,0:T(8,128)(2,1)S(1)} %get-tuple-element.43), channel_id=1, source_target_pairs={{0,8},{8,16},{16,24},{1,9},{9,17},{17,25},{2,10},{10,18},{18,26},{... | collective-permute-start | bytes 2457608 | tf_op jit(solution)/shard_map/ppermute | solution.py:487
  37.7 30.0 %collective-permute-start.8 = (bf16[20,5,16,256]{3,2,1,0:T(8,128)(2,1)S(1)}, bf16[20,5,16,256]{3,2,1,0:T(8,128)(2,1)}, u32[]{:S(2)}, u32[]{:S(2)}) collective-permute-start(bf16[20,5,16,256]{3,2,1,0:T(8,128)(2,1)S(1)} %get-tuple-element.44), channel_id=1, source_target_pairs={{8,0},{16,8},{24,16},{9,1},{17,9},{25,17},{10,2},{18,10},{26,18},{... | collective-permute-start | bytes 2457608 | tf_op jit(solution)/shard_map/ppermute | solution.py:487
  40.2 27.5 %copy-start.1 = (s32[16,16,256]{2,1,0:T(8,128)S(1)}, s32[16,16,256]{2,1,0:T(8,128)}, u32[]{:S(2)}) copy-start(s32[16,16,256]{2,1,0:T(8,128)} %refs_3_.5) | copy-start | bytes 786436
  71.1 11.4 %collective-permute-start.9 = (f32[5,16,256]{2,1,0:T(8,128)S(1)}, f32[5,16,256]{2,1,0:T(8,128)S(1)}, u32[]{:S(2)}, u32[]{:S(2)}) collective-permute-start(f32[5,16,256]{2,1,0:T(8,128)S(1)} %get-tuple-element.46), channel_id=1, source_target_pairs={{0,1},{1,2},{2,3},{3,4},{4,5},{5,6},{6,7},{8,9},{9,10},{10,11},{11... | collective-permute-start | bytes 245768 | tf_op jit(solution)/shard_map/ppermute | solution.py:487
  75.8 6.8 %collective-permute-start.10 = (f32[5,16,256]{2,1,0:T(8,128)S(1)}, f32[5,16,256]{2,1,0:T(8,128)S(1)}, u32[]{:S(2)}, u32[]{:S(2)}) collective-permute-start(f32[5,16,256]{2,1,0:T(8,128)S(1)} %get-tuple-element.47), channel_id=1, source_target_pairs={{1,0},{2,1},{3,2},{4,3},{5,4},{6,5},{7,6},{9,8},{10,9},{11,10},{12... | collective-permute-start | bytes 245768 | tf_op jit(solution)/shard_map/ppermute | solution.py:487
  77.7 4.9 %collective-permute-start.11 = (f32[5,16,256]{2,1,0:T(8,128)S(1)}, f32[5,16,256]{2,1,0:T(8,128)S(1)}, u32[]{:S(2)}, u32[]{:S(2)}) collective-permute-start(f32[5,16,256]{2,1,0:T(8,128)S(1)} %get-tuple-element.48), channel_id=1, source_target_pairs={{0,8},{8,16},{16,24},{1,9},{9,17},{17,25},{2,10},{10,18},{18,26},{... | collective-permute-start | bytes 245768 | tf_op jit(solution)/shard_map/ppermute | solution.py:487
  80.5 5.8 %collective-permute-start.12 = (f32[5,16,256]{2,1,0:T(8,128)S(1)}, f32[5,16,256]{2,1,0:T(8,128)S(1)}, u32[]{:S(2)}, u32[]{:S(2)}) collective-permute-start(f32[5,16,256]{2,1,0:T(8,128)S(1)} %get-tuple-element.49), channel_id=1, source_target_pairs={{8,0},{16,8},{24,16},{9,1},{17,9},{25,17},{10,2},{18,10},{26,18},{... | collective-permute-start | bytes 245768 | tf_op jit(solution)/shard_map/ppermute | solution.py:487
  89.5 10.8 %collective-permute-start.13 = (f32[5,16,256]{2,1,0:T(8,128)S(1)}, f32[5,16,256]{2,1,0:T(8,128)S(1)}, u32[]{:S(2)}, u32[]{:S(2)}) collective-permute-start(f32[5,16,256]{2,1,0:T(8,128)S(1)} %get-tuple-element.55), channel_id=1, source_target_pairs={{0,1},{1,2},{2,3},{3,4},{4,5},{5,6},{6,7},{8,9},{9,10},{10,11},{11... | collective-permute-start | bytes 245768 | tf_op jit(solution)/shard_map/ppermute | solution.py:487
  94.0 6.3 %collective-permute-start.14 = (f32[5,16,256]{2,1,0:T(8,128)S(1)}, f32[5,16,256]{2,1,0:T(8,128)S(1)}, u32[]{:S(2)}, u32[]{:S(2)}) collective-permute-start(f32[5,16,256]{2,1,0:T(8,128)S(1)} %get-tuple-element.56), channel_id=1, source_target_pairs={{1,0},{2,1},{3,2},{4,3},{5,4},{6,5},{7,6},{9,8},{10,9},{11,10},{12... | collective-permute-start | bytes 245768 | tf_op jit(solution)/shard_map/ppermute | solution.py:487
  95.9 4.4 %collective-permute-start.15 = (f32[5,16,256]{2,1,0:T(8,128)S(1)}, f32[5,16,256]{2,1,0:T(8,128)S(1)}, u32[]{:S(2)}, u32[]{:S(2)}) collective-permute-start(f32[5,16,256]{2,1,0:T(8,128)S(1)} %get-tuple-element.57), channel_id=1, source_target_pairs={{0,8},{8,16},{16,24},{1,9},{9,17},{17,25},{2,10},{10,18},{18,26},{... | collective-permute-start | bytes 245768 | tf_op jit(solution)/shard_map/ppermute | solution.py:487
  98.1 5.8 %collective-permute-start.16 = (f32[5,16,256]{2,1,0:T(8,128)S(1)}, f32[5,16,256]{2,1,0:T(8,128)S(1)}, u32[]{:S(2)}, u32[]{:S(2)}) collective-permute-start(f32[5,16,256]{2,1,0:T(8,128)S(1)} %get-tuple-element.58), channel_id=1, source_target_pairs={{8,0},{16,8},{24,16},{9,1},{17,9},{25,17},{10,2},{18,10},{26,18},{... | collective-permute-start | bytes 245768 | tf_op jit(solution)/shard_map/ppermute | solution.py:487

commit v12 on v11

--- a/solution.py
+++ b/solution.py
@@ -176,16 +176,13 @@
     return ref[n].astype(F32) + ref[n + 1].astype(F32)
 
 
-def faces_kernel(pick, amp, base, *refs):
-    u = refs[0:4]
-    w = refs[4:8]
-    tails = refs[8:12]
-    scratch = refs[12]
+def faces_kernel(across, pick, amp, base, *refs):
+    u, w, tails, scratch = refs[0:2], refs[2:4], refs[4:6], refs[6]
     nv, nx, ny, nz = base.shape
 
     def body(j, carry):
-        lines = [base[j, 0], base[j, nx - 1], *edge_lines(base[j], scratch)]
-        for f in range(4):
+        lines = [base[j, 0], base[j, nx - 1]] if across == "chord" else edge_lines(base[j], scratch)
+        for f in range(2):
             for n, value in enumerate((summed(pick, amp, u[f], w[f], j), lines[f])):
                 hi = value.astype(BF16)
                 tails[f][2 * n, j] = hi
@@ -195,19 +192,20 @@
     lax.fori_loop(0, nv, body, 0)
 
 
-def faces(pick, amp, base, u_faces, w_faces):
+def faces(across, pick, amp, base, u_faces, w_faces):
     nv, nx, ny, nz = base.shape
     whole = lambda a: pl.BlockSpec(a.shape, lambda s: (0,) * a.ndim)
     return pl.pallas_call(
-        faces_kernel,
+        lambda *refs: faces_kernel(across, *refs),
         grid=(1,),
         in_specs=[in_smem()] * 2 + [whole(a) for a in (base, *u_faces, *w_faces)],
         out_specs=[pl.BlockSpec((TAIL,) + a.shape[1:], lambda s: (a.shape[0] // TAIL - 1, 0, 0, 0)) for a in u_faces],
         out_shape=[sds(a.shape, BF16) for a in u_faces],
-        input_output_aliases={3: 0, 4: 1, 5: 2, 6: 3},
+        input_output_aliases={3: 0, 4: 1},
         scratch_shapes=[pltpu.VMEM((nz // LANES, nx * ny, LANES), F32)],
         compiler_params=params(36),
-        name="faces",
+        cost_estimate=pl.CostEstimate(flops=10**7, bytes_accessed=5 * 10**6, transcendentals=0),
+        name="faces_" + across,
     )(pick, amp, base, *u_faces, *w_faces)
 
 
@@ -537,8 +535,13 @@
     wide = kron_rows(mix, ny)
     lw_y = within(wide, ny, np.eye(ny, dtype=np.float32))
     lw_x = lw_y if nx == ny else within(kron_rows(mix, nx), nx, np.eye(nx, dtype=np.float32))
-    w_faces = [*mix_chord(lw_y[0], adjoint), *mix_normal(lw_x[1], adjoint)]
-    halo = exchange(faces(pick, amp, base, own, w_faces))
+    w_normal = mix_normal(lw_x[1], adjoint)
+    y_faces = faces("normal", pick, amp, base, own[2:], w_normal)
+    *y_faces, lw_chord = lax.optimization_barrier((*y_faces, lw_y[0]))
+    y_halo = exchange_axis("normal", *y_faces)
+    w_chord = mix_chord(lw_chord, adjoint)
+    halo = exchange_axis("chord", *faces("chord", pick, amp, base, own[:2], w_chord)) + y_halo
+    w_faces = [*w_chord, *w_normal]
     local = main(pick, amp, main_rows(wide, ny), direct, adjoint)
     field, *sides = boundary(1.0 / nm, pick, amp, local, cell, w_faces, halo)
     sides, base_halo = sides[:4], sides[4:]

time: 110 us -> 108 us (0.982)
  waiting for transfers between devices: 15.9 us -> 13 us
    ppermute x12, waiting for transfers between devices: 12.2 us -> 8.42 us  [exchange_axis(): return [lax.ppermute(hi, axis, up), lax.ppermute(lo, axis, down)]]
  transfers between devices with their start and end apart: 17 -> 17, of which waited for: 6 -> 7; matrix products, arithmetic and copies ran while one was open for 1% -> 1% of each run, Pallas kernels for 28% -> 30%
where the time goes in v12:
time: 108 us; the launch traced here: 106 us
  Pallas kernels  48.6 us (45%)
  starting transfers between devices  42.8 us (40%)
  waiting for transfers between devices  13 us (12%)
    ppermute x12, starting transfers between devices, exchange_axis(): return [lax.ppermute(hi, axis, up), lax.ppermute(lo, axis, down)]  33.8 us
    pallas_call x1, Pallas kernels, main(): pl.pallas_call(main_kernel, in_specs=[in_smem(), in_smem(), in_vmem(), in...  22.6 us
    ppermute x5, starting transfers between devices, sum_over(): lax.ppermute(values, axis, [(i, i ^ bit) for i in range(count)])  9 us
    ppermute x12, waiting for transfers between devices, exchange_axis(): return [lax.ppermute(hi, axis, up), lax.ppermute(lo, axis, down)]  8.42 us
    pallas_call x2, Pallas kernels, apply_step(): pl.pallas_call(lambda *refs: step_kernel(last, *refs), in_specs=[in_vmem(...  7.27 us
    pallas_call x1, Pallas kernels, mix_normal(): pl.pallas_call(mix_normal_kernel, in_specs=[in_vmem(), in_hbm()], out_spe...  5.79 us
    pallas_call x1, Pallas kernels, pack(): pl.pallas_call(direct_kernel, in_specs=[in_hbm()], out_specs=[in_vmem()]...  5.19 us
    ppermute x5, waiting for transfers between devices, sum_over(): lax.ppermute(values, axis, [(i, i ^ bit) for i in range(count)])  4.58 us
  transfers between devices with their start and end apart: 17, of which 7 were waited for; matrix products, arithmetic and copies ran while one was open for 1% of the time, Pallas kernels for 30%

profile of v12, /device:TPU:5, one launch (start us, length us, event | category | flops | bytes accessed | tf_op | source)
XLA Modules:
  0.0 105.9 jit_solution(991405347471489059)
XLA Ops:
  0.0 0.0 copy-start.9
  0.0 5.2 %pack_direct.1 = (bf16[20,5,16,256]{3,2,1,0:T(8,128)(2,1)S(1)}, bf16[20,5,16,256]{3,2,1,0:T(8,128)(2,1)S(1)}, bf16[20,5,16,256]{3,2,1,0:T(8,128)(2,1)S(1)}, bf16...) custom-call(bf16[16,5,16,16,256]{4,3,2,1,0:T(8,128)(2,1)} %u_hbm.1), custom_call_target="tpu_custom_call" | custom-call | flops 15728640 | bytes 10485760 | tf_op jit(solution)/shard_map/pack_direct/pallas_call | solution.py:88
  5.2 0.1 reduce_sum.9
  5.3 0.1 collective-permute-start
  5.4 0.0 copy-done.9
  5.4 2.3 %collective-permute-done = f32[16]{0:T(128)S(1)} collective-permute-done((f32[16]{0:T(128)S(1)}, f32[16]{0:T(128)S(1)}, u32[]{:S(2)}, u32[]{:S(2)}) %collective-permute-start) | collective-permute-done | bytes 96 | tf_op jit(solution)/shard_map/ppermute | solution.py:499
  7.8 1.3 %collective-permute-start.1 = (f32[16]{0:T(128)S(1)}, f32[16]{0:T(128)S(1)}, u32[]{:S(2)}, u32[]{:S(2)}) collective-permute-start(f32[16]{0:T(128)S(1)} %add.18), channel_id=1, source_target_pairs={{0,2},{1,3},{2,0},{3,1},{4,6},{5,7},{6,4},{7,5},{8,10},{9,11},{10,... | collective-permute-start | bytes 200 | tf_op jit(solution)/shard_map/ppermute | solution.py:499
  9.1 0.0 copy-done.8
  9.1 0.2 fusion.6
  9.3 0.9 collective-permute-done.1
  10.2 2.3 %collective-permute-start.2 = (f32[16]{0:T(128)S(1)}, f32[16]{0:T(128)S(1)}, u32[]{:S(2)}, u32[]{:S(2)}) collective-permute-start(f32[16]{0:T(128)S(1)} %add.19), channel_id=1, source_target_pairs={{0,4},{1,5},{2,6},{3,7},{4,0},{5,1},{6,2},{7,3},{8,12},{9,13},{10,... | collective-permute-start | bytes 200 | tf_op jit(solution)/shard_map/ppermute | solution.py:499
  12.5 0.0 copy-done.7
  12.5 0.0 copy-done.10
  12.5 0.4 multiply_convert_fusion
  12.9 0.6 collective-permute-done.2
  13.5 4.1 %collective-permute-start.3 = (f32[16]{0:T(128)S(1)}, f32[16]{0:T(128)S(1)}, u32[]{:S(2)}, u32[]{:S(2)}) collective-permute-start(f32[16]{0:T(128)S(1)} %add.20), channel_id=1, source_target_pairs={{0,8},{8,0},{16,24},{24,16},{1,9},{9,1},{17,25},{25,17},{2,10},{10... | collective-permute-start | bytes 200 | tf_op jit(solution)/shard_map/ppermute | solution.py:499
  17.6 0.8 collective-permute-done.3
  18.4 1.2 %collective-permute-start.4 = (f32[16]{0:T(128)S(1)}, f32[16]{0:T(128)S(1)}, u32[]{:S(2)}, u32[]{:S(2)}) collective-permute-start(f32[16]{0:T(128)S(1)} %add.21), channel_id=1, source_target_pairs={{0,16},{8,24},{16,0},{24,8},{1,17},{9,25},{17,1},{25,9},{2,18},{10... | collective-permute-start | bytes 200 | tf_op jit(solution)/shard_map/ppermute | solution.py:499
  19.6 5.8 %mix_normal.1 = (f32[16,80,256]{2,1,0:T(8,128)S(1)}, f32[16,80,256]{2,1,0:T(8,128)S(1)}) custom-call(bf16[80,160]{1,0:T(8,128)(2,1)S(1)} %get-tuple-element.70.lw, bf16[16,5,16,16,256]{4,3,2,1,0:T(8,128)(2,1)} %hi.1), custom_call_target="tpu_custom_call" | custom-call | flops 15728640 | bytes 15728640 | tf_op jit(solution)/shard_map/mix_normal/pallas_call | solution.py:153
  25.4 0.0 collective-permute-done.4
  25.5 0.0 copy-done
  25.5 0.0 copy-done.2
  25.5 0.0 copy-done.3
  25.5 1.1 %faces_normal.1 = (bf16[20,5,16,256]{3,2,1,0:T(8,128)(2,1)S(1)}, bf16[20,5,16,256]{3,2,1,0:T(8,128)(2,1)S(1)}) custom-call(s32[16]{0:T(128)S(1)} %copy-done.3, f32[16]{0:T(128)S(1)} %add_rsqrt_fusion.amp.refs_1_, f32[5,16,16,256]{3,2,1,0:T(8,128)S(1)} %copy-done, ...), custom_call_target="tpu_custom_call", output_to_operand_aliasing={{0}: (3, {}), {1}: (4, {})} | custom-call | flops 10000000 | bytes 5000000 | tf_op jit(solution)/shard_map/faces_normal/pallas_call | solution.py:198
  26.6 3.1 %collective-permute-start.5 = (bf16[20,5,16,256]{3,2,1,0:T(8,128)(2,1)S(1)}, bf16[20,5,16,256]{3,2,1,0:T(8,128)(2,1)}, u32[]{:S(2)}, u32[]{:S(2)}) collective-permute-start(bf16[20,5,16,256]{3,2,1,0:T(8,128)(2,1)S(1)} %get-tuple-element.45), channel_id=1, source_target_pairs={{0,1},{1,2},{2,3},{3,4},{4,5},{5,6},{6,7},{8,9},{9,10},{10,11},{11... | collective-permute-start | bytes 2457608 | tf_op jit(solution)/shard_map/ppermute | solution.py:485
  29.8 3.0 %collective-permute-start.6 = (bf16[20,5,16,256]{3,2,1,0:T(8,128)(2,1)S(1)}, bf16[20,5,16,256]{3,2,1,0:T(8,128)(2,1)}, u32[]{:S(2)}, u32[]{:S(2)}) collective-permute-start(bf16[20,5,16,256]{3,2,1,0:T(8,128)(2,1)S(1)} %get-tuple-element.46), channel_id=1, source_target_pairs={{1,0},{2,1},{3,2},{4,3},{5,4},{6,5},{7,6},{9,8},{10,9},{11,10},{12... | collective-permute-start | bytes 2457608 | tf_op jit(solution)/shard_map/ppermute | solution.py:485
  32.8 2.3 %mix_chord.1 = (f32[16,80,256]{2,1,0:T(8,128)S(1)}, f32[16,80,256]{2,1,0:T(8,128)S(1)}) custom-call(bf16[80,160]{1,0:T(8,128)(2,1)S(1)} %get-tuple-element.42.lw, bf16[16,5,16,16,256]{4,3,2,1,0:T(8,128)(2,1)} %hi.1, bf16[16,5,16,16,256]{4,3,2,1,0:T(8,128)(2,1)} %hi.1), custom_call_target="tpu_custom_call" | custom-call | flops 100000000 | bytes 6000000 | tf_op jit(solution)/shard_map/mix_chord/pallas_call | solution.py:118
  35.1 0.0 copy-start.4
  35.1 0.0 copy-start.5
  35.1 0.0 copy-start.6
  35.1 1.0 faces_chord.1
  36.1 3.2 %collective-permute-start.7 = (bf16[20,5,16,256]{3,2,1,0:T(8,128)(2,1)S(1)}, bf16[20,5,16,256]{3,2,1,0:T(8,128)(2,1)}, u32[]{:S(2)}, u32[]{:S(2)}) collective-permute-start(bf16[20,5,16,256]{3,2,1,0:T(8,128)(2,1)S(1)} %get-tuple-element.49), channel_id=1, source_target_pairs={{0,8},{8,16},{16,24},{1,9},{9,17},{17,25},{2,10},{10,18},{18,26},{... | collective-permute-start | bytes 2457608 | tf_op jit(solution)/shard_map/ppermute | solution.py:485
  39.3 2.0 %collective-permute-start.8 = (bf16[20,5,16,256]{3,2,1,0:T(8,128)(2,1)S(1)}, bf16[20,5,16,256]{3,2,1,0:T(8,128)(2,1)}, u32[]{:S(2)}, u32[]{:S(2)}) collective-permute-start(bf16[20,5,16,256]{3,2,1,0:T(8,128)(2,1)S(1)} %get-tuple-element.50), channel_id=1, source_target_pairs={{8,0},{16,8},{24,16},{9,1},{17,9},{25,17},{10,2},{18,10},{26,18},{... | collective-permute-start | bytes 2457608 | tf_op jit(solution)/shard_map/ppermute | solution.py:485
  41.4 0.1 pad_maximum_fusion.1.refs_0_
  41.5 0.0 copy-done.4
  41.5 0.0 copy-done.5
  41.5 0.0 copy-done.6
  41.6 0.0 copy-start.1
  41.6 22.6 %main.1.refs_2_ = f32[16,80,256]{2,1,0:T(8,128)S(1)} custom-call(s32[16]{0:T(128)S(1)} %copy-done.3, f32[16]{0:T(128)S(1)} %add_rsqrt_fusion.amp.refs_1_, bf16[320,160]{1,0:T(8,128)(2,1)S(1)} %pad_maximum_fusion.lw, bf16[16,5,16,16,256]{4,3,2,1,0:T(8,128)(2,1)} %u_hbm.1, bf16[16,5,16,16,256]{4,3,2,1,0:T(8,128)(2,1)} %hi.1), custom_call_target="tpu_custom_call" | custom-call | flops 1000000 | bytes 100000 | tf_op jit(solution)/shard_map/main/pallas_call | solution.py:314
  64.2 1.2 %collective-permute-done.5.refs_8_ = bf16[20,5,16,256]{3,2,1,0:T(8,128)(2,1)} collective-permute-done((bf16[20,5,16,256]{3,2,1,0:T(8,128)(2,1)S(1)}, bf16[20,5,16,256]{3,2,1,0:T(8,128)(2,1)}, u32[]{:S(2)}, u32[]{:S(2)}) %collective-permute-start.5) | collective-permute-done | bytes 819232 | tf_op jit(solution)/shard_map/ppermute | solution.py:485
  65.4 0.0 collective-permute-done.6.refs_9_
  65.4 0.0 collective-permute-done.7.refs_10_
  65.4 0.0 collective-permute-done.8.refs_11_
  65.4 0.0 copy-done.1
  65.4 3.4 %boundary.1 = (f32[16,80,256]{2,1,0:T(8,128)S(1)}, f32[5,16,256]{2,1,0:T(8,128)S(1)}, f32[5,16,256]{2,1,0:T(8,128)S(1)}, f32[5,16,256]{2,1,0:T(8,128)S(1)}, f32[...) custom-call(s32[16]{0:T(128)S(1)} %copy-done.3, ...), custom_call_target="tpu_custom_call" | custom-call | tf_op jit(solution)/shard_map/boundary/pallas_call | solution.py:391
  68.8 5.0 %collective-permute-start.9 = (f32[5,16,256]{2,1,0:T(8,128)S(1)}, f32[5,16,256]{2,1,0:T(8,128)S(1)}, u32[]{:S(2)}, u32[]{:S(2)}) collective-permute-start(f32[5,16,256]{2,1,0:T(8,128)S(1)} %get-tuple-element.52), channel_id=1, source_target_pairs={{0,1},{1,2},{2,3},{3,4},{4,5},{5,6},{6,7},{8,9},{9,10},{10,11},{11... | collective-permute-start | bytes 245768 | tf_op jit(solution)/shard_map/ppermute | solution.py:485
  73.8 1.9 %collective-permute-start.10 = (f32[5,16,256]{2,1,0:T(8,128)S(1)}, f32[5,16,256]{2,1,0:T(8,128)S(1)}, u32[]{:S(2)}, u32[]{:S(2)}) collective-permute-start(f32[5,16,256]{2,1,0:T(8,128)S(1)} %get-tuple-element.53), channel_id=1, source_target_pairs={{1,0},{2,1},{3,2},{4,3},{5,4},{6,5},{7,6},{9,8},{10,9},{11,10},{12... | collective-permute-start | bytes 245768 | tf_op jit(solution)/shard_map/ppermute | solution.py:485
  75.7 2.8 %collective-permute-start.11 = (f32[5,16,256]{2,1,0:T(8,128)S(1)}, f32[5,16,256]{2,1,0:T(8,128)S(1)}, u32[]{:S(2)}, u32[]{:S(2)}) collective-permute-start(f32[5,16,256]{2,1,0:T(8,128)S(1)} %get-tuple-element.54), channel_id=1, source_target_pairs={{0,8},{8,16},{16,24},{1,9},{9,17},{17,25},{2,10},{10,18},{18,26},{... | collective-permute-start | bytes 245768 | tf_op jit(solution)/shard_map/ppermute | solution.py:485
  78.5 1.9 %collective-permute-start.12 = (f32[5,16,256]{2,1,0:T(8,128)S(1)}, f32[5,16,256]{2,1,0:T(8,128)S(1)}, u32[]{:S(2)}, u32[]{:S(2)}) collective-permute-start(f32[5,16,256]{2,1,0:T(8,128)S(1)} %get-tuple-element.55), channel_id=1, source_target_pairs={{8,0},{16,8},{24,16},{9,1},{17,9},{25,17},{10,2},{18,10},{26,18},{... | collective-permute-start | bytes 245768 | tf_op jit(solution)/shard_map/ppermute | solution.py:485
  80.5 0.1 pad_maximum_fusion.2.refs_1_
  80.5 0.0 collective-permute-done.9.refs_5_
  80.5 0.0 collective-permute-done.10.refs_6_
  80.6 0.0 collective-permute-done.11.refs_7_
  80.6 3.7 %collective-permute-done.12.refs_8_ = f32[5,16,256]{2,1,0:T(8,128)S(1)} collective-permute-done((f32[5,16,256]{2,1,0:T(8,128)S(1)}, f32[5,16,256]{2,1,0:T(8,128)S(1)}, u32[]{:S(2)}, u32[]{:S(2)}) %collective-permute-start.12) | collective-permute-done | bytes 81952 | tf_op jit(solution)/shard_map/ppermute | solution.py:485
  84.3 3.2 %step_one.1 = (f32[16,80,256]{2,1,0:T(8,128)S(1)}, f32[5,16,256]{2,1,0:T(8,128)S(1)}, f32[5,16,256]{2,1,0:T(8,128)S(1)}, f32[5,16,256]{2,1,0:T(8,128)S(1)}, f32[5,16,256]{2,1,0:T(8,128)S(1)}) custom-call(bf16[240,240]{1,0:T(8,128)(2,1)S(1)} %pad_maximum_fusion.1.refs_0_, bf16[80,240]{1,0:T(8,128)(2,1)S(1)} %pad_maximum_fusion.2.refs_1_, ...), custom_call_target="tpu_custom_call" | custom-call | tf_op jit(solution)/shard_map/step_one/pallas_call | solution.py:470
  87.5 4.5 %collective-permute-start.13 = (f32[5,16,256]{2,1,0:T(8,128)S(1)}, f32[5,16,256]{2,1,0:T(8,128)S(1)}, u32[]{:S(2)}, u32[]{:S(2)}) collective-permute-start(f32[5,16,256]{2,1,0:T(8,128)S(1)} %get-tuple-element.61), channel_id=1, source_target_pairs={{0,1},{1,2},{2,3},{3,4},{4,5},{5,6},{6,7},{8,9},{9,10},{10,11},{11... | collective-permute-start | bytes 245768 | tf_op jit(solution)/shard_map/ppermute | solution.py:485
  92.0 1.9 %collective-permute-start.14 = (f32[5,16,256]{2,1,0:T(8,128)S(1)}, f32[5,16,256]{2,1,0:T(8,128)S(1)}, u32[]{:S(2)}, u32[]{:S(2)}) collective-permute-start(f32[5,16,256]{2,1,0:T(8,128)S(1)} %get-tuple-element.62), channel_id=1, source_target_pairs={{1,0},{2,1},{3,2},{4,3},{5,4},{6,5},{7,6},{9,8},{10,9},{11,10},{12... | collective-permute-start | bytes 245768 | tf_op jit(solution)/shard_map/ppermute | solution.py:485
  94.0 2.1 %collective-permute-start.15 = (f32[5,16,256]{2,1,0:T(8,128)S(1)}, f32[5,16,256]{2,1,0:T(8,128)S(1)}, u32[]{:S(2)}, u32[]{:S(2)}) collective-permute-start(f32[5,16,256]{2,1,0:T(8,128)S(1)} %get-tuple-element.63), channel_id=1, source_target_pairs={{0,8},{8,16},{16,24},{1,9},{9,17},{17,25},{2,10},{10,18},{18,26},{... | collective-permute-start | bytes 245768 | tf_op jit(solution)/shard_map/ppermute | solution.py:485
  96.1 2.2 %collective-permute-start.16 = (f32[5,16,256]{2,1,0:T(8,128)S(1)}, f32[5,16,256]{2,1,0:T(8,128)S(1)}, u32[]{:S(2)}, u32[]{:S(2)}) collective-permute-start(f32[5,16,256]{2,1,0:T(8,128)S(1)} %get-tuple-element.64), channel_id=1, source_target_pairs={{8,0},{16,8},{24,16},{9,1},{17,9},{25,17},{10,2},{18,10},{26,18},{... | collective-permute-start | bytes 245768 | tf_op jit(solution)/shard_map/ppermute | solution.py:485
  98.3 0.0 collective-permute-done.13.refs_5_
  98.3 0.0 collective-permute-done.14.refs_6_
  98.3 0.0 collective-permute-done.15.refs_7_
  98.3 3.5 %collective-permute-done.16.refs_8_ = f32[5,16,256]{2,1,0:T(8,128)S(1)} collective-permute-done((f32[5,16,256]{2,1,0:T(8,128)S(1)}, f32[5,16,256]{2,1,0:T(8,128)S(1)}, u32[]{:S(2)}, u32[]{:S(2)}) %collective-permute-start.16) | collective-permute-done | bytes 81952 | tf_op jit(solution)/shard_map/ppermute | solution.py:485
  101.9 4.1 %step_two.1 = f32[5,16,16,256]{3,2,1,0:T(8,128)} custom-call(bf16[240,240]{1,0:T(8,128)(2,1)S(1)} %pad_maximum_fusion.1.refs_0_, bf16[80,240]{1,0:T(8,128)(2,1)S(1)} %pad_maximum_fusion.2.refs_1_, f32[5,16,16,256]{3,2,1,0:T(8,128)S(1)} %copy-done, s32[16,16,256]{2,1,0:T(8,128)S(1)} %copy-done.1, f32[16,80,256]{2,1,0:T(8,128)S(1)} %get-tuple-element.60.refs_4_, ...), custom_call_target="tpu_custom_call" | custom-call | tf_op jit(solution)/shard_map/step_two/pallas_call | solution.py:470
  (18 shorter events, 0.1 us)
Async XLA Ops:
  0.0 9.1 %copy-start.8 = (f32[10,160,1]{1,0,2:T(8,128)S(1)}, f32[10,160,1]{1,0,2:T(8,128)}, u32[]{:S(2)}) copy-start(f32[10,160,1]{1,0,2:T(8,128)} %constant.26) | copy-start | bytes 19204
  0.0 12.5 %copy-start.7 = (f32[80,160]{1,0:T(8,128)S(1)}, f32[80,160]{1,0:T(8,128)}, u32[]{:S(2)}) copy-start(f32[80,160]{1,0:T(8,128)} %constant.19.clone) | copy-start | bytes 153604
  0.0 12.5 %copy-start.10 = (f32[80,5,1]{0,1,2:T(8,128)S(1)}, f32[80,5,1]{0,1,2:T(8,128)}, u32[]{:S(2)}) copy-start(f32[80,5,1]{0,1,2:T(8,128)} %constant.27) | copy-start | bytes 4804
  0.0 5.4 %copy-start.9 = (f32[3,5,5]{2,0,1:T(4,128)S(1)}, f32[3,5,5]{2,0,1:T(4,128)}, u32[]{:S(2)}) copy-start(f32[3,5,5]{2,0,1:T(4,128)} %param.18) | copy-start | bytes 904
  5.3 2.4 %collective-permute-start = (f32[16]{0:T(128)S(1)}, f32[16]{0:T(128)S(1)}, u32[]{:S(2)}, u32[]{:S(2)}) collective-permute-start(f32[16]{0:T(128)S(1)} %reduce_sum.9), channel_id=1, source_target_pairs={{0,1},{1,0},{2,3},{3,2},{4,5},{5,4},{6,7},{7,6},{8,9},{9,8},{10,11... | collective-permute-start | bytes 200 | tf_op jit(solution)/shard_map/ppermute | solution.py:499
  7.8 2.4 %collective-permute-start.1 = (f32[16]{0:T(128)S(1)}, f32[16]{0:T(128)S(1)}, u32[]{:S(2)}, u32[]{:S(2)}) collective-permute-start(f32[16]{0:T(128)S(1)} %add.18), channel_id=1, source_target_pairs={{0,2},{1,3},{2,0},{3,1},{4,6},{5,7},{6,4},{7,5},{8,10},{9,11},{10,... | collective-permute-start | bytes 200 | tf_op jit(solution)/shard_map/ppermute | solution.py:499
  10.2 3.3 %collective-permute-start.2 = (f32[16]{0:T(128)S(1)}, f32[16]{0:T(128)S(1)}, u32[]{:S(2)}, u32[]{:S(2)}) collective-permute-start(f32[16]{0:T(128)S(1)} %add.19), channel_id=1, source_target_pairs={{0,4},{1,5},{2,6},{3,7},{4,0},{5,1},{6,2},{7,3},{8,12},{9,13},{10,... | collective-permute-start | bytes 200 | tf_op jit(solution)/shard_map/ppermute | solution.py:499
  13.5 4.9 %collective-permute-start.3 = (f32[16]{0:T(128)S(1)}, f32[16]{0:T(128)S(1)}, u32[]{:S(2)}, u32[]{:S(2)}) collective-permute-start(f32[16]{0:T(128)S(1)} %add.20), channel_id=1, source_target_pairs={{0,8},{8,0},{16,24},{24,16},{1,9},{9,1},{17,25},{25,17},{2,10},{10... | collective-permute-start | bytes 200 | tf_op jit(solution)/shard_map/ppermute | solution.py:499
  18.4 7.0 %collective-permute-start.4 = (f32[16]{0:T(128)S(1)}, f32[16]{0:T(128)S(1)}, u32[]{:S(2)}, u32[]{:S(2)}) collective-permute-start(f32[16]{0:T(128)S(1)} %add.21), channel_id=1, source_target_pairs={{0,16},{8,24},{16,0},{24,8},{1,17},{9,25},{17,1},{25,9},{2,18},{10... | collective-permute-start | bytes 200 | tf_op jit(solution)/shard_map/ppermute | solution.py:499
  19.6 5.8 %copy-start = (f32[5,16,16,256]{3,2,1,0:T(8,128)S(1)}, f32[5,16,16,256]{3,2,1,0:T(8,128)}, u32[]{:S(2)}) copy-start(f32[5,16,16,256]{3,2,1,0:T(8,128)} %refs_2_.7) | copy-start | bytes 3932164
  19.6 5.8 %copy-start.2 = (bf16[20,5,16,256]{3,2,1,0:T(8,128)(2,1)S(1)}, bf16[20,5,16,256]{3,2,1,0:T(8,128)(2,1)}, u32[]{:S(2)}) copy-start(bf16[20,5,16,256]{3,2,1,0:T(8,128)(2,1)} %get-tuple-element.37.refs_4_) | copy-start | bytes 2457604
  19.6 5.8 %copy-start.3 = (s32[16]{0:T(128)S(1)}, s32[16]{0:T(128)}, u32[]{:S(2)}) copy-start(s32[16]{0:T(128)} %refs_0_.5) | copy-start | bytes 196
  26.6 38.8 %collective-permute-start.5 = (bf16[20,5,16,256]{3,2,1,0:T(8,128)(2,1)S(1)}, bf16[20,5,16,256]{3,2,1,0:T(8,128)(2,1)}, u32[]{:S(2)}, u32[]{:S(2)}) collective-permute-start(bf16[20,5,16,256]{3,2,1,0:T(8,128)(2,1)S(1)} %get-tuple-element.45), channel_id=1, source_target_pairs={{0,1},{1,2},{2,3},{3,4},{4,5},{5,6},{6,7},{8,9},{9,10},{10,11},{11... | collective-permute-start | bytes 2457608 | tf_op jit(solution)/shard_map/ppermute | solution.py:485
  29.8 35.6 %collective-permute-start.6 = (bf16[20,5,16,256]{3,2,1,0:T(8,128)(2,1)S(1)}, bf16[20,5,16,256]{3,2,1,0:T(8,128)(2,1)}, u32[]{:S(2)}, u32[]{:S(2)}) collective-permute-start(bf16[20,5,16,256]{3,2,1,0:T(8,128)(2,1)S(1)} %get-tuple-element.46), channel_id=1, source_target_pairs={{1,0},{2,1},{3,2},{4,3},{5,4},{6,5},{7,6},{9,8},{10,9},{11,10},{12... | collective-permute-start | bytes 2457608 | tf_op jit(solution)/shard_map/ppermute | solution.py:485
  35.1 6.4 %copy-start.4 = (f32[1,80,160]{2,1,0:T(8,128)S(1)}, f32[1,80,160]{2,1,0:T(8,128)}, u32[]{:S(2)}) copy-start(f32[1,80,160]{2,1,0:T(8,128)} %constant.24) | copy-start | bytes 153604
  35.1 6.4 %copy-start.5 = (f32[1,80,160]{2,1,0:T(8,128)S(1)}, f32[1,80,160]{2,1,0:T(8,128)}, u32[]{:S(2)}) copy-start(f32[1,80,160]{2,1,0:T(8,128)} %constant.23) | copy-start | bytes 153604
  35.1 6.4 %copy-start.6 = (f32[1,80,160]{2,1,0:T(8,128)S(1)}, f32[1,80,160]{2,1,0:T(8,128)}, u32[]{:S(2)}) copy-start(f32[1,80,160]{2,1,0:T(8,128)} %constant.22) | copy-start | bytes 153604
  36.1 29.3 %collective-permute-start.7 = (bf16[20,5,16,256]{3,2,1,0:T(8,128)(2,1)S(1)}, bf16[20,5,16,256]{3,2,1,0:T(8,128)(2,1)}, u32[]{:S(2)}, u32[]{:S(2)}) collective-permute-start(bf16[20,5,16,256]{3,2,1,0:T(8,128)(2,1)S(1)} %get-tuple-element.49), channel_id=1, source_target_pairs={{0,8},{8,16},{16,24},{1,9},{9,17},{17,25},{2,10},{10,18},{18,26},{... | collective-permute-start | bytes 2457608 | tf_op jit(solution)/shard_map/ppermute | solution.py:485
  39.3 26.1 %collective-permute-start.8 = (bf16[20,5,16,256]{3,2,1,0:T(8,128)(2,1)S(1)}, bf16[20,5,16,256]{3,2,1,0:T(8,128)(2,1)}, u32[]{:S(2)}, u32[]{:S(2)}) collective-permute-start(bf16[20,5,16,256]{3,2,1,0:T(8,128)(2,1)S(1)} %get-tuple-element.50), channel_id=1, source_target_pairs={{8,0},{16,8},{24,16},{9,1},{17,9},{25,17},{10,2},{18,10},{26,18},{... | collective-permute-start | bytes 2457608 | tf_op jit(solution)/shard_map/ppermute | solution.py:485
  41.6 23.8 %copy-start.1 = (s32[16,16,256]{2,1,0:T(8,128)S(1)}, s32[16,16,256]{2,1,0:T(8,128)}, u32[]{:S(2)}) copy-start(s32[16,16,256]{2,1,0:T(8,128)} %refs_3_.5) | copy-start | bytes 786436
  68.8 11.8 %collective-permute-start.9 = (f32[5,16,256]{2,1,0:T(8,128)S(1)}, f32[5,16,256]{2,1,0:T(8,128)S(1)}, u32[]{:S(2)}, u32[]{:S(2)}) collective-permute-start(f32[5,16,256]{2,1,0:T(8,128)S(1)} %get-tuple-element.52), channel_id=1, source_target_pairs={{0,1},{1,2},{2,3},{3,4},{4,5},{5,6},{6,7},{8,9},{9,10},{10,11},{11... | collective-permute-start | bytes 245768 | tf_op jit(solution)/shard_map/ppermute | solution.py:485
  73.8 6.8 %collective-permute-start.10 = (f32[5,16,256]{2,1,0:T(8,128)S(1)}, f32[5,16,256]{2,1,0:T(8,128)S(1)}, u32[]{:S(2)}, u32[]{:S(2)}) collective-permute-start(f32[5,16,256]{2,1,0:T(8,128)S(1)} %get-tuple-element.53), channel_id=1, source_target_pairs={{1,0},{2,1},{3,2},{4,3},{5,4},{6,5},{7,6},{9,8},{10,9},{11,10},{12... | collective-permute-start | bytes 245768 | tf_op jit(solution)/shard_map/ppermute | solution.py:485
  75.7 4.9 %collective-permute-start.11 = (f32[5,16,256]{2,1,0:T(8,128)S(1)}, f32[5,16,256]{2,1,0:T(8,128)S(1)}, u32[]{:S(2)}, u32[]{:S(2)}) collective-permute-start(f32[5,16,256]{2,1,0:T(8,128)S(1)} %get-tuple-element.54), channel_id=1, source_target_pairs={{0,8},{8,16},{16,24},{1,9},{9,17},{17,25},{2,10},{10,18},{18,26},{... | collective-permute-start | bytes 245768 | tf_op jit(solution)/shard_map/ppermute | solution.py:485
  78.5 5.8 %collective-permute-start.12 = (f32[5,16,256]{2,1,0:T(8,128)S(1)}, f32[5,16,256]{2,1,0:T(8,128)S(1)}, u32[]{:S(2)}, u32[]{:S(2)}) collective-permute-start(f32[5,16,256]{2,1,0:T(8,128)S(1)} %get-tuple-element.55), channel_id=1, source_target_pairs={{8,0},{16,8},{24,16},{9,1},{17,9},{25,17},{10,2},{18,10},{26,18},{... | collective-permute-start | bytes 245768 | tf_op jit(solution)/shard_map/ppermute | solution.py:485
  87.5 10.8 %collective-permute-start.13 = (f32[5,16,256]{2,1,0:T(8,128)S(1)}, f32[5,16,256]{2,1,0:T(8,128)S(1)}, u32[]{:S(2)}, u32[]{:S(2)}) collective-permute-start(f32[5,16,256]{2,1,0:T(8,128)S(1)} %get-tuple-element.61), channel_id=1, source_target_pairs={{0,1},{1,2},{2,3},{3,4},{4,5},{5,6},{6,7},{8,9},{9,10},{10,11},{11... | collective-permute-start | bytes 245768 | tf_op jit(solution)/shard_map/ppermute | solution.py:485
  92.0 6.3 %collective-permute-start.14 = (f32[5,16,256]{2,1,0:T(8,128)S(1)}, f32[5,16,256]{2,1,0:T(8,128)S(1)}, u32[]{:S(2)}, u32[]{:S(2)}) collective-permute-start(f32[5,16,256]{2,1,0:T(8,128)S(1)} %get-tuple-element.62), channel_id=1, source_target_pairs={{1,0},{2,1},{3,2},{4,3},{5,4},{6,5},{7,6},{9,8},{10,9},{11,10},{12... | collective-permute-start | bytes 245768 | tf_op jit(solution)/shard_map/ppermute | solution.py:485
  94.0 4.4 %collective-permute-start.15 = (f32[5,16,256]{2,1,0:T(8,128)S(1)}, f32[5,16,256]{2,1,0:T(8,128)S(1)}, u32[]{:S(2)}, u32[]{:S(2)}) collective-permute-start(f32[5,16,256]{2,1,0:T(8,128)S(1)} %get-tuple-element.63), channel_id=1, source_target_pairs={{0,8},{8,16},{16,24},{1,9},{9,17},{17,25},{2,10},{10,18},{18,26},{... | collective-permute-start | bytes 245768 | tf_op jit(solution)/shard_map/ppermute | solution.py:485
  96.1 5.8 %collective-permute-start.16 = (f32[5,16,256]{2,1,0:T(8,128)S(1)}, f32[5,16,256]{2,1,0:T(8,128)S(1)}, u32[]{:S(2)}, u32[]{:S(2)}) collective-permute-start(f32[5,16,256]{2,1,0:T(8,128)S(1)} %get-tuple-element.64), channel_id=1, source_target_pairs={{8,0},{16,8},{24,16},{9,1},{17,9},{25,17},{10,2},{18,10},{26,18},{... | collective-permute-start | bytes 245768 | tf_op jit(solution)/shard_map/ppermute | solution.py:485

commit v13 on v12

--- a/solution.py
+++ b/solution.py
@@ -380,7 +380,7 @@
         write_lines(g, x, ny, ylo, yhi)
         return carry
 
-    lax.fori_loop(0, nx, plane, 0, unroll=2)
+    lax.fori_loop(0, nx, plane, 0, unroll=4)
     xlo[...] = field[0].reshape(xlo.shape)
     xhi[...] = field[nx - 1].reshape(xhi.shape)
 
@@ -443,7 +443,7 @@
             out[x] = h
         return carry
 
-    lax.fori_loop(0, nx, plane, 0, unroll=4)
+    lax.fori_loop(0, nx, plane, 0, unroll=8)
 
     def finish(x, carry):
         change = c0[x] - c0[x + 2]

time: 108 us -> 107 us (level)
  no operation moved by 1% of the time
where the time goes in v13:
time: 107 us; the launch traced here: 106 us
  Pallas kernels  48.1 us (45%)
  starting transfers between devices  42.8 us (40%)
  waiting for transfers between devices  13.1 us (12%)
    ppermute x12, starting transfers between devices, exchange_axis(): return [lax.ppermute(hi, axis, up), lax.ppermute(lo, axis, down)]  33.8 us
    pallas_call x1, Pallas kernels, main(): pl.pallas_call(main_kernel, in_specs=[in_smem(), in_smem(), in_vmem(), in...  22.5 us
    ppermute x5, starting transfers between devices, sum_over(): lax.ppermute(values, axis, [(i, i ^ bit) for i in range(count)])  9 us
    ppermute x12, waiting for transfers between devices, exchange_axis(): return [lax.ppermute(hi, axis, up), lax.ppermute(lo, axis, down)]  8.49 us
    pallas_call x2, Pallas kernels, apply_step(): pl.pallas_call(lambda *refs: step_kernel(last, *refs), in_specs=[in_vmem(...  6.86 us
    pallas_call x1, Pallas kernels, mix_normal(): pl.pallas_call(mix_normal_kernel, in_specs=[in_vmem(), in_hbm()], out_spe...  5.79 us
    pallas_call x1, Pallas kernels, pack(): pl.pallas_call(direct_kernel, in_specs=[in_hbm()], out_specs=[in_vmem()]...  5.19 us
    ppermute x5, waiting for transfers between devices, sum_over(): lax.ppermute(values, axis, [(i, i ^ bit) for i in range(count)])  4.58 us
  transfers between devices with their start and end apart: 17, of which 7 were waited for; matrix products, arithmetic and copies ran while one was open for 1% of the time, Pallas kernels for 30%

profile of v13, /device:TPU:5, one launch (start us, length us, event | category | flops | bytes accessed | tf_op | source)
XLA Modules:
  0.0 105.5 jit_solution(13836266145161892523)
XLA Ops:
  0.0 0.0 copy-start.9
  0.0 5.2 %pack_direct.1 = (bf16[20,5,16,256]{3,2,1,0:T(8,128)(2,1)S(1)}, bf16[20,5,16,256]{3,2,1,0:T(8,128)(2,1)S(1)}, bf16[20,5,16,256]{3,2,1,0:T(8,128)(2,1)S(1)}, bf16...) custom-call(bf16[16,5,16,16,256]{4,3,2,1,0:T(8,128)(2,1)} %u_hbm.1), custom_call_target="tpu_custom_call" | custom-call | flops 15728640 | bytes 10485760 | tf_op jit(solution)/shard_map/pack_direct/pallas_call | solution.py:88
  5.2 0.1 reduce_sum.9
  5.3 0.1 collective-permute-start
  5.4 0.0 copy-done.9
  5.4 2.3 %collective-permute-done = f32[16]{0:T(128)S(1)} collective-permute-done((f32[16]{0:T(128)S(1)}, f32[16]{0:T(128)S(1)}, u32[]{:S(2)}, u32[]{:S(2)}) %collective-permute-start) | collective-permute-done | bytes 96 | tf_op jit(solution)/shard_map/ppermute | solution.py:499
  7.8 1.3 %collective-permute-start.1 = (f32[16]{0:T(128)S(1)}, f32[16]{0:T(128)S(1)}, u32[]{:S(2)}, u32[]{:S(2)}) collective-permute-start(f32[16]{0:T(128)S(1)} %add.18), channel_id=1, source_target_pairs={{0,2},{1,3},{2,0},{3,1},{4,6},{5,7},{6,4},{7,5},{8,10},{9,11},{10,... | collective-permute-start | bytes 200 | tf_op jit(solution)/shard_map/ppermute | solution.py:499
  9.1 0.0 copy-done.8
  9.1 0.2 fusion.6
  9.3 0.9 collective-permute-done.1
  10.2 2.3 %collective-permute-start.2 = (f32[16]{0:T(128)S(1)}, f32[16]{0:T(128)S(1)}, u32[]{:S(2)}, u32[]{:S(2)}) collective-permute-start(f32[16]{0:T(128)S(1)} %add.19), channel_id=1, source_target_pairs={{0,4},{1,5},{2,6},{3,7},{4,0},{5,1},{6,2},{7,3},{8,12},{9,13},{10,... | collective-permute-start | bytes 200 | tf_op jit(solution)/shard_map/ppermute | solution.py:499
  12.5 0.0 copy-done.7
  12.5 0.0 copy-done.10
  12.5 0.4 multiply_convert_fusion
  12.9 0.6 collective-permute-done.2
  13.5 4.1 %collective-permute-start.3 = (f32[16]{0:T(128)S(1)}, f32[16]{0:T(128)S(1)}, u32[]{:S(2)}, u32[]{:S(2)}) collective-permute-start(f32[16]{0:T(128)S(1)} %add.20), channel_id=1, source_target_pairs={{0,8},{8,0},{16,24},{24,16},{1,9},{9,1},{17,25},{25,17},{2,10},{10... | collective-permute-start | bytes 200 | tf_op jit(solution)/shard_map/ppermute | solution.py:499
  17.6 0.8 collective-permute-done.3
  18.4 1.2 %collective-permute-start.4 = (f32[16]{0:T(128)S(1)}, f32[16]{0:T(128)S(1)}, u32[]{:S(2)}, u32[]{:S(2)}) collective-permute-start(f32[16]{0:T(128)S(1)} %add.21), channel_id=1, source_target_pairs={{0,16},{8,24},{16,0},{24,8},{1,17},{9,25},{17,1},{25,9},{2,18},{10... | collective-permute-start | bytes 200 | tf_op jit(solution)/shard_map/ppermute | solution.py:499
  19.6 5.8 %mix_normal.1 = (f32[16,80,256]{2,1,0:T(8,128)S(1)}, f32[16,80,256]{2,1,0:T(8,128)S(1)}) custom-call(bf16[80,160]{1,0:T(8,128)(2,1)S(1)} %get-tuple-element.70.lw, bf16[16,5,16,16,256]{4,3,2,1,0:T(8,128)(2,1)} %hi.1), custom_call_target="tpu_custom_call" | custom-call | flops 15728640 | bytes 15728640 | tf_op jit(solution)/shard_map/mix_normal/pallas_call | solution.py:153
  25.4 0.0 collective-permute-done.4
  25.5 0.0 copy-done
  25.5 0.0 copy-done.2
  25.5 0.0 copy-done.3
  25.5 1.1 %faces_normal.1 = (bf16[20,5,16,256]{3,2,1,0:T(8,128)(2,1)S(1)}, bf16[20,5,16,256]{3,2,1,0:T(8,128)(2,1)S(1)}) custom-call(s32[16]{0:T(128)S(1)} %copy-done.3, f32[16]{0:T(128)S(1)} %add_rsqrt_fusion.amp.refs_1_, f32[5,16,16,256]{3,2,1,0:T(8,128)S(1)} %copy-done, ...), custom_call_target="tpu_custom_call", output_to_operand_aliasing={{0}: (3, {}), {1}: (4, {})} | custom-call | flops 10000000 | bytes 5000000 | tf_op jit(solution)/shard_map/faces_normal/pallas_call | solution.py:198
  26.6 3.1 %collective-permute-start.5 = (bf16[20,5,16,256]{3,2,1,0:T(8,128)(2,1)S(1)}, bf16[20,5,16,256]{3,2,1,0:T(8,128)(2,1)}, u32[]{:S(2)}, u32[]{:S(2)}) collective-permute-start(bf16[20,5,16,256]{3,2,1,0:T(8,128)(2,1)S(1)} %get-tuple-element.45), channel_id=1, source_target_pairs={{0,1},{1,2},{2,3},{3,4},{4,5},{5,6},{6,7},{8,9},{9,10},{10,11},{11... | collective-permute-start | bytes 2457608 | tf_op jit(solution)/shard_map/ppermute | solution.py:485
  29.8 3.0 %collective-permute-start.6 = (bf16[20,5,16,256]{3,2,1,0:T(8,128)(2,1)S(1)}, bf16[20,5,16,256]{3,2,1,0:T(8,128)(2,1)}, u32[]{:S(2)}, u32[]{:S(2)}) collective-permute-start(bf16[20,5,16,256]{3,2,1,0:T(8,128)(2,1)S(1)} %get-tuple-element.46), channel_id=1, source_target_pairs={{1,0},{2,1},{3,2},{4,3},{5,4},{6,5},{7,6},{9,8},{10,9},{11,10},{12... | collective-permute-start | bytes 2457608 | tf_op jit(solution)/shard_map/ppermute | solution.py:485
  32.8 2.3 %mix_chord.1 = (f32[16,80,256]{2,1,0:T(8,128)S(1)}, f32[16,80,256]{2,1,0:T(8,128)S(1)}) custom-call(bf16[80,160]{1,0:T(8,128)(2,1)S(1)} %get-tuple-element.42.lw, bf16[16,5,16,16,256]{4,3,2,1,0:T(8,128)(2,1)} %hi.1, bf16[16,5,16,16,256]{4,3,2,1,0:T(8,128)(2,1)} %hi.1), custom_call_target="tpu_custom_call" | custom-call | flops 100000000 | bytes 6000000 | tf_op jit(solution)/shard_map/mix_chord/pallas_call | solution.py:118
  35.1 0.0 copy-start.4
  35.1 0.0 copy-start.5
  35.1 0.0 copy-start.6
  35.1 1.0 faces_chord.1
  36.1 3.2 %collective-permute-start.7 = (bf16[20,5,16,256]{3,2,1,0:T(8,128)(2,1)S(1)}, bf16[20,5,16,256]{3,2,1,0:T(8,128)(2,1)}, u32[]{:S(2)}, u32[]{:S(2)}) collective-permute-start(bf16[20,5,16,256]{3,2,1,0:T(8,128)(2,1)S(1)} %get-tuple-element.49), channel_id=1, source_target_pairs={{0,8},{8,16},{16,24},{1,9},{9,17},{17,25},{2,10},{10,18},{18,26},{... | collective-permute-start | bytes 2457608 | tf_op jit(solution)/shard_map/ppermute | solution.py:485
  39.3 2.0 %collective-permute-start.8 = (bf16[20,5,16,256]{3,2,1,0:T(8,128)(2,1)S(1)}, bf16[20,5,16,256]{3,2,1,0:T(8,128)(2,1)}, u32[]{:S(2)}, u32[]{:S(2)}) collective-permute-start(bf16[20,5,16,256]{3,2,1,0:T(8,128)(2,1)S(1)} %get-tuple-element.50), channel_id=1, source_target_pairs={{8,0},{16,8},{24,16},{9,1},{17,9},{25,17},{10,2},{18,10},{26,18},{... | collective-permute-start | bytes 2457608 | tf_op jit(solution)/shard_map/ppermute | solution.py:485
  41.4 0.1 pad_maximum_fusion.1.refs_0_
  41.5 0.0 copy-done.4
  41.5 0.0 copy-done.5
  41.5 0.0 copy-done.6
  41.6 0.0 copy-start.1
  41.6 22.5 %main.1.refs_2_ = f32[16,80,256]{2,1,0:T(8,128)S(1)} custom-call(s32[16]{0:T(128)S(1)} %copy-done.3, f32[16]{0:T(128)S(1)} %add_rsqrt_fusion.amp.refs_1_, bf16[320,160]{1,0:T(8,128)(2,1)S(1)} %pad_maximum_fusion.lw, bf16[16,5,16,16,256]{4,3,2,1,0:T(8,128)(2,1)} %u_hbm.1, bf16[16,5,16,16,256]{4,3,2,1,0:T(8,128)(2,1)} %hi.1), custom_call_target="tpu_custom_call" | custom-call | flops 1000000 | bytes 100000 | tf_op jit(solution)/shard_map/main/pallas_call | solution.py:314
  64.2 1.2 %collective-permute-done.5.refs_8_ = bf16[20,5,16,256]{3,2,1,0:T(8,128)(2,1)} collective-permute-done((bf16[20,5,16,256]{3,2,1,0:T(8,128)(2,1)S(1)}, bf16[20,5,16,256]{3,2,1,0:T(8,128)(2,1)}, u32[]{:S(2)}, u32[]{:S(2)}) %collective-permute-start.5) | collective-permute-done | bytes 819232 | tf_op jit(solution)/shard_map/ppermute | solution.py:485
  65.4 0.0 collective-permute-done.6.refs_9_
  65.4 0.0 collective-permute-done.7.refs_10_
  65.4 0.0 collective-permute-done.8.refs_11_
  65.4 0.0 copy-done.1
  65.4 3.4 %boundary.1 = (f32[16,80,256]{2,1,0:T(8,128)S(1)}, f32[5,16,256]{2,1,0:T(8,128)S(1)}, f32[5,16,256]{2,1,0:T(8,128)S(1)}, f32[5,16,256]{2,1,0:T(8,128)S(1)}, f32[...) custom-call(s32[16]{0:T(128)S(1)} %copy-done.3, ...), custom_call_target="tpu_custom_call" | custom-call | tf_op jit(solution)/shard_map/boundary/pallas_call | solution.py:391
  68.8 5.0 %collective-permute-start.9 = (f32[5,16,256]{2,1,0:T(8,128)S(1)}, f32[5,16,256]{2,1,0:T(8,128)S(1)}, u32[]{:S(2)}, u32[]{:S(2)}) collective-permute-start(f32[5,16,256]{2,1,0:T(8,128)S(1)} %get-tuple-element.52), channel_id=1, source_target_pairs={{0,1},{1,2},{2,3},{3,4},{4,5},{5,6},{6,7},{8,9},{9,10},{10,11},{11... | collective-permute-start | bytes 245768 | tf_op jit(solution)/shard_map/ppermute | solution.py:485
  73.8 1.9 %collective-permute-start.10 = (f32[5,16,256]{2,1,0:T(8,128)S(1)}, f32[5,16,256]{2,1,0:T(8,128)S(1)}, u32[]{:S(2)}, u32[]{:S(2)}) collective-permute-start(f32[5,16,256]{2,1,0:T(8,128)S(1)} %get-tuple-element.53), channel_id=1, source_target_pairs={{1,0},{2,1},{3,2},{4,3},{5,4},{6,5},{7,6},{9,8},{10,9},{11,10},{12... | collective-permute-start | bytes 245768 | tf_op jit(solution)/shard_map/ppermute | solution.py:485
  75.7 2.8 %collective-permute-start.11 = (f32[5,16,256]{2,1,0:T(8,128)S(1)}, f32[5,16,256]{2,1,0:T(8,128)S(1)}, u32[]{:S(2)}, u32[]{:S(2)}) collective-permute-start(f32[5,16,256]{2,1,0:T(8,128)S(1)} %get-tuple-element.54), channel_id=1, source_target_pairs={{0,8},{8,16},{16,24},{1,9},{9,17},{17,25},{2,10},{10,18},{18,26},{... | collective-permute-start | bytes 245768 | tf_op jit(solution)/shard_map/ppermute | solution.py:485
  78.5 1.9 %collective-permute-start.12 = (f32[5,16,256]{2,1,0:T(8,128)S(1)}, f32[5,16,256]{2,1,0:T(8,128)S(1)}, u32[]{:S(2)}, u32[]{:S(2)}) collective-permute-start(f32[5,16,256]{2,1,0:T(8,128)S(1)} %get-tuple-element.55), channel_id=1, source_target_pairs={{8,0},{16,8},{24,16},{9,1},{17,9},{25,17},{10,2},{18,10},{26,18},{... | collective-permute-start | bytes 245768 | tf_op jit(solution)/shard_map/ppermute | solution.py:485
  80.4 0.1 pad_maximum_fusion.2.refs_1_
  80.5 0.0 collective-permute-done.9.refs_5_
  80.5 0.0 collective-permute-done.10.refs_6_
  80.5 0.0 collective-permute-done.11.refs_7_
  80.6 3.7 %collective-permute-done.12.refs_8_ = f32[5,16,256]{2,1,0:T(8,128)S(1)} collective-permute-done((f32[5,16,256]{2,1,0:T(8,128)S(1)}, f32[5,16,256]{2,1,0:T(8,128)S(1)}, u32[]{:S(2)}, u32[]{:S(2)}) %collective-permute-start.12) | collective-permute-done | bytes 81952 | tf_op jit(solution)/shard_map/ppermute | solution.py:485
  84.3 3.0 %step_one.1 = (f32[16,80,256]{2,1,0:T(8,128)S(1)}, f32[5,16,256]{2,1,0:T(8,128)S(1)}, f32[5,16,256]{2,1,0:T(8,128)S(1)}, f32[5,16,256]{2,1,0:T(8,128)S(1)}, f32[5,16,256]{2,1,0:T(8,128)S(1)}) custom-call(bf16[240,240]{1,0:T(8,128)(2,1)S(1)} %pad_maximum_fusion.1.refs_0_, bf16[80,240]{1,0:T(8,128)(2,1)S(1)} %pad_maximum_fusion.2.refs_1_, ...), custom_call_target="tpu_custom_call" | custom-call | tf_op jit(solution)/shard_map/step_one/pallas_call | solution.py:470
  87.3 4.5 %collective-permute-start.13 = (f32[5,16,256]{2,1,0:T(8,128)S(1)}, f32[5,16,256]{2,1,0:T(8,128)S(1)}, u32[]{:S(2)}, u32[]{:S(2)}) collective-permute-start(f32[5,16,256]{2,1,0:T(8,128)S(1)} %get-tuple-element.61), channel_id=1, source_target_pairs={{0,1},{1,2},{2,3},{3,4},{4,5},{5,6},{6,7},{8,9},{9,10},{10,11},{11... | collective-permute-start | bytes 245768 | tf_op jit(solution)/shard_map/ppermute | solution.py:485
  91.8 1.9 %collective-permute-start.14 = (f32[5,16,256]{2,1,0:T(8,128)S(1)}, f32[5,16,256]{2,1,0:T(8,128)S(1)}, u32[]{:S(2)}, u32[]{:S(2)}) collective-permute-start(f32[5,16,256]{2,1,0:T(8,128)S(1)} %get-tuple-element.62), channel_id=1, source_target_pairs={{1,0},{2,1},{3,2},{4,3},{5,4},{6,5},{7,6},{9,8},{10,9},{11,10},{12... | collective-permute-start | bytes 245768 | tf_op jit(solution)/shard_map/ppermute | solution.py:485
  93.7 2.1 %collective-permute-start.15 = (f32[5,16,256]{2,1,0:T(8,128)S(1)}, f32[5,16,256]{2,1,0:T(8,128)S(1)}, u32[]{:S(2)}, u32[]{:S(2)}) collective-permute-start(f32[5,16,256]{2,1,0:T(8,128)S(1)} %get-tuple-element.63), channel_id=1, source_target_pairs={{0,8},{8,16},{16,24},{1,9},{9,17},{17,25},{2,10},{10,18},{18,26},{... | collective-permute-start | bytes 245768 | tf_op jit(solution)/shard_map/ppermute | solution.py:485
  95.9 2.2 %collective-permute-start.16 = (f32[5,16,256]{2,1,0:T(8,128)S(1)}, f32[5,16,256]{2,1,0:T(8,128)S(1)}, u32[]{:S(2)}, u32[]{:S(2)}) collective-permute-start(f32[5,16,256]{2,1,0:T(8,128)S(1)} %get-tuple-element.64), channel_id=1, source_target_pairs={{8,0},{16,8},{24,16},{9,1},{17,9},{25,17},{10,2},{18,10},{26,18},{... | collective-permute-start | bytes 245768 | tf_op jit(solution)/shard_map/ppermute | solution.py:485
  98.1 0.0 collective-permute-done.13.refs_5_
  98.1 0.0 collective-permute-done.14.refs_6_
  98.1 0.0 collective-permute-done.15.refs_7_
  98.1 3.5 %collective-permute-done.16.refs_8_ = f32[5,16,256]{2,1,0:T(8,128)S(1)} collective-permute-done((f32[5,16,256]{2,1,0:T(8,128)S(1)}, f32[5,16,256]{2,1,0:T(8,128)S(1)}, u32[]{:S(2)}, u32[]{:S(2)}) %collective-permute-start.16) | collective-permute-done | bytes 81952 | tf_op jit(solution)/shard_map/ppermute | solution.py:485
  101.6 3.9 %step_two.1 = f32[5,16,16,256]{3,2,1,0:T(8,128)} custom-call(bf16[240,240]{1,0:T(8,128)(2,1)S(1)} %pad_maximum_fusion.1.refs_0_, bf16[80,240]{1,0:T(8,128)(2,1)S(1)} %pad_maximum_fusion.2.refs_1_, f32[5,16,16,256]{3,2,1,0:T(8,128)S(1)} %copy-done, s32[16,16,256]{2,1,0:T(8,128)S(1)} %copy-done.1, f32[16,80,256]{2,1,0:T(8,128)S(1)} %get-tuple-element.60.refs_4_, ...), custom_call_target="tpu_custom_call" | custom-call | tf_op jit(solution)/shard_map/step_two/pallas_call | solution.py:470
  (18 shorter events, 0.1 us)
Async XLA Ops:
  0.0 9.1 %copy-start.8 = (f32[10,160,1]{1,0,2:T(8,128)S(1)}, f32[10,160,1]{1,0,2:T(8,128)}, u32[]{:S(2)}) copy-start(f32[10,160,1]{1,0,2:T(8,128)} %constant.26) | copy-start | bytes 19204
  0.0 12.5 %copy-start.7 = (f32[80,160]{1,0:T(8,128)S(1)}, f32[80,160]{1,0:T(8,128)}, u32[]{:S(2)}) copy-start(f32[80,160]{1,0:T(8,128)} %constant.19.clone) | copy-start | bytes 153604
  0.0 12.5 %copy-start.10 = (f32[80,5,1]{0,1,2:T(8,128)S(1)}, f32[80,5,1]{0,1,2:T(8,128)}, u32[]{:S(2)}) copy-start(f32[80,5,1]{0,1,2:T(8,128)} %constant.27) | copy-start | bytes 4804
  0.0 5.4 %copy-start.9 = (f32[3,5,5]{2,0,1:T(4,128)S(1)}, f32[3,5,5]{2,0,1:T(4,128)}, u32[]{:S(2)}) copy-start(f32[3,5,5]{2,0,1:T(4,128)} %param.18) | copy-start | bytes 904
  5.3 2.4 %collective-permute-start = (f32[16]{0:T(128)S(1)}, f32[16]{0:T(128)S(1)}, u32[]{:S(2)}, u32[]{:S(2)}) collective-permute-start(f32[16]{0:T(128)S(1)} %reduce_sum.9), channel_id=1, source_target_pairs={{0,1},{1,0},{2,3},{3,2},{4,5},{5,4},{6,7},{7,6},{8,9},{9,8},{10,11... | collective-permute-start | bytes 200 | tf_op jit(solution)/shard_map/ppermute | solution.py:499
  7.8 2.4 %collective-permute-start.1 = (f32[16]{0:T(128)S(1)}, f32[16]{0:T(128)S(1)}, u32[]{:S(2)}, u32[]{:S(2)}) collective-permute-start(f32[16]{0:T(128)S(1)} %add.18), channel_id=1, source_target_pairs={{0,2},{1,3},{2,0},{3,1},{4,6},{5,7},{6,4},{7,5},{8,10},{9,11},{10,... | collective-permute-start | bytes 200 | tf_op jit(solution)/shard_map/ppermute | solution.py:499
  10.2 3.3 %collective-permute-start.2 = (f32[16]{0:T(128)S(1)}, f32[16]{0:T(128)S(1)}, u32[]{:S(2)}, u32[]{:S(2)}) collective-permute-start(f32[16]{0:T(128)S(1)} %add.19), channel_id=1, source_target_pairs={{0,4},{1,5},{2,6},{3,7},{4,0},{5,1},{6,2},{7,3},{8,12},{9,13},{10,... | collective-permute-start | bytes 200 | tf_op jit(solution)/shard_map/ppermute | solution.py:499
  13.5 4.9 %collective-permute-start.3 = (f32[16]{0:T(128)S(1)}, f32[16]{0:T(128)S(1)}, u32[]{:S(2)}, u32[]{:S(2)}) collective-permute-start(f32[16]{0:T(128)S(1)} %add.20), channel_id=1, source_target_pairs={{0,8},{8,0},{16,24},{24,16},{1,9},{9,1},{17,25},{25,17},{2,10},{10... | collective-permute-start | bytes 200 | tf_op jit(solution)/shard_map/ppermute | solution.py:499
  18.4 7.0 %collective-permute-start.4 = (f32[16]{0:T(128)S(1)}, f32[16]{0:T(128)S(1)}, u32[]{:S(2)}, u32[]{:S(2)}) collective-permute-start(f32[16]{0:T(128)S(1)} %add.21), channel_id=1, source_target_pairs={{0,16},{8,24},{16,0},{24,8},{1,17},{9,25},{17,1},{25,9},{2,18},{10... | collective-permute-start | bytes 200 | tf_op jit(solution)/shard_map/ppermute | solution.py:499
  19.6 5.8 %copy-start = (f32[5,16,16,256]{3,2,1,0:T(8,128)S(1)}, f32[5,16,16,256]{3,2,1,0:T(8,128)}, u32[]{:S(2)}) copy-start(f32[5,16,16,256]{3,2,1,0:T(8,128)} %refs_2_.7) | copy-start | bytes 3932164
  19.6 5.8 %copy-start.2 = (bf16[20,5,16,256]{3,2,1,0:T(8,128)(2,1)S(1)}, bf16[20,5,16,256]{3,2,1,0:T(8,128)(2,1)}, u32[]{:S(2)}) copy-start(bf16[20,5,16,256]{3,2,1,0:T(8,128)(2,1)} %get-tuple-element.37.refs_4_) | copy-start | bytes 2457604
  19.6 5.8 %copy-start.3 = (s32[16]{0:T(128)S(1)}, s32[16]{0:T(128)}, u32[]{:S(2)}) copy-start(s32[16]{0:T(128)} %refs_0_.5) | copy-start | bytes 196
  26.6 38.8 %collective-permute-start.5 = (bf16[20,5,16,256]{3,2,1,0:T(8,128)(2,1)S(1)}, bf16[20,5,16,256]{3,2,1,0:T(8,128)(2,1)}, u32[]{:S(2)}, u32[]{:S(2)}) collective-permute-start(bf16[20,5,16,256]{3,2,1,0:T(8,128)(2,1)S(1)} %get-tuple-element.45), channel_id=1, source_target_pairs={{0,1},{1,2},{2,3},{3,4},{4,5},{5,6},{6,7},{8,9},{9,10},{10,11},{11... | collective-permute-start | bytes 2457608 | tf_op jit(solution)/shard_map/ppermute | solution.py:485
  29.8 35.6 %collective-permute-start.6 = (bf16[20,5,16,256]{3,2,1,0:T(8,128)(2,1)S(1)}, bf16[20,5,16,256]{3,2,1,0:T(8,128)(2,1)}, u32[]{:S(2)}, u32[]{:S(2)}) collective-permute-start(bf16[20,5,16,256]{3,2,1,0:T(8,128)(2,1)S(1)} %get-tuple-element.46), channel_id=1, source_target_pairs={{1,0},{2,1},{3,2},{4,3},{5,4},{6,5},{7,6},{9,8},{10,9},{11,10},{12... | collective-permute-start | bytes 2457608 | tf_op jit(solution)/shard_map/ppermute | solution.py:485
  35.1 6.4 %copy-start.4 = (f32[1,80,160]{2,1,0:T(8,128)S(1)}, f32[1,80,160]{2,1,0:T(8,128)}, u32[]{:S(2)}) copy-start(f32[1,80,160]{2,1,0:T(8,128)} %constant.24) | copy-start | bytes 153604
  35.1 6.4 %copy-start.5 = (f32[1,80,160]{2,1,0:T(8,128)S(1)}, f32[1,80,160]{2,1,0:T(8,128)}, u32[]{:S(2)}) copy-start(f32[1,80,160]{2,1,0:T(8,128)} %constant.23) | copy-start | bytes 153604
  35.1 6.4 %copy-start.6 = (f32[1,80,160]{2,1,0:T(8,128)S(1)}, f32[1,80,160]{2,1,0:T(8,128)}, u32[]{:S(2)}) copy-start(f32[1,80,160]{2,1,0:T(8,128)} %constant.22) | copy-start | bytes 153604
  36.1 29.3 %collective-permute-start.7 = (bf16[20,5,16,256]{3,2,1,0:T(8,128)(2,1)S(1)}, bf16[20,5,16,256]{3,2,1,0:T(8,128)(2,1)}, u32[]{:S(2)}, u32[]{:S(2)}) collective-permute-start(bf16[20,5,16,256]{3,2,1,0:T(8,128)(2,1)S(1)} %get-tuple-element.49), channel_id=1, source_target_pairs={{0,8},{8,16},{16,24},{1,9},{9,17},{17,25},{2,10},{10,18},{18,26},{... | collective-permute-start | bytes 2457608 | tf_op jit(solution)/shard_map/ppermute | solution.py:485
  39.3 26.1 %collective-permute-start.8 = (bf16[20,5,16,256]{3,2,1,0:T(8,128)(2,1)S(1)}, bf16[20,5,16,256]{3,2,1,0:T(8,128)(2,1)}, u32[]{:S(2)}, u32[]{:S(2)}) collective-permute-start(bf16[20,5,16,256]{3,2,1,0:T(8,128)(2,1)S(1)} %get-tuple-element.50), channel_id=1, source_target_pairs={{8,0},{16,8},{24,16},{9,1},{17,9},{25,17},{10,2},{18,10},{26,18},{... | collective-permute-start | bytes 2457608 | tf_op jit(solution)/shard_map/ppermute | solution.py:485
  41.6 23.8 %copy-start.1 = (s32[16,16,256]{2,1,0:T(8,128)S(1)}, s32[16,16,256]{2,1,0:T(8,128)}, u32[]{:S(2)}) copy-start(s32[16,16,256]{2,1,0:T(8,128)} %refs_3_.5) | copy-start | bytes 786436
  68.8 11.8 %collective-permute-start.9 = (f32[5,16,256]{2,1,0:T(8,128)S(1)}, f32[5,16,256]{2,1,0:T(8,128)S(1)}, u32[]{:S(2)}, u32[]{:S(2)}) collective-permute-start(f32[5,16,256]{2,1,0:T(8,128)S(1)} %get-tuple-element.52), channel_id=1, source_target_pairs={{0,1},{1,2},{2,3},{3,4},{4,5},{5,6},{6,7},{8,9},{9,10},{10,11},{11... | collective-permute-start | bytes 245768 | tf_op jit(solution)/shard_map/ppermute | solution.py:485
  73.8 6.8 %collective-permute-start.10 = (f32[5,16,256]{2,1,0:T(8,128)S(1)}, f32[5,16,256]{2,1,0:T(8,128)S(1)}, u32[]{:S(2)}, u32[]{:S(2)}) collective-permute-start(f32[5,16,256]{2,1,0:T(8,128)S(1)} %get-tuple-element.53), channel_id=1, source_target_pairs={{1,0},{2,1},{3,2},{4,3},{5,4},{6,5},{7,6},{9,8},{10,9},{11,10},{12... | collective-permute-start | bytes 245768 | tf_op jit(solution)/shard_map/ppermute | solution.py:485
  75.7 4.9 %collective-permute-start.11 = (f32[5,16,256]{2,1,0:T(8,128)S(1)}, f32[5,16,256]{2,1,0:T(8,128)S(1)}, u32[]{:S(2)}, u32[]{:S(2)}) collective-permute-start(f32[5,16,256]{2,1,0:T(8,128)S(1)} %get-tuple-element.54), channel_id=1, source_target_pairs={{0,8},{8,16},{16,24},{1,9},{9,17},{17,25},{2,10},{10,18},{18,26},{... | collective-permute-start | bytes 245768 | tf_op jit(solution)/shard_map/ppermute | solution.py:485
  78.5 5.8 %collective-permute-start.12 = (f32[5,16,256]{2,1,0:T(8,128)S(1)}, f32[5,16,256]{2,1,0:T(8,128)S(1)}, u32[]{:S(2)}, u32[]{:S(2)}) collective-permute-start(f32[5,16,256]{2,1,0:T(8,128)S(1)} %get-tuple-element.55), channel_id=1, source_target_pairs={{8,0},{16,8},{24,16},{9,1},{17,9},{25,17},{10,2},{18,10},{26,18},{... | collective-permute-start | bytes 245768 | tf_op jit(solution)/shard_map/ppermute | solution.py:485
  87.3 10.8 %collective-permute-start.13 = (f32[5,16,256]{2,1,0:T(8,128)S(1)}, f32[5,16,256]{2,1,0:T(8,128)S(1)}, u32[]{:S(2)}, u32[]{:S(2)}) collective-permute-start(f32[5,16,256]{2,1,0:T(8,128)S(1)} %get-tuple-element.61), channel_id=1, source_target_pairs={{0,1},{1,2},{2,3},{3,4},{4,5},{5,6},{6,7},{8,9},{9,10},{10,11},{11... | collective-permute-start | bytes 245768 | tf_op jit(solution)/shard_map/ppermute | solution.py:485
  91.8 6.3 %collective-permute-start.14 = (f32[5,16,256]{2,1,0:T(8,128)S(1)}, f32[5,16,256]{2,1,0:T(8,128)S(1)}, u32[]{:S(2)}, u32[]{:S(2)}) collective-permute-start(f32[5,16,256]{2,1,0:T(8,128)S(1)} %get-tuple-element.62), channel_id=1, source_target_pairs={{1,0},{2,1},{3,2},{4,3},{5,4},{6,5},{7,6},{9,8},{10,9},{11,10},{12... | collective-permute-start | bytes 245768 | tf_op jit(solution)/shard_map/ppermute | solution.py:485
  93.7 4.4 %collective-permute-start.15 = (f32[5,16,256]{2,1,0:T(8,128)S(1)}, f32[5,16,256]{2,1,0:T(8,128)S(1)}, u32[]{:S(2)}, u32[]{:S(2)}) collective-permute-start(f32[5,16,256]{2,1,0:T(8,128)S(1)} %get-tuple-element.63), channel_id=1, source_target_pairs={{0,8},{8,16},{16,24},{1,9},{9,17},{17,25},{2,10},{10,18},{18,26},{... | collective-permute-start | bytes 245768 | tf_op jit(solution)/shard_map/ppermute | solution.py:485
  95.9 5.8 %collective-permute-start.16 = (f32[5,16,256]{2,1,0:T(8,128)S(1)}, f32[5,16,256]{2,1,0:T(8,128)S(1)}, u32[]{:S(2)}, u32[]{:S(2)}) collective-permute-start(f32[5,16,256]{2,1,0:T(8,128)S(1)} %get-tuple-element.64), channel_id=1, source_target_pairs={{8,0},{16,8},{24,16},{9,1},{17,9},{25,17},{10,2},{18,10},{26,18},{... | collective-permute-start | bytes 245768 | tf_op jit(solution)/shard_map/ppermute | solution.py:485
